TPU v7x, 32 devices: a whole 2x2x4 slice. The times are simulated.
32 devices in a mesh: dp: 2 (over x), frame: 8 (over z, core), tile: 2 (over y).
Axes of the slice: x: 2, y: 2, z: 4, core: 2. Of those that a mesh axis runs over, the one named last changes fastest.
Arguments:
- clip_input: bfloat16 [2, 8, 18, 32, 640], P('dp', 'frame', 'tile'), may hold values from -36 to 36
- cotangent: bfloat16 [2, 8, 18, 32, 640], P('dp', 'frame', 'tile'), may hold values from -6 to 6
- norm_gain: float32 [640], replicated, may hold values from 0.25 to 1.75
- conv_weight: bfloat16 [9, 640, 640], P(None, ('frame', 'tile')), may hold values from -0.078125 to 0.078125
- attn_weight: bfloat16 [640, 2560], P(('frame', 'tile')), may hold values from -0.25 to 0.25
- query_gain: float32 [64], replicated, may hold values from 0.5 to 1.5
- key_gain: float32 [64], replicated, may hold values from 0.5 to 1.5
- logit_scale: float32 [10], replicated, may hold values from 0.5 to 4
Outputs:
- mid_grad: bfloat16 [2, 8, 18, 32, 640], P('dp', 'frame', 'tile')
- value_grad: float32 [640, 640], P(('frame', 'tile'))
- out_proj_grad: float32 [640, 640], P(('frame', 'tile'))
- query_gain_grad: float32 [64], replicated
- key_gain_grad: float32 [64], replicated
- scale_grad: float32 [10], replicated
All inputs are finite; a program needn't handle non-finite values.
Results may differ from a plain program's by a relative error of at most 0.013.
The roundings to bfloat16 on the way count: a program that leaves them out, or rounds other values in their place, can miss the bound.
Values may be sent and summed in bfloat16 or wider, within the bound.
No kernel may reach another device: no remote copies, remote signals or barrier semaphores. Data moves between devices by JAX's collectives and lax.ppermute only.
A program may use at most 128 MiB of HBM per device.

v0:
```python
import math

import jax
import jax.numpy as jnp
from jax import lax
from jax.sharding import PartitionSpec as P

GROUPS = 32


def extended(x, sides, width):
    for axis, dim in sides:
        devices, length = (lax.axis_size(axis), x.shape[dim])
        up = [(i, (i + 1) % devices) for i in range(devices - 1)]
        down = [(j, i) for i, j in up]
        last = lax.slice_in_dim(x, length - width, length, axis=dim)
        first = lax.slice_in_dim(x, 0, width, axis=dim)
        before = lax.ppermute(last, axis, up)
        after = lax.ppermute(first, axis, down)
        x = jnp.concatenate([before, x, after], axis=dim)
    return x


def layer_stats(vec):
    mean = jnp.mean(vec, axis=-1, keepdims=True)
    cent = vec - mean
    var = jnp.mean(cent * cent, axis=-1, keepdims=True)
    rstd = lax.rsqrt(var + 1e-05)
    return (cent * rstd, rstd)


def layer_back(dhat, hat, rstd):
    first = jnp.mean(dhat, axis=-1, keepdims=True)
    second = jnp.mean(dhat * hat, axis=-1, keepdims=True)
    return rstd * (dhat - first - hat * second)


def attention_pass(mid, cot, weights, query_gain, key_gain, logit_scale):
    frames, count, width = mid.shape
    heads = logit_scale.shape[0]
    depth = width // heads
    total = frames * count
    high = lax.Precision.HIGHEST
    f32 = jnp.float32
    flat = mid.reshape(total, width)
    w_inner = weights[:, : 3 * width]
    proj = jnp.dot(flat, w_inner, preferred_element_type=f32)
    query = proj[:, :width].reshape(frames, count, heads, depth)
    keyed = proj[:, width : 2 * width].reshape(frames, count, heads, depth)
    value = proj[:, 2 * width :].astype(jnp.bfloat16).reshape(frames, count, heads, depth)
    q_hat, q_rstd = layer_stats(query)
    k_hat, k_rstd = layer_stats(keyed)
    q_norm = q_hat * query_gain
    k_norm = k_hat * key_gain
    root = math.sqrt(depth)
    raw = jnp.einsum("fnhd,gnhd->nhfg", q_norm, k_norm, precision=high) / root
    scale = logit_scale[None, :, None, None]
    expo = jnp.exp(raw * scale)
    probs = expo / jnp.sum(expo, axis=-1, keepdims=True)
    probs_b = probs.astype(jnp.bfloat16)
    mixed = jnp.einsum("nhfg,gnhd->fnhd", probs_b, value, preferred_element_type=f32)
    mixed = mixed.astype(jnp.bfloat16).reshape(total, width)
    cot_flat = cot.reshape(total, width)
    w_out = weights[:, 3 * width :]
    d_mixed = lax.dot_general(cot_flat, w_out, (((1,), (1,)), ((), ())), preferred_element_type=f32)
    d_mixed = d_mixed.astype(jnp.bfloat16).reshape(frames, count, heads, depth)
    d_probs = jnp.einsum("fnhd,gnhd->nhfg", d_mixed, value, preferred_element_type=f32)
    d_value = jnp.einsum("nhfg,fnhd->gnhd", probs_b, d_mixed, preferred_element_type=f32)
    d_value = d_value.astype(jnp.bfloat16)
    d_logits = probs * (d_probs - jnp.sum(probs * d_probs, axis=-1, keepdims=True))
    scale_term = jnp.sum(d_logits * raw, axis=(0, 2, 3))
    d_raw = d_logits * scale / root
    d_qn = jnp.einsum("nhfg,gnhd->fnhd", d_raw, k_norm, precision=high)
    d_kn = jnp.einsum("nhfg,fnhd->gnhd", d_raw, q_norm, precision=high)
    qgain_term = jnp.sum(d_qn * q_hat, axis=(0, 1, 2))
    kgain_term = jnp.sum(d_kn * k_hat, axis=(0, 1, 2))
    d_query = layer_back(d_qn * query_gain, q_hat, q_rstd).astype(jnp.bfloat16)
    d_key = layer_back(d_kn * key_gain, k_hat, k_rstd).astype(jnp.bfloat16)
    d_cat = jnp.concatenate(
        [d_query.reshape(total, width), d_key.reshape(total, width), d_value.reshape(total, width)],
        axis=1,
    )
    d_mid = lax.dot_general(d_cat, w_inner, (((1,), (1,)), ((), ())), preferred_element_type=f32)
    d_mid = d_mid.astype(jnp.bfloat16).reshape(frames, count, width)
    return (d_mid, mixed, d_value.reshape(total, width), scale_term, qgain_term, kgain_term)


def local(
    clip_input, cotangent, norm_gain, conv_weight, attn_weight, query_gain, key_gain, logit_scale
):
    source = clip_input[0]
    cot = cotangent[0]
    frames_here, rows, cols, width = source.shape
    positions = rows * cols
    per_group = width // GROUPS
    cot_flat = cot.reshape(frames_here, positions, width)
    attn_full = lax.all_gather(attn_weight, ("frame", "tile"), axis=0, tiled=True)
    xf = source.astype(jnp.float32).reshape(frames_here, positions, GROUPS, per_group)
    sums, squares = lax.psum((jnp.sum(xf, axis=(1, 3)), jnp.sum(xf * xf, axis=(1, 3))), "tile")
    count = positions * lax.axis_size("tile") * per_group
    mean = sums / count
    rstd = lax.rsqrt(squares / count - mean * mean + 1e-05)
    normed = (xf - mean[:, None, :, None]) * rstd[:, None, :, None]
    zed = normed.reshape(frames_here, rows, cols, width) * norm_gain
    act = jax.nn.silu(zed).astype(jnp.bfloat16)
    padded = extended(act, (("tile", 1),), 1)
    padded = jnp.pad(padded, ((0, 0), (0, 0), (1, 1), (0, 0)))
    slabs = []
    for row_off in (-1, 0, 1):
        for col_off in (-1, 0, 1):
            slabs.append(
                padded[:, 1 + row_off : 1 + row_off + rows, 1 + col_off : 1 + col_off + cols, :]
            )
    stacked = jnp.stack(slabs, axis=3).reshape(frames_here * positions, 9, width)
    full_conv = lax.all_gather(conv_weight, ("frame", "tile"), axis=1, tiled=True)
    pre = jnp.dot(
        stacked.reshape(frames_here * positions, 9 * width),
        full_conv.reshape(9 * width, width),
        preferred_element_type=jnp.float32,
    )
    mid = (source.astype(jnp.float32) + pre.reshape(frames_here, rows, cols, width)).astype(
        jnp.bfloat16
    )
    mid_flat = mid.reshape(frames_here, positions, width)
    mid_tiled, cot_tiled = (
        lax.all_to_all(mid_flat, "frame", split_axis=1, concat_axis=0, tiled=True),
        lax.all_to_all(cot_flat, "frame", split_axis=1, concat_axis=0, tiled=True),
    )
    d_mid, mixed, d_value, scale_term, qgain_term, kgain_term = attention_pass(
        mid_tiled, cot_tiled, attn_full, query_gain, key_gain, logit_scale
    )
    d_back = lax.all_to_all(d_mid, "frame", split_axis=0, concat_axis=1, tiled=True)
    mid_grad = (
        cot.astype(jnp.float32) + d_back.reshape(frames_here, rows, cols, width).astype(jnp.float32)
    ).astype(jnp.bfloat16)
    tiled_mid = mid_tiled.reshape(-1, width)
    tiled_cot = cot_tiled.reshape(-1, width)
    contract = (((0,), (0,)), ((), ()))
    value_term = lax.dot_general(tiled_mid, d_value, contract, preferred_element_type=jnp.float32)
    out_term = lax.dot_general(mixed, tiled_cot, contract, preferred_element_type=jnp.float32)
    shares = lax.psum_scatter(
        jnp.concatenate([value_term, out_term], axis=1),
        ("frame", "tile"),
        scatter_dimension=0,
        tiled=True,
    )
    summed = lax.psum(shares.astype(jnp.bfloat16), "dp").astype(jnp.float32)
    scale_sum, qgain_sum, kgain_sum = lax.psum(
        (scale_term, qgain_term, kgain_term), ("dp", "frame", "tile")
    )
    tokens_all = lax.axis_size("dp") * mid_tiled.shape[0] * rows * lax.axis_size("tile") * cols
    factor = 1.0 / math.sqrt(tokens_all)
    value_grad = summed[:, :width] * factor
    out_proj_grad = summed[:, width:] * factor
    return (
        mid_grad[None],
        value_grad,
        out_proj_grad,
        qgain_sum * factor,
        kgain_sum * factor,
        scale_sum * factor,
    )


def solution(mesh):
    in_specs = (
        P("dp", "frame", "tile", None, None),
        P("dp", "frame", "tile", None, None),
        P(),
        P(None, ("frame", "tile"), None),
        P(("frame", "tile"), None),
        P(),
        P(),
        P(),
    )
    out_specs = (
        P("dp", "frame", "tile", None, None),
        P(("frame", "tile"), None),
        P(("frame", "tile"), None),
        P(),
        P(),
        P(),
    )
    return jax.shard_map(local, mesh=mesh, in_specs=in_specs, out_specs=out_specs, check_vma=False)
```

profile of v0, /device:TPU:0, one launch (start us, length us, event | category | flops | bytes accessed | tf_op | source)
XLA Modules:
  0.0 317.7 jit_solution(850922302177832545)
XLA Ops:
  10.2 5.9 %all-reduce.2 = (f32[1,32]{1,0:T(1,128)S(1)}, f32[1,32]{1,0:T(1,128)S(1)}) all-reduce(f32[1,32]{1,0:T(1,128)S(1)} %bitcast.150, f32[1,32]{1,0:T(1,128)S(1)} %bitcast.151), channel_id=1, replica_groups=mesh['dp'=2,'frame'=8,'tile'=2] {'tile'}, use_global_device_ids=true, to_apply=%region_5.6 | all-reduce | flops 64 | bytes 512 | tf_op jit(solution)/shard_map/psum | solution.py:99
  19.0 4.5 %collective-permute-start = (bf16[1,1,32,640]{3,2,1,0:T(8,128)(2,1)S(1)}, bf16[1,1,32,640]{3,2,1,0:T(8,128)(2,1)S(1)}, u32[]{:S(2)}, u32[]{:S(2)}) collective-permute-start(bf16[1,1,32,640]{3,2,1,0:T(8,128)(2,1)S(1)} %get-tuple-element.63), channel_id=1, source_target_pairs={{0,1},{2,3},{4,5},{6,7},{8,9},{10,11},{12,13},{14,15},{16,17},{18,... | collective-permute-start | bytes 122888 | tf_op jit(solution)/shard_map/ppermute | solution.py:18
  24.7 3.0 reduce.8
  28.4 5.9 %all-to-all-start.1 = ((bf16[8,2,11520]{2,1,0:T(2,128)(2,1)}), bf16[8,2,11520]{2,1,0:T(2,128)(2,1)S(1)}, u32[]{:S(2)}, u32[]{:S(2)}) async-start(bf16[8,2,11520]{2,1,0:T(2,128)(2,1)} %reshape.270), calls=%async_computation.1 | async-start | bytes 737280 | tf_op jit(solution)/shard_map/all_to_all | solution.py:127
  36.2 4.2 %copy.120 = bf16[1,9,32,9,640]{4,3,2,1,0:T(8,128)(2,1)} copy(bf16[1,9,32,9,640]{4,2,1,3,0:T(8,128)(2,1)S(1)} %fusion.80) | data formatting | bytes 6635520 | tf_op jit(solution)/shard_map/stack | solution.py:114
  40.4 7.3 %dot_general.38 = bf16[9,32,5760]{2,1,0:T(8,128)(2,1)} reshape(bf16[1,9,32,9,640]{4,3,2,1,0:T(8,128)(2,1)} %copy.120) | data formatting | bytes 6635520 | tf_op jit(solution)/shard_map/dot_general | solution.py:116
  47.8 38.3 %all-gather.3.cloned.1.call-done = bf16[9,640,640]{2,1,0:T(8,128)(2,1)} async-done(((bf16[9,40,640]{2,1,0:T(8,128)(2,1)}), bf16[9,640,640]{2,1,0:T(8,128)(2,1)}) %all-gather.3.cloned.1.call-update) | async-done | bytes 7372816 | tf_op jit(solution)/shard_map/all_gather | solution.py:115
  86.1 6.9 %fusion.26 = bf16[9,32,640]{2,1,0:T(8,128)(2,1)S(1)} fusion(bf16[9,32,5760]{2,1,0:T(8,128)(2,1)} %dot_general.38, bf16[5760,640,1]{1,0,2:T(8,128)(2,1)} %bitcast.152, bf16[1,1,9,32,640]{4,3,2,1,0:T(8,128)(2,1)S(1)} %copy-done.3), kind=kOutput, calls=%fused_computation.51 | convolution fusion | flops 2123919360 | bytes 11427840 | tf_op jit(solution)/shard_map/dot_general | solution.py:116
  93.6 2.9 reduce.9
  97.3 3.4 %all-to-all-start = ((bf16[8,2,11520]{2,1,0:T(2,128)(2,1)}), bf16[8,2,11520]{2,1,0:T(2,128)(2,1)S(1)}, u32[]{:S(2)}, u32[]{:S(2)}) async-start(bf16[8,2,11520]{2,1,0:T(2,128)(2,1)} %reshape.272), calls=%async_computation | async-start | bytes 737280 | tf_op jit(solution)/shard_map/all_to_all | solution.py:126
  101.3 36.2 %all-gather.5.cloned.1.call-done = bf16[640,2560]{1,0:T(8,128)(2,1)} async-done(((bf16[40,2560]{1,0:T(8,128)(2,1)}), bf16[640,2560]{1,0:T(8,128)(2,1)}) %all-gather.5.cloned.1.call-update) | async-done | bytes 3276816 | tf_op jit(solution)/shard_map/all_gather | solution.py:97
  150.1 2.8 reshape.253
  152.9 3.0 reduce_sum.161
  158.0 6.4 %multiply_reduce_fusion.4 = (f32[8,36,10]{0,2,1:T(8,128)}, f32[8,36,10,64]{3,0,2,1:T(8,128)}, f32[8,36,10]{0,2,1:T(8,128)}, f32[8,36,10,64]{3,0,2,1:T(8,128)}) fusion(f32[8,36,10]{0,2,1:T(8,128)} %copy.128, f32[8,36,10,64]{3,2,1,0:T(8,128)S(1)} %reshape.254, f32[8,36,10]{0,2,1:T(8,128)} %copy.123, f32[8,36,10,64]{3,2,1,0:T(8,128)} %reshape.253), kind=kLoop, calls=%fused_computation.31 | loop fusion | flops 1100160 | bytes 2995200 | tf_op jit(solution)/shard_map/reduce_sum | solution.py:27
  167.3 6.1 %fusion.18 = (f32[36,10,8]{2,1,0:T(8,128)S(1)}, f32[36,10,8,8]{2,3,1,0:T(8,128)S(1)}) fusion(f32[10]{0:T(128)S(1)} %broadcast_multiply_fusion.9, f32[8,36,10,64]{3,0,2,1:T(8,128)} %get-tuple-element.58, f32[64]{0:T(128)S(1)} %copy-done.21, f32[8,36,10]{0,2,1:T(8,128)S(1)} %copy.131, f32[8,36,10,64]{3,0,2,1:T(8,128)S(1)} %copy-done, f32[64]{0:T(128)S(1)} %copy-done.22, ...), kind=kOutput, calls=%fused_computation.43 | convolution fusion | flops 18475200 | bytes 1601832 | tf_op jit(solution)/shard_map/fnhd,gnhd->nhfg/dot_general | solution.py:56
  182.2 3.0 copy.155
  191.0 5.5 %fusion.5 = (f32[64]{0:T(128)}, f32[8,36,10]{0,2,1:T(8,128)}, f32[8,36,10]{0,2,1:T(8,128)}, f32[36,10,64,8]{2,3,1,0:T(8,128)}) fusion(f32[8,36,10,64]{3,0,2,1:T(8,128)S(1)} %copy-done.2, f32[8,36,10]{0,2,1:T(8,128)S(1)} %copy-done.18, f32[64]{0:T(128)S(1)} %copy-done.21, f32[36,10,8,8]{2,3,1,0:T(8,128)S(1)} %get-tuple-element.72, f32[10]{0:T(128)S(1)} %copy-done.23, ...), kind=kOutput, calls=%fused_computation.10 | convolution fusion | flops 19393856 | bytes 2350888 | tf_op jit(solution)/shard_map/nhfg,fnhd->gnhd/dot_general | solution.py:74
  206.1 3.1 multiply_convert_fusion
  210.5 2.8 reshape.259
  213.2 7.3 %fusion.6 = (f32[64]{0:T(128)}, f32[8,36,10]{0,2,1:T(8,128)}, f32[8,36,10]{0,2,1:T(8,128)}, f32[36,10,64,8]{2,3,1,0:T(8,128)}) fusion(f32[8,36,10,64]{3,0,2,1:T(8,128)S(1)} %copy-done.1, f32[8,36,10]{0,2,1:T(8,128)S(1)} %copy-done.16, f32[64]{0:T(128)S(1)} %copy-done.22, f32[36,10,8,8]{2,3,1,0:T(8,128)} %copy-done.28, f32[10]{0:T(128)S(1)} %copy-done.23, ...), kind=kOutput, calls=%fused_computation.13 | convolution fusion | flops 19393856 | bytes 2350888 | tf_op jit(solution)/shard_map/nhfg,gnhd->fnhd/dot_general | solution.py:73
  232.1 2.8 fusion.23
  235.7 4.0 %all-to-all-start.2 = ((bf16[8,36,640]{2,1,0:T(8,128)(2,1)}), bf16[8,36,640]{2,1,0:T(8,128)(2,1)S(1)}, u32[]{:S(2)}, u32[]{:S(2)}) async-start(bf16[8,36,640]{2,1,0:T(8,128)(2,1)} %reshape.261), calls=%async_computation.2 | async-start | bytes 819200 | tf_op jit(solution)/shard_map/all_to_all | solution.py:132
  239.8 39.9 %all-reduce.1 = (f32[64]{0:T(128)S(1)}, f32[64]{0:T(128)S(1)}, f32[10]{0:T(128)S(1)}) all-reduce(f32[64]{0:T(128)S(1)} %copy-done.25, f32[64]{0:T(128)S(1)} %copy-done.24, f32[10]{0:T(128)S(1)} %get-tuple-element.71), channel_id=1, replica_groups=mesh['dp'=2,'frame'=8,'tile'=2] {'dp','frame','tile'}, use_global_device_ids=true, to_apply=%region_19.20 | all-reduce | flops 138 | bytes 1104 | tf_op jit(solution)/shard_map/psum | solution.py:148
  284.0 24.2 %all-reduce.5.cloned.1.call-done = bf16[40,1280]{0,1:T(8,128)(2,1)} async-done(((bf16[40,1280]{0,1:T(8,128)(2,1)}), bf16[40,1280]{0,1:T(8,128)(2,1)}) %all-reduce.5.cloned.1.call-update) | async-done | bytes 102416 | tf_op jit(solution)/shard_map/psum | solution.py:147
  (171 shorter events, 73.5 us)
Async XLA Ops:
  7.2 16.4 %copy-start.13 = (bf16[1,1,9,32,640]{4,3,2,1,0:T(8,128)(2,1)S(1)}, bf16[1,1,9,32,640]{4,3,2,1,0:T(8,128)(2,1)}, u32[]{:S(2)}) copy-start(bf16[1,1,9,32,640]{4,3,2,1,0:T(8,128)(2,1)} %param.9) | copy-start | bytes 1105924
  7.2 78.9 %all-gather.3.cloned.1.call-start = ((), (), s32[]{:S(2)}) async-start(), calls=%async_computation.4 | async-start | bytes 7833600 | tf_op jit(solution)/shard_map/all_gather | solution.py:115
  7.9 129.6 %all-gather.5.cloned.1.call-start = ((), (), s32[]{:S(2)}) async-start(), calls=%async_computation.5 | async-start | bytes 3481600 | tf_op jit(solution)/shard_map/all_gather | solution.py:97
  17.7 16.7 %collective-permute-start.1 = (bf16[1,1,32,640]{3,2,1,0:T(8,128)(2,1)S(1)}, bf16[1,1,32,640]{3,2,1,0:T(8,128)(2,1)S(1)}, u32[]{:S(2)}, u32[]{:S(2)}) collective-permute-start(bf16[1,1,32,640]{3,2,1,0:T(8,128)(2,1)S(1)} %get-tuple-element.64), channel_id=1, source_target_pairs={{1,0},{3,2},{5,4},{7,6},{9,8},{11,10},{13,12},{15,14},{17,16},{19,... | collective-permute-start | bytes 122888 | tf_op jit(solution)/shard_map/ppermute | solution.py:19
  19.0 15.4 %collective-permute-start = (bf16[1,1,32,640]{3,2,1,0:T(8,128)(2,1)S(1)}, bf16[1,1,32,640]{3,2,1,0:T(8,128)(2,1)S(1)}, u32[]{:S(2)}, u32[]{:S(2)}) collective-permute-start(bf16[1,1,32,640]{3,2,1,0:T(8,128)(2,1)S(1)} %get-tuple-element.63), channel_id=1, source_target_pairs={{0,1},{2,3},{4,5},{6,7},{8,9},{10,11},{12,13},{14,15},{16,17},{18,... | collective-permute-start | bytes 122888 | tf_op jit(solution)/shard_map/ppermute | solution.py:18
  28.4 68.8 %all-to-all-start.1 = ((bf16[8,2,11520]{2,1,0:T(2,128)(2,1)}), bf16[8,2,11520]{2,1,0:T(2,128)(2,1)S(1)}, u32[]{:S(2)}, u32[]{:S(2)}) async-start(bf16[8,2,11520]{2,1,0:T(2,128)(2,1)} %reshape.270), calls=%async_computation.1 | async-start | bytes 737280 | tf_op jit(solution)/shard_map/all_to_all | solution.py:127
  93.6 7.4 %copy-start.23 = (f32[10]{0:T(128)S(1)}, f32[10]{0:T(128)}, u32[]{:S(2)}) copy-start(f32[10]{0:T(128)} %param.15) | copy-start | bytes 124
  97.3 43.7 %all-to-all-start = ((bf16[8,2,11520]{2,1,0:T(2,128)(2,1)}), bf16[8,2,11520]{2,1,0:T(2,128)(2,1)S(1)}, u32[]{:S(2)}, u32[]{:S(2)}) async-start(bf16[8,2,11520]{2,1,0:T(2,128)(2,1)} %reshape.272), calls=%async_computation | async-start | bytes 737280 | tf_op jit(solution)/shard_map/all_to_all | solution.py:126
  100.7 180.6 %reduce-scatter.4.cloned.1.call-start = ((), (), s32[]{:S(2)}) async-start(), calls=%async_computation.7 | async-start | bytes 3481600
  101.0 75.2 %copy-start.26 = (f32[10]{0:T(128)}, f32[10]{0:T(128)S(1)}, u32[]{:S(2)}) copy-start(f32[10]{0:T(128)S(1)} %broadcast_multiply_fusion.9) | copy-start | bytes 124
  101.3 39.6 %copy-start.8 = (bf16[288,1,640]{2,1,0:T(2,128)(2,1)}, bf16[288,1,640]{2,1,0:T(2,128)(2,1)S(1)}, u32[]{:S(2)}) copy-start(bf16[288,1,640]{2,1,0:T(2,128)(2,1)S(1)} %reshape.271) | copy-start | bytes 1105924
  164.4 2.9 copy-start.21
  164.4 2.9 copy-start.22
  165.8 7.6 %copy-start.17 = (f32[8,36,10]{0,2,1:T(8,128)}, f32[8,36,10]{0,2,1:T(8,128)S(1)}, u32[]{:S(2)}) copy-start(f32[8,36,10]{0,2,1:T(8,128)S(1)} %copy.131) | copy-start | bytes 34564
  167.3 6.2 %copy-start.15 = (f32[8,36,10]{0,2,1:T(8,128)}, f32[8,36,10]{0,2,1:T(8,128)S(1)}, u32[]{:S(2)}) copy-start(f32[8,36,10]{0,2,1:T(8,128)S(1)} %copy.126) | copy-start | bytes 34564
  167.3 6.2 %copy-start.4 = (bf16[8,36,10,64]{3,2,1,0:T(8,128)(2,1)S(1)}, bf16[8,36,10,64]{3,2,1,0:T(8,128)(2,1)}, u32[]{:S(2)}) copy-start(bf16[8,36,10,64]{3,2,1,0:T(8,128)(2,1)} %reshape.256) | copy-start | bytes 1105924
  175.5 5.8 %copy-start.10 = (bf16[288,640]{1,0:T(8,128)(2,1)}, bf16[288,640]{1,0:T(8,128)(2,1)S(1)}, u32[]{:S(2)}) copy-start(bf16[288,640]{1,0:T(8,128)(2,1)S(1)} %reshape.260) | copy-start | bytes 1105924
  190.9 5.5 %copy-start.28 = (f32[36,10,8,8]{2,3,1,0:T(8,128)}, f32[36,10,8,8]{2,3,1,0:T(8,128)S(1)}, u32[]{:S(2)}) copy-start(f32[36,10,8,8]{2,3,1,0:T(8,128)S(1)} %get-tuple-element.72) | copy-start | bytes 276484
  220.6 7.7 %copy-start.12 = (f32[36,10,64,8]{2,3,1,0:T(8,128)S(1)}, f32[36,10,64,8]{2,3,1,0:T(8,128)}, u32[]{:S(2)}) copy-start(f32[36,10,64,8]{2,3,1,0:T(8,128)} %get-tuple-element.70) | copy-start | bytes 2211844
  234.9 4.9 %copy-start.24 = (f32[64]{0:T(128)S(1)}, f32[64]{0:T(128)}, u32[]{:S(2)}) copy-start(f32[64]{0:T(128)} %get-tuple-element.42) | copy-start | bytes 772
  234.9 4.9 %copy-start.25 = (f32[64]{0:T(128)S(1)}, f32[64]{0:T(128)}, u32[]{:S(2)}) copy-start(f32[64]{0:T(128)} %get-tuple-element.44) | copy-start | bytes 772
  235.7 47.4 %copy-start.14 = (bf16[1,1,9,32,640]{4,3,2,1,0:T(8,128)(2,1)S(1)}, bf16[1,1,9,32,640]{4,3,2,1,0:T(8,128)(2,1)}, u32[]{:S(2)}) copy-start(bf16[1,1,9,32,640]{4,3,2,1,0:T(8,128)(2,1)} %param.9) | copy-start | bytes 1105924
  235.7 45.5 %all-to-all-start.2 = ((bf16[8,36,640]{2,1,0:T(8,128)(2,1)}), bf16[8,36,640]{2,1,0:T(8,128)(2,1)S(1)}, u32[]{:S(2)}, u32[]{:S(2)}) async-start(bf16[8,36,640]{2,1,0:T(8,128)(2,1)} %reshape.261), calls=%async_computation.2 | async-start | bytes 819200 | tf_op jit(solution)/shard_map/all_to_all | solution.py:132
  239.7 68.5 %all-reduce.5.cloned.1.call-start = ((), (), s32[]{:S(2)}) async-start(), calls=%async_computation.6 | async-start | bytes 655360 | tf_op jit(solution)/shard_map/psum | solution.py:147
  (19 other events, 31.4 us)
Sparse Core Ops, SparseCore 0:
  10.3 75.7 all-gather.2
  88.4 49.0 all-gather.4
  185.3 68.5 reduce-scatter.3
  283.3 24.9 all-reduce.4
where the time goes:
time: 324 us; the launch traced here: 318 us
  waiting for transfers between devices  100 us (31%)
  local copies, waits for them, and re-layouts  62.3 us (19%)
  blocking collectives  45.8 us (14%)
  matrix products  38.4 us (12%)
  other arithmetic  36.8 us (11%)
  starting transfers between devices  19.5 us (6%)
  between operations  14.7 us (5%)
    psum x1, blocking collectives, local(): lax.psum((scale_term, qgain_term, kgain_term), ('dp', 'frame', 'tile'))  39.9 us
    all_gather x1, waiting for transfers between devices, local(): lax.all_gather(conv_weight, ('frame', 'tile'), axis=1, tiled=True)  38.3 us
    all_gather x1, waiting for transfers between devices, local(): lax.all_gather(attn_weight, ('frame', 'tile'), axis=0, tiled=True)  36.2 us
    psum x1, waiting for transfers between devices, local(): summed = lax.psum(shares.astype(jnp.bfloat16), 'dp').astype(jnp.float32)  24.2 us
    unnamed x82, local copies, waits for them, and re-layouts  14.4 us
    dot_general x1, matrix products, attention_pass(): d_qn = jnp.einsum('nhfg,gnhd->fnhd', d_raw, k_norm, precision=high)  7.35 us
    dot_general x1, local copies, waits for them, and re-layouts, local(): jnp.dot(stacked.reshape(frames_here * positions, 9 * width), full_conv.re...  7.33 us
    dot_general x1, matrix products, local(): jnp.dot(stacked.reshape(frames_here * positions, 9 * width), full_conv.re...  6.87 us
  transfers between devices with their start and end apart: 9, of which 3 were waited for; matrix products, arithmetic and copies ran while one was open for 27% of the time, Pallas kernels for 0%

commit v1 on v0

v1 whole, which is shorter than its diff:
```python
import functools
import math

import jax
import jax.numpy as jnp
from jax import lax
from jax.experimental import pallas as pl
from jax.experimental.pallas import tpu as pltpu
from jax.sharding import PartitionSpec as P

GROUPS = 32
EPS = 1e-05
SLOT = 16
BF = jnp.bfloat16
F32 = jnp.float32
VMEM_BYTES = 48 * 1024 * 1024


def swap(x, axis):
    return lax.ppermute(x, axis, [(i, i ^ 1) for i in range(lax.axis_size(axis))])


def round_up(value, unit):
    return -(-value // unit) * unit


def dot(a, b):
    return lax.dot_general(a, b, (((1,), (0,)), ((), ())), preferred_element_type=F32)


def dot_t(a, b):
    return lax.dot_general(a, b, (((1,), (1,)), ((), ())), preferred_element_type=F32)


def dot_rows(a, b):
    return lax.dot_general(a, b, (((0,), (0,)), ((), ())), preferred_element_type=F32)


def halves(x):
    high = x.astype(BF)
    return high, (x - high.astype(F32)).astype(BF)


def picker(rows, cols, depth, offset):
    row = lax.broadcasted_iota(jnp.int32, (rows, cols), 0)
    col = lax.broadcasted_iota(jnp.int32, (rows, cols), 1)
    return (col - row // depth == offset).astype(F32).astype(BF)


def spreader(rows, cols, depth, offset):
    row = lax.broadcasted_iota(jnp.int32, (rows, cols), 0)
    col = lax.broadcasted_iota(jnp.int32, (rows, cols), 1)
    return (row - col // depth == offset).astype(F32).astype(BF)


def head_sums(x, pick):
    high, low = halves(x)
    return dot(high, pick) + dot(low, pick)


def spread(x, both):
    high, low = halves(x)
    return dot(jnp.concatenate([high, low], axis=1), both)


def conv_kernel(place, mine, other, weights, out, padded, *, rows, cols, part, blocks, count):
    x, core, tile = (place[0], place[1], place[2])
    whole = 2 * rows * cols
    half = rows * cols
    col = lax.broadcasted_iota(jnp.int32, (whole, part), 0) % cols
    zero = jnp.zeros((cols, padded.shape[1]), BF)
    padded[pl.ds(0, cols), :] = zero
    padded[pl.ds(cols + whole, cols), :] = zero
    for dc, source in ((0, mine), (1, other)):
        for dx in (0, 1):
            first, second = source[dx], source[2 + dx]
            padded[pl.ds(cols, half), :] = jnp.where(tile == 0, first, second)
            padded[pl.ds(cols + half, half), :] = jnp.where(tile == 0, second, first)
            taps = dot(padded[pl.ds(0, whole), :], weights[0])
            taps += dot(padded[pl.ds(cols, whole), :], weights[1])
            taps += dot(padded[pl.ds(2 * cols, whole), :], weights[2])
            left = pltpu.roll(taps[:, :part], 1, 0)
            right = pltpu.roll(taps[:, 2 * part :], whole - 1, 0)
            pre = taps[:, part : 2 * part] + jnp.where(col > 0, left, 0.0)
            pre = (pre + jnp.where(col < cols - 1, right, 0.0)).astype(BF)
            for t in (0, 1):
                for f in range(blocks):
                    start = t * half + f * count
                    out[x ^ dx, f, t, core ^ dc] = pre[start : start + count]


def attend_kernel(
    place, pre, pair, weights, qgain, kgain, scale,
    grads, sums, d_raw, q_hat, k_hat, q_rstd, k_rstd, d_value,
    mid_s, cot_s, doubled_k, doubled_v, doubled_acc,
    *, heads, count, padded,
):
    frames = pair.shape[0]
    width = pair.shape[-1]
    depth = width // heads
    total = frames * padded
    lanes = scale.shape[-1]
    me = place[0]
    mid_s[...] = jnp.zeros_like(mid_s)
    cot_s[...] = jnp.zeros_like(cot_s)
    for z in range(frames // 2):
        for e in (0, 1):
            f = 2 * z + e
            parts = [
                pre[x, z, c, t, e].astype(F32) for x in (0, 1) for c in (0, 1) for t in (0, 1)
            ]
            whole = jnp.concatenate(parts, axis=1)
            mid_s[pl.ds(f * padded, count), :] = pair[f, 0].astype(F32) + whole
            cot_s[pl.ds(f * padded, count), :] = pair[f, 1].astype(F32)
    mid = mid_s[...].astype(BF)
    cot = cot_s[...].astype(BF)
    pick = picker(width, lanes, depth, 0)
    both = jnp.concatenate([spreader(lanes, width, depth, 0)] * 2, axis=0)

    def stats(vec):
        cent = vec - spread(head_sums(vec, pick) / depth, both)
        var = head_sums(cent * cent, pick) / depth
        rstd = lax.rsqrt(var + EPS)
        return cent * spread(rstd, both), rstd

    hat, rstd = stats(dot(mid, weights[0 ^ me]))
    q_hat[...] = hat
    q_rstd[...] = rstd
    q_norm = hat * qgain[...]
    hat, rstd = stats(dot(mid, weights[1 ^ me]))
    k_hat[...] = hat
    k_rstd[...] = rstd
    hat = hat * kgain[...]
    doubled_k[pl.ds(0, total), :] = hat
    doubled_k[pl.ds(total, total), :] = hat
    value = dot(mid, weights[2 ^ me]).astype(BF).astype(F32)
    doubled_v[pl.ds(0, total), :] = value
    doubled_v[pl.ds(total, total), :] = value
    d_mixed = dot_t(cot, weights[3 ^ me]).astype(BF).astype(F32)

    raw = jnp.zeros((total, lanes), F32)
    d_probs = jnp.zeros((total, lanes), F32)
    for s in range(frames):
        here = picker(width, lanes, depth, SLOT * s)
        raw += head_sums(q_norm * doubled_k[pl.ds(s * padded, total), :], here)
        d_probs += head_sums(d_mixed * doubled_v[pl.ds(s * padded, total), :], here)
    raw = raw / math.sqrt(depth)

    def over_frames(x):
        step = SLOT
        while step < lanes:
            x = x + pltpu.roll(x, step, 1)
            step *= 2
        return x

    expo = jnp.exp(raw * scale[...])
    probs = expo / over_frames(expo)
    probs_b = probs.astype(BF)
    d_logits = probs * (d_probs - over_frames(probs * d_probs))
    sums[...] = jnp.sum(d_logits * raw, axis=0, keepdims=True)
    d_raw[...] = d_logits * scale[...] / math.sqrt(depth)

    mixed = jnp.zeros((total, width), F32)
    doubled_acc[...] = jnp.zeros_like(doubled_acc)
    for s in range(frames):
        weight = dot(probs_b, spreader(lanes, width, depth, SLOT * s))
        mixed += weight * doubled_v[pl.ds(s * padded, total), :]
        doubled_acc[pl.ds(s * padded, total), :] += weight * d_mixed
    mixed = mixed.astype(BF)
    dv = (doubled_acc[pl.ds(0, total), :] + doubled_acc[pl.ds(total, total), :]).astype(BF)
    d_value[...] = dv
    v_term = dot_rows(mid, dv).astype(BF)
    o_term = dot_rows(mixed, cot).astype(BF)
    core = place[1]
    rows = grads.shape[2]
    for z in range(frames // 2):
        for c in (0, 1):
            start = (2 * z + c) * rows
            grads[core ^ c, z, :, pl.ds(0, width)] = v_term[start : start + rows]
            grads[core ^ c, z, :, pl.ds(width, width)] = o_term[start : start + rows]


def back_kernel(
    place, d_raw, q_hat, k_hat, q_rstd, k_rstd, d_value, weights, qgain, kgain,
    d_mid, sums, doubled_k, doubled_acc,
    *, heads, padded,
):
    total, width = q_hat.shape
    depth = width // heads
    frames = total // padded
    lanes = d_raw.shape[-1]
    me = place[0]
    pick = picker(width, lanes, depth, 0)
    both = jnp.concatenate([spreader(lanes, width, depth, 0)] * 2, axis=0)
    k_norm = k_hat[...] * kgain[...]
    doubled_k[pl.ds(0, total), :] = k_norm
    doubled_k[pl.ds(total, total), :] = k_norm
    q_norm = q_hat[...] * qgain[...]
    doubled_acc[...] = jnp.zeros_like(doubled_acc)
    high, low = halves(d_raw[...])
    pair = jnp.concatenate([high, low], axis=1)
    d_qn = jnp.zeros((total, width), F32)
    for s in range(frames):
        one = spreader(lanes, width, depth, SLOT * s)
        weight = dot(pair, jnp.concatenate([one, one], axis=0))
        d_qn += weight * doubled_k[pl.ds(s * padded, total), :]
        doubled_acc[pl.ds(s * padded, total), :] += weight * q_norm
    d_kn = doubled_acc[pl.ds(0, total), :] + doubled_acc[pl.ds(total, total), :]

    def back(dhat, hat, rstd):
        first = spread(head_sums(dhat, pick) / depth, both)
        second = spread(head_sums(dhat * hat, pick) / depth, both)
        return (spread(rstd, both) * (dhat - first - hat * second)).astype(BF)

    sums[pl.ds(0, 1), :] = jnp.sum(d_qn * q_hat[...], axis=0, keepdims=True)
    sums[pl.ds(1, 1), :] = jnp.sum(d_kn * k_hat[...], axis=0, keepdims=True)
    d_query = back(d_qn * qgain[...], q_hat[...], q_rstd[...])
    d_key = back(d_kn * kgain[...], k_hat[...], k_rstd[...])
    out = dot_t(d_query, weights[0 ^ me]) + dot_t(d_key, weights[1 ^ me])
    out += dot_t(d_value[...], weights[2 ^ me])
    for f in range(frames):
        d_mid[f] = out[f * padded : (f + 1) * padded].astype(BF)


def specs(number):
    smem = pl.BlockSpec(memory_space=pltpu.SMEM)
    return [smem] + [pl.BlockSpec(memory_space=pltpu.VMEM)] * (number - 1)


def call(kernel, outs, scratch, *args):
    return pl.pallas_call(
        kernel,
        out_shape=[jax.ShapeDtypeStruct(shape, dtype) for shape, dtype in outs],
        in_specs=specs(len(args)),
        out_specs=[pl.BlockSpec(memory_space=pltpu.VMEM)] * len(outs),
        scratch_shapes=[pltpu.VMEM(shape, dtype) for shape, dtype in scratch],
        compiler_params=pltpu.CompilerParams(vmem_limit_bytes=VMEM_BYTES),
    )(*args)


def local(
    clip_input, cotangent, norm_gain, conv_weight, attn_weight, query_gain, key_gain, logit_scale
):
    source = clip_input[0, 0]
    cot = cotangent[0, 0]
    rows, cols, width = source.shape
    heads = logit_scale.shape[0]
    depth = width // heads
    tokens = rows * cols
    clips, frames, tiles = (lax.axis_size(name) for name in ("dp", "frame", "tile"))
    square = ("frame", "tile")
    ranks = frames * tiles
    share = conv_weight.shape[1]
    count = tokens // frames
    part = width // 8
    x = lax.axis_index("dp") % 2
    core = lax.axis_index("frame") % 2
    tile = lax.axis_index("tile")

    mine = lax.dynamic_slice_in_dim(conv_weight, x * (width // 2), width // 2, axis=2)
    mine = mine.reshape(3, 3, share, 4, part).transpose(3, 0, 2, 1, 4)
    mine = mine.reshape(4, 3, share, 3 * part)
    spread_out = jnp.broadcast_to(mine[None], (frames // 2,) + mine.shape)
    conv_in = lax.all_to_all(spread_out.reshape((ranks,) + mine.shape[1:]), square, 0, 0, tiled=True)
    conv_full = conv_in.transpose(1, 0, 2, 3).reshape(3, width, 3 * part)

    flat = source.reshape(tokens, width)
    xf = flat.astype(F32)
    sums = jnp.stack([jnp.sum(xf, axis=0), jnp.sum(xf * xf, axis=0)])
    sums = (sums + swap(sums, "tile")).reshape(2, GROUPS, width // GROUPS).sum(axis=-1)
    size = tokens * tiles * (width // GROUPS)
    mean = sums[0] / size
    rstd = lax.rsqrt(sums[1] / size - mean * mean + EPS)
    mean = jnp.repeat(mean, width // GROUPS)
    rstd = jnp.repeat(rstd, width // GROUPS)
    act = jax.nn.silu((xf - mean) * rstd * norm_gain).astype(BF)

    act = jnp.stack([act, swap(act, "dp")])
    act = jnp.concatenate([act, swap(act, "tile")])
    act_other = swap(act, "frame")

    pair = jnp.stack([flat.reshape(frames, count, width), cot.reshape(frames, count, width)], axis=1)
    pair = lax.all_to_all(pair, "frame", 0, 0, tiled=True)

    kinds = attn_weight.reshape(share, 4, width).transpose(1, 0, 2)
    kinds = jnp.broadcast_to(kinds[None], (frames // 2,) + kinds.shape).reshape(ranks, share, width)
    own = lax.all_to_all(kinds, square, 0, 0, tiled=True).reshape(1, width, width)
    own = jnp.concatenate([own, swap(own, "tile")])
    attn = jnp.concatenate([own, swap(own, "frame")])

    place = jnp.stack([x, core, tile]).astype(jnp.int32)
    (pre,) = call(
        functools.partial(
            conv_kernel, rows=rows, cols=cols, part=part, blocks=frames, count=count
        ),
        [((2, frames, tiles, 2, count, part), BF)],
        [((tiles * tokens + 2 * cols, width), BF)],
        place,
        act,
        act_other,
        conv_full,
    )
    groups = None
    if clips > 2:
        groups = [[2 * ranks * g + i for i in range(2 * ranks)] for g in range(clips // 2)]
    pre = lax.all_to_all(
        pre.reshape(2 * ranks, 2, count, part),
        ("dp",) + square,
        0,
        0,
        axis_index_groups=groups,
        tiled=True,
    ).reshape(2, frames // 2, 2, tiles, 2, count, part)

    lanes = frames * SLOT
    padded = round_up(count, 8)
    total = frames * padded
    scale = jnp.tile(jnp.pad(logit_scale, (0, SLOT - heads)), frames)[None]
    qgain = jnp.tile(query_gain, heads)[None]
    kgain = jnp.tile(key_gain, heads)[None]
    place = jnp.stack([2 * core + tile, core]).astype(jnp.int32)
    plane = (total, width)
    double = (2 * total, width)
    grads, scale_sums, d_raw, q_hat, k_hat, q_rstd, k_rstd, d_value = call(
        functools.partial(attend_kernel, heads=heads, count=count, padded=padded),
        [
            ((2, frames // 2, tiles * share, 2 * width), BF),
            ((1, lanes), F32),
            ((total, lanes), F32),
            (plane, F32),
            (plane, F32),
            ((total, lanes), F32),
            ((total, lanes), F32),
            (plane, BF),
        ],
        [(plane, F32), (plane, F32), (double, F32), (double, F32), (double, F32)],
        place,
        pre,
        pair,
        attn,
        qgain,
        kgain,
        scale,
    )

    chip = (grads[0].astype(F32) + swap(grads[1], "frame").astype(F32)).astype(BF)
    same_core = [[i for i in range(ranks) if (i // tiles) % 2 == c] for c in (0, 1)]
    chip = lax.all_to_all(
        chip.reshape(ranks // 2, share, 2 * width),
        square,
        0,
        0,
        axis_index_groups=same_core,
        tiled=True,
    )
    shares = jnp.sum(chip.astype(F32), axis=0)

    d_mid, gain_sums = call(
        functools.partial(back_kernel, heads=heads, padded=padded),
        [((frames, padded, width), BF), ((2, width), F32)],
        [(double, F32), (double, F32)],
        place,
        d_raw,
        q_hat,
        k_hat,
        q_rstd,
        k_rstd,
        d_value,
        attn,
        qgain,
        kgain,
    )
    d_back = lax.all_to_all(d_mid, "frame", 0, 0, tiled=True)[:, :count].reshape(rows, cols, width)
    mid_grad = (cot.astype(F32) + d_back.astype(F32)).astype(BF)

    if clips == 2:
        shares = shares.astype(BF)
        summed = shares.astype(F32) + swap(shares, "dp").astype(F32)
    else:
        summed = lax.psum(shares.astype(BF), "dp").astype(F32)
    gains = gain_sums.reshape(2, heads, depth).sum(axis=1)
    by_head = scale_sums.reshape(frames, SLOT).sum(axis=0)[:heads]
    scale_sum, qgain_sum, kgain_sum = lax.psum(
        (by_head, gains[0], gains[1]), ("dp", "frame", "tile")
    )
    factor = 1.0 / math.sqrt(clips * frames * tiles * tokens)
    return (
        mid_grad[None, None],
        summed[:, :width] * factor,
        summed[:, width:] * factor,
        qgain_sum * factor,
        kgain_sum * factor,
        scale_sum * factor,
    )


def solution(mesh):
    in_specs = (
        P("dp", "frame", "tile", None, None),
        P("dp", "frame", "tile", None, None),
        P(),
        P(None, ("frame", "tile"), None),
        P(("frame", "tile"), None),
        P(),
        P(),
        P(),
    )
    out_specs = (
        P("dp", "frame", "tile", None, None),
        P(("frame", "tile"), None),
        P(("frame", "tile"), None),
        P(),
        P(),
        P(),
    )
    return jax.shard_map(local, mesh=mesh, in_specs=in_specs, out_specs=out_specs, check_vma=False)
```

time: 324 us -> 220 us (0.68); the launches traced: 318 us -> 219 us
  local copies, waits for them, and re-layouts: 62.3 us -> 15.6 us
  matrix products: 38.4 us -> 0 us
  Pallas kernels: 0 us -> 24.6 us
  other arithmetic: 36.8 us -> 13 us
  starting transfers between devices: 19.5 us -> 36.2 us
  between operations: 14.7 us -> 1 us
  waiting for transfers between devices: 100 us -> 86.5 us
  blocking collectives: 45.8 us -> 41.9 us
    all_gather x2 -> x0, waiting for transfers between devices: 74.5 us -> none  [the longest x1 38.3 us: local(): lax.all_gather(conv_weight, ('frame', 'tile'), axis=1, tiled=True)]
    all_to_all x3 -> x6, waiting for transfers between devices: 0.01 us -> 46.2 us  [the longest x1 15.7 us: local(): lax.all_to_all(pre.reshape(2 * ranks, 2, count, part), ('dp',) + square,...]
    ppermute x2 -> x8, waiting for transfers between devices: 0.01 us -> 40.2 us  [swap(): lax.ppermute(x, axis, [(i, i ^ 1) for i in range(lax.axis_size(axis))])]
    dot_general x12 -> x0, matrix products: 38.4 us -> none  [the longest x1 7.35 us: attention_pass(): d_qn = jnp.einsum('nhfg,gnhd->fnhd', d_raw, k_norm, precision=high)]
    pallas_call x0 -> x3, Pallas kernels: none -> 24.6 us  [call(): pl.pallas_call(kernel, out_shape=[jax.ShapeDtypeStruct(shape, dtype) for...]
    psum x1 -> x0, waiting for transfers between devices: 24.2 us -> none  [local(): summed = lax.psum(shares.astype(jnp.bfloat16), 'dp').astype(jnp.float32)]
    all_to_all x3 -> x6, starting transfers between devices: 13.4 us -> 28.2 us  [the longest x1 7.43 us: local(): lax.all_to_all(kinds, square, 0, 0, tiled=True).reshape(1, width, width)]
    unnamed x82 -> x14, local copies, waits for them, and re-layouts: 14.4 us -> 0.04 us
  transfers between devices with their start and end apart: 9 -> 14, of which waited for: 3 -> 9; matrix products, arithmetic and copies ran while one was open for 27% -> 9% of each run, Pallas kernels for 0% -> 6%
where the time goes in v1:
time: 220 us; the launch traced here: 219 us
  waiting for transfers between devices  86.5 us (39%)
  blocking collectives  41.9 us (19%)
  starting transfers between devices  36.2 us (16%)
  Pallas kernels  24.6 us (11%)
  local copies, waits for them, and re-layouts  15.6 us (7%)
  other arithmetic  13 us (6%)
    psum x1, blocking collectives, local(): lax.psum((by_head, gains[0], gains[1]), ('dp', 'frame', 'tile'))  41.9 us
    ppermute x8, waiting for transfers between devices, swap(): lax.ppermute(x, axis, [(i, i ^ 1) for i in range(lax.axis_size(axis))])  40.2 us
    pallas_call x3, Pallas kernels, call(): pl.pallas_call(kernel, out_shape=[jax.ShapeDtypeStruct(shape, dtype) for...  24.6 us
    all_to_all x1, waiting for transfers between devices, local(): lax.all_to_all(pre.reshape(2 * ranks, 2, count, part), ('dp',) + square,...  15.7 us
    all_to_all x1, waiting for transfers between devices, local(): lax.all_to_all(kinds, square, 0, 0, tiled=True).reshape(1, width, width)  13.7 us
    all_to_all x1, waiting for transfers between devices, local(): lax.all_to_all(d_mid, 'frame', 0, 0, tiled=True)[:, :count]  11.7 us
    ppermute x8, starting transfers between devices, swap(): lax.ppermute(x, axis, [(i, i ^ 1) for i in range(lax.axis_size(axis))])  8.03 us
    all_to_all x1, starting transfers between devices, local(): lax.all_to_all(kinds, square, 0, 0, tiled=True).reshape(1, width, width)  7.43 us
  transfers between devices with their start and end apart: 14, of which 9 were waited for; matrix products, arithmetic and copies ran while one was open for 9% of the time, Pallas kernels for 6%

profile of v1, /device:TPU:0, one launch (start us, length us, event | category | flops | bytes accessed | tf_op | source)
XLA Modules:
  0.0 218.8 jit_solution(1815558475647999626)
XLA Ops:
  2.7 7.4 %all-to-all-start.3 = ((bf16[16,40,640]{2,1,0:T(8,128)(2,1)}), bf16[16,40,640]{2,1,0:T(8,128)(2,1)}, u32[]{:S(2)}, u32[]{:S(2)}) async-start(bf16[16,40,640]{2,1,0:T(8,128)(2,1)} %bitcast.16), calls=%async_computation.3 | async-start | bytes 1638400 | tf_op jit(solution)/shard_map/all_to_all | solution.py:287
  10.3 1.9 collective-permute-start
  13.2 2.4 %collective-permute-done = f32[2,640]{1,0:T(2,128)S(1)} collective-permute-done((f32[2,640]{1,0:T(2,128)S(1)}, f32[2,640]{1,0:T(2,128)S(1)}, u32[]{:S(2)}, u32[]{:S(2)}) %collective-permute-start) | collective-permute-done | bytes 5152 | tf_op jit(solution)/shard_map/ppermute | solution.py:20
  16.2 13.7 %all-to-all-done.3 = bf16[16,40,640]{2,1,0:T(8,128)(2,1)} async-done(((bf16[16,40,640]{2,1,0:T(8,128)(2,1)}), bf16[16,40,640]{2,1,0:T(8,128)(2,1)}, u32[]{:S(2)}, u32[]{:S(2)}) %all-to-all-start.3) | async-done | bytes 819232 | tf_op jit(solution)/shard_map/all_to_all | solution.py:287
  31.0 5.1 %all-to-all-start = ((bf16[16,3,40,240]{3,2,1,0:T(8,128)(2,1)}), bf16[16,3,40,240]{3,2,1,0:T(8,128)(2,1)}, u32[]{:S(2)}, u32[]{:S(2)}) async-start(bf16[16,3,40,240]{3,2,1,0:T(8,128)(2,1)} %bitcast.10), calls=%async_computation | async-start | bytes 1966080 | tf_op jit(solution)/shard_map/all_to_all | solution.py:264
  38.1 9.1 %collective-permute-done.1 = bf16[288,640]{1,0:T(8,128)(2,1)S(1)} collective-permute-done((bf16[288,640]{1,0:T(8,128)(2,1)S(1)}, bf16[288,640]{1,0:T(8,128)(2,1)S(1)}, u32[]{:S(2)}, u32[]{:S(2)}) %collective-permute-start.1) | collective-permute-done | bytes 368672 | tf_op jit(solution)/shard_map/ppermute | solution.py:20
  49.4 21.7 %collective-permute-done.2 = bf16[2,288,640]{2,1,0:T(8,128)(2,1)S(1)} collective-permute-done((bf16[2,288,640]{2,1,0:T(8,128)(2,1)S(1)}, bf16[2,288,640]{2,1,0:T(8,128)(2,1)S(1)}, u32[]{:S(2)}, u32[]{:S(2)}) %collective-permute-start.2) | collective-permute-done | bytes 737312 | tf_op jit(solution)/shard_map/ppermute | solution.py:20
  71.3 1.8 stack_reshape_reshape_squeeze.3
  73.2 1.8 stack_reshape_squeeze.3
  77.9 5.5 %all-to-all-start.2 = ((bf16[8,2,36,640]{3,1,2,0:T(2,128)(2,1)}), bf16[8,2,36,640]{3,1,2,0:T(2,128)(2,1)}, u32[]{:S(2)}, u32[]{:S(2)}) async-start(bf16[8,2,36,640]{3,1,2,0:T(2,128)(2,1)} %copy.28), calls=%async_computation.2 | async-start | bytes 1474560 | tf_op jit(solution)/shard_map/all_to_all | solution.py:283
  83.4 5.2 %collective-permute-done.4 = bf16[1,640,640]{2,1,0:T(8,128)(2,1)} collective-permute-done((bf16[1,640,640]{2,1,0:T(8,128)(2,1)}, bf16[1,640,640]{2,1,0:T(8,128)(2,1)}, u32[]{:S(2)}, u32[]{:S(2)}) %collective-permute-start.4) | collective-permute-done | bytes 819232 | tf_op jit(solution)/shard_map/ppermute | solution.py:20
  88.6 2.8 %pad_maximum_fusion.1 = bf16[2,640,640]{2,1,0:T(8,128)(2,1)} fusion(bf16[1,640,640]{2,1,0:T(8,128)(2,1)} %collective-permute-done.4, bf16[1,640,640]{2,1,0:T(8,128)(2,1)} %bitcast.17), kind=kLoop, calls=%fused_computation.1 | loop fusion | flops 819200 | bytes 3276800 | tf_op jit(solution)/shard_map/concatenate | solution.py:288
  92.8 4.2 %shard_map.127 = bf16[2,8,2,2,36,80]{5,4,3,2,1,0:T(8,128)(2,1)S(1)} custom-call(s32[3]{0:T(128)S(1)} %pad_add_fusion.1.place, bf16[4,288,640]{2,1,0:T(8,128)(2,1)S(1)} %pad_maximum_fusion.2.mine, bf16[4,288,640]{2,1,0:T(8,128)(2,1)S(1)} %collective-permute-done.3.other, bf16[3,640,240]{2,1,0:T(8,128)(2,1)S(1)} %bitcast.55), custom_call_target="tpu_custom_call" | custom-call | tf_op jit(solution)/shard_map/pallas_call | solution.py:231
  98.4 5.1 %all-to-all-done.2 = bf16[8,2,36,640]{3,1,2,0:T(2,128)(2,1)} async-done(((bf16[8,2,36,640]{3,1,2,0:T(2,128)(2,1)}), bf16[8,2,36,640]{3,1,2,0:T(2,128)(2,1)}, u32[]{:S(2)}, u32[]{:S(2)}) %all-to-all-start.2) | async-done | bytes 737312 | tf_op jit(solution)/shard_map/all_to_all | solution.py:283
  103.4 3.1 %all-to-all-start.1 = ((bf16[32,2,36,80]{3,1,2,0:T(2,128)(2,1)}), bf16[32,2,36,80]{3,1,2,0:T(2,128)(2,1)S(1)}, u32[]{:S(2)}, u32[]{:S(2)}) async-start(bf16[32,2,36,80]{3,1,2,0:T(2,128)(2,1)} %copy.26), calls=%async_computation.1 | async-start | bytes 1179648 | tf_op jit(solution)/shard_map/all_to_all | solution.py:306
  108.1 15.7 %all-to-all-done.1 = bf16[32,2,36,80]{3,1,2,0:T(2,128)(2,1)S(1)} async-done(((bf16[32,2,36,80]{3,1,2,0:T(2,128)(2,1)}), bf16[32,2,36,80]{3,1,2,0:T(2,128)(2,1)S(1)}, u32[]{:S(2)}, u32[]{:S(2)}) %all-to-all-start.1) | async-done | bytes 368672 | tf_op jit(solution)/shard_map/all_to_all | solution.py:306
  124.0 3.3 %pad_maximum_fusion.weights = bf16[4,640,640]{2,1,0:T(8,128)(2,1)} fusion(bf16[2,640,640]{2,1,0:T(8,128)(2,1)} %collective-permute-done.5, bf16[1,640,640]{2,1,0:T(8,128)(2,1)} %collective-permute-done.4, bf16[1,640,640]{2,1,0:T(8,128)(2,1)} %bitcast.17), kind=kLoop, calls=%fused_computation | loop fusion | flops 3276800 | bytes 6553600 | tf_op jit(solution)/shard_map/concatenate | solution.py:289
  127.3 11.9 %shard_map.128 = (bf16[2,4,80,1280]{3,2,1,0:T(8,128)(2,1)S(1)}, f32[1,128]{1,0:T(1,128)S(1)}, f32[320,128]{1,0:T(8,128)S(1)}, f32[320,640]{1,0:T(8,128)S(1)}, f3...) custom-call(s32[2]{0:T(128)S(1)} %pad_add_fusion.place, ...), custom_call_target="tpu_custom_call" | custom-call | tf_op jit(solution)/shard_map/pallas_call | solution.py:231
  140.1 8.5 %shard_map.129 = (bf16[8,40,640]{2,1,0:T(8,128)(2,1)}, f32[2,640]{1,0:T(2,128)S(1)}) custom-call(s32[2]{0:T(128)S(1)} %pad_add_fusion.place, f32[320,128]{1,0:T(8,128)S(1)} %get-tuple-element.16.d_raw, f32[320,640]{1,0:T(8,128)S(1)} %get-tuple-element.17.q_hat, f32[320,640]{1,0:T(8,128)S(1)} %get-tuple-element.18.k_hat, ...), custom_call_target="tpu_custom_call" | custom-call | tf_op jit(solution)/shard_map/pallas_call | solution.py:231
  148.6 3.5 %all-to-all-start.4 = ((bf16[8,40,640]{2,1,0:T(8,128)(2,1)}), bf16[8,40,640]{2,1,0:T(8,128)(2,1)S(1)}, u32[]{:S(2)}, u32[]{:S(2)}) async-start(bf16[8,40,640]{2,1,0:T(8,128)(2,1)} %get-tuple-element.22), calls=%async_computation.4 | async-start | bytes 819200 | tf_op jit(solution)/shard_map/all_to_all | solution.py:373
  153.2 11.7 %all-to-all-done.4 = bf16[8,40,640]{2,1,0:T(8,128)(2,1)S(1)} async-done(((bf16[8,40,640]{2,1,0:T(8,128)(2,1)}), bf16[8,40,640]{2,1,0:T(8,128)(2,1)S(1)}, u32[]{:S(2)}, u32[]{:S(2)}) %all-to-all-start.4) | async-done | bytes 409632 | tf_op jit(solution)/shard_map/all_to_all | solution.py:373
  164.9 3.5 %all-to-all-start.5 = ((bf16[8,40,1280]{2,1,0:T(8,128)(2,1)}), bf16[8,40,1280]{2,1,0:T(8,128)(2,1)S(1)}, u32[]{:S(2)}, u32[]{:S(2)}) async-start(bf16[8,40,1280]{2,1,0:T(8,128)(2,1)} %bitcast.20), calls=%async_computation.5 | async-start | bytes 1638400 | tf_op jit(solution)/shard_map/all_to_all | solution.py:348
  169.8 41.9 %all-reduce.1 = (f32[64]{0:T(128)S(1)}, f32[64]{0:T(128)S(1)}, f32[10]{0:T(128)S(1)}) all-reduce(f32[64]{0:T(128)S(1)} %get-tuple-element.34, f32[64]{0:T(128)S(1)} %get-tuple-element.33, f32[10]{0:T(128)S(1)} %bitcast.62), channel_id=1, replica_groups=mesh['dp'=2,'frame'=8,'tile'=2] {'dp','frame','tile'}, use_global_device_ids=true, to_apply=%region_5.6 | all-reduce | flops 138 | bytes 1104 | tf_op jit(solution)/shard_map/psum | solution.py:383
  213.0 2.3 %collective-permute-start.7 = (bf16[40,1280]{1,0:T(8,128)(2,1)S(1)}, bf16[40,1280]{1,0:T(8,128)(2,1)S(1)}, u32[]{:S(2)}, u32[]{:S(2)}) collective-permute-start(bf16[40,1280]{1,0:T(8,128)(2,1)S(1)} %reduce_sum.60), channel_id=1, source_target_pairs={{0,16},{16,0},{1,17},{17,1},{2,18},{18,2},{3,19},{19,3},{4,20},{20... | collective-permute-start | bytes 307208 | tf_op jit(solution)/shard_map/ppermute | solution.py:20
  (83 shorter events, 24.4 us)
Async XLA Ops:
  0.6 11.7 %copy-start = (bf16[9,40,640]{2,1,0:T(8,128)(2,1)S(1)}, bf16[9,40,640]{2,1,0:T(8,128)(2,1)}, u32[]{:S(2)}) copy-start(bf16[9,40,640]{2,1,0:T(8,128)(2,1)} %param.11) | copy-start | bytes 1382404
  1.7 8.5 %copy-start.1 = (bf16[1,1,9,32,640]{4,3,2,1,0:T(8,128)(2,1)S(1)}, bf16[1,1,9,32,640]{4,3,2,1,0:T(8,128)(2,1)}, u32[]{:S(2)}) copy-start(bf16[1,1,9,32,640]{4,3,2,1,0:T(8,128)(2,1)} %param.8) | copy-start | bytes 1105924
  2.7 27.2 %all-to-all-start.3 = ((bf16[16,40,640]{2,1,0:T(8,128)(2,1)}), bf16[16,40,640]{2,1,0:T(8,128)(2,1)}, u32[]{:S(2)}, u32[]{:S(2)}) async-start(bf16[16,40,640]{2,1,0:T(8,128)(2,1)} %bitcast.16), calls=%async_computation.3 | async-start | bytes 1638400 | tf_op jit(solution)/shard_map/all_to_all | solution.py:287
  10.3 5.3 %collective-permute-start = (f32[2,640]{1,0:T(2,128)S(1)}, f32[2,640]{1,0:T(2,128)S(1)}, u32[]{:S(2)}, u32[]{:S(2)}) collective-permute-start(f32[2,640]{1,0:T(2,128)S(1)} %pad_maximum_fusion.5), channel_id=1, source_target_pairs={{0,1},{1,0},{2,3},{3,2},{4,5},{5,4},{6,7},{7,6},{8,9},{9,8},{10,11... | collective-permute-start | bytes 15368 | tf_op jit(solution)/shard_map/ppermute | solution.py:20
  15.8 20.2 %copy-start.3 = (f32[640]{0:T(1024)S(1)}, f32[640]{0:T(1024)}, u32[]{:S(2)}) copy-start(f32[640]{0:T(1024)} %param.10) | copy-start | bytes 7684
  31.0 46.9 %all-to-all-start = ((bf16[16,3,40,240]{3,2,1,0:T(8,128)(2,1)}), bf16[16,3,40,240]{3,2,1,0:T(8,128)(2,1)}, u32[]{:S(2)}, u32[]{:S(2)}) async-start(bf16[16,3,40,240]{3,2,1,0:T(8,128)(2,1)} %bitcast.10), calls=%async_computation | async-start | bytes 1966080 | tf_op jit(solution)/shard_map/all_to_all | solution.py:264
  36.3 10.9 %collective-permute-start.1 = (bf16[288,640]{1,0:T(8,128)(2,1)S(1)}, bf16[288,640]{1,0:T(8,128)(2,1)S(1)}, u32[]{:S(2)}, u32[]{:S(2)}) collective-permute-start(bf16[288,640]{1,0:T(8,128)(2,1)S(1)} %multiply_convert_fusion), channel_id=1, source_target_pairs={{0,16},{16,0},{1,17},{17,1},{2,18},{18,2},{3,19},{19,3},{4,20},{20... | collective-permute-start | bytes 1105928 | tf_op jit(solution)/shard_map/ppermute | solution.py:20
  47.3 23.8 %collective-permute-start.2 = (bf16[2,288,640]{2,1,0:T(8,128)(2,1)S(1)}, bf16[2,288,640]{2,1,0:T(8,128)(2,1)S(1)}, u32[]{:S(2)}, u32[]{:S(2)}) collective-permute-start(bf16[2,288,640]{2,1,0:T(8,128)(2,1)S(1)} %pad_maximum_fusion.4), channel_id=1, source_target_pairs={{0,1},{1,0},{2,3},{3,2},{4,5},{5,4},{6,7},{7,6},{8,9},{9,8},{10,11... | collective-permute-start | bytes 2211848 | tf_op jit(solution)/shard_map/ppermute | solution.py:20
  49.1 39.6 %collective-permute-start.4 = (bf16[1,640,640]{2,1,0:T(8,128)(2,1)}, bf16[1,640,640]{2,1,0:T(8,128)(2,1)}, u32[]{:S(2)}, u32[]{:S(2)}) collective-permute-start(bf16[1,640,640]{2,1,0:T(8,128)(2,1)} %bitcast.17), channel_id=1, source_target_pairs={{0,1},{1,0},{2,3},{3,2},{4,5},{5,4},{6,7},{7,6},{8,9},{9,8},{10,11... | collective-permute-start | bytes 2457608 | tf_op jit(solution)/shard_map/ppermute | solution.py:20
  71.3 21.5 %collective-permute-start.3 = (bf16[4,288,640]{2,1,0:T(8,128)(2,1)S(1)}, bf16[4,288,640]{2,1,0:T(8,128)(2,1)S(1)}, u32[]{:S(2)}, u32[]{:S(2)}) collective-permute-start(bf16[4,288,640]{2,1,0:T(8,128)(2,1)S(1)} %pad_maximum_fusion.2.mine), channel_id=1, source_target_pairs={{0,2},{2,0},{4,6},{6,4},{8,10},{10,8},{12,14},{14,12},{1,3},{3,1},... | collective-permute-start | bytes 4423688 | tf_op jit(solution)/shard_map/ppermute | solution.py:20
  77.9 25.6 %all-to-all-start.2 = ((bf16[8,2,36,640]{3,1,2,0:T(2,128)(2,1)}), bf16[8,2,36,640]{3,1,2,0:T(2,128)(2,1)}, u32[]{:S(2)}, u32[]{:S(2)}) async-start(bf16[8,2,36,640]{3,1,2,0:T(2,128)(2,1)} %copy.28), calls=%async_computation.2 | async-start | bytes 1474560 | tf_op jit(solution)/shard_map/all_to_all | solution.py:283
  91.4 32.5 %collective-permute-start.5 = (bf16[2,640,640]{2,1,0:T(8,128)(2,1)}, bf16[2,640,640]{2,1,0:T(8,128)(2,1)}, u32[]{:S(2)}, u32[]{:S(2)}) collective-permute-start(bf16[2,640,640]{2,1,0:T(8,128)(2,1)} %pad_maximum_fusion.1), channel_id=1, source_target_pairs={{0,2},{2,0},{4,6},{6,4},{8,10},{10,8},{12,14},{14,12},{1,3},{3,1},... | collective-permute-start | bytes 4915208 | tf_op jit(solution)/shard_map/ppermute | solution.py:20
  97.0 9.5 %copy-start.4 = (f32[64]{0:T(128)S(1)}, f32[64]{0:T(128)}, u32[]{:S(2)}) copy-start(f32[64]{0:T(128)} %param.14) | copy-start | bytes 772
  97.1 9.6 %copy-start.5 = (f32[64]{0:T(128)S(1)}, f32[64]{0:T(128)}, u32[]{:S(2)}) copy-start(f32[64]{0:T(128)} %param.13) | copy-start | bytes 772
  97.1 9.7 %copy-start.6 = (f32[10]{0:T(128)S(1)}, f32[10]{0:T(128)}, u32[]{:S(2)}) copy-start(f32[10]{0:T(128)} %param.15) | copy-start | bytes 124
  103.4 20.4 %all-to-all-start.1 = ((bf16[32,2,36,80]{3,1,2,0:T(2,128)(2,1)}), bf16[32,2,36,80]{3,1,2,0:T(2,128)(2,1)S(1)}, u32[]{:S(2)}, u32[]{:S(2)}) async-start(bf16[32,2,36,80]{3,1,2,0:T(2,128)(2,1)} %copy.26), calls=%async_computation.1 | async-start | bytes 1179648 | tf_op jit(solution)/shard_map/all_to_all | solution.py:306
  140.1 11.9 %collective-permute-start.6 = (bf16[4,80,1280]{2,1,0:T(8,128)(2,1)}, bf16[4,80,1280]{2,1,0:T(8,128)(2,1)S(1)}, u32[]{:S(2)}, u32[]{:S(2)}) collective-permute-start(bf16[4,80,1280]{2,1,0:T(8,128)(2,1)} %slice_bitcast_fusion), channel_id=1, source_target_pairs={{0,2},{2,0},{4,6},{6,4},{8,10},{10,8},{12,14},{14,12},{1,3},{3,1},... | collective-permute-start | bytes 2457608 | tf_op jit(solution)/shard_map/ppermute | solution.py:20
  148.6 16.3 %all-to-all-start.4 = ((bf16[8,40,640]{2,1,0:T(8,128)(2,1)}), bf16[8,40,640]{2,1,0:T(8,128)(2,1)S(1)}, u32[]{:S(2)}, u32[]{:S(2)}) async-start(bf16[8,40,640]{2,1,0:T(8,128)(2,1)} %get-tuple-element.22), calls=%async_computation.4 | async-start | bytes 819200 | tf_op jit(solution)/shard_map/all_to_all | solution.py:373
  164.9 48.0 %all-to-all-start.5 = ((bf16[8,40,1280]{2,1,0:T(8,128)(2,1)}), bf16[8,40,1280]{2,1,0:T(8,128)(2,1)S(1)}, u32[]{:S(2)}, u32[]{:S(2)}) async-start(bf16[8,40,1280]{2,1,0:T(8,128)(2,1)} %bitcast.20), calls=%async_computation.5 | async-start | bytes 1638400 | tf_op jit(solution)/shard_map/all_to_all | solution.py:348
  212.8 2.6 %copy-start.2 = (bf16[1,1,9,32,640]{4,3,2,1,0:T(8,128)(2,1)S(1)}, bf16[1,1,9,32,640]{4,3,2,1,0:T(8,128)(2,1)}, u32[]{:S(2)}) copy-start(bf16[1,1,9,32,640]{4,3,2,1,0:T(8,128)(2,1)} %param.9) | copy-start | bytes 1105924
  213.0 5.0 %collective-permute-start.7 = (bf16[40,1280]{1,0:T(8,128)(2,1)S(1)}, bf16[40,1280]{1,0:T(8,128)(2,1)S(1)}, u32[]{:S(2)}, u32[]{:S(2)}) collective-permute-start(bf16[40,1280]{1,0:T(8,128)(2,1)S(1)} %reduce_sum.60), channel_id=1, source_target_pairs={{0,16},{16,0},{1,17},{17,1},{2,18},{18,2},{3,19},{19,3},{4,20},{20... | collective-permute-start | bytes 307208 | tf_op jit(solution)/shard_map/ppermute | solution.py:20

commit v2 on v1

v2 whole, which is shorter than its diff:
```python
import functools
import math

import jax
import jax.numpy as jnp
from jax import lax
from jax.experimental import pallas as pl
from jax.experimental.pallas import tpu as pltpu
from jax.sharding import PartitionSpec as P

GROUPS = 32
EPS = 1e-05
SLOT = 16
BF = jnp.bfloat16
F32 = jnp.float32
VMEM_BYTES = 48 * 1024 * 1024


def swap(x, axis):
    return lax.ppermute(x, axis, [(i, i ^ 1) for i in range(lax.axis_size(axis))])


def round_up(value, unit):
    return -(-value // unit) * unit


def dot(a, b):
    return lax.dot_general(a, b, (((1,), (0,)), ((), ())), preferred_element_type=F32)


def dot_t(a, b):
    return lax.dot_general(a, b, (((1,), (1,)), ((), ())), preferred_element_type=F32)


def dot_rows(a, b):
    return lax.dot_general(a, b, (((0,), (0,)), ((), ())), preferred_element_type=F32)


def halves(x):
    high = x.astype(BF)
    return high, (x - high.astype(F32)).astype(BF)


def picker(rows, cols, depth, offset):
    row = lax.broadcasted_iota(jnp.int32, (rows, cols), 0)
    col = lax.broadcasted_iota(jnp.int32, (rows, cols), 1)
    return (col - row // depth == offset).astype(F32).astype(BF)


def spreader(rows, cols, depth, offset):
    row = lax.broadcasted_iota(jnp.int32, (rows, cols), 0)
    col = lax.broadcasted_iota(jnp.int32, (rows, cols), 1)
    return (row - col // depth == offset).astype(F32).astype(BF)


def head_sums(x, pick):
    high, low = halves(x)
    return dot(high, pick) + dot(low, pick)


def spread(x, both):
    high, low = halves(x)
    return dot(jnp.concatenate([high, low], axis=1), both)


def over_slots(x):
    step = SLOT
    while step < x.shape[1]:
        x = x + pltpu.roll(x, step, 1)
        step *= 2
    return x


def each(number, body):
    if number > 8:
        lax.fori_loop(0, number, lambda i, _: body(i), None)
    else:
        for i in range(number):
            body(i)


def act_kernel(place, gain, first, *rest, cols, part):
    second, (act, kept) = (rest[:-2], rest[-2:])
    half, width = first.shape
    tile, chosen = (place[2], place[3])
    upper = first[...]
    lower = jnp.concatenate([ref[...] for ref in second], axis=0) if len(second) > 1 else second[0][...]
    upper, lower = (jnp.where(tile == 0, upper, lower), jnp.where(tile == 0, lower, upper))
    kept[pl.ds(0, half), :] = dot(upper, picker(width, part, 1, -part * chosen)).astype(BF)
    kept[pl.ds(half, half), :] = dot(lower, picker(width, part, 1, -part * chosen)).astype(BF)
    upper, lower = (upper.astype(F32), lower.astype(F32))
    total = jnp.sum(upper, axis=0, keepdims=True) + jnp.sum(lower, axis=0, keepdims=True)
    square = jnp.sum(upper * upper, axis=0, keepdims=True)
    square = square + jnp.sum(lower * lower, axis=0, keepdims=True)
    both = jnp.concatenate([total, square, jnp.zeros((6, width), F32)], axis=0)
    high, low = halves(both)
    lowest = (both - high.astype(F32) - low.astype(F32)).astype(BF)
    per_group = width // GROUPS
    pick = picker(width, 128, per_group, 0)
    back = spreader(128, width, per_group, 0)
    both = (dot(high, pick) + dot(low, pick) + dot(lowest, pick)) / (2 * half * per_group)
    mean = both[0:1]
    rstd = lax.rsqrt(both[1:2] - mean * mean + EPS)
    both = jnp.concatenate([mean, rstd, jnp.zeros((6, 128), F32)], axis=0)
    high, low = halves(both)
    lowest = (both - high.astype(F32) - low.astype(F32)).astype(BF)
    both = dot(high, back) + dot(low, back) + dot(lowest, back)
    mean = both[0:1]
    scale = both[1:2] * gain[...]
    act[pl.ds(0, cols), :] = jnp.zeros((cols, width), BF)
    act[pl.ds(cols + 2 * half, cols), :] = jnp.zeros((cols, width), BF)
    for start, x in ((cols, upper), (cols + half, lower)):
        zed = (x - mean) * scale
        act[pl.ds(start, half), :] = (zed / (1.0 + jnp.exp(-zed))).astype(BF)


def conv_kernel(place, weights, *refs, cols, part, blocks, count):
    acts, kept, out = (refs[:4], refs[4:8], refs[8])
    x, core = (place[0], place[1])
    whole = kept[0].shape[0]
    half = whole // 2
    third = count // 3
    col = lax.broadcasted_iota(jnp.int32, (whole, part), 0) % cols
    for dc in (0, 1):
        for dx in (0, 1):
            act, plus = (acts[2 * dc + dx], kept[2 * dc + dx])
            taps = dot(act[pl.ds(0, whole), :], weights[0])
            taps += dot(act[pl.ds(cols, whole), :], weights[1])
            taps += dot(act[pl.ds(2 * cols, whole), :], weights[2])
            left = pltpu.roll(taps[:, :part], 1, 0)
            right = pltpu.roll(taps[:, 2 * part :], whole - 1, 0)
            pre = taps[:, part : 2 * part] + jnp.where(col > 0, left, 0.0)
            pre = pre + jnp.where(col < cols - 1, right, 0.0)
            mid = (plus[...].astype(F32) + pre).astype(BF)
            if blocks > 8:
                out[x ^ dx, core ^ dc] = mid
                continue
            for t in (0, 1):
                for f in range(blocks):
                    start = t * half + f * count
                    three = [mid[start + third * j : start + third * (j + 1)] for j in range(3)]
                    out[x ^ dx, f, t, core ^ dc] = jnp.concatenate(three, axis=1)


def attend_kernel(
    mid_in, weights, qgain, kgain, scale,
    mid_out, q_hat, k_hat, q_rstd, k_rstd, value_out, raw_out, probs_out, mixed_out,
    mid_s, doubled, mixed_s, raw_s,
    *, heads, count, padded, part,
):
    total, width = mid_s.shape
    frames = total // padded
    depth = width // heads
    lanes = scale.shape[-1]
    third = count // 3
    mid_s[...] = jnp.zeros_like(mid_s)

    def unpack(z):
        for e in (0, 1):
            blocks = [mid_in[x, z, c, t, e] for x in (0, 1) for c in (0, 1) for t in (0, 1)]
            for j in range(3):
                piece = [b[:, j * part : (j + 1) * part] for b in blocks]
                start = (2 * z + e) * padded + j * third
                mid_s[pl.ds(start, third), :] = jnp.concatenate(piece, axis=1).astype(F32)

    for z in range(frames // 2):
        unpack(z)
    mid = mid_s[...].astype(BF)
    mid_out[...] = mid
    pick = picker(width, lanes, depth, 0)
    both = jnp.concatenate([spreader(lanes, width, depth, 0)] * 2, axis=0)

    def stats(vec):
        cent = vec - spread(head_sums(vec, pick) / depth, both)
        var = head_sums(cent * cent, pick) / depth
        rstd = lax.rsqrt(var + EPS)
        return cent * spread(rstd, both), rstd

    hat, rstd = stats(dot(mid, weights[:, pl.ds(0, width)]))
    q_hat[...] = hat
    q_rstd[...] = rstd
    q_norm = hat * qgain[...]
    hat, rstd = stats(dot(mid, weights[:, pl.ds(width, width)]))
    k_hat[...] = hat
    k_rstd[...] = rstd
    hat = hat * kgain[...]
    doubled[pl.ds(0, total), :] = hat
    doubled[pl.ds(total, total), :] = hat
    raw_s[...] = jnp.zeros_like(raw_s)

    def logits(s):
        here = picker(width, lanes, depth, SLOT * s)
        raw_s[...] += head_sums(q_norm * doubled[pl.ds(s * padded, total), :], here)

    each(frames, logits)
    raw = raw_s[...] / math.sqrt(depth)
    raw_out[...] = raw
    expo = jnp.exp(raw * scale[...])
    probs = expo / over_slots(expo)
    probs_out[...] = probs
    probs_b = probs.astype(BF)

    value = dot(mid, weights[:, pl.ds(2 * width, width)]).astype(BF)
    value_out[...] = value
    value = value.astype(F32)
    doubled[pl.ds(0, total), :] = value
    doubled[pl.ds(total, total), :] = value
    mixed_s[...] = jnp.zeros_like(mixed_s)

    def mix(s):
        weight = dot(probs_b, spreader(lanes, width, depth, SLOT * s))
        mixed_s[...] += weight * doubled[pl.ds(s * padded, total), :]

    each(frames, mix)
    mixed_out[...] = mixed_s[...].astype(BF)


def middle_kernel(
    place, cot_in, weights, mid, mixed, value_in, raw, probs_in, scale,
    grads, sums, d_raw, d_value,
    cot_s, doubled, doubled_acc, probs_s,
    *, heads, count, padded,
):
    total, width = mid.shape
    frames = total // padded
    depth = width // heads
    lanes = scale.shape[-1]
    x, core = (place[0], place[1])
    cot_s[...] = jnp.zeros_like(cot_s)

    def unpack(f):
        cot_s[pl.ds(f * padded, count), :] = cot_in[f].astype(F32)

    each(frames, unpack)
    cot = cot_s[...].astype(BF)
    rows = grads.shape[3]

    def store(kind, term):
        for z in range(frames // 2):
            for c in (0, 1):
                start = (2 * z + c) * rows
                grads[x ^ kind, core ^ c, z] = term[start : start + rows]

    store(1, dot_rows(mixed[...], cot).astype(BF))
    d_mixed = dot_t(cot, weights[:, pl.ds(3 * width, width)]).astype(BF).astype(F32)
    value = value_in[...].astype(F32)
    doubled[pl.ds(0, total), :] = value
    doubled[pl.ds(total, total), :] = value
    doubled_acc[...] = jnp.zeros_like(doubled_acc)
    probs_s[...] = jnp.zeros_like(probs_s)
    probs = probs_in[...]
    probs_b = probs.astype(BF)

    def shift(s):
        here = picker(width, lanes, depth, SLOT * s)
        probs_s[...] += head_sums(d_mixed * doubled[pl.ds(s * padded, total), :], here)
        weight = dot(probs_b, spreader(lanes, width, depth, SLOT * s))
        doubled_acc[pl.ds(s * padded, total), :] += weight * d_mixed

    each(frames, shift)
    d_probs = probs_s[...]
    dv = (doubled_acc[pl.ds(0, total), :] + doubled_acc[pl.ds(total, total), :]).astype(BF)
    d_value[...] = dv
    store(0, dot_rows(mid[...], dv).astype(BF))
    d_logits = probs * (d_probs - over_slots(probs * d_probs))
    sums[...] = jnp.sum(d_logits * raw[...], axis=0, keepdims=True)
    d_raw[...] = d_logits * scale[...] / math.sqrt(depth)


def back_kernel(
    d_raw, q_hat, k_hat, q_rstd, k_rstd, d_value, weights, qgain, kgain, scale_sums,
    d_mid,
    doubled, doubled_acc, d_qn_s,
    *, heads, count, padded,
):
    total, width = q_hat.shape
    depth = width // heads
    frames = total // padded
    lanes = d_raw.shape[-1]
    pick = picker(width, lanes, depth, 0)
    both = jnp.concatenate([spreader(lanes, width, depth, 0)] * 2, axis=0)
    k_norm = k_hat[...] * kgain[...]
    doubled[pl.ds(0, total), :] = k_norm
    doubled[pl.ds(total, total), :] = k_norm
    q_norm = q_hat[...] * qgain[...]
    doubled_acc[...] = jnp.zeros_like(doubled_acc)
    d_qn_s[...] = jnp.zeros_like(d_qn_s)
    high, low = halves(d_raw[...])
    pair = jnp.concatenate([high, low], axis=1)

    def shift(s):
        one = spreader(lanes, width, depth, SLOT * s)
        weight = dot(pair, jnp.concatenate([one, one], axis=0))
        d_qn_s[...] += weight * doubled[pl.ds(s * padded, total), :]
        doubled_acc[pl.ds(s * padded, total), :] += weight * q_norm

    each(frames, shift)
    d_qn = d_qn_s[...]
    d_kn = doubled_acc[pl.ds(0, total), :] + doubled_acc[pl.ds(total, total), :]

    def back(dhat, hat, rstd):
        first = spread(head_sums(dhat, pick) / depth, both)
        second = spread(head_sums(dhat * hat, pick) / depth, both)
        return (spread(rstd, both) * (dhat - first - hat * second)).astype(BF)

    d_query = back(d_qn * qgain[...], q_hat[...], q_rstd[...])
    d_key = back(d_kn * kgain[...], k_hat[...], k_rstd[...])
    out = dot_t(d_query, weights[:, pl.ds(0, width)])
    out += dot_t(d_key, weights[:, pl.ds(width, width)])
    out += dot_t(d_value[...], weights[:, pl.ds(2 * width, width)])

    row = lax.broadcasted_iota(jnp.int32, (width, 128), 0)
    col = lax.broadcasted_iota(jnp.int32, (width, 128), 1)
    fold = (row % depth == col).astype(F32)

    def folded(d_norm, hat):
        sums = jnp.sum(d_norm * hat, axis=0, keepdims=True)
        sums = jnp.broadcast_to(sums, (8, width))
        return jnp.dot(sums, fold, precision=lax.Precision.HIGHEST, preferred_element_type=F32)[0:1]

    by_head = over_slots(jnp.broadcast_to(scale_sums[...], (8, lanes)))[0:1, :128]
    small = [folded(d_qn, q_hat[...]), folded(d_kn, k_hat[...]), by_head]
    small.append(jnp.zeros((1, width - 384), F32))
    small = jnp.concatenate(small, axis=1)
    high, low = halves(small)
    lowest = (small - high.astype(F32) - low.astype(F32)).astype(BF)
    spare = [high.astype(F32), low.astype(F32), lowest.astype(F32)]
    if padded - count > 3:
        spare.append(jnp.zeros((padded - count - 3, width), F32))
    spare = jnp.concatenate(spare, axis=0)
    for f in range(frames):
        tokens = out[f * padded : f * padded + count]
        d_mid[f] = jnp.concatenate([tokens, spare], axis=0).astype(BF)


def call(kernel, outs, scratch, *args):
    smem = pl.BlockSpec(memory_space=pltpu.SMEM)
    vmem = pl.BlockSpec(memory_space=pltpu.VMEM)
    return pl.pallas_call(
        kernel,
        out_shape=[jax.ShapeDtypeStruct(shape, dtype) for shape, dtype in outs],
        in_specs=[smem if arg.dtype == jnp.int32 else vmem for arg in args],
        out_specs=[vmem] * len(outs),
        scratch_shapes=[pltpu.VMEM(shape, dtype) for shape, dtype in scratch],
        compiler_params=pltpu.CompilerParams(vmem_limit_bytes=VMEM_BYTES),
    )(*args)


def local(
    clip_input, cotangent, norm_gain, conv_weight, attn_weight, query_gain, key_gain, logit_scale
):
    source = clip_input[0, 0]
    cot = cotangent[0, 0]
    rows, cols, width = source.shape
    heads = logit_scale.shape[0]
    depth = width // heads
    tokens = rows * cols
    clips, frames, tiles = (lax.axis_size(name) for name in ("dp", "frame", "tile"))
    square = ("frame", "tile")
    ranks = frames * tiles
    share = conv_weight.shape[1]
    count = tokens // frames
    third = count // 3
    part = width // 8
    x = lax.axis_index("dp") % 2
    core = lax.axis_index("frame") % 2
    tile = lax.axis_index("tile")
    place = jnp.stack([x, core, tile, 4 * x + 2 * core + tile]).astype(jnp.int32)

    mine = lax.dynamic_slice_in_dim(conv_weight, x * (width // 2), width // 2, axis=2)
    mine = mine.reshape(3, 3, share, 4, part).transpose(3, 0, 2, 1, 4)
    mine = mine.reshape(4, 3, share, 3 * part)
    spread_out = jnp.broadcast_to(mine[None], (frames // 2,) + mine.shape)
    conv_in = lax.all_to_all(spread_out.reshape((ranks,) + mine.shape[1:]), square, 0, 0, tiled=True)
    conv_full = conv_in.transpose(1, 0, 2, 3).reshape(3, width, 3 * part)
    attn_full = lax.all_gather(attn_weight, square, axis=0, tiled=True)

    flat = source.reshape(tokens, width)
    half = tokens // 2
    along_x = swap(flat, "dp")
    along_y = swap(flat, "tile")
    across = (swap(along_x[:half], "tile"), swap(along_y[half:], "dp"))
    own = ((flat, along_y), (along_x,) + across)
    gain = norm_gain[None]
    acts, kept = ([], [])
    for other in (False, True):
        for pieces in own:
            if other:
                pieces = [swap(piece, "frame") for piece in pieces]
            act, keep = call(
                functools.partial(act_kernel, cols=cols, part=part),
                [((tiles * tokens + 2 * cols, width), BF), ((tiles * tokens, part), BF)],
                [],
                place,
                gain,
                *pieces,
            )
            acts.append(act)
            kept.append(keep)

    blocked = (2, frames, tiles, 2, third, 3 * part)
    plain = (2, 2, tiles * tokens, part)
    (mid,) = call(
        functools.partial(conv_kernel, cols=cols, part=part, blocks=frames, count=count),
        [(plain if frames > 8 else blocked, BF)],
        [],
        place,
        conv_full,
        *acts,
        *kept,
    )
    if frames > 8:
        mid = mid.reshape(2, 2, tiles, frames, 3, third, part).transpose(0, 3, 2, 1, 5, 4, 6)
    groups = None
    if clips > 2:
        groups = [[2 * ranks * g + i for i in range(2 * ranks)] for g in range(clips // 2)]
    mid = lax.all_to_all(
        mid.reshape(2 * ranks, 2 * third, 3 * part),
        ("dp",) + square,
        0,
        0,
        axis_index_groups=groups,
        tiled=True,
    ).reshape(2, frames // 2, 2, tiles, 2, third, 3 * part)

    cot_blocks, mid = lax.optimization_barrier((cot.reshape(frames, count, width), mid))
    cot_blocks = lax.all_to_all(cot_blocks, "frame", 0, 0, tiled=True)

    lanes = frames * SLOT
    padded = round_up(count + 3, 8)
    total = frames * padded
    scale = jnp.tile(jnp.pad(logit_scale, (0, SLOT - heads)), frames)[None]
    qgain = jnp.tile(query_gain, heads)[None]
    kgain = jnp.tile(key_gain, heads)[None]
    plane = (total, width)
    double = (2 * total, width)
    narrow = (total, lanes)
    mid, q_hat, k_hat, q_rstd, k_rstd, value, raw, probs, mixed = call(
        functools.partial(attend_kernel, heads=heads, count=count, padded=padded, part=part),
        [
            (plane, BF), (plane, F32), (plane, F32), (narrow, F32), (narrow, F32),
            (plane, BF), (narrow, F32), (narrow, F32), (plane, BF),
        ],
        [(plane, F32), (double, F32), (plane, F32), (narrow, F32)],
        mid, attn_full, qgain, kgain, scale,
    )
    grads, scale_sums, d_raw, d_value = call(
        functools.partial(middle_kernel, heads=heads, count=count, padded=padded),
        [
            ((2, 2, frames // 2, tiles * share, width), BF),
            ((1, lanes), F32), (narrow, F32), (plane, BF),
        ],
        [(plane, F32), (double, F32), (double, F32), (narrow, F32)],
        place, cot_blocks, attn_full, mid, mixed, value, raw, probs, scale,
    )

    chip = (grads[:, 0].astype(F32) + swap(grads[:, 1], "frame").astype(F32)).astype(BF)
    shares = (chip[0].astype(F32) + swap(chip[1], "dp").astype(F32)).astype(BF)
    same_core = [[i for i in range(ranks) if (i // tiles) % 2 == c] for c in (0, 1)]
    shares = lax.all_to_all(
        shares.reshape(ranks // 2, share, width),
        square,
        0,
        0,
        axis_index_groups=same_core,
        tiled=True,
    )
    shares = jnp.sum(shares.astype(F32), axis=0)

    (d_mid,) = call(
        functools.partial(back_kernel, heads=heads, count=count, padded=padded),
        [((frames, padded, width), BF)],
        [(double, F32), (double, F32), (plane, F32)],
        d_raw, q_hat, k_hat, q_rstd, k_rstd, d_value, attn_full, qgain, kgain, scale_sums,
    )
    d_back = lax.all_to_all(d_mid, "frame", 0, 0, tiled=True)
    small = jnp.sum(d_back[:, count : count + 3].astype(F32), axis=(0, 1))
    d_back = d_back[:, :count].reshape(rows, cols, width)
    mid_grad = (cot.astype(F32) + d_back.astype(F32)).astype(BF)

    small = small + swap(small, "tile")
    if clips == 2:
        small = small + swap(small, "dp")
    else:
        small = lax.psum(small, "dp")
        same_clip = [[i for i in range(clips) if i % 2 == c] for c in (0, 1)]
        shares = lax.psum(shares, "dp", axis_index_groups=same_clip)
    theirs = swap(shares, "dp")
    factor = 1.0 / math.sqrt(clips * frames * tiles * tokens)
    value_grad = jnp.where(x == 0, shares, theirs) * factor
    out_proj_grad = jnp.where(x == 0, theirs, shares) * factor
    scale_sum = small[256 : 256 + heads]
    return (
        mid_grad[None, None],
        value_grad,
        out_proj_grad,
        small[:depth] * factor,
        small[128 : 128 + depth] * factor,
        scale_sum * factor,
    )


def solution(mesh):
    in_specs = (
        P("dp", "frame", "tile", None, None),
        P("dp", "frame", "tile", None, None),
        P(),
        P(None, ("frame", "tile"), None),
        P(("frame", "tile"), None),
        P(),
        P(),
        P(),
    )
    out_specs = (
        P("dp", "frame", "tile", None, None),
        P(("frame", "tile"), None),
        P(("frame", "tile"), None),
        P(),
        P(),
        P(),
    )
    return jax.shard_map(local, mesh=mesh, in_specs=in_specs, out_specs=out_specs, check_vma=False)
```

time: 220 us -> 169 us (0.77)
  blocking collectives: 41.9 us -> 0 us
  waiting for transfers between devices: 86.5 us -> 56.1 us
  between operations: 1 us -> 14.4 us
  Pallas kernels: 24.6 us -> 36.1 us
  other arithmetic: 13 us -> 5 us
  local copies, waits for them, and re-layouts: 15.6 us -> 20 us
    psum x1 -> x0, blocking collectives: 41.9 us -> none  [local(): lax.psum((by_head, gains[0], gains[1]), ('dp', 'frame', 'tile'))]
    all_to_all x5 -> x4, waiting for transfers between devices: 46.2 us -> 29.7 us  [the longest x1 12.2 us: local(): lax.all_to_all(mid.reshape(2 * ranks, 2 * third, 3 * part), ('dp',) + squ...]
    ppermute x8 -> x14, waiting for transfers between devices: 40.2 us -> 25.6 us  [swap(): lax.ppermute(x, axis, [(i, i ^ 1) for i in range(lax.axis_size(axis))])]
    unnamed x14 -> x60, local copies, waits for them, and re-layouts: 0.04 us -> 13.9 us
    pallas_call x3 -> x8, Pallas kernels: 24.6 us -> 36.1 us  [call(): pl.pallas_call(kernel, out_shape=[jax.ShapeDtypeStruct(shape, dtype) for...]
    concatenate x3 -> x0, other arithmetic: 6.25 us -> none  [the longest x1 3.3 us: local(): attn = jnp.concatenate([own, swap(own, 'frame')])]
    all_to_all x5 -> x4, starting transfers between devices: 23.1 us -> 17.4 us  [the longest x1 4.84 us: local(): d_back = lax.all_to_all(d_mid, 'frame', 0, 0, tiled=True)]
    another operation x5 -> x1, local copies, waits for them, and re-layouts: 5.3 us -> 0.84 us  [local(): cot.reshape(frames, count, width)]
  transfers between devices with their start and end apart: 14 -> 20, of which waited for: 9 -> 9; matrix products, arithmetic and copies ran while one was open for 9% -> 6% of each run, Pallas kernels for 6% -> 18%
where the time goes in v2:
time: 169 us; the launch traced here: 168 us
  waiting for transfers between devices  56.1 us (33%)
  starting transfers between devices  36.1 us (21%)
  Pallas kernels  36.1 us (21%)
  local copies, waits for them, and re-layouts  20 us (12%)
  between operations  14.4 us (9%)
  other arithmetic  5 us (3%)
    pallas_call x8, Pallas kernels, call(): pl.pallas_call(kernel, out_shape=[jax.ShapeDtypeStruct(shape, dtype) for...  36.1 us
    ppermute x14, waiting for transfers between devices, swap(): lax.ppermute(x, axis, [(i, i ^ 1) for i in range(lax.axis_size(axis))])  25.6 us
    unnamed x60, local copies, waits for them, and re-layouts  13.9 us
    all_to_all x1, waiting for transfers between devices, local(): lax.all_to_all(mid.reshape(2 * ranks, 2 * third, 3 * part), ('dp',) + squ...  12.2 us
    ppermute x14, starting transfers between devices, swap(): lax.ppermute(x, axis, [(i, i ^ 1) for i in range(lax.axis_size(axis))])  11.2 us
    all_to_all x1, waiting for transfers between devices, local(): d_back = lax.all_to_all(d_mid, 'frame', 0, 0, tiled=True)  10.3 us
    all_to_all x1, starting transfers between devices, local(): lax.all_to_all(spread_out.reshape((ranks,) + mine.shape[1:]), square, 0,...  7.56 us
    all_to_all x1, waiting for transfers between devices, local(): lax.all_to_all(shares.reshape(ranks // 2, share, width), square, 0, 0, ax...  7.2 us
  transfers between devices with their start and end apart: 20, of which 9 were waited for; matrix products, arithmetic and copies ran while one was open for 6% of the time, Pallas kernels for 18%

profile of v2, /device:TPU:0, one launch (start us, length us, event | category | flops | bytes accessed | tf_op | source)
XLA Modules:
  0.0 167.7 jit_solution(6242631417017645202)
XLA Ops:
  10.2 7.6 %all-to-all-start = ((bf16[16,3,40,240]{3,2,1,0:T(8,128)(2,1)}), bf16[16,3,40,240]{3,2,1,0:T(8,128)(2,1)}, u32[]{:S(2)}, u32[]{:S(2)}) async-start(bf16[16,3,40,240]{3,2,1,0:T(8,128)(2,1)} %bitcast.5), calls=%async_computation | async-start | bytes 1966080 | tf_op jit(solution)/shard_map/all_to_all | solution.py:374
  19.3 1.9 %collective-permute-start = (bf16[288,640]{1,0:T(8,128)(2,1)S(1)}, bf16[288,640]{1,0:T(8,128)(2,1)S(1)}, u32[]{:S(2)}, u32[]{:S(2)}) collective-permute-start(bf16[288,640]{1,0:T(8,128)(2,1)S(1)} %bitcast.30), channel_id=1, source_target_pairs={{0,1},{1,0},{2,3},{3,2},{4,5},{5,4},{6,7},{7,6},{8,9},{9,8},{10,11... | collective-permute-start | bytes 1105928 | tf_op jit(solution)/shard_map/ppermute | solution.py:20
  21.2 7.5 %collective-permute-done.1.first = bf16[288,640]{1,0:T(8,128)(2,1)S(1)} collective-permute-done((bf16[288,640]{1,0:T(8,128)(2,1)S(1)}, bf16[288,640]{1,0:T(8,128)(2,1)S(1)}, u32[]{:S(2)}, u32[]{:S(2)}) %collective-permute-start.1) | collective-permute-done | bytes 368672 | tf_op jit(solution)/shard_map/ppermute | solution.py:20
  28.7 1.7 %collective-permute-start.2 = (bf16[144,640]{1,0:T(8,128)(2,1)S(1)}, bf16[144,640]{1,0:T(8,128)(2,1)S(1)}, u32[]{:S(2)}, u32[]{:S(2)}) collective-permute-start(bf16[144,640]{1,0:T(8,128)(2,1)S(1)} %slice.44), channel_id=1, source_target_pairs={{0,1},{1,0},{2,3},{3,2},{4,5},{5,4},{6,7},{7,6},{8,9},{9,8},{10,11... | collective-permute-start | bytes 552968 | tf_op jit(solution)/shard_map/ppermute | solution.py:20
  30.4 6.8 %collective-permute-done.rest_0_ = bf16[288,640]{1,0:T(8,128)(2,1)S(1)} collective-permute-done((bf16[288,640]{1,0:T(8,128)(2,1)S(1)}, bf16[288,640]{1,0:T(8,128)(2,1)S(1)}, u32[]{:S(2)}, u32[]{:S(2)}) %collective-permute-start) | collective-permute-done | bytes 368672 | tf_op jit(solution)/shard_map/ppermute | solution.py:20
  39.0 3.7 %collective-permute-done.2.rest_0_ = bf16[144,640]{1,0:T(8,128)(2,1)S(1)} collective-permute-done((bf16[144,640]{1,0:T(8,128)(2,1)S(1)}, bf16[144,640]{1,0:T(8,128)(2,1)S(1)}, u32[]{:S(2)}, u32[]{:S(2)}) %collective-permute-start.2) | collective-permute-done | bytes 184352 | tf_op jit(solution)/shard_map/ppermute | solution.py:20
  42.8 1.7 %collective-permute-done.3.rest_1_ = bf16[144,640]{1,0:T(8,128)(2,1)} collective-permute-done((bf16[144,640]{1,0:T(8,128)(2,1)S(1)}, bf16[144,640]{1,0:T(8,128)(2,1)}, u32[]{:S(2)}, u32[]{:S(2)}) %collective-permute-start.3) | collective-permute-done | bytes 184352 | tf_op jit(solution)/shard_map/ppermute | solution.py:20
  44.6 1.7 %shard_map.127 = (bf16[640,640]{1,0:T(8,128)(2,1)S(1)}, bf16[576,80]{1,0:T(8,128)(2,1)S(1)}) custom-call(s32[4]{0:T(128)S(1)} %pad_add_fusion.place, f32[1,640]{1,0:T(1,128)S(1)} %broadcast_in_dim.13.gain, bf16[288,640]{1,0:T(8,128)(2,1)S(1)} %bitcast.32, bf16[288,640]{1,0:T(8,128)(2,1)S(1)} %collective-permute-done.rest_0_), custom_call_target="tpu_custom_call" | custom-call | tf_op jit(solution)/shard_map/pallas_call | solution.py:339
  46.3 2.1 %shard_map.128 = (bf16[640,640]{1,0:T(8,128)(2,1)S(1)}, bf16[576,80]{1,0:T(8,128)(2,1)S(1)}) custom-call(s32[4]{0:T(128)S(1)} %pad_add_fusion.place, f32[1,640]{1,0:T(1,128)S(1)} %broadcast_in_dim.13.gain, bf16[288,640]{1,0:T(8,128)(2,1)S(1)} %collective-permute-done.1.first, bf16[144,640]{1,0:T(8,128)(2,1)S(1)} %collective-permute-done.2.rest_0_, ...), custom_call_target="tpu_custom_call" | custom-call | tf_op jit(solution)/shard_map/pallas_call | solution.py:339
  49.1 2.3 %shard_map.129 = (bf16[640,640]{1,0:T(8,128)(2,1)S(1)}, bf16[576,80]{1,0:T(8,128)(2,1)S(1)}) custom-call(s32[4]{0:T(128)S(1)} %pad_add_fusion.place, f32[1,640]{1,0:T(1,128)S(1)} %broadcast_in_dim.13.gain, bf16[288,640]{1,0:T(8,128)(2,1)} %collective-permute-done.4.first, bf16[288,640]{1,0:T(8,128)(2,1)} %collective-permute-done.5.rest_0_), custom_call_target="tpu_custom_call" | custom-call | tf_op jit(solution)/shard_map/pallas_call | solution.py:339
  52.4 2.3 %shard_map.130 = (bf16[640,640]{1,0:T(8,128)(2,1)S(1)}, bf16[576,80]{1,0:T(8,128)(2,1)S(1)}) custom-call(s32[4]{0:T(128)S(1)} %pad_add_fusion.place, f32[1,640]{1,0:T(1,128)S(1)} %broadcast_in_dim.13.gain, bf16[288,640]{1,0:T(8,128)(2,1)} %collective-permute-done.6.first, bf16[144,640]{1,0:T(8,128)(2,1)} %collective-permute-done.7.rest_0_, ...), custom_call_target="tpu_custom_call" | custom-call | tf_op jit(solution)/shard_map/pallas_call | solution.py:339
  57.3 4.3 %shard_map.131 = bf16[2,8,2,2,12,240]{5,4,3,2,1,0:T(8,128)(2,1)S(1)} custom-call(s32[4]{0:T(128)S(1)} %pad_add_fusion.place, bf16[3,640,240]{2,1,0:T(8,128)(2,1)S(1)} %bitcast.28, bf16[640,640]{1,0:T(8,128)(2,1)S(1)} %get-tuple-element.29.refs_0_, bf16[640,640]{1,0:T(8,128)(2,1)S(1)} %get-tuple-element.30.refs_1_, bf16[640,640]{1,0:T(8,128)(2,1)S(1)} %copy-done.6, ...), custom_call_target="tpu_custom_call" | custom-call | tf_op jit(solution)/shard_map/pallas_call | solution.py:339
  62.6 4.3 %all-to-all-start.1 = ((bf16[32,24,240]{2,1,0:T(8,128)(2,1)}), bf16[32,24,240]{2,1,0:T(8,128)(2,1)S(1)}, u32[]{:S(2)}, u32[]{:S(2)}) async-start(bf16[32,24,240]{2,1,0:T(8,128)(2,1)} %reshape.60), calls=%async_computation.1 | async-start | bytes 786432 | tf_op jit(solution)/shard_map/all_to_all | solution.py:417
  67.8 12.2 %all-to-all-done.1 = bf16[32,24,240]{2,1,0:T(8,128)(2,1)S(1)} async-done(((bf16[32,24,240]{2,1,0:T(8,128)(2,1)}), bf16[32,24,240]{2,1,0:T(8,128)(2,1)S(1)}, u32[]{:S(2)}, u32[]{:S(2)}) %all-to-all-start.1) | async-done | bytes 368672 | tf_op jit(solution)/shard_map/all_to_all | solution.py:417
  80.3 3.6 %all-to-all-start.2 = ((bf16[8,36,640]{2,1,0:T(8,128)(2,1)}), bf16[8,36,640]{2,1,0:T(8,128)(2,1)S(1)}, u32[]{:S(2)}, u32[]{:S(2)}) async-start(bf16[8,36,640]{2,1,0:T(8,128)(2,1)} %reshape_squeeze.6), calls=%async_computation.2 | async-start | bytes 819200 | tf_op jit(solution)/shard_map/all_to_all | solution.py:427
  84.5 8.2 %shard_map.132 = (bf16[320,640]{1,0:T(8,128)(2,1)S(1)}, f32[320,640]{1,0:T(8,128)S(1)}, f32[320,640]{1,0:T(8,128)S(1)}, f32[320,128]{1,0:T(8,128)S(1)}, f32[320,...) custom-call(bf16[2,4,2,2,2,12,240]{6,5,4,3,2,1,0:T(8,128)(2,1)S(1)} , ...), custom_call_target="tpu_custom_call" | custom-call | tf_op jit(solution)/shard_map/pallas_call | solution.py:339
  102.5 6.5 %shard_map.133 = (bf16[2,2,4,80,640]{4,3,2,1,0:T(8,128)(2,1)S(1)}, f32[1,128]{1,0:T(1,128)S(1)}, f32[320,128]{1,0:T(8,128)S(1)}, bf16[320,640]{1,0:T(8,128)(2,1)S(1)}) custom-call(s32[4]{0:T(128)S(1)} %pad_add_fusion.place, bf16[8,36,640]{2,1,0:T(8,128)(2,1)S(1)} %all-to-all-done.2.cot_in, bf16[640,2560]{1,0:T(8,128)(2,1)} %all-gather.2.cloned.1.call-done.weights, ...), custom_call_target="tpu_custom_call" | custom-call | tf_op jit(solution)/shard_map/pallas_call | solution.py:339
  110.5 8.5 %shard_map.134 = bf16[8,40,640]{2,1,0:T(8,128)(2,1)} custom-call(f32[320,128]{1,0:T(8,128)S(1)} %get-tuple-element.44.d_raw, f32[320,640]{1,0:T(8,128)S(1)} %copy-done.2, f32[320,640]{1,0:T(8,128)S(1)} %copy-done.4, f32[320,128]{1,0:T(8,128)S(1)} %copy-done.15, f32[320,128]{1,0:T(8,128)S(1)} %copy-done.17, bf16[320,640]{1,0:T(8,128)(2,1)S(1)} %get-tuple-element.49.d_value, ...), custom_call_target="tpu_custom_call" | custom-call | tf_op jit(solution)/shard_map/pallas_call | solution.py:339
  118.9 4.8 %all-to-all-start.3 = ((bf16[8,40,640]{2,1,0:T(8,128)(2,1)}), bf16[8,40,640]{2,1,0:T(8,128)(2,1)S(1)}, u32[]{:S(2)}, u32[]{:S(2)}) async-start(bf16[8,40,640]{2,1,0:T(8,128)(2,1)} %shard_map.134), calls=%async_computation.3 | async-start | bytes 819200 | tf_op jit(solution)/shard_map/all_to_all | solution.py:476
  126.3 10.3 %all-to-all-done.3 = bf16[8,40,640]{2,1,0:T(8,128)(2,1)S(1)} async-done(((bf16[8,40,640]{2,1,0:T(8,128)(2,1)}), bf16[8,40,640]{2,1,0:T(8,128)(2,1)S(1)}, u32[]{:S(2)}, u32[]{:S(2)}) %all-to-all-start.3) | async-done | bytes 409632 | tf_op jit(solution)/shard_map/all_to_all | solution.py:476
  139.1 4.6 %all-to-all-start.4 = ((bf16[8,40,640]{2,1,0:T(8,128)(2,1)}), bf16[8,40,640]{2,1,0:T(8,128)(2,1)S(1)}, u32[]{:S(2)}, u32[]{:S(2)}) async-start(bf16[8,40,640]{2,1,0:T(8,128)(2,1)} %bitcast.13), calls=%async_computation.4 | async-start | bytes 819200 | tf_op jit(solution)/shard_map/all_to_all | solution.py:460
  145.4 2.2 %collective-permute-done.13 = f32[640]{0:T(1024)S(1)} collective-permute-done((f32[640]{0:T(1024)S(1)}, f32[640]{0:T(1024)S(1)}, u32[]{:S(2)}, u32[]{:S(2)}) %collective-permute-start.13) | collective-permute-done | bytes 2592 | tf_op jit(solution)/shard_map/ppermute | solution.py:20
  148.1 7.2 %all-to-all-done.4 = bf16[8,40,640]{2,1,0:T(8,128)(2,1)S(1)} async-done(((bf16[8,40,640]{2,1,0:T(8,128)(2,1)}), bf16[8,40,640]{2,1,0:T(8,128)(2,1)S(1)}, u32[]{:S(2)}, u32[]{:S(2)}) %all-to-all-start.4) | async-done | bytes 409632 | tf_op jit(solution)/shard_map/all_to_all | solution.py:460
  156.5 3.6 %collective-permute-done.11 = f32[40,640]{1,0:T(8,128)S(1)} collective-permute-done((f32[40,640]{1,0:T(8,128)S(1)}, f32[40,640]{1,0:T(8,128)S(1)}, u32[]{:S(2)}, u32[]{:S(2)}) %collective-permute-start.11) | collective-permute-done | bytes 102432 | tf_op jit(solution)/shard_map/ppermute | solution.py:20
  (121 shorter events, 33.3 us)
Async XLA Ops:
  7.2 77.3 %all-gather.2.cloned.1.call-start = ((), (), s32[]{:S(2)}) async-start(), calls=%async_computation.5 | async-start | bytes 3481600 | tf_op jit(solution)/shard_map/all_gather | solution.py:376
  10.2 34.3 %copy-start.26 = (f32[640]{0:T(1024)S(1)}, f32[640]{0:T(1024)}, u32[]{:S(2)}) copy-start(f32[640]{0:T(1024)} %param.10) | copy-start | bytes 7684
  10.2 45.4 %all-to-all-start = ((bf16[16,3,40,240]{3,2,1,0:T(8,128)(2,1)}), bf16[16,3,40,240]{3,2,1,0:T(8,128)(2,1)}, u32[]{:S(2)}, u32[]{:S(2)}) async-start(bf16[16,3,40,240]{3,2,1,0:T(8,128)(2,1)} %bitcast.5), calls=%async_computation | async-start | bytes 1966080 | tf_op jit(solution)/shard_map/all_to_all | solution.py:374
  17.7 10.9 %collective-permute-start.1 = (bf16[288,640]{1,0:T(8,128)(2,1)S(1)}, bf16[288,640]{1,0:T(8,128)(2,1)S(1)}, u32[]{:S(2)}, u32[]{:S(2)}) collective-permute-start(bf16[288,640]{1,0:T(8,128)(2,1)S(1)} %bitcast.29), channel_id=1, source_target_pairs={{0,16},{16,0},{1,17},{17,1},{2,18},{18,2},{3,19},{19,3},{4,20},{20... | collective-permute-start | bytes 1105928 | tf_op jit(solution)/shard_map/ppermute | solution.py:20
  19.3 17.9 %collective-permute-start = (bf16[288,640]{1,0:T(8,128)(2,1)S(1)}, bf16[288,640]{1,0:T(8,128)(2,1)S(1)}, u32[]{:S(2)}, u32[]{:S(2)}) collective-permute-start(bf16[288,640]{1,0:T(8,128)(2,1)S(1)} %bitcast.30), channel_id=1, source_target_pairs={{0,1},{1,0},{2,3},{3,2},{4,5},{5,4},{6,7},{7,6},{8,9},{9,8},{10,11... | collective-permute-start | bytes 1105928 | tf_op jit(solution)/shard_map/ppermute | solution.py:20
  21.2 27.9 %collective-permute-start.4 = (bf16[288,640]{1,0:T(8,128)(2,1)S(1)}, bf16[288,640]{1,0:T(8,128)(2,1)}, u32[]{:S(2)}, u32[]{:S(2)}) collective-permute-start(bf16[288,640]{1,0:T(8,128)(2,1)S(1)} %bitcast.31), channel_id=1, source_target_pairs={{0,2},{2,0},{4,6},{6,4},{8,10},{10,8},{12,14},{14,12},{1,3},{3,1},... | collective-permute-start | bytes 1105928 | tf_op jit(solution)/shard_map/ppermute | solution.py:20
  28.7 14.1 %collective-permute-start.2 = (bf16[144,640]{1,0:T(8,128)(2,1)S(1)}, bf16[144,640]{1,0:T(8,128)(2,1)S(1)}, u32[]{:S(2)}, u32[]{:S(2)}) collective-permute-start(bf16[144,640]{1,0:T(8,128)(2,1)S(1)} %slice.44), channel_id=1, source_target_pairs={{0,1},{1,0},{2,3},{3,2},{4,5},{5,4},{6,7},{7,6},{8,9},{9,8},{10,11... | collective-permute-start | bytes 552968 | tf_op jit(solution)/shard_map/ppermute | solution.py:20
  37.3 11.9 %collective-permute-start.5 = (bf16[288,640]{1,0:T(8,128)(2,1)S(1)}, bf16[288,640]{1,0:T(8,128)(2,1)}, u32[]{:S(2)}, u32[]{:S(2)}) collective-permute-start(bf16[288,640]{1,0:T(8,128)(2,1)S(1)} %collective-permute-done.rest_0_), channel_id=1, source_target_pairs={{0,2},{2,0},{4,6},{6,4},{8,10},{10,8},{12,14},{14,12},{1,3},{3,1},... | collective-permute-start | bytes 1105928 | tf_op jit(solution)/shard_map/ppermute | solution.py:20
  37.3 7.2 %collective-permute-start.3 = (bf16[144,640]{1,0:T(8,128)(2,1)S(1)}, bf16[144,640]{1,0:T(8,128)(2,1)}, u32[]{:S(2)}, u32[]{:S(2)}) collective-permute-start(bf16[144,640]{1,0:T(8,128)(2,1)S(1)} %slice.45), channel_id=1, source_target_pairs={{0,16},{16,0},{1,17},{17,1},{2,18},{18,2},{3,19},{19,3},{4,20},{20... | collective-permute-start | bytes 552968 | tf_op jit(solution)/shard_map/ppermute | solution.py:20
  38.8 13.5 %collective-permute-start.6 = (bf16[288,640]{1,0:T(8,128)(2,1)S(1)}, bf16[288,640]{1,0:T(8,128)(2,1)}, u32[]{:S(2)}, u32[]{:S(2)}) collective-permute-start(bf16[288,640]{1,0:T(8,128)(2,1)S(1)} %collective-permute-done.1.first), channel_id=1, source_target_pairs={{0,2},{2,0},{4,6},{6,4},{8,10},{10,8},{12,14},{14,12},{1,3},{3,1},... | collective-permute-start | bytes 1105928 | tf_op jit(solution)/shard_map/ppermute | solution.py:20
  42.8 9.6 %collective-permute-start.7 = (bf16[144,640]{1,0:T(8,128)(2,1)S(1)}, bf16[144,640]{1,0:T(8,128)(2,1)}, u32[]{:S(2)}, u32[]{:S(2)}) collective-permute-start(bf16[144,640]{1,0:T(8,128)(2,1)S(1)} %collective-permute-done.2.rest_0_), channel_id=1, source_target_pairs={{0,2},{2,0},{4,6},{6,4},{8,10},{10,8},{12,14},{14,12},{1,3},{3,1},... | collective-permute-start | bytes 552968 | tf_op jit(solution)/shard_map/ppermute | solution.py:20
  44.5 7.9 %collective-permute-start.8 = (bf16[144,640]{1,0:T(8,128)(2,1)}, bf16[144,640]{1,0:T(8,128)(2,1)}, u32[]{:S(2)}, u32[]{:S(2)}) collective-permute-start(bf16[144,640]{1,0:T(8,128)(2,1)} %collective-permute-done.3.rest_1_), channel_id=1, source_target_pairs={{0,2},{2,0},{4,6},{6,4},{8,10},{10,8},{12,14},{14,12},{1,3},{3,1},... | collective-permute-start | bytes 552968 | tf_op jit(solution)/shard_map/ppermute | solution.py:20
  62.6 17.4 %all-to-all-start.1 = ((bf16[32,24,240]{2,1,0:T(8,128)(2,1)}), bf16[32,24,240]{2,1,0:T(8,128)(2,1)S(1)}, u32[]{:S(2)}, u32[]{:S(2)}) async-start(bf16[32,24,240]{2,1,0:T(8,128)(2,1)} %reshape.60), calls=%async_computation.1 | async-start | bytes 786432 | tf_op jit(solution)/shard_map/all_to_all | solution.py:417
  66.9 17.0 %copy-start.27 = (f32[64]{0:T(128)S(1)}, f32[64]{0:T(128)}, u32[]{:S(2)}) copy-start(f32[64]{0:T(128)} %param.14) | copy-start | bytes 772
  66.9 17.1 %copy-start.28 = (f32[64]{0:T(128)S(1)}, f32[64]{0:T(128)}, u32[]{:S(2)}) copy-start(f32[64]{0:T(128)} %param.13) | copy-start | bytes 772
  66.9 17.2 %copy-start.29 = (f32[10]{0:T(128)S(1)}, f32[10]{0:T(128)}, u32[]{:S(2)}) copy-start(f32[10]{0:T(128)} %param.15) | copy-start | bytes 124
  80.3 18.4 %all-to-all-start.2 = ((bf16[8,36,640]{2,1,0:T(8,128)(2,1)}), bf16[8,36,640]{2,1,0:T(8,128)(2,1)S(1)}, u32[]{:S(2)}, u32[]{:S(2)}) async-start(bf16[8,36,640]{2,1,0:T(8,128)(2,1)} %reshape_squeeze.6), calls=%async_computation.2 | async-start | bytes 819200 | tf_op jit(solution)/shard_map/all_to_all | solution.py:427
  109.2 14.6 %collective-permute-start.9 = (bf16[2,4,80,640]{3,2,1,0:T(8,128)(2,1)S(1)}, bf16[2,4,80,640]{3,2,1,0:T(8,128)(2,1)}, u32[]{:S(2)}, u32[]{:S(2)}) collective-permute-start(bf16[2,4,80,640]{3,2,1,0:T(8,128)(2,1)S(1)} %slice_bitcast_fusion.1), channel_id=1, source_target_pairs={{0,2},{2,0},{4,6},{6,4},{8,10},{10,8},{12,14},{14,12},{1,3},{3,1},... | collective-permute-start | bytes 2457608 | tf_op jit(solution)/shard_map/ppermute | solution.py:20
  118.9 17.7 %all-to-all-start.3 = ((bf16[8,40,640]{2,1,0:T(8,128)(2,1)}), bf16[8,40,640]{2,1,0:T(8,128)(2,1)S(1)}, u32[]{:S(2)}, u32[]{:S(2)}) async-start(bf16[8,40,640]{2,1,0:T(8,128)(2,1)} %shard_map.134), calls=%async_computation.3 | async-start | bytes 819200 | tf_op jit(solution)/shard_map/all_to_all | solution.py:476
  125.2 13.1 %collective-permute-start.10 = (bf16[4,80,640]{2,1,0:T(8,128)(2,1)S(1)}, bf16[4,80,640]{2,1,0:T(8,128)(2,1)S(1)}, u32[]{:S(2)}, u32[]{:S(2)}) collective-permute-start(bf16[4,80,640]{2,1,0:T(8,128)(2,1)S(1)} %slice_bitcast_fusion.2), channel_id=1, source_target_pairs={{0,16},{16,0},{1,17},{17,1},{2,18},{18,2},{3,19},{19,3},{4,20},{20... | collective-permute-start | bytes 1228808 | tf_op jit(solution)/shard_map/ppermute | solution.py:20
  136.7 7.2 %collective-permute-start.12 = (f32[640]{0:T(1024)S(1)}, f32[640]{0:T(1024)S(1)}, u32[]{:S(2)}, u32[]{:S(2)}) collective-permute-start(f32[640]{0:T(1024)S(1)} %convert_reduce_fusion.1), channel_id=1, source_target_pairs={{0,1},{1,0},{2,3},{3,2},{4,5},{5,4},{6,7},{7,6},{8,9},{9,8},{10,11... | collective-permute-start | bytes 7688 | tf_op jit(solution)/shard_map/ppermute | solution.py:20
  139.1 16.2 %all-to-all-start.4 = ((bf16[8,40,640]{2,1,0:T(8,128)(2,1)}), bf16[8,40,640]{2,1,0:T(8,128)(2,1)S(1)}, u32[]{:S(2)}, u32[]{:S(2)}) async-start(bf16[8,40,640]{2,1,0:T(8,128)(2,1)} %bitcast.13), calls=%async_computation.4 | async-start | bytes 819200 | tf_op jit(solution)/shard_map/all_to_all | solution.py:460
  143.9 3.7 %collective-permute-start.13 = (f32[640]{0:T(1024)S(1)}, f32[640]{0:T(1024)S(1)}, u32[]{:S(2)}, u32[]{:S(2)}) collective-permute-start(f32[640]{0:T(1024)S(1)} %add.42), channel_id=1, source_target_pairs={{0,16},{16,0},{1,17},{17,1},{2,18},{18,2},{3,19},{19,3},{4,20},{20... | collective-permute-start | bytes 7688 | tf_op jit(solution)/shard_map/ppermute | solution.py:20
  155.4 4.7 %collective-permute-start.11 = (f32[40,640]{1,0:T(8,128)S(1)}, f32[40,640]{1,0:T(8,128)S(1)}, u32[]{:S(2)}, u32[]{:S(2)}) collective-permute-start(f32[40,640]{1,0:T(8,128)S(1)} %convert_reduce_fusion), channel_id=1, source_target_pairs={{0,16},{16,0},{1,17},{17,1},{2,18},{18,2},{3,19},{19,3},{4,20},{20... | collective-permute-start | bytes 307208 | tf_op jit(solution)/shard_map/ppermute | solution.py:20
  (26 other events, 60.0 us)
Sparse Core Ops, SparseCore 0:
  10.3 58.5 all-gather.1

commit v3 on v2

--- a/solution.py
+++ b/solution.py
@@ -13,7 +13,6 @@
 SLOT = 16
 BF = jnp.bfloat16
 F32 = jnp.float32
-VMEM_BYTES = 48 * 1024 * 1024
 
 
 def swap(x, axis):
@@ -79,67 +78,81 @@
             body(i)
 
 
-def act_kernel(place, gain, first, *rest, cols, part):
-    second, (act, kept) = (rest[:-2], rest[-2:])
-    half, width = first.shape
+def act_kernel(place, gain, *refs, cols, part):
+    blocks, (acts, kept) = (refs[:-2], refs[-2:])
+    half, width = blocks[0].shape
     tile, chosen = (place[2], place[3])
-    upper = first[...]
-    lower = jnp.concatenate([ref[...] for ref in second], axis=0) if len(second) > 1 else second[0][...]
-    upper, lower = (jnp.where(tile == 0, upper, lower), jnp.where(tile == 0, lower, upper))
-    kept[pl.ds(0, half), :] = dot(upper, picker(width, part, 1, -part * chosen)).astype(BF)
-    kept[pl.ds(half, half), :] = dot(lower, picker(width, part, 1, -part * chosen)).astype(BF)
-    upper, lower = (upper.astype(F32), lower.astype(F32))
-    total = jnp.sum(upper, axis=0, keepdims=True) + jnp.sum(lower, axis=0, keepdims=True)
-    square = jnp.sum(upper * upper, axis=0, keepdims=True)
-    square = square + jnp.sum(lower * lower, axis=0, keepdims=True)
-    both = jnp.concatenate([total, square, jnp.zeros((6, width), F32)], axis=0)
-    high, low = halves(both)
-    lowest = (both - high.astype(F32) - low.astype(F32)).astype(BF)
+    choice = picker(width, part, 1, -part * chosen)
     per_group = width // GROUPS
     pick = picker(width, 128, per_group, 0)
     back = spreader(128, width, per_group, 0)
+
+    def thirds(x):
+        high, low = halves(x)
+        return high, low, (x - high.astype(F32) - low.astype(F32)).astype(BF)
+
+    totals, squares = ([], [])
+    for frame in range(4):
+        total, square = (0.0, 0.0)
+        for dy in (0, 1):
+            x = blocks[2 * frame + dy][...]
+            start = pl.multiple_of((tile ^ dy) * half, half)
+            kept[frame, pl.ds(start, half), :] = dot(x, choice).astype(BF)
+            x = x.astype(F32)
+            total = total + jnp.sum(x, axis=0, keepdims=True)
+            square = square + jnp.sum(x * x, axis=0, keepdims=True)
+        totals.append(total)
+        squares.append(square)
+    high, low, lowest = thirds(jnp.concatenate(totals + squares, axis=0))
     both = (dot(high, pick) + dot(low, pick) + dot(lowest, pick)) / (2 * half * per_group)
-    mean = both[0:1]
-    rstd = lax.rsqrt(both[1:2] - mean * mean + EPS)
-    both = jnp.concatenate([mean, rstd, jnp.zeros((6, 128), F32)], axis=0)
-    high, low = halves(both)
-    lowest = (both - high.astype(F32) - low.astype(F32)).astype(BF)
+    mean = both[0:4]
+    rstd = lax.rsqrt(both[4:8] - mean * mean + EPS)
+    high, low, lowest = thirds(jnp.concatenate([mean, rstd], axis=0))
     both = dot(high, back) + dot(low, back) + dot(lowest, back)
-    mean = both[0:1]
-    scale = both[1:2] * gain[...]
-    act[pl.ds(0, cols), :] = jnp.zeros((cols, width), BF)
-    act[pl.ds(cols + 2 * half, cols), :] = jnp.zeros((cols, width), BF)
-    for start, x in ((cols, upper), (cols + half, lower)):
-        zed = (x - mean) * scale
-        act[pl.ds(start, half), :] = (zed / (1.0 + jnp.exp(-zed))).astype(BF)
-
-
-def conv_kernel(place, weights, *refs, cols, part, blocks, count):
-    acts, kept, out = (refs[:4], refs[4:8], refs[8])
+    scales = both[4:8] * gain[...]
+    for frame in range(4):
+        acts[frame, pl.ds(0, cols), :] = jnp.zeros((cols, width), BF)
+        acts[frame, pl.ds(cols + 2 * half, cols), :] = jnp.zeros((cols, width), BF)
+        for dy in (0, 1):
+            x = blocks[2 * frame + dy][...].astype(F32)
+            zed = (x - both[frame : frame + 1]) * scales[frame : frame + 1]
+            start = pl.multiple_of(cols + (tile ^ dy) * half, cols)
+            acts[frame, pl.ds(start, half), :] = (zed / (1.0 + jnp.exp(-zed))).astype(BF)
+
+
+def conv_kernel(place, weights, acts, kept, out, *, cols, part, blocks, count):
     x, core = (place[0], place[1])
-    whole = kept[0].shape[0]
+    whole = kept.shape[1]
     half = whole // 2
     third = count // 3
     col = lax.broadcasted_iota(jnp.int32, (whole, part), 0) % cols
-    for dc in (0, 1):
-        for dx in (0, 1):
-            act, plus = (acts[2 * dc + dx], kept[2 * dc + dx])
-            taps = dot(act[pl.ds(0, whole), :], weights[0])
-            taps += dot(act[pl.ds(cols, whole), :], weights[1])
-            taps += dot(act[pl.ds(2 * cols, whole), :], weights[2])
+    for dx in (0, 1):
+        mids = []
+        for dc in (0, 1):
+            frame = 2 * dc + dx
+            taps = dot(acts[frame, pl.ds(0, whole), :], weights[0])
+            taps += dot(acts[frame, pl.ds(cols, whole), :], weights[1])
+            taps += dot(acts[frame, pl.ds(2 * cols, whole), :], weights[2])
             left = pltpu.roll(taps[:, :part], 1, 0)
             right = pltpu.roll(taps[:, 2 * part :], whole - 1, 0)
             pre = taps[:, part : 2 * part] + jnp.where(col > 0, left, 0.0)
             pre = pre + jnp.where(col < cols - 1, right, 0.0)
-            mid = (plus[...].astype(F32) + pre).astype(BF)
-            if blocks > 8:
-                out[x ^ dx, core ^ dc] = mid
-                continue
+            mids.append((kept[frame].astype(F32) + pre).astype(BF))
+        if blocks > 8:
+            for dc in (0, 1):
+                out[x ^ dx, dc] = mids[dc]
+            continue
+        for f in range(blocks):
             for t in (0, 1):
-                for f in range(blocks):
-                    start = t * half + f * count
-                    three = [mid[start + third * j : start + third * (j + 1)] for j in range(3)]
-                    out[x ^ dx, f, t, core ^ dc] = jnp.concatenate(three, axis=1)
+                start = t * half + f * count
+                rows = [
+                    jnp.concatenate(
+                        [mid[start + third * j : start + third * (j + 1)] for j in range(3)], axis=1
+                    )
+                    for mid in mids
+                ]
+                index = ((x ^ dx) * blocks + f) * 2 + t
+                out[index] = jnp.concatenate(rows, axis=0)
 
 
 def attend_kernel(
@@ -157,7 +170,12 @@
 
     def unpack(z):
         for e in (0, 1):
-            blocks = [mid_in[x, z, c, t, e] for x in (0, 1) for c in (0, 1) for t in (0, 1)]
+            blocks = [
+                mid_in[(x * frames + 2 * z + c) * 2 + t, pl.ds((e ^ c) * third, third), :]
+                for x in (0, 1)
+                for c in (0, 1)
+                for t in (0, 1)
+            ]
             for j in range(3):
                 piece = [b[:, j * part : (j + 1) * part] for b in blocks]
                 start = (2 * z + e) * padded + j * third
@@ -225,7 +243,7 @@
     frames = total // padded
     depth = width // heads
     lanes = scale.shape[-1]
-    x, core = (place[0], place[1])
+    x, core, tile, plane = (place[0], place[1], place[2], place[4])
     cot_s[...] = jnp.zeros_like(cot_s)
 
     def unpack(f):
@@ -233,13 +251,15 @@
 
     each(frames, unpack)
     cot = cot_s[...].astype(BF)
-    rows = grads.shape[3]
+    rows = grads.shape[4]
 
     def store(kind, term):
         for z in range(frames // 2):
             for c in (0, 1):
-                start = (2 * z + c) * rows
-                grads[x ^ kind, core ^ c, z] = term[start : start + rows]
+                for t in (0, 1):
+                    start = (4 * z + 2 * c + t) * rows
+                    block = term[start : start + rows]
+                    grads[x ^ kind, core ^ c, tile ^ t, plane ^ z] = block
 
     store(1, dot_rows(mixed[...], cot).astype(BF))
     d_mixed = dot_t(cot, weights[:, pl.ds(3 * width, width)]).astype(BF).astype(F32)
@@ -333,7 +353,7 @@
         d_mid[f] = jnp.concatenate([tokens, spare], axis=0).astype(BF)
 
 
-def call(kernel, outs, scratch, *args):
+def call(kernel, mebibytes, outs, scratch, *args):
     smem = pl.BlockSpec(memory_space=pltpu.SMEM)
     vmem = pl.BlockSpec(memory_space=pltpu.VMEM)
     return pl.pallas_call(
@@ -342,7 +362,7 @@
         in_specs=[smem if arg.dtype == jnp.int32 else vmem for arg in args],
         out_specs=[vmem] * len(outs),
         scratch_shapes=[pltpu.VMEM(shape, dtype) for shape, dtype in scratch],
-        compiler_params=pltpu.CompilerParams(vmem_limit_bytes=VMEM_BYTES),
+        compiler_params=pltpu.CompilerParams(vmem_limit_bytes=mebibytes << 20),
     )(*args)
 
 
@@ -365,63 +385,54 @@
     x = lax.axis_index("dp") % 2
     core = lax.axis_index("frame") % 2
     tile = lax.axis_index("tile")
-    place = jnp.stack([x, core, tile, 4 * x + 2 * core + tile]).astype(jnp.int32)
+    plane = lax.axis_index("frame") // 2
+    place = jnp.stack([x, core, tile, 4 * x + 2 * core + tile, plane]).astype(jnp.int32)
+    flat = source.reshape(tokens, width)
 
     mine = lax.dynamic_slice_in_dim(conv_weight, x * (width // 2), width // 2, axis=2)
     mine = mine.reshape(3, 3, share, 4, part).transpose(3, 0, 2, 1, 4)
     mine = mine.reshape(4, 3, share, 3 * part)
+    mine, _ = lax.optimization_barrier((mine, swap(flat[:8, :128], "dp")))
     spread_out = jnp.broadcast_to(mine[None], (frames // 2,) + mine.shape)
     conv_in = lax.all_to_all(spread_out.reshape((ranks,) + mine.shape[1:]), square, 0, 0, tiled=True)
     conv_full = conv_in.transpose(1, 0, 2, 3).reshape(3, width, 3 * part)
     attn_full = lax.all_gather(attn_weight, square, axis=0, tiled=True)
 
-    flat = source.reshape(tokens, width)
     half = tokens // 2
     along_x = swap(flat, "dp")
     along_y = swap(flat, "tile")
-    across = (swap(along_x[:half], "tile"), swap(along_y[half:], "dp"))
-    own = ((flat, along_y), (along_x,) + across)
-    gain = norm_gain[None]
-    acts, kept = ([], [])
-    for other in (False, True):
-        for pieces in own:
-            if other:
-                pieces = [swap(piece, "frame") for piece in pieces]
-            act, keep = call(
-                functools.partial(act_kernel, cols=cols, part=part),
-                [((tiles * tokens + 2 * cols, width), BF), ((tiles * tokens, part), BF)],
-                [],
-                place,
-                gain,
-                *pieces,
-            )
-            acts.append(act)
-            kept.append(keep)
-
-    blocked = (2, frames, tiles, 2, third, 3 * part)
+    across = jnp.concatenate([swap(along_x[:half], "tile"), swap(along_y[half:], "dp")])
+    pieces = [flat, along_y, along_x, across]
+    pieces += [swap(piece, "frame") for piece in pieces]
+    acts, kept = call(
+        functools.partial(act_kernel, cols=cols, part=part),
+        20,
+        [((4, tiles * tokens + 2 * cols, width), BF), ((4, tiles * tokens, part), BF)],
+        [],
+        place,
+        norm_gain[None],
+        *pieces,
+    )
+
+    blocked = (2 * ranks, 2 * third, 3 * part)
     plain = (2, 2, tiles * tokens, part)
     (mid,) = call(
         functools.partial(conv_kernel, cols=cols, part=part, blocks=frames, count=count),
+        16,
         [(plain if frames > 8 else blocked, BF)],
         [],
         place,
         conv_full,
-        *acts,
-        *kept,
+        acts,
+        kept,
     )
     if frames > 8:
         mid = mid.reshape(2, 2, tiles, frames, 3, third, part).transpose(0, 3, 2, 1, 5, 4, 6)
+        mid = mid.reshape(blocked)
     groups = None
     if clips > 2:
         groups = [[2 * ranks * g + i for i in range(2 * ranks)] for g in range(clips // 2)]
-    mid = lax.all_to_all(
-        mid.reshape(2 * ranks, 2 * third, 3 * part),
-        ("dp",) + square,
-        0,
-        0,
-        axis_index_groups=groups,
-        tiled=True,
-    ).reshape(2, frames // 2, 2, tiles, 2, third, 3 * part)
+    mid = lax.all_to_all(mid, ("dp",) + square, 0, 0, axis_index_groups=groups, tiled=True)
 
     cot_blocks, mid = lax.optimization_barrier((cot.reshape(frames, count, width), mid))
     cot_blocks = lax.all_to_all(cot_blocks, "frame", 0, 0, tiled=True)
@@ -432,47 +443,49 @@
     scale = jnp.tile(jnp.pad(logit_scale, (0, SLOT - heads)), frames)[None]
     qgain = jnp.tile(query_gain, heads)[None]
     kgain = jnp.tile(key_gain, heads)[None]
-    plane = (total, width)
+    full = (total, width)
     double = (2 * total, width)
     narrow = (total, lanes)
     mid, q_hat, k_hat, q_rstd, k_rstd, value, raw, probs, mixed = call(
         functools.partial(attend_kernel, heads=heads, count=count, padded=padded, part=part),
+        20,
         [
-            (plane, BF), (plane, F32), (plane, F32), (narrow, F32), (narrow, F32),
-            (plane, BF), (narrow, F32), (narrow, F32), (plane, BF),
+            (full, BF), (full, F32), (full, F32), (narrow, F32), (narrow, F32),
+            (full, BF), (narrow, F32), (narrow, F32), (full, BF),
         ],
-        [(plane, F32), (double, F32), (plane, F32), (narrow, F32)],
+        [(full, F32), (double, F32), (full, F32), (narrow, F32)],
         mid, attn_full, qgain, kgain, scale,
     )
     grads, scale_sums, d_raw, d_value = call(
         functools.partial(middle_kernel, heads=heads, count=count, padded=padded),
+        20,
         [
-            ((2, 2, frames // 2, tiles * share, width), BF),
-            ((1, lanes), F32), (narrow, F32), (plane, BF),
+            ((2, 2, 2, frames // 2, share, width), BF),
+            ((1, lanes), F32), (narrow, F32), (full, BF),
         ],
-        [(plane, F32), (double, F32), (double, F32), (narrow, F32)],
+        [(full, F32), (double, F32), (double, F32), (narrow, F32)],
         place, cot_blocks, attn_full, mid, mixed, value, raw, probs, scale,
     )
-
-    chip = (grads[:, 0].astype(F32) + swap(grads[:, 1], "frame").astype(F32)).astype(BF)
-    shares = (chip[0].astype(F32) + swap(chip[1], "dp").astype(F32)).astype(BF)
-    same_core = [[i for i in range(ranks) if (i // tiles) % 2 == c] for c in (0, 1)]
-    shares = lax.all_to_all(
-        shares.reshape(ranks // 2, share, width),
-        square,
-        0,
-        0,
-        axis_index_groups=same_core,
-        tiled=True,
-    )
-    shares = jnp.sum(shares.astype(F32), axis=0)
-
     (d_mid,) = call(
         functools.partial(back_kernel, heads=heads, count=count, padded=padded),
+        20,
         [((frames, padded, width), BF)],
-        [(double, F32), (double, F32), (plane, F32)],
+        [(double, F32), (double, F32), (full, F32)],
         d_raw, q_hat, k_hat, q_rstd, k_rstd, d_value, attn_full, qgain, kgain, scale_sums,
     )
+
+    def add(mine, theirs):
+        return (mine.astype(F32) + theirs.astype(F32)).astype(BF)
+
+    shares = add(grads[:, 0], swap(grads[:, 1], "frame"))
+    shares = add(shares[0], swap(shares[1], "dp"))
+    shares = add(shares[0], swap(shares[1], "tile"))
+    step = frames // 4
+    while step > 0:
+        pairs = [(i, i ^ (2 * step)) for i in range(frames)]
+        shares = add(shares[:step], lax.ppermute(shares[step:], "frame", pairs))
+        step //= 2
+    shares = shares[0]
     d_back = lax.all_to_all(d_mid, "frame", 0, 0, tiled=True)
     small = jnp.sum(d_back[:, count : count + 3].astype(F32), axis=(0, 1))
     d_back = d_back[:, :count].reshape(rows, cols, width)
@@ -485,7 +498,8 @@
         small = lax.psum(small, "dp")
         same_clip = [[i for i in range(clips) if i % 2 == c] for c in (0, 1)]
         shares = lax.psum(shares, "dp", axis_index_groups=same_clip)
-    theirs = swap(shares, "dp")
+    theirs = swap(shares, "dp").astype(F32)
+    shares = shares.astype(F32)
     factor = 1.0 / math.sqrt(clips * frames * tiles * tokens)
     value_grad = jnp.where(x == 0, shares, theirs) * factor
     out_proj_grad = jnp.where(x == 0, theirs, shares) * factor

time: 169 us -> 165 us (0.976)
  Pallas kernels: 36.1 us -> 27.7 us
  local copies, waits for them, and re-layouts: 20 us -> 25.4 us
    pallas_call x8 -> x5, Pallas kernels: 36.1 us -> 27.7 us  [call(): pl.pallas_call(kernel, out_shape=[jax.ShapeDtypeStruct(shape, dtype) for...]
    ppermute x0 -> x2, waiting for transfers between devices: none -> 7.95 us  [local(): shares = add(shares[:step], lax.ppermute(shares[step:], 'frame', pairs))]
    all_to_all x2 -> x1, waiting for transfers between devices: 19.4 us -> 12.3 us  [local(): lax.all_to_all(mid, ('dp',) + square, 0, 0, axis_index_groups=groups, til...]
    unnamed x60 -> x61, local copies, waits for them, and re-layouts: 13.9 us -> 19.8 us
    all_to_all x2 -> x1, starting transfers between devices: 8.9 us -> 4.25 us  [local(): lax.all_to_all(mid, ('dp',) + square, 0, 0, axis_index_groups=groups, til...]
  transfers between devices with their start and end apart: 20 -> 21, of which waited for: 9 -> 11; matrix products, arithmetic and copies ran while one was open for 6% -> 6% of each run, Pallas kernels for 18% -> 14%
where the time goes in v3:
time: 165 us; the launch traced here: 164 us
  waiting for transfers between devices  56.4 us (34%)
  starting transfers between devices  34.5 us (21%)
  Pallas kernels  27.7 us (17%)
  local copies, waits for them, and re-layouts  25.4 us (15%)
  between operations  14.4 us (9%)
  other arithmetic  5.2 us (3%)
    pallas_call x5, Pallas kernels, call(): pl.pallas_call(kernel, out_shape=[jax.ShapeDtypeStruct(shape, dtype) for...  27.7 us
    ppermute x14, waiting for transfers between devices, swap(): lax.ppermute(x, axis, [(i, i ^ 1) for i in range(lax.axis_size(axis))])  25.2 us
    unnamed x61, local copies, waits for them, and re-layouts  19.8 us
    ppermute x14, starting transfers between devices, swap(): lax.ppermute(x, axis, [(i, i ^ 1) for i in range(lax.axis_size(axis))])  12.7 us
    all_to_all x1, waiting for transfers between devices, local(): lax.all_to_all(mid, ('dp',) + square, 0, 0, axis_index_groups=groups, til...  12.3 us
    all_to_all x1, waiting for transfers between devices, local(): d_back = lax.all_to_all(d_mid, 'frame', 0, 0, tiled=True)  10.3 us
    ppermute x2, waiting for transfers between devices, local(): shares = add(shares[:step], lax.ppermute(shares[step:], 'frame', pairs))  7.95 us
    all_to_all x1, starting transfers between devices, local(): lax.all_to_all(spread_out.reshape((ranks,) + mine.shape[1:]), square, 0,...  7.56 us
  transfers between devices with their start and end apart: 21, of which 11 were waited for; matrix products, arithmetic and copies ran while one was open for 6% of the time, Pallas kernels for 14%

profile of v3, /device:TPU:0, one launch (start us, length us, event | category | flops | bytes accessed | tf_op | source)
XLA Modules:
  0.0 163.7 jit_solution(10840515602881712260)
XLA Ops:
  10.2 7.6 %all-to-all-start = ((bf16[16,3,40,240]{3,2,1,0:T(8,128)(2,1)}), bf16[16,3,40,240]{3,2,1,0:T(8,128)(2,1)}, u32[]{:S(2)}, u32[]{:S(2)}) async-start(bf16[16,3,40,240]{3,2,1,0:T(8,128)(2,1)} %bitcast.6), calls=%async_computation | async-start | bytes 1966080 | tf_op jit(solution)/shard_map/all_to_all | solution.py:397
  19.4 1.9 %collective-permute-start = (bf16[288,640]{1,0:T(8,128)(2,1)S(1)}, bf16[288,640]{1,0:T(8,128)(2,1)S(1)}, u32[]{:S(2)}, u32[]{:S(2)}) collective-permute-start(bf16[288,640]{1,0:T(8,128)(2,1)S(1)} %bitcast.37), channel_id=1, source_target_pairs={{0,1},{1,0},{2,3},{3,2},{4,5},{5,4},{6,7},{7,6},{8,9},{9,8},{10,11... | collective-permute-start | bytes 1105928 | tf_op jit(solution)/shard_map/ppermute | solution.py:19
  21.2 7.5 %collective-permute-done.1.refs_2_ = bf16[288,640]{1,0:T(8,128)(2,1)S(1)} collective-permute-done((bf16[288,640]{1,0:T(8,128)(2,1)S(1)}, bf16[288,640]{1,0:T(8,128)(2,1)S(1)}, u32[]{:S(2)}, u32[]{:S(2)}) %collective-permute-start.1) | collective-permute-done | bytes 368672 | tf_op jit(solution)/shard_map/ppermute | solution.py:19
  28.7 1.7 %collective-permute-start.2 = (bf16[144,640]{1,0:T(8,128)(2,1)S(1)}, bf16[144,640]{1,0:T(8,128)(2,1)S(1)}, u32[]{:S(2)}, u32[]{:S(2)}) collective-permute-start(bf16[144,640]{1,0:T(8,128)(2,1)S(1)} %slice.69), channel_id=1, source_target_pairs={{0,1},{1,0},{2,3},{3,2},{4,5},{5,4},{6,7},{7,6},{8,9},{9,8},{10,11... | collective-permute-start | bytes 552968 | tf_op jit(solution)/shard_map/ppermute | solution.py:19
  30.5 6.8 %collective-permute-done.refs_1_ = bf16[288,640]{1,0:T(8,128)(2,1)S(1)} collective-permute-done((bf16[288,640]{1,0:T(8,128)(2,1)S(1)}, bf16[288,640]{1,0:T(8,128)(2,1)S(1)}, u32[]{:S(2)}, u32[]{:S(2)}) %collective-permute-start) | collective-permute-done | bytes 368672 | tf_op jit(solution)/shard_map/ppermute | solution.py:19
  39.3 3.5 %collective-permute-done.2 = bf16[144,640]{1,0:T(8,128)(2,1)S(1)} collective-permute-done((bf16[144,640]{1,0:T(8,128)(2,1)S(1)}, bf16[144,640]{1,0:T(8,128)(2,1)S(1)}, u32[]{:S(2)}, u32[]{:S(2)}) %collective-permute-start.2) | collective-permute-done | bytes 184352 | tf_op jit(solution)/shard_map/ppermute | solution.py:19
  45.8 4.7 %shard_map.127 = (bf16[4,640,640]{2,1,0:T(8,128)(2,1)S(1)}, bf16[4,576,80]{2,1,0:T(8,128)(2,1)S(1)}) custom-call(s32[5]{0:T(128)S(1)} %stack.23.place, f32[1,640]{1,0:T(1,128)S(1)} %broadcast_in_dim.5.gain, bf16[288,640]{1,0:T(8,128)(2,1)S(1)} %bitcast.39, bf16[288,640]{1,0:T(8,128)(2,1)S(1)} %collective-permute-done.refs_1_, ...), custom_call_target="tpu_custom_call" | custom-call | tf_op jit(solution)/shard_map/pallas_call | solution.py:359
  50.5 1.7 %copy-done.4 = bf16[4,640,640]{2,1,0:T(8,128)(2,1)} copy-done((bf16[4,640,640]{2,1,0:T(8,128)(2,1)}, bf16[4,640,640]{2,1,0:T(8,128)(2,1)S(1)}, u32[]{:S(2)}) %copy-start.4) | copy-done | bytes 3276824
  53.5 2.0 %copy-done.5 = bf16[4,640,640]{2,1,0:T(8,128)(2,1)S(1)} copy-done((bf16[4,640,640]{2,1,0:T(8,128)(2,1)S(1)}, bf16[4,640,640]{2,1,0:T(8,128)(2,1)}, u32[]{:S(2)}) %copy-start.5) | copy-done | bytes 3276824
  55.4 5.1 %shard_map.128 = bf16[32,24,240]{2,1,0:T(8,128)(2,1)} custom-call(s32[5]{0:T(128)S(1)} %stack.23.place, bf16[3,640,240]{2,1,0:T(8,128)(2,1)S(1)} %bitcast.35, bf16[4,640,640]{2,1,0:T(8,128)(2,1)S(1)} %copy-done.5, bf16[4,576,80]{2,1,0:T(8,128)(2,1)S(1)} %get-tuple-element.24.kept), custom_call_target="tpu_custom_call" | custom-call | tf_op jit(solution)/shard_map/pallas_call | solution.py:359
  60.5 4.2 %all-to-all-start.1 = ((bf16[32,24,240]{2,1,0:T(8,128)(2,1)}), bf16[32,24,240]{2,1,0:T(8,128)(2,1)S(1)}, u32[]{:S(2)}, u32[]{:S(2)}) async-start(bf16[32,24,240]{2,1,0:T(8,128)(2,1)} %shard_map.128), calls=%async_computation.1 | async-start | bytes 786432 | tf_op jit(solution)/shard_map/all_to_all | solution.py:435
  65.6 12.3 %all-to-all-done.1.mid_in = bf16[32,24,240]{2,1,0:T(8,128)(2,1)S(1)} async-done(((bf16[32,24,240]{2,1,0:T(8,128)(2,1)}), bf16[32,24,240]{2,1,0:T(8,128)(2,1)S(1)}, u32[]{:S(2)}, u32[]{:S(2)}) %all-to-all-start.1) | async-done | bytes 368672 | tf_op jit(solution)/shard_map/all_to_all | solution.py:435
  77.9 3.6 %all-to-all-start.2 = ((bf16[8,36,640]{2,1,0:T(8,128)(2,1)}), bf16[8,36,640]{2,1,0:T(8,128)(2,1)S(1)}, u32[]{:S(2)}, u32[]{:S(2)}) async-start(bf16[8,36,640]{2,1,0:T(8,128)(2,1)} %reshape_squeeze.6), calls=%async_computation.2 | async-start | bytes 819200 | tf_op jit(solution)/shard_map/all_to_all | solution.py:438
  81.8 1.9 %copy-done.1 = bf16[640,2560]{1,0:T(8,128)(2,1)S(1)} copy-done((bf16[640,2560]{1,0:T(8,128)(2,1)S(1)}, bf16[640,2560]{1,0:T(8,128)(2,1)}, u32[]{:S(2)}) %copy-start.1) | copy-done | bytes 3276824
  83.7 6.3 %shard_map.129 = (bf16[320,640]{1,0:T(8,128)(2,1)S(1)}, f32[320,640]{1,0:T(8,128)S(1)}, f32[320,640]{1,0:T(8,128)S(1)}, f32[320,128]{1,0:T(8,128)S(1)}, f32[320,...) custom-call(bf16[32,24,240]{2,1,0:T(8,128)(2,1)S(1)} %all-to-all-don, ...), custom_call_target="tpu_custom_call" | custom-call | tf_op jit(solution)/shard_map/pallas_call | solution.py:359
  95.2 1.9 %copy-done.2 = bf16[640,2560]{1,0:T(8,128)(2,1)S(1)} copy-done((bf16[640,2560]{1,0:T(8,128)(2,1)S(1)}, bf16[640,2560]{1,0:T(8,128)(2,1)}, u32[]{:S(2)}) %copy-start.2) | copy-done | bytes 3276824
  102.0 5.1 %shard_map.130 = (bf16[2,2,2,4,40,640]{5,4,3,2,1,0:T(8,128)(2,1)S(1)}, f32[1,128]{1,0:T(1,128)S(1)}, f32[320,128]{1,0:T(8,128)S(1)}, bf16[320,640]{1,0:T(8,128)(2,1)S(1)}) custom-call(s32[5]{0:T(128)S(1)} %stack.23.place, bf16[8,36,640]{2,1,0:T(8,128)(2,1)S(1)} %all-to-all-done.2.cot_in, bf16[640,2560]{1,0:T(8,128)(2,1)S(1)} %copy-done.2, ...), custom_call_target="tpu_custom_call" | custom-call | tf_op jit(solution)/shard_map/pallas_call | solution.py:359
  108.6 6.6 %shard_map.131 = bf16[8,40,640]{2,1,0:T(8,128)(2,1)} custom-call(f32[320,128]{1,0:T(8,128)S(1)} %get-tuple-element.32.d_raw, f32[320,640]{1,0:T(8,128)S(1)} %get-tuple-element.33.q_hat, f32[320,640]{1,0:T(8,128)S(1)} %copy-done.7, f32[320,128]{1,0:T(8,128)S(1)} %get-tuple-element.35.q_rstd, f32[320,128]{1,0:T(8,128)S(1)} %copy-done.18, ...), custom_call_target="tpu_custom_call" | custom-call | tf_op jit(solution)/shard_map/pallas_call | solution.py:359
  115.1 4.8 %all-to-all-start.3 = ((bf16[8,40,640]{2,1,0:T(8,128)(2,1)}), bf16[8,40,640]{2,1,0:T(8,128)(2,1)S(1)}, u32[]{:S(2)}, u32[]{:S(2)}) async-start(bf16[8,40,640]{2,1,0:T(8,128)(2,1)} %shard_map.131), calls=%async_computation.3 | async-start | bytes 819200 | tf_op jit(solution)/shard_map/all_to_all | solution.py:489
  122.5 10.3 %all-to-all-done.3 = bf16[8,40,640]{2,1,0:T(8,128)(2,1)S(1)} async-done(((bf16[8,40,640]{2,1,0:T(8,128)(2,1)}), bf16[8,40,640]{2,1,0:T(8,128)(2,1)S(1)}, u32[]{:S(2)}, u32[]{:S(2)}) %all-to-all-start.3) | async-done | bytes 409632 | tf_op jit(solution)/shard_map/all_to_all | solution.py:489
  137.7 3.4 %collective-permute-done.10 = bf16[4,40,640]{2,1,0:T(8,128)(2,1)S(1)} collective-permute-done((bf16[4,40,640]{2,1,0:T(8,128)(2,1)S(1)}, bf16[4,40,640]{2,1,0:T(8,128)(2,1)S(1)}, u32[]{:S(2)}, u32[]{:S(2)}) %collective-permute-start.10) | collective-permute-done | bytes 204832 | tf_op jit(solution)/shard_map/ppermute | solution.py:19
  143.4 4.4 %collective-permute-done.11 = bf16[2,40,640]{2,1,0:T(8,128)(2,1)S(1)} collective-permute-done((bf16[2,40,640]{2,1,0:T(8,128)(2,1)S(1)}, bf16[2,40,640]{2,1,0:T(8,128)(2,1)S(1)}, u32[]{:S(2)}, u32[]{:S(2)}) %collective-permute-start.11) | collective-permute-done | bytes 102432 | tf_op jit(solution)/shard_map/ppermute | solution.py:486
  148.4 3.6 %collective-permute-done.12 = bf16[1,40,640]{2,1,0:T(8,128)(2,1)S(1)} collective-permute-done((bf16[1,40,640]{2,1,0:T(8,128)(2,1)S(1)}, bf16[1,40,640]{2,1,0:T(8,128)(2,1)S(1)}, u32[]{:S(2)}, u32[]{:S(2)}) %collective-permute-start.12) | collective-permute-done | bytes 51232 | tf_op jit(solution)/shard_map/ppermute | solution.py:486
  153.2 2.9 %collective-permute-done.13 = bf16[40,640]{1,0:T(8,128)(2,1)S(1)} collective-permute-done((bf16[40,640]{1,0:T(8,128)(2,1)S(1)}, bf16[40,640]{1,0:T(8,128)(2,1)S(1)}, u32[]{:S(2)}, u32[]{:S(2)}) %collective-permute-start.13) | collective-permute-done | bytes 51232 | tf_op jit(solution)/shard_map/ppermute | solution.py:19
  (123 shorter events, 35.6 us)
Async XLA Ops:
  7.2 74.6 %all-gather.2.cloned.1.call-start = ((), (), s32[]{:S(2)}) async-start(), calls=%async_computation.4 | async-start | bytes 3481600 | tf_op jit(solution)/shard_map/all_gather | solution.py:399
  10.2 32.8 %copy-start.26 = (f32[640]{0:T(1024)S(1)}, f32[640]{0:T(1024)}, u32[]{:S(2)}) copy-start(f32[640]{0:T(1024)} %param.10) | copy-start | bytes 7684
  10.2 42.0 %all-to-all-start = ((bf16[16,3,40,240]{3,2,1,0:T(8,128)(2,1)}), bf16[16,3,40,240]{3,2,1,0:T(8,128)(2,1)}, u32[]{:S(2)}, u32[]{:S(2)}) async-start(bf16[16,3,40,240]{3,2,1,0:T(8,128)(2,1)} %bitcast.6), calls=%async_computation | async-start | bytes 1966080 | tf_op jit(solution)/shard_map/all_to_all | solution.py:397
  17.8 10.9 %collective-permute-start.1 = (bf16[288,640]{1,0:T(8,128)(2,1)S(1)}, bf16[288,640]{1,0:T(8,128)(2,1)S(1)}, u32[]{:S(2)}, u32[]{:S(2)}) collective-permute-start(bf16[288,640]{1,0:T(8,128)(2,1)S(1)} %bitcast.36), channel_id=1, source_target_pairs={{0,16},{16,0},{1,17},{17,1},{2,18},{18,2},{3,19},{19,3},{4,20},{20... | collective-permute-start | bytes 1105928 | tf_op jit(solution)/shard_map/ppermute | solution.py:19
  19.4 17.9 %collective-permute-start = (bf16[288,640]{1,0:T(8,128)(2,1)S(1)}, bf16[288,640]{1,0:T(8,128)(2,1)S(1)}, u32[]{:S(2)}, u32[]{:S(2)}) collective-permute-start(bf16[288,640]{1,0:T(8,128)(2,1)S(1)} %bitcast.37), channel_id=1, source_target_pairs={{0,1},{1,0},{2,3},{3,2},{4,5},{5,4},{6,7},{7,6},{8,9},{9,8},{10,11... | collective-permute-start | bytes 1105928 | tf_op jit(solution)/shard_map/ppermute | solution.py:19
  28.7 14.1 %collective-permute-start.2 = (bf16[144,640]{1,0:T(8,128)(2,1)S(1)}, bf16[144,640]{1,0:T(8,128)(2,1)S(1)}, u32[]{:S(2)}, u32[]{:S(2)}) collective-permute-start(bf16[144,640]{1,0:T(8,128)(2,1)S(1)} %slice.69), channel_id=1, source_target_pairs={{0,1},{1,0},{2,3},{3,2},{4,5},{5,4},{6,7},{7,6},{8,9},{9,8},{10,11... | collective-permute-start | bytes 552968 | tf_op jit(solution)/shard_map/ppermute | solution.py:19
  37.3 5.6 %collective-permute-start.3 = (bf16[144,640]{1,0:T(8,128)(2,1)S(1)}, bf16[144,640]{1,0:T(8,128)(2,1)S(1)}, u32[]{:S(2)}, u32[]{:S(2)}) collective-permute-start(bf16[144,640]{1,0:T(8,128)(2,1)S(1)} %slice.70), channel_id=1, source_target_pairs={{0,16},{16,0},{1,17},{17,1},{2,18},{18,2},{3,19},{19,3},{4,20},{20... | collective-permute-start | bytes 552968 | tf_op jit(solution)/shard_map/ppermute | solution.py:19
  38.8 4.3 %collective-permute-start.4 = (bf16[288,640]{1,0:T(8,128)(2,1)S(1)}, bf16[288,640]{1,0:T(8,128)(2,1)S(1)}, u32[]{:S(2)}, u32[]{:S(2)}) collective-permute-start(bf16[288,640]{1,0:T(8,128)(2,1)S(1)} %bitcast.38), channel_id=1, source_target_pairs={{0,2},{2,0},{4,6},{6,4},{8,10},{10,8},{12,14},{14,12},{1,3},{3,1},... | collective-permute-start | bytes 1105928 | tf_op jit(solution)/shard_map/ppermute | solution.py:19
  38.8 4.3 %collective-permute-start.5 = (bf16[288,640]{1,0:T(8,128)(2,1)S(1)}, bf16[288,640]{1,0:T(8,128)(2,1)S(1)}, u32[]{:S(2)}, u32[]{:S(2)}) collective-permute-start(bf16[288,640]{1,0:T(8,128)(2,1)S(1)} %collective-permute-done.refs_1_), channel_id=1, source_target_pairs={{0,2},{2,0},{4,6},{6,4},{8,10},{10,8},{12,14},{14,12},{1,3},{3,1},... | collective-permute-start | bytes 1105928 | tf_op jit(solution)/shard_map/ppermute | solution.py:19
  39.3 3.8 %collective-permute-start.6 = (bf16[288,640]{1,0:T(8,128)(2,1)S(1)}, bf16[288,640]{1,0:T(8,128)(2,1)S(1)}, u32[]{:S(2)}, u32[]{:S(2)}) collective-permute-start(bf16[288,640]{1,0:T(8,128)(2,1)S(1)} %collective-permute-done.1.refs_2_), channel_id=1, source_target_pairs={{0,2},{2,0},{4,6},{6,4},{8,10},{10,8},{12,14},{14,12},{1,3},{3,1},... | collective-permute-start | bytes 1105928 | tf_op jit(solution)/shard_map/ppermute | solution.py:19
  42.9 1.9 %collective-permute-start.7 = (bf16[288,640]{1,0:T(8,128)(2,1)S(1)}, bf16[288,640]{1,0:T(8,128)(2,1)}, u32[]{:S(2)}, u32[]{:S(2)}) collective-permute-start(bf16[288,640]{1,0:T(8,128)(2,1)S(1)} %constant_dynamic-update-slice_fusion.refs_3_), channel_id=1, source_target_pairs={{0,2},{2,0},{4,6},{6,4},{8,10},{10,8},{12,14},{14,12},{1,3},{3,1},... | collective-permute-start | bytes 1105928 | tf_op jit(solution)/shard_map/ppermute | solution.py:19
  60.5 21.1 %copy-start.28 = (f32[64]{0:T(128)S(1)}, f32[64]{0:T(128)}, u32[]{:S(2)}) copy-start(f32[64]{0:T(128)} %param.13) | copy-start | bytes 772
  60.5 21.2 %copy-start.29 = (f32[10]{0:T(128)S(1)}, f32[10]{0:T(128)}, u32[]{:S(2)}) copy-start(f32[10]{0:T(128)} %param.15) | copy-start | bytes 124
  60.5 17.4 %all-to-all-start.1 = ((bf16[32,24,240]{2,1,0:T(8,128)(2,1)}), bf16[32,24,240]{2,1,0:T(8,128)(2,1)S(1)}, u32[]{:S(2)}, u32[]{:S(2)}) async-start(bf16[32,24,240]{2,1,0:T(8,128)(2,1)} %shard_map.128), calls=%async_computation.1 | async-start | bytes 786432 | tf_op jit(solution)/shard_map/all_to_all | solution.py:435
  77.9 17.4 %all-to-all-start.2 = ((bf16[8,36,640]{2,1,0:T(8,128)(2,1)}), bf16[8,36,640]{2,1,0:T(8,128)(2,1)S(1)}, u32[]{:S(2)}, u32[]{:S(2)}) async-start(bf16[8,36,640]{2,1,0:T(8,128)(2,1)} %reshape_squeeze.6), calls=%async_computation.2 | async-start | bytes 819200 | tf_op jit(solution)/shard_map/all_to_all | solution.py:438
  108.1 11.9 %collective-permute-start.8 = (bf16[2,2,4,40,640]{4,3,2,1,0:T(8,128)(2,1)}, bf16[2,2,4,40,640]{4,3,2,1,0:T(8,128)(2,1)}, u32[]{:S(2)}, u32[]{:S(2)}) collective-permute-start(bf16[2,2,4,40,640]{4,3,2,1,0:T(8,128)(2,1)} %slice_bitcast_fusion.1), channel_id=1, source_target_pairs={{0,2},{2,0},{4,6},{6,4},{8,10},{10,8},{12,14},{14,12},{1,3},{3,1},... | collective-permute-start | bytes 2457608 | tf_op jit(solution)/shard_map/ppermute | solution.py:19
  115.1 17.7 %all-to-all-start.3 = ((bf16[8,40,640]{2,1,0:T(8,128)(2,1)}), bf16[8,40,640]{2,1,0:T(8,128)(2,1)S(1)}, u32[]{:S(2)}, u32[]{:S(2)}) async-start(bf16[8,40,640]{2,1,0:T(8,128)(2,1)} %shard_map.131), calls=%async_computation.3 | async-start | bytes 819200 | tf_op jit(solution)/shard_map/all_to_all | solution.py:489
  121.4 13.1 %collective-permute-start.9 = (bf16[2,4,40,640]{3,2,1,0:T(8,128)(2,1)S(1)}, bf16[2,4,40,640]{3,2,1,0:T(8,128)(2,1)S(1)}, u32[]{:S(2)}, u32[]{:S(2)}) collective-permute-start(bf16[2,4,40,640]{3,2,1,0:T(8,128)(2,1)S(1)} %slice_bitcast_fusion.2), channel_id=1, source_target_pairs={{0,16},{16,0},{1,17},{17,1},{2,18},{18,2},{3,19},{19,3},{4,20},{20... | collective-permute-start | bytes 1228808 | tf_op jit(solution)/shard_map/ppermute | solution.py:19
  132.9 3.7 %collective-permute-start.14 = (f32[640]{0:T(1024)S(1)}, f32[640]{0:T(1024)S(1)}, u32[]{:S(2)}, u32[]{:S(2)}) collective-permute-start(f32[640]{0:T(1024)S(1)} %convert_reduce_fusion), channel_id=1, source_target_pairs={{0,1},{1,0},{2,3},{3,2},{4,5},{5,4},{6,7},{7,6},{8,9},{9,8},{10,11... | collective-permute-start | bytes 7688 | tf_op jit(solution)/shard_map/ppermute | solution.py:19
  134.6 6.4 %collective-permute-start.10 = (bf16[4,40,640]{2,1,0:T(8,128)(2,1)S(1)}, bf16[4,40,640]{2,1,0:T(8,128)(2,1)S(1)}, u32[]{:S(2)}, u32[]{:S(2)}) collective-permute-start(bf16[4,40,640]{2,1,0:T(8,128)(2,1)S(1)} %slice_bitcast_fusion.4), channel_id=1, source_target_pairs={{0,1},{1,0},{2,3},{3,2},{4,5},{5,4},{6,7},{7,6},{8,9},{9,8},{10,11... | collective-permute-start | bytes 614408 | tf_op jit(solution)/shard_map/ppermute | solution.py:19
  136.6 6.8 %collective-permute-start.15 = (f32[640]{0:T(1024)S(1)}, f32[640]{0:T(1024)S(1)}, u32[]{:S(2)}, u32[]{:S(2)}) collective-permute-start(f32[640]{0:T(1024)S(1)} %add.55), channel_id=1, source_target_pairs={{0,16},{16,0},{1,17},{17,1},{2,18},{18,2},{3,19},{19,3},{4,20},{20... | collective-permute-start | bytes 7688 | tf_op jit(solution)/shard_map/ppermute | solution.py:19
  141.1 6.6 %collective-permute-start.11 = (bf16[2,40,640]{2,1,0:T(8,128)(2,1)S(1)}, bf16[2,40,640]{2,1,0:T(8,128)(2,1)S(1)}, u32[]{:S(2)}, u32[]{:S(2)}) collective-permute-start(bf16[2,40,640]{2,1,0:T(8,128)(2,1)S(1)} %slice.78), channel_id=1, source_target_pairs={{0,8},{2,10},{4,12},{6,14},{8,0},{10,2},{12,4},{14,6},{1,9},{3,11}... | collective-permute-start | bytes 307208 | tf_op jit(solution)/shard_map/ppermute | solution.py:486
  147.8 4.2 %collective-permute-start.12 = (bf16[1,40,640]{2,1,0:T(8,128)(2,1)S(1)}, bf16[1,40,640]{2,1,0:T(8,128)(2,1)S(1)}, u32[]{:S(2)}, u32[]{:S(2)}) collective-permute-start(bf16[1,40,640]{2,1,0:T(8,128)(2,1)S(1)} %slice.80), channel_id=1, source_target_pairs={{0,4},{2,6},{4,0},{6,2},{8,12},{10,14},{12,8},{14,10},{1,5},{3,7},... | collective-permute-start | bytes 153608 | tf_op jit(solution)/shard_map/ppermute | solution.py:486
  152.0 4.2 %collective-permute-start.13 = (bf16[40,640]{1,0:T(8,128)(2,1)S(1)}, bf16[40,640]{1,0:T(8,128)(2,1)S(1)}, u32[]{:S(2)}, u32[]{:S(2)}) collective-permute-start(bf16[40,640]{1,0:T(8,128)(2,1)S(1)} %fusion.5), channel_id=1, source_target_pairs={{0,16},{16,0},{1,17},{17,1},{2,18},{18,2},{3,19},{19,3},{4,20},{20... | collective-permute-start | bytes 153608 | tf_op jit(solution)/shard_map/ppermute | solution.py:19
  (27 other events, 78.2 us)
Sparse Core Ops, SparseCore 0:
  10.3 58.4 all-gather.1

commit v4 on v3

--- a/solution.py
+++ b/solution.py
@@ -156,9 +156,9 @@
 
 
 def attend_kernel(
-    mid_in, weights, qgain, kgain, scale,
-    mid_out, q_hat, k_hat, q_rstd, k_rstd, value_out, raw_out, probs_out, mixed_out,
-    mid_s, doubled, mixed_s, raw_s,
+    place, mid_in, cot_in, weights, qgain, kgain, scale,
+    kept, sent, sums, d_raw, q_hat, k_hat, q_rstd, k_rstd, d_value,
+    mid_s, cot_s, doubled, doubled_v, mixed_s, raw_s, probs_s,
     *, heads, count, padded, part,
 ):
     total, width = mid_s.shape
@@ -166,10 +166,12 @@
     depth = width // heads
     lanes = scale.shape[-1]
     third = count // 3
+    x, core, tile, plane = (place[0], place[1], place[2], place[4])
     mid_s[...] = jnp.zeros_like(mid_s)
-
-    def unpack(z):
+    cot_s[...] = jnp.zeros_like(cot_s)
+    for z in range(frames // 2):
         for e in (0, 1):
+            f = 2 * z + e
             blocks = [
                 mid_in[(x * frames + 2 * z + c) * 2 + t, pl.ds((e ^ c) * third, third), :]
                 for x in (0, 1)
@@ -178,13 +180,11 @@
             ]
             for j in range(3):
                 piece = [b[:, j * part : (j + 1) * part] for b in blocks]
-                start = (2 * z + e) * padded + j * third
+                start = f * padded + j * third
                 mid_s[pl.ds(start, third), :] = jnp.concatenate(piece, axis=1).astype(F32)
-
-    for z in range(frames // 2):
-        unpack(z)
+            cot_s[pl.ds(f * padded, count), :] = cot_in[f].astype(F32)
     mid = mid_s[...].astype(BF)
-    mid_out[...] = mid
+    cot = cot_s[...].astype(BF)
     pick = picker(width, lanes, depth, 0)
     both = jnp.concatenate([spreader(lanes, width, depth, 0)] * 2, axis=0)
 
@@ -204,127 +204,101 @@
     hat = hat * kgain[...]
     doubled[pl.ds(0, total), :] = hat
     doubled[pl.ds(total, total), :] = hat
+    value = dot(mid, weights[:, pl.ds(2 * width, width)]).astype(BF).astype(F32)
+    doubled_v[pl.ds(0, total), :] = value
+    doubled_v[pl.ds(total, total), :] = value
+    d_mixed = dot_t(cot, weights[:, pl.ds(3 * width, width)]).astype(BF).astype(F32)
     raw_s[...] = jnp.zeros_like(raw_s)
+    probs_s[...] = jnp.zeros_like(probs_s)
 
     def logits(s):
         here = picker(width, lanes, depth, SLOT * s)
         raw_s[...] += head_sums(q_norm * doubled[pl.ds(s * padded, total), :], here)
+        probs_s[...] += head_sums(d_mixed * doubled_v[pl.ds(s * padded, total), :], here)
 
     each(frames, logits)
     raw = raw_s[...] / math.sqrt(depth)
-    raw_out[...] = raw
     expo = jnp.exp(raw * scale[...])
     probs = expo / over_slots(expo)
-    probs_out[...] = probs
     probs_b = probs.astype(BF)
-
-    value = dot(mid, weights[:, pl.ds(2 * width, width)]).astype(BF)
-    value_out[...] = value
-    value = value.astype(F32)
-    doubled[pl.ds(0, total), :] = value
-    doubled[pl.ds(total, total), :] = value
+    d_probs = probs_s[...]
+    d_logits = probs * (d_probs - over_slots(probs * d_probs))
+    sums[...] = jnp.sum(d_logits * raw, axis=0, keepdims=True)
+    d_raw[...] = d_logits * scale[...] / math.sqrt(depth)
     mixed_s[...] = jnp.zeros_like(mixed_s)
+    doubled[...] = jnp.zeros_like(doubled)
 
     def mix(s):
         weight = dot(probs_b, spreader(lanes, width, depth, SLOT * s))
-        mixed_s[...] += weight * doubled[pl.ds(s * padded, total), :]
+        mixed_s[...] += weight * doubled_v[pl.ds(s * padded, total), :]
+        doubled[pl.ds(s * padded, total), :] += weight * d_mixed
 
     each(frames, mix)
-    mixed_out[...] = mixed_s[...].astype(BF)
-
-
-def middle_kernel(
-    place, cot_in, weights, mid, mixed, value_in, raw, probs_in, scale,
-    grads, sums, d_raw, d_value,
-    cot_s, doubled, doubled_acc, probs_s,
-    *, heads, count, padded,
-):
-    total, width = mid.shape
-    frames = total // padded
-    depth = width // heads
-    lanes = scale.shape[-1]
-    x, core, tile, plane = (place[0], place[1], place[2], place[4])
-    cot_s[...] = jnp.zeros_like(cot_s)
-
-    def unpack(f):
-        cot_s[pl.ds(f * padded, count), :] = cot_in[f].astype(F32)
-
-    each(frames, unpack)
-    cot = cot_s[...].astype(BF)
-    rows = grads.shape[4]
+    dv = (doubled[pl.ds(0, total), :] + doubled[pl.ds(total, total), :]).astype(BF)
+    d_value[...] = dv
+    rows = kept.shape[3]
 
     def store(kind, term):
         for z in range(frames // 2):
-            for c in (0, 1):
-                for t in (0, 1):
-                    start = (4 * z + 2 * c + t) * rows
-                    block = term[start : start + rows]
-                    grads[x ^ kind, core ^ c, tile ^ t, plane ^ z] = block
-
-    store(1, dot_rows(mixed[...], cot).astype(BF))
-    d_mixed = dot_t(cot, weights[:, pl.ds(3 * width, width)]).astype(BF).astype(F32)
-    value = value_in[...].astype(F32)
-    doubled[pl.ds(0, total), :] = value
-    doubled[pl.ds(total, total), :] = value
+            for t in (0, 1):
+                start = (4 * z + t) * rows
+                first = term[start : start + rows]
+                second = term[start + 2 * rows : start + 3 * rows]
+                kept[x ^ kind, tile ^ t, plane ^ z] = jnp.where(core == 0, first, second)
+                sent[x ^ kind, tile ^ t, plane ^ z] = jnp.where(core == 0, second, first)
+
+    store(1, dot_rows(mixed_s[...].astype(BF), cot).astype(BF))
+    store(0, dot_rows(mid, dv).astype(BF))
+
+
+def slope_kernel(
+    d_raw, q_hat, k_hat, qgain, kgain,
+    d_qn, d_kn,
+    doubled, doubled_acc,
+    *, heads, padded,
+):
+    total, width = q_hat.shape
+    depth = width // heads
+    frames = total // padded
+    lanes = d_raw.shape[-1]
+    k_norm = k_hat[...] * kgain[...]
+    doubled[pl.ds(0, total), :] = k_norm
+    doubled[pl.ds(total, total), :] = k_norm
+    q_norm = q_hat[...] * qgain[...]
     doubled_acc[...] = jnp.zeros_like(doubled_acc)
-    probs_s[...] = jnp.zeros_like(probs_s)
-    probs = probs_in[...]
-    probs_b = probs.astype(BF)
+    d_qn[...] = jnp.zeros_like(d_qn)
+    high, low = halves(d_raw[...])
+    pair = jnp.concatenate([high, low], axis=1)
 
     def shift(s):
-        here = picker(width, lanes, depth, SLOT * s)
-        probs_s[...] += head_sums(d_mixed * doubled[pl.ds(s * padded, total), :], here)
-        weight = dot(probs_b, spreader(lanes, width, depth, SLOT * s))
-        doubled_acc[pl.ds(s * padded, total), :] += weight * d_mixed
+        one = spreader(lanes, width, depth, SLOT * s)
+        weight = dot(pair, jnp.concatenate([one, one], axis=0))
+        d_qn[...] += weight * doubled[pl.ds(s * padded, total), :]
+        doubled_acc[pl.ds(s * padded, total), :] += weight * q_norm
 
     each(frames, shift)
-    d_probs = probs_s[...]
-    dv = (doubled_acc[pl.ds(0, total), :] + doubled_acc[pl.ds(total, total), :]).astype(BF)
-    d_value[...] = dv
-    store(0, dot_rows(mid[...], dv).astype(BF))
-    d_logits = probs * (d_probs - over_slots(probs * d_probs))
-    sums[...] = jnp.sum(d_logits * raw[...], axis=0, keepdims=True)
-    d_raw[...] = d_logits * scale[...] / math.sqrt(depth)
+    d_kn[...] = doubled_acc[pl.ds(0, total), :] + doubled_acc[pl.ds(total, total), :]
 
 
 def back_kernel(
-    d_raw, q_hat, k_hat, q_rstd, k_rstd, d_value, weights, qgain, kgain, scale_sums,
+    d_qn, d_kn, q_hat, k_hat, q_rstd, k_rstd, d_value, weights, qgain, kgain, scale_sums,
     d_mid,
-    doubled, doubled_acc, d_qn_s,
     *, heads, count, padded,
 ):
     total, width = q_hat.shape
     depth = width // heads
     frames = total // padded
-    lanes = d_raw.shape[-1]
+    lanes = scale_sums.shape[-1]
     pick = picker(width, lanes, depth, 0)
     both = jnp.concatenate([spreader(lanes, width, depth, 0)] * 2, axis=0)
-    k_norm = k_hat[...] * kgain[...]
-    doubled[pl.ds(0, total), :] = k_norm
-    doubled[pl.ds(total, total), :] = k_norm
-    q_norm = q_hat[...] * qgain[...]
-    doubled_acc[...] = jnp.zeros_like(doubled_acc)
-    d_qn_s[...] = jnp.zeros_like(d_qn_s)
-    high, low = halves(d_raw[...])
-    pair = jnp.concatenate([high, low], axis=1)
-
-    def shift(s):
-        one = spreader(lanes, width, depth, SLOT * s)
-        weight = dot(pair, jnp.concatenate([one, one], axis=0))
-        d_qn_s[...] += weight * doubled[pl.ds(s * padded, total), :]
-        doubled_acc[pl.ds(s * padded, total), :] += weight * q_norm
-
-    each(frames, shift)
-    d_qn = d_qn_s[...]
-    d_kn = doubled_acc[pl.ds(0, total), :] + doubled_acc[pl.ds(total, total), :]
 
     def back(dhat, hat, rstd):
         first = spread(head_sums(dhat, pick) / depth, both)
         second = spread(head_sums(dhat * hat, pick) / depth, both)
         return (spread(rstd, both) * (dhat - first - hat * second)).astype(BF)
 
-    d_query = back(d_qn * qgain[...], q_hat[...], q_rstd[...])
-    d_key = back(d_kn * kgain[...], k_hat[...], k_rstd[...])
+    d_query = back(d_qn[...] * qgain[...], q_hat[...], q_rstd[...])
+    d_key = back(d_kn[...] * kgain[...], k_hat[...], k_rstd[...])
     out = dot_t(d_query, weights[:, pl.ds(0, width)])
     out += dot_t(d_key, weights[:, pl.ds(width, width)])
     out += dot_t(d_value[...], weights[:, pl.ds(2 * width, width)])
@@ -339,7 +313,7 @@
         return jnp.dot(sums, fold, precision=lax.Precision.HIGHEST, preferred_element_type=F32)[0:1]
 
     by_head = over_slots(jnp.broadcast_to(scale_sums[...], (8, lanes)))[0:1, :128]
-    small = [folded(d_qn, q_hat[...]), folded(d_kn, k_hat[...]), by_head]
+    small = [folded(d_qn[...], q_hat[...]), folded(d_kn[...], k_hat[...]), by_head]
     small.append(jnp.zeros((1, width - 384), F32))
     small = jnp.concatenate(small, axis=1)
     high, low = halves(small)
@@ -392,9 +366,10 @@
     mine = lax.dynamic_slice_in_dim(conv_weight, x * (width // 2), width // 2, axis=2)
     mine = mine.reshape(3, 3, share, 4, part).transpose(3, 0, 2, 1, 4)
     mine = mine.reshape(4, 3, share, 3 * part)
-    mine, _ = lax.optimization_barrier((mine, swap(flat[:8, :128], "dp")))
     spread_out = jnp.broadcast_to(mine[None], (frames // 2,) + mine.shape)
     conv_in = lax.all_to_all(spread_out.reshape((ranks,) + mine.shape[1:]), square, 0, 0, tiled=True)
+    cot_blocks, conv_in = lax.optimization_barrier((cot.reshape(frames, count, width), conv_in))
+    cot_blocks = lax.all_to_all(cot_blocks, "frame", 0, 0, tiled=True)
     conv_full = conv_in.transpose(1, 0, 2, 3).reshape(3, width, 3 * part)
     attn_full = lax.all_gather(attn_weight, square, axis=0, tiled=True)
 
@@ -432,10 +407,8 @@
     groups = None
     if clips > 2:
         groups = [[2 * ranks * g + i for i in range(2 * ranks)] for g in range(clips // 2)]
+    mid, cot_blocks = lax.optimization_barrier((mid, cot_blocks))
     mid = lax.all_to_all(mid, ("dp",) + square, 0, 0, axis_index_groups=groups, tiled=True)
-
-    cot_blocks, mid = lax.optimization_barrier((cot.reshape(frames, count, width), mid))
-    cot_blocks = lax.all_to_all(cot_blocks, "frame", 0, 0, tiled=True)
 
     lanes = frames * SLOT
     padded = round_up(count + 3, 8)
@@ -446,38 +419,41 @@
     full = (total, width)
     double = (2 * total, width)
     narrow = (total, lanes)
-    mid, q_hat, k_hat, q_rstd, k_rstd, value, raw, probs, mixed = call(
+    kept, sent, scale_sums, d_raw, q_hat, k_hat, q_rstd, k_rstd, d_value = call(
         functools.partial(attend_kernel, heads=heads, count=count, padded=padded, part=part),
         20,
         [
-            (full, BF), (full, F32), (full, F32), (narrow, F32), (narrow, F32),
-            (full, BF), (narrow, F32), (narrow, F32), (full, BF),
+            ((2, 2, frames // 2, share, width), BF),
+            ((2, 2, frames // 2, share, width), BF),
+            ((1, lanes), F32), (narrow, F32),
+            (full, F32), (full, F32), (narrow, F32), (narrow, F32), (full, BF),
         ],
-        [(full, F32), (double, F32), (full, F32), (narrow, F32)],
-        mid, attn_full, qgain, kgain, scale,
-    )
-    grads, scale_sums, d_raw, d_value = call(
-        functools.partial(middle_kernel, heads=heads, count=count, padded=padded),
-        20,
         [
-            ((2, 2, 2, frames // 2, share, width), BF),
-            ((1, lanes), F32), (narrow, F32), (full, BF),
+            (full, F32), (full, F32), (double, F32), (double, F32), (full, F32),
+            (narrow, F32), (narrow, F32),
         ],
-        [(full, F32), (double, F32), (double, F32), (narrow, F32)],
-        place, cot_blocks, attn_full, mid, mixed, value, raw, probs, scale,
-    )
+        place, mid, cot_blocks, attn_full, qgain, kgain, scale,
+    )
+    d_qn, d_kn = call(
+        functools.partial(slope_kernel, heads=heads, padded=padded),
+        16,
+        [(full, F32), (full, F32)],
+        [(double, F32), (double, F32)],
+        d_raw, q_hat, k_hat, qgain, kgain,
+    )
+
+    def add(mine, theirs):
+        return (mine.astype(F32) + theirs.astype(F32)).astype(BF)
+
+    shares = add(kept, swap(sent, "frame"))
+    shares, d_qn = lax.optimization_barrier((shares, d_qn))
     (d_mid,) = call(
         functools.partial(back_kernel, heads=heads, count=count, padded=padded),
-        20,
+        16,
         [((frames, padded, width), BF)],
-        [(double, F32), (double, F32), (full, F32)],
-        d_raw, q_hat, k_hat, q_rstd, k_rstd, d_value, attn_full, qgain, kgain, scale_sums,
-    )
-
-    def add(mine, theirs):
-        return (mine.astype(F32) + theirs.astype(F32)).astype(BF)
-
-    shares = add(grads[:, 0], swap(grads[:, 1], "frame"))
+        [],
+        d_qn, d_kn, q_hat, k_hat, q_rstd, k_rstd, d_value, attn_full, qgain, kgain, scale_sums,
+    )
     shares = add(shares[0], swap(shares[1], "dp"))
     shares = add(shares[0], swap(shares[1], "tile"))
     step = frames // 4

time: 165 us -> 153 us (0.927)
  local copies, waits for them, and re-layouts: 25.4 us -> 10.3 us
  waiting for transfers between devices: 56.4 us -> 60.7 us
  other arithmetic: 5.2 us -> 3.07 us
  starting transfers between devices: 34.5 us -> 36.6 us
    unnamed x61 -> x25, local copies, waits for them, and re-layouts: 19.8 us -> 4.63 us
    ppermute x2, waiting for transfers between devices: 7.95 us -> 1.2 us  [local(): shares = add(shares[:step], lax.ppermute(shares[step:], 'frame', pairs))]
    all_to_all x1, waiting for transfers between devices: 0.01 us -> 6.55 us  [local(): lax.all_to_all(spread_out.reshape((ranks,) + mine.shape[1:]), square, 0,...]
    all_to_all x1, waiting for transfers between devices: 0.01 us -> 6.06 us  [local(): cot_blocks = lax.all_to_all(cot_blocks, 'frame', 0, 0, tiled=True)]
    all_to_all x1, waiting for transfers between devices: 10.3 us -> 5.16 us  [local(): d_back = lax.all_to_all(d_mid, 'frame', 0, 0, tiled=True)]
    ppermute x14, waiting for transfers between devices: 25.2 us -> 28.4 us  [swap(): lax.ppermute(x, axis, [(i, i ^ 1) for i in range(lax.axis_size(axis))])]
    all_to_all x1, starting transfers between devices: 3.64 us -> 5.59 us  [local(): cot_blocks = lax.all_to_all(cot_blocks, 'frame', 0, 0, tiled=True)]
  transfers between devices with their start and end apart: 21 -> 21, of which waited for: 11 -> 14; matrix products, arithmetic and copies ran while one was open for 6% -> 6% of each run, Pallas kernels for 14% -> 11%
where the time goes in v4:
time: 153 us; the launch traced here: 152 us
  waiting for transfers between devices  60.7 us (40%)
  starting transfers between devices  36.6 us (24%)
  Pallas kernels  27.4 us (18%)
  between operations  14.4 us (9%)
  local copies, waits for them, and re-layouts  10.3 us (7%)
  other arithmetic  3.07 us (2%)
    ppermute x14, waiting for transfers between devices, swap(): lax.ppermute(x, axis, [(i, i ^ 1) for i in range(lax.axis_size(axis))])  28.4 us
    pallas_call x5, Pallas kernels, call(): pl.pallas_call(kernel, out_shape=[jax.ShapeDtypeStruct(shape, dtype) for...  27.4 us
    ppermute x14, starting transfers between devices, swap(): lax.ppermute(x, axis, [(i, i ^ 1) for i in range(lax.axis_size(axis))])  14.1 us
    all_to_all x1, waiting for transfers between devices, local(): lax.all_to_all(mid, ('dp',) + square, 0, 0, axis_index_groups=groups, til...  12.6 us
    all_to_all x1, starting transfers between devices, local(): lax.all_to_all(spread_out.reshape((ranks,) + mine.shape[1:]), square, 0,...  7.52 us
    all_to_all x1, waiting for transfers between devices, local(): lax.all_to_all(spread_out.reshape((ranks,) + mine.shape[1:]), square, 0,...  6.55 us
    all_to_all x1, waiting for transfers between devices, local(): cot_blocks = lax.all_to_all(cot_blocks, 'frame', 0, 0, tiled=True)  6.06 us
    all_to_all x1, starting transfers between devices, local(): cot_blocks = lax.all_to_all(cot_blocks, 'frame', 0, 0, tiled=True)  5.59 us
  transfers between devices with their start and end apart: 21, of which 14 were waited for; matrix products, arithmetic and copies ran while one was open for 6% of the time, Pallas kernels for 11%

profile of v4, /device:TPU:0, one launch (start us, length us, event | category | flops | bytes accessed | tf_op | source)
XLA Modules:
  0.0 152.4 jit_solution(5141761626507339533)
XLA Ops:
  10.1 7.5 %all-to-all-start = ((bf16[16,3,40,240]{3,2,1,0:T(8,128)(2,1)}), bf16[16,3,40,240]{3,2,1,0:T(8,128)(2,1)S(1)}, u32[]{:S(2)}, u32[]{:S(2)}) async-start(bf16[16,3,40,240]{3,2,1,0:T(8,128)(2,1)} %bitcast.6), calls=%async_computation | async-start | bytes 1966080 | tf_op jit(solution)/shard_map/all_to_all | solution.py:370
  17.7 1.6 %collective-permute-start.1 = (bf16[288,640]{1,0:T(8,128)(2,1)S(1)}, bf16[288,640]{1,0:T(8,128)(2,1)S(1)}, u32[]{:S(2)}, u32[]{:S(2)}) collective-permute-start(bf16[288,640]{1,0:T(8,128)(2,1)S(1)} %bitcast.27), channel_id=1, source_target_pairs={{0,16},{16,0},{1,17},{17,1},{2,18},{18,2},{3,19},{19,3},{4,20},{20... | collective-permute-start | bytes 1105928 | tf_op jit(solution)/shard_map/ppermute | solution.py:19
  19.2 1.9 %collective-permute-start = (bf16[288,640]{1,0:T(8,128)(2,1)S(1)}, bf16[288,640]{1,0:T(8,128)(2,1)S(1)}, u32[]{:S(2)}, u32[]{:S(2)}) collective-permute-start(bf16[288,640]{1,0:T(8,128)(2,1)S(1)} %bitcast.28), channel_id=1, source_target_pairs={{0,1},{1,0},{2,3},{3,2},{4,5},{5,4},{6,7},{7,6},{8,9},{9,8},{10,11... | collective-permute-start | bytes 1105928 | tf_op jit(solution)/shard_map/ppermute | solution.py:19
  21.2 7.5 %collective-permute-done.1.refs_2_ = bf16[288,640]{1,0:T(8,128)(2,1)S(1)} collective-permute-done((bf16[288,640]{1,0:T(8,128)(2,1)S(1)}, bf16[288,640]{1,0:T(8,128)(2,1)S(1)}, u32[]{:S(2)}, u32[]{:S(2)}) %collective-permute-start.1) | collective-permute-done | bytes 368672 | tf_op jit(solution)/shard_map/ppermute | solution.py:19
  29.4 1.6 %collective-permute-start.2 = (bf16[144,640]{1,0:T(8,128)(2,1)}, bf16[144,640]{1,0:T(8,128)(2,1)}, u32[]{:S(2)}, u32[]{:S(2)}) collective-permute-start(bf16[144,640]{1,0:T(8,128)(2,1)} %slice.60), channel_id=1, source_target_pairs={{0,1},{1,0},{2,3},{3,2},{4,5},{5,4},{6,7},{7,6},{8,9},{9,8},{10,11... | collective-permute-start | bytes 552968 | tf_op jit(solution)/shard_map/ppermute | solution.py:19
  31.0 6.3 %collective-permute-done.refs_1_ = bf16[288,640]{1,0:T(8,128)(2,1)S(1)} collective-permute-done((bf16[288,640]{1,0:T(8,128)(2,1)S(1)}, bf16[288,640]{1,0:T(8,128)(2,1)S(1)}, u32[]{:S(2)}, u32[]{:S(2)}) %collective-permute-start) | collective-permute-done | bytes 368672 | tf_op jit(solution)/shard_map/ppermute | solution.py:19
  40.3 6.5 %all-to-all-done = bf16[16,3,40,240]{3,2,1,0:T(8,128)(2,1)S(1)} async-done(((bf16[16,3,40,240]{3,2,1,0:T(8,128)(2,1)}), bf16[16,3,40,240]{3,2,1,0:T(8,128)(2,1)S(1)}, u32[]{:S(2)}, u32[]{:S(2)}) %all-to-all-start) | async-done | bytes 921632 | tf_op jit(solution)/shard_map/all_to_all | solution.py:370
  47.8 5.6 %all-to-all-start.1 = ((bf16[8,36,640]{2,1,0:T(8,128)(2,1)}), bf16[8,36,640]{2,1,0:T(8,128)(2,1)S(1)}, u32[]{:S(2)}, u32[]{:S(2)}) async-start(bf16[8,36,640]{2,1,0:T(8,128)(2,1)} %reshape_squeeze.6), calls=%async_computation.1 | async-start | bytes 819200 | tf_op jit(solution)/shard_map/all_to_all | solution.py:372
  56.5 1.6 %collective-permute-done.7.refs_7_ = bf16[288,640]{1,0:T(8,128)(2,1)} collective-permute-done((bf16[288,640]{1,0:T(8,128)(2,1)S(1)}, bf16[288,640]{1,0:T(8,128)(2,1)}, u32[]{:S(2)}, u32[]{:S(2)}) %collective-permute-start.7) | collective-permute-done | bytes 368672 | tf_op jit(solution)/shard_map/ppermute | solution.py:19
  58.2 4.7 %shard_map.127 = (bf16[4,640,640]{2,1,0:T(8,128)(2,1)S(1)}, bf16[4,576,80]{2,1,0:T(8,128)(2,1)S(1)}) custom-call(s32[5]{0:T(128)S(1)} %stack.23.place, f32[1,640]{1,0:T(1,128)S(1)} %broadcast_in_dim.13.gain, bf16[288,640]{1,0:T(8,128)(2,1)S(1)} %bitcast.30, bf16[288,640]{1,0:T(8,128)(2,1)S(1)} %collective-permute-done.refs_1_, ...), custom_call_target="tpu_custom_call" | custom-call | tf_op jit(solution)/shard_map/pallas_call | solution.py:333
  62.9 5.1 %shard_map.128 = bf16[32,24,240]{2,1,0:T(8,128)(2,1)} custom-call(s32[5]{0:T(128)S(1)} %stack.23.place, bf16[3,640,240]{2,1,0:T(8,128)(2,1)S(1)} %bitcast.26, bf16[4,640,640]{2,1,0:T(8,128)(2,1)S(1)} %get-tuple-element.26.acts, bf16[4,576,80]{2,1,0:T(8,128)(2,1)S(1)} %get-tuple-element.27.kept), custom_call_target="tpu_custom_call" | custom-call | tf_op jit(solution)/shard_map/pallas_call | solution.py:333
  68.0 6.1 %all-to-all-done.1.cot_in = bf16[8,36,640]{2,1,0:T(8,128)(2,1)S(1)} async-done(((bf16[8,36,640]{2,1,0:T(8,128)(2,1)}), bf16[8,36,640]{2,1,0:T(8,128)(2,1)S(1)}, u32[]{:S(2)}, u32[]{:S(2)}) %all-to-all-start.1) | async-done | bytes 368672 | tf_op jit(solution)/shard_map/all_to_all | solution.py:372
  74.1 3.6 %all-to-all-start.2 = ((bf16[32,24,240]{2,1,0:T(8,128)(2,1)}), bf16[32,24,240]{2,1,0:T(8,128)(2,1)S(1)}, u32[]{:S(2)}, u32[]{:S(2)}) async-start(bf16[32,24,240]{2,1,0:T(8,128)(2,1)} %shard_map.128), calls=%async_computation.2 | async-start | bytes 786432 | tf_op jit(solution)/shard_map/all_to_all | solution.py:411
  78.0 12.6 %all-to-all-done.2.mid_in = bf16[32,24,240]{2,1,0:T(8,128)(2,1)S(1)} async-done(((bf16[32,24,240]{2,1,0:T(8,128)(2,1)}), bf16[32,24,240]{2,1,0:T(8,128)(2,1)S(1)}, u32[]{:S(2)}, u32[]{:S(2)}) %all-to-all-start.2) | async-done | bytes 368672 | tf_op jit(solution)/shard_map/all_to_all | solution.py:411
  90.6 1.9 %copy-done.1 = bf16[640,2560]{1,0:T(8,128)(2,1)S(1)} copy-done((bf16[640,2560]{1,0:T(8,128)(2,1)S(1)}, bf16[640,2560]{1,0:T(8,128)(2,1)}, u32[]{:S(2)}) %copy-start.1) | copy-done | bytes 3276824
  92.5 10.6 %shard_map.129 = (bf16[2,2,4,40,640]{4,3,2,1,0:T(8,128)(2,1)S(1)}, bf16[2,2,4,40,640]{4,3,2,1,0:T(8,128)(2,1)S(1)}, f32[1,128]{1,0:T(1,128)S(1)}, f32[320,128]{1...) custom-call(s32[5]{0:T(128)S(1)} %stack.23.place, ...), custom_call_target="tpu_custom_call" | custom-call | tf_op jit(solution)/shard_map/pallas_call | solution.py:333
  103.2 2.0 %shard_map.130 = (f32[320,640]{1,0:T(8,128)S(1)}, f32[320,640]{1,0:T(8,128)S(1)}) custom-call(f32[320,128]{1,0:T(8,128)S(1)} %get-tuple-element.33.d_raw, f32[320,640]{1,0:T(8,128)S(1)} %get-tuple-element.34.q_hat, f32[320,640]{1,0:T(8,128)S(1)} %get-tuple-element.35.k_hat, f32[1,640]{1,0:T(1,128)S(1)} %broadcast_in_dim_tile.9.qgain, ...), custom_call_target="tpu_custom_call" | custom-call | tf_op jit(solution)/shard_map/pallas_call | solution.py:333
  107.5 5.1 %shard_map.131 = bf16[8,40,640]{2,1,0:T(8,128)(2,1)} custom-call(f32[320,640]{1,0:T(8,128)S(1)} %get-tuple-element.37.d_qn, f32[320,640]{1,0:T(8,128)S(1)} %get-tuple-element.38.d_kn, f32[320,640]{1,0:T(8,128)S(1)} %get-tuple-element.34.q_hat, f32[320,640]{1,0:T(8,128)S(1)} %get-tuple-element.35.k_hat, f32[320,128]{1,0:T(8,128)S(1)} %get-tuple-element.39.q_rstd, ...), custom_call_target="tpu_custom_call" | custom-call | tf_op jit(solution)/shard_map/pallas_call | solution.py:333
  112.6 3.5 %all-to-all-start.3 = ((bf16[8,40,640]{2,1,0:T(8,128)(2,1)}), bf16[8,40,640]{2,1,0:T(8,128)(2,1)S(1)}, u32[]{:S(2)}, u32[]{:S(2)}) async-start(bf16[8,40,640]{2,1,0:T(8,128)(2,1)} %shard_map.131), calls=%async_computation.3 | async-start | bytes 819200 | tf_op jit(solution)/shard_map/all_to_all | solution.py:465
  119.2 4.9 %collective-permute-done.10 = bf16[4,40,640]{2,1,0:T(8,128)(2,1)S(1)} collective-permute-done((bf16[4,40,640]{2,1,0:T(8,128)(2,1)S(1)}, bf16[4,40,640]{2,1,0:T(8,128)(2,1)S(1)}, u32[]{:S(2)}, u32[]{:S(2)}) %collective-permute-start.10) | collective-permute-done | bytes 204832 | tf_op jit(solution)/shard_map/ppermute | solution.py:19
  124.1 2.2 %collective-permute-start.11 = (bf16[2,40,640]{2,1,0:T(8,128)(2,1)S(1)}, bf16[2,40,640]{2,1,0:T(8,128)(2,1)S(1)}, u32[]{:S(2)}, u32[]{:S(2)}) collective-permute-start(bf16[2,40,640]{2,1,0:T(8,128)(2,1)S(1)} %slice.66), channel_id=1, source_target_pairs={{0,8},{2,10},{4,12},{6,14},{8,0},{10,2},{12,4},{14,6},{1,9},{3,11}... | collective-permute-start | bytes 307208 | tf_op jit(solution)/shard_map/ppermute | solution.py:462
  126.3 5.2 %all-to-all-done.3 = bf16[8,40,640]{2,1,0:T(8,128)(2,1)S(1)} async-done(((bf16[8,40,640]{2,1,0:T(8,128)(2,1)}), bf16[8,40,640]{2,1,0:T(8,128)(2,1)S(1)}, u32[]{:S(2)}, u32[]{:S(2)}) %all-to-all-start.3) | async-done | bytes 409632 | tf_op jit(solution)/shard_map/all_to_all | solution.py:465
  136.6 2.4 %collective-permute-done.15 = f32[640]{0:T(1024)S(1)} collective-permute-done((f32[640]{0:T(1024)S(1)}, f32[640]{0:T(1024)S(1)}, u32[]{:S(2)}, u32[]{:S(2)}) %collective-permute-start.15) | collective-permute-done | bytes 2592 | tf_op jit(solution)/shard_map/ppermute | solution.py:19
  142.2 2.7 %collective-permute-done.13 = bf16[40,640]{1,0:T(8,128)(2,1)S(1)} collective-permute-done((bf16[40,640]{1,0:T(8,128)(2,1)S(1)}, bf16[40,640]{1,0:T(8,128)(2,1)S(1)}, u32[]{:S(2)}, u32[]{:S(2)}) %collective-permute-start.13) | collective-permute-done | bytes 51232 | tf_op jit(solution)/shard_map/ppermute | solution.py:19
  (86 shorter events, 25.4 us)
Async XLA Ops:
  7.2 83.4 %all-gather.2.cloned.1.call-start = ((), (), s32[]{:S(2)}) async-start(), calls=%async_computation.4 | async-start | bytes 3481600 | tf_op jit(solution)/shard_map/all_gather | solution.py:374
  10.1 29.3 %copy-start.6 = (bf16[1,1,9,32,640]{4,3,2,1,0:T(8,128)(2,1)S(1)}, bf16[1,1,9,32,640]{4,3,2,1,0:T(8,128)(2,1)}, u32[]{:S(2)}) copy-start(bf16[1,1,9,32,640]{4,3,2,1,0:T(8,128)(2,1)} %param.9) | copy-start | bytes 1105924
  10.1 36.7 %all-to-all-start = ((bf16[16,3,40,240]{3,2,1,0:T(8,128)(2,1)}), bf16[16,3,40,240]{3,2,1,0:T(8,128)(2,1)S(1)}, u32[]{:S(2)}, u32[]{:S(2)}) async-start(bf16[16,3,40,240]{3,2,1,0:T(8,128)(2,1)} %bitcast.6), calls=%async_computation | async-start | bytes 1966080 | tf_op jit(solution)/shard_map/all_to_all | solution.py:370
  17.7 38.7 %copy-start.8 = (f32[640]{0:T(1024)S(1)}, f32[640]{0:T(1024)}, u32[]{:S(2)}) copy-start(f32[640]{0:T(1024)} %param.10) | copy-start | bytes 7684
  17.7 11.0 %collective-permute-start.1 = (bf16[288,640]{1,0:T(8,128)(2,1)S(1)}, bf16[288,640]{1,0:T(8,128)(2,1)S(1)}, u32[]{:S(2)}, u32[]{:S(2)}) collective-permute-start(bf16[288,640]{1,0:T(8,128)(2,1)S(1)} %bitcast.27), channel_id=1, source_target_pairs={{0,16},{16,0},{1,17},{17,1},{2,18},{18,2},{3,19},{19,3},{4,20},{20... | collective-permute-start | bytes 1105928 | tf_op jit(solution)/shard_map/ppermute | solution.py:19
  19.2 18.0 %collective-permute-start = (bf16[288,640]{1,0:T(8,128)(2,1)S(1)}, bf16[288,640]{1,0:T(8,128)(2,1)S(1)}, u32[]{:S(2)}, u32[]{:S(2)}) collective-permute-start(bf16[288,640]{1,0:T(8,128)(2,1)S(1)} %bitcast.28), channel_id=1, source_target_pairs={{0,1},{1,0},{2,3},{3,2},{4,5},{5,4},{6,7},{7,6},{8,9},{9,8},{10,11... | collective-permute-start | bytes 1105928 | tf_op jit(solution)/shard_map/ppermute | solution.py:19
  29.4 25.0 %collective-permute-start.2 = (bf16[144,640]{1,0:T(8,128)(2,1)}, bf16[144,640]{1,0:T(8,128)(2,1)}, u32[]{:S(2)}, u32[]{:S(2)}) collective-permute-start(bf16[144,640]{1,0:T(8,128)(2,1)} %slice.60), channel_id=1, source_target_pairs={{0,1},{1,0},{2,3},{3,2},{4,5},{5,4},{6,7},{7,6},{8,9},{9,8},{10,11... | collective-permute-start | bytes 552968 | tf_op jit(solution)/shard_map/ppermute | solution.py:19
  38.0 17.4 %collective-permute-start.3 = (bf16[144,640]{1,0:T(8,128)(2,1)}, bf16[144,640]{1,0:T(8,128)(2,1)}, u32[]{:S(2)}, u32[]{:S(2)}) collective-permute-start(bf16[144,640]{1,0:T(8,128)(2,1)} %slice.61), channel_id=1, source_target_pairs={{0,16},{16,0},{1,17},{17,1},{2,18},{18,2},{3,19},{19,3},{4,20},{20... | collective-permute-start | bytes 552968 | tf_op jit(solution)/shard_map/ppermute | solution.py:19
  47.8 26.3 %all-to-all-start.1 = ((bf16[8,36,640]{2,1,0:T(8,128)(2,1)}), bf16[8,36,640]{2,1,0:T(8,128)(2,1)S(1)}, u32[]{:S(2)}, u32[]{:S(2)}) async-start(bf16[8,36,640]{2,1,0:T(8,128)(2,1)} %reshape_squeeze.6), calls=%async_computation.1 | async-start | bytes 819200 | tf_op jit(solution)/shard_map/all_to_all | solution.py:372
  53.4 3.2 %collective-permute-start.4 = (bf16[288,640]{1,0:T(8,128)(2,1)S(1)}, bf16[288,640]{1,0:T(8,128)(2,1)S(1)}, u32[]{:S(2)}, u32[]{:S(2)}) collective-permute-start(bf16[288,640]{1,0:T(8,128)(2,1)S(1)} %bitcast.29), channel_id=1, source_target_pairs={{0,2},{2,0},{4,6},{6,4},{8,10},{10,8},{12,14},{14,12},{1,3},{3,1},... | collective-permute-start | bytes 1105928 | tf_op jit(solution)/shard_map/ppermute | solution.py:19
  53.9 2.7 %collective-permute-start.5 = (bf16[288,640]{1,0:T(8,128)(2,1)S(1)}, bf16[288,640]{1,0:T(8,128)(2,1)S(1)}, u32[]{:S(2)}, u32[]{:S(2)}) collective-permute-start(bf16[288,640]{1,0:T(8,128)(2,1)S(1)} %collective-permute-done.refs_1_), channel_id=1, source_target_pairs={{0,2},{2,0},{4,6},{6,4},{8,10},{10,8},{12,14},{14,12},{1,3},{3,1},... | collective-permute-start | bytes 1105928 | tf_op jit(solution)/shard_map/ppermute | solution.py:19
  53.9 2.7 %collective-permute-start.6 = (bf16[288,640]{1,0:T(8,128)(2,1)S(1)}, bf16[288,640]{1,0:T(8,128)(2,1)S(1)}, u32[]{:S(2)}, u32[]{:S(2)}) collective-permute-start(bf16[288,640]{1,0:T(8,128)(2,1)S(1)} %collective-permute-done.1.refs_2_), channel_id=1, source_target_pairs={{0,2},{2,0},{4,6},{6,4},{8,10},{10,8},{12,14},{14,12},{1,3},{3,1},... | collective-permute-start | bytes 1105928 | tf_op jit(solution)/shard_map/ppermute | solution.py:19
  56.3 1.9 %collective-permute-start.7 = (bf16[288,640]{1,0:T(8,128)(2,1)S(1)}, bf16[288,640]{1,0:T(8,128)(2,1)}, u32[]{:S(2)}, u32[]{:S(2)}) collective-permute-start(bf16[288,640]{1,0:T(8,128)(2,1)S(1)} %constant_dynamic-update-slice_fusion.refs_3_), channel_id=1, source_target_pairs={{0,2},{2,0},{4,6},{6,4},{8,10},{10,8},{12,14},{14,12},{1,3},{3,1},... | collective-permute-start | bytes 1105928 | tf_op jit(solution)/shard_map/ppermute | solution.py:19
  62.9 14.9 %copy-start.11 = (f32[10]{0:T(128)S(1)}, f32[10]{0:T(128)}, u32[]{:S(2)}) copy-start(f32[10]{0:T(128)} %param.15) | copy-start | bytes 124
  74.1 16.5 %all-to-all-start.2 = ((bf16[32,24,240]{2,1,0:T(8,128)(2,1)}), bf16[32,24,240]{2,1,0:T(8,128)(2,1)S(1)}, u32[]{:S(2)}, u32[]{:S(2)}) async-start(bf16[32,24,240]{2,1,0:T(8,128)(2,1)} %shard_map.128), calls=%async_computation.2 | async-start | bytes 786432 | tf_op jit(solution)/shard_map/all_to_all | solution.py:411
  103.2 2.4 %collective-permute-start.8 = (bf16[2,2,4,40,640]{4,3,2,1,0:T(8,128)(2,1)S(1)}, bf16[2,2,4,40,640]{4,3,2,1,0:T(8,128)(2,1)S(1)}, u32[]{:S(2)}, u32[]{:S(2)}) collective-permute-start(bf16[2,2,4,40,640]{4,3,2,1,0:T(8,128)(2,1)S(1)} %get-tuple-element.32), channel_id=1, source_target_pairs={{0,2},{2,0},{4,6},{6,4},{8,10},{10,8},{12,14},{14,12},{1,3},{3,1},... | collective-permute-start | bytes 2457608 | tf_op jit(solution)/shard_map/ppermute | solution.py:19
  105.8 11.7 %collective-permute-start.9 = (bf16[2,4,40,640]{3,2,1,0:T(8,128)(2,1)S(1)}, bf16[2,4,40,640]{3,2,1,0:T(8,128)(2,1)S(1)}, u32[]{:S(2)}, u32[]{:S(2)}) collective-permute-start(bf16[2,4,40,640]{3,2,1,0:T(8,128)(2,1)S(1)} %slice_bitcast_fusion), channel_id=1, source_target_pairs={{0,16},{16,0},{1,17},{17,1},{2,18},{18,2},{3,19},{19,3},{4,20},{20... | collective-permute-start | bytes 1228808 | tf_op jit(solution)/shard_map/ppermute | solution.py:19
  112.6 19.0 %all-to-all-start.3 = ((bf16[8,40,640]{2,1,0:T(8,128)(2,1)}), bf16[8,40,640]{2,1,0:T(8,128)(2,1)S(1)}, u32[]{:S(2)}, u32[]{:S(2)}) async-start(bf16[8,40,640]{2,1,0:T(8,128)(2,1)} %shard_map.131), calls=%async_computation.3 | async-start | bytes 819200 | tf_op jit(solution)/shard_map/all_to_all | solution.py:465
  117.6 6.4 %collective-permute-start.10 = (bf16[4,40,640]{2,1,0:T(8,128)(2,1)S(1)}, bf16[4,40,640]{2,1,0:T(8,128)(2,1)S(1)}, u32[]{:S(2)}, u32[]{:S(2)}) collective-permute-start(bf16[4,40,640]{2,1,0:T(8,128)(2,1)S(1)} %slice_bitcast_fusion.1), channel_id=1, source_target_pairs={{0,1},{1,0},{2,3},{3,2},{4,5},{5,4},{6,7},{7,6},{8,9},{9,8},{10,11... | collective-permute-start | bytes 614408 | tf_op jit(solution)/shard_map/ppermute | solution.py:19
  124.1 12.3 %collective-permute-start.11 = (bf16[2,40,640]{2,1,0:T(8,128)(2,1)S(1)}, bf16[2,40,640]{2,1,0:T(8,128)(2,1)S(1)}, u32[]{:S(2)}, u32[]{:S(2)}) collective-permute-start(bf16[2,40,640]{2,1,0:T(8,128)(2,1)S(1)} %slice.66), channel_id=1, source_target_pairs={{0,8},{2,10},{4,12},{6,14},{8,0},{10,2},{12,4},{14,6},{1,9},{3,11}... | collective-permute-start | bytes 307208 | tf_op jit(solution)/shard_map/ppermute | solution.py:462
  131.7 3.7 %collective-permute-start.14 = (f32[640]{0:T(1024)S(1)}, f32[640]{0:T(1024)S(1)}, u32[]{:S(2)}, u32[]{:S(2)}) collective-permute-start(f32[640]{0:T(1024)S(1)} %convert_reduce_fusion), channel_id=1, source_target_pairs={{0,1},{1,0},{2,3},{3,2},{4,5},{5,4},{6,7},{7,6},{8,9},{9,8},{10,11... | collective-permute-start | bytes 7688 | tf_op jit(solution)/shard_map/ppermute | solution.py:19
  135.4 3.6 %collective-permute-start.15 = (f32[640]{0:T(1024)S(1)}, f32[640]{0:T(1024)S(1)}, u32[]{:S(2)}, u32[]{:S(2)}) collective-permute-start(f32[640]{0:T(1024)S(1)} %add.55), channel_id=1, source_target_pairs={{0,16},{16,0},{1,17},{17,1},{2,18},{18,2},{3,19},{19,3},{4,20},{20... | collective-permute-start | bytes 7688 | tf_op jit(solution)/shard_map/ppermute | solution.py:19
  136.5 4.2 %collective-permute-start.12 = (bf16[1,40,640]{2,1,0:T(8,128)(2,1)S(1)}, bf16[1,40,640]{2,1,0:T(8,128)(2,1)S(1)}, u32[]{:S(2)}, u32[]{:S(2)}) collective-permute-start(bf16[1,40,640]{2,1,0:T(8,128)(2,1)S(1)} %slice.68), channel_id=1, source_target_pairs={{0,4},{2,6},{4,0},{6,2},{8,12},{10,14},{12,8},{14,10},{1,5},{3,7},... | collective-permute-start | bytes 153608 | tf_op jit(solution)/shard_map/ppermute | solution.py:462
  140.7 4.2 %collective-permute-start.13 = (bf16[40,640]{1,0:T(8,128)(2,1)S(1)}, bf16[40,640]{1,0:T(8,128)(2,1)S(1)}, u32[]{:S(2)}, u32[]{:S(2)}) collective-permute-start(bf16[40,640]{1,0:T(8,128)(2,1)S(1)} %fusion.4), channel_id=1, source_target_pairs={{0,16},{16,0},{1,17},{17,1},{2,18},{18,2},{3,19},{19,3},{4,20},{20... | collective-permute-start | bytes 153608 | tf_op jit(solution)/shard_map/ppermute | solution.py:19
  (9 other events, 59.5 us)
Sparse Core Ops, SparseCore 0:
  10.3 65.1 all-gather.1

commit v5 on v4

--- a/solution.py
+++ b/solution.py
@@ -76,6 +76,36 @@
     else:
         for i in range(number):
             body(i)
+
+
+def pack_kernel(place, weights, cot, out):
+    share, width = (weights.shape[0], cot.shape[1])
+    frames = out.shape[0]
+    count = cot.shape[0] // frames
+    x = place[0]
+    chosen = [
+        jnp.where(x == 0, weights[:, pl.ds(c * width, width)], weights[:, pl.ds((2 + c) * width, width)])
+        for c in (0, 1)
+    ]
+    for f in range(frames):
+        out[f, pl.ds(0, share), :] = chosen[f % 2]
+        out[f, pl.ds(share, count), :] = cot[pl.ds(f * count, count), :]
+
+
+def join_kernel(place, *refs):
+    pieces, out = (refs[:-1], refs[-1])
+    x, core, tile = (place[0], place[1], place[2])
+    frames = out.shape[1]
+    for dc in (0, 1):
+        own, by_tile, by_clip, low, high = pieces[5 * dc : 5 * dc + 5]
+        own_kind = 2 * x + (core ^ dc)
+        other_kind = 2 * (x ^ 1) + (core ^ dc)
+        for f in range(frames):
+            out[own_kind, f, tile] = own[f]
+            out[own_kind, f, tile ^ 1] = by_tile[f]
+            out[other_kind, f, tile] = by_clip[f]
+            part, index = (low, f) if f < frames // 2 else (high, f - frames // 2)
+            out[other_kind, f, tile ^ 1] = part[index]
 
 
 def act_kernel(place, gain, *refs, cols, part):
@@ -166,6 +196,7 @@
     depth = width // heads
     lanes = scale.shape[-1]
     third = count // 3
+    share = kept.shape[3]
     x, core, tile, plane = (place[0], place[1], place[2], place[4])
     mid_s[...] = jnp.zeros_like(mid_s)
     cot_s[...] = jnp.zeros_like(cot_s)
@@ -182,7 +213,7 @@
                 piece = [b[:, j * part : (j + 1) * part] for b in blocks]
                 start = f * padded + j * third
                 mid_s[pl.ds(start, third), :] = jnp.concatenate(piece, axis=1).astype(F32)
-            cot_s[pl.ds(f * padded, count), :] = cot_in[f].astype(F32)
+            cot_s[pl.ds(f * padded, count), :] = cot_in[f, pl.ds(share, count), :].astype(F32)
     mid = mid_s[...].astype(BF)
     cot = cot_s[...].astype(BF)
     pick = picker(width, lanes, depth, 0)
@@ -194,20 +225,20 @@
         rstd = lax.rsqrt(var + EPS)
         return cent * spread(rstd, both), rstd
 
-    hat, rstd = stats(dot(mid, weights[:, pl.ds(0, width)]))
+    hat, rstd = stats(dot(mid, weights[0]))
     q_hat[...] = hat
     q_rstd[...] = rstd
     q_norm = hat * qgain[...]
-    hat, rstd = stats(dot(mid, weights[:, pl.ds(width, width)]))
+    hat, rstd = stats(dot(mid, weights[1]))
     k_hat[...] = hat
     k_rstd[...] = rstd
     hat = hat * kgain[...]
     doubled[pl.ds(0, total), :] = hat
     doubled[pl.ds(total, total), :] = hat
-    value = dot(mid, weights[:, pl.ds(2 * width, width)]).astype(BF).astype(F32)
+    value = dot(mid, weights[2]).astype(BF).astype(F32)
     doubled_v[pl.ds(0, total), :] = value
     doubled_v[pl.ds(total, total), :] = value
-    d_mixed = dot_t(cot, weights[:, pl.ds(3 * width, width)]).astype(BF).astype(F32)
+    d_mixed = dot_t(cot, weights[3]).astype(BF).astype(F32)
     raw_s[...] = jnp.zeros_like(raw_s)
     probs_s[...] = jnp.zeros_like(probs_s)
 
@@ -299,9 +330,9 @@
 
     d_query = back(d_qn[...] * qgain[...], q_hat[...], q_rstd[...])
     d_key = back(d_kn[...] * kgain[...], k_hat[...], k_rstd[...])
-    out = dot_t(d_query, weights[:, pl.ds(0, width)])
-    out += dot_t(d_key, weights[:, pl.ds(width, width)])
-    out += dot_t(d_value[...], weights[:, pl.ds(2 * width, width)])
+    out = dot_t(d_query, weights[0])
+    out += dot_t(d_key, weights[1])
+    out += dot_t(d_value[...], weights[2])
 
     row = lax.broadcasted_iota(jnp.int32, (width, 128), 0)
     col = lax.broadcasted_iota(jnp.int32, (width, 128), 1)
@@ -363,15 +394,35 @@
     place = jnp.stack([x, core, tile, 4 * x + 2 * core + tile, plane]).astype(jnp.int32)
     flat = source.reshape(tokens, width)
 
+    (packed,) = call(
+        pack_kernel,
+        12,
+        [((frames, share + count, width), BF)],
+        [],
+        place,
+        attn_weight,
+        cot.reshape(tokens, width),
+    )
+    packed = lax.all_to_all(packed, "frame", 0, 0, tiled=True)
+    own = packed[:, :share]
+    by_tile = swap(own, "tile")
+    by_clip = swap(own, "dp")
+    middle = frames // 2
+    parts = [own, by_tile, by_clip, swap(by_clip[:middle], "tile"), swap(by_tile[middle:], "dp")]
+    parts += [swap(piece, "frame") for piece in parts]
+    (attn_full,) = call(
+        join_kernel, 16, [((4, frames, tiles, share, width), BF)], [], place, *parts
+    )
+    attn_full = attn_full.reshape(4, width, width)
+
     mine = lax.dynamic_slice_in_dim(conv_weight, x * (width // 2), width // 2, axis=2)
     mine = mine.reshape(3, 3, share, 4, part).transpose(3, 0, 2, 1, 4)
     mine = mine.reshape(4, 3, share, 3 * part)
     spread_out = jnp.broadcast_to(mine[None], (frames // 2,) + mine.shape)
-    conv_in = lax.all_to_all(spread_out.reshape((ranks,) + mine.shape[1:]), square, 0, 0, tiled=True)
-    cot_blocks, conv_in = lax.optimization_barrier((cot.reshape(frames, count, width), conv_in))
-    cot_blocks = lax.all_to_all(cot_blocks, "frame", 0, 0, tiled=True)
+    spread_out = spread_out.reshape((ranks,) + mine.shape[1:])
+    spread_out, packed = lax.optimization_barrier((spread_out, packed))
+    conv_in = lax.all_to_all(spread_out, square, 0, 0, tiled=True)
     conv_full = conv_in.transpose(1, 0, 2, 3).reshape(3, width, 3 * part)
-    attn_full = lax.all_gather(attn_weight, square, axis=0, tiled=True)
 
     half = tokens // 2
     along_x = swap(flat, "dp")
@@ -407,7 +458,6 @@
     groups = None
     if clips > 2:
         groups = [[2 * ranks * g + i for i in range(2 * ranks)] for g in range(clips // 2)]
-    mid, cot_blocks = lax.optimization_barrier((mid, cot_blocks))
     mid = lax.all_to_all(mid, ("dp",) + square, 0, 0, axis_index_groups=groups, tiled=True)
 
     lanes = frames * SLOT
@@ -432,7 +482,7 @@
             (full, F32), (full, F32), (double, F32), (double, F32), (full, F32),
             (narrow, F32), (narrow, F32),
         ],
-        place, mid, cot_blocks, attn_full, qgain, kgain, scale,
+        place, mid, packed, attn_full, qgain, kgain, scale,
     )
     d_qn, d_kn = call(
         functools.partial(slope_kernel, heads=heads, padded=padded),

time: 153 us -> 159 us (1.039)
  between operations: 14.4 us -> 1.04 us
  waiting for transfers between devices: 60.7 us -> 68.2 us
  starting transfers between devices: 36.6 us -> 42.7 us
  local copies, waits for them, and re-layouts: 10.3 us -> 13.5 us
  Pallas kernels: 27.4 us -> 30.2 us
    all_to_all x1, waiting for transfers between devices: 12.6 us -> 0.01 us  [local(): lax.all_to_all(mid, ('dp',) + square, 0, 0, axis_index_groups=groups, til...]
    ppermute x14 -> x23, waiting for transfers between devices: 28.4 us -> 40.9 us  [swap(): lax.ppermute(x, axis, [(i, i ^ 1) for i in range(lax.axis_size(axis))])]
    all_to_all x2, waiting for transfers between devices: 12.6 us -> 20.7 us  [the longest x1 20.7 us: local(): packed = lax.all_to_all(packed, 'frame', 0, 0, tiled=True)]
    unnamed x25 -> x31, local copies, waits for them, and re-layouts: 4.63 us -> 9.64 us
    ppermute x14 -> x23, starting transfers between devices: 14.1 us -> 18.5 us  [swap(): lax.ppermute(x, axis, [(i, i ^ 1) for i in range(lax.axis_size(axis))])]
    pallas_call x5 -> x7, Pallas kernels: 27.4 us -> 30.2 us  [call(): pl.pallas_call(kernel, out_shape=[jax.ShapeDtypeStruct(shape, dtype) for...]
    all_to_all x1, starting transfers between devices: 3.6 us -> 6.17 us  [local(): lax.all_to_all(mid, ('dp',) + square, 0, 0, axis_index_groups=groups, til...]
    all_to_all x2, starting transfers between devices: 13.1 us -> 10.7 us  [the longest x1 6.33 us: local(): packed = lax.all_to_all(packed, 'frame', 0, 0, tiled=True)]
  transfers between devices with their start and end apart: 21 -> 29, of which waited for: 14 -> 15; matrix products, arithmetic and copies ran while one was open for 6% -> 3% of each run, Pallas kernels for 11% -> 11%
where the time goes in v5:
time: 159 us
  waiting for transfers between devices  68.2 us (43%)
  starting transfers between devices  42.7 us (27%)
  Pallas kernels  30.2 us (19%)
  local copies, waits for them, and re-layouts  13.5 us (8%)
  other arithmetic  3.07 us (2%)
    ppermute x23, waiting for transfers between devices, swap(): lax.ppermute(x, axis, [(i, i ^ 1) for i in range(lax.axis_size(axis))])  40.9 us
    pallas_call x7, Pallas kernels, call(): pl.pallas_call(kernel, out_shape=[jax.ShapeDtypeStruct(shape, dtype) for...  30.2 us
    all_to_all x1, waiting for transfers between devices, local(): packed = lax.all_to_all(packed, 'frame', 0, 0, tiled=True)  20.7 us
    ppermute x23, starting transfers between devices, swap(): lax.ppermute(x, axis, [(i, i ^ 1) for i in range(lax.axis_size(axis))])  18.5 us
    unnamed x31, local copies, waits for them, and re-layouts  9.64 us
    all_to_all x1, starting transfers between devices, local(): packed = lax.all_to_all(packed, 'frame', 0, 0, tiled=True)  6.33 us
    all_to_all x1, starting transfers between devices, local(): lax.all_to_all(mid, ('dp',) + square, 0, 0, axis_index_groups=groups, til...  6.17 us
    all_to_all x1, waiting for transfers between devices, local(): d_back = lax.all_to_all(d_mid, 'frame', 0, 0, tiled=True)  5.16 us
  transfers between devices with their start and end apart: 29, of which 15 were waited for; matrix products, arithmetic and copies ran while one was open for 3% of the time, Pallas kernels for 11%

profile of v5, /device:TPU:0, one launch (start us, length us, event | category | flops | bytes accessed | tf_op | source)
XLA Modules:
  0.0 158.6 jit_solution(4806693620568387030)
XLA Ops:
  4.2 6.3 %all-to-all-start = ((bf16[8,76,640]{2,1,0:T(8,128)(2,1)}), bf16[8,76,640]{2,1,0:T(8,128)(2,1)S(1)}, u32[]{:S(2)}, u32[]{:S(2)}) async-start(bf16[8,76,640]{2,1,0:T(8,128)(2,1)} %shard_map.127), calls=%async_computation | async-start | bytes 1638400 | tf_op jit(solution)/shard_map/all_to_all | solution.py:406
  11.5 20.7 %all-to-all-done.cot_in = bf16[8,76,640]{2,1,0:T(8,128)(2,1)S(1)} async-done(((bf16[8,76,640]{2,1,0:T(8,128)(2,1)}), bf16[8,76,640]{2,1,0:T(8,128)(2,1)S(1)}, u32[]{:S(2)}, u32[]{:S(2)}) %all-to-all-start) | async-done | bytes 778272 | tf_op jit(solution)/shard_map/all_to_all | solution.py:406
  33.3 4.3 %all-to-all-start.1 = ((bf16[16,3,40,240]{3,2,1,0:T(8,128)(2,1)}), bf16[16,3,40,240]{3,2,1,0:T(8,128)(2,1)}, u32[]{:S(2)}, u32[]{:S(2)}) async-start(bf16[16,3,40,240]{3,2,1,0:T(8,128)(2,1)} %bitcast.6), calls=%async_computation.1 | async-start | bytes 1966080 | tf_op jit(solution)/shard_map/all_to_all | solution.py:424
  39.2 1.7 %collective-permute-start = (bf16[288,640]{1,0:T(8,128)(2,1)S(1)}, bf16[288,640]{1,0:T(8,128)(2,1)S(1)}, u32[]{:S(2)}, u32[]{:S(2)}) collective-permute-start(bf16[288,640]{1,0:T(8,128)(2,1)S(1)} %bitcast.31), channel_id=1, source_target_pairs={{0,1},{1,0},{2,3},{3,2},{4,5},{5,4},{6,7},{7,6},{8,9},{9,8},{10,11... | collective-permute-start | bytes 1105928 | tf_op jit(solution)/shard_map/ppermute | solution.py:19
  41.0 7.5 %collective-permute-done.1.refs_2_ = bf16[288,640]{1,0:T(8,128)(2,1)S(1)} collective-permute-done((bf16[288,640]{1,0:T(8,128)(2,1)S(1)}, bf16[288,640]{1,0:T(8,128)(2,1)S(1)}, u32[]{:S(2)}, u32[]{:S(2)}) %collective-permute-start.1) | collective-permute-done | bytes 368672 | tf_op jit(solution)/shard_map/ppermute | solution.py:19
  48.5 1.7 %collective-permute-start.2 = (bf16[144,640]{1,0:T(8,128)(2,1)S(1)}, bf16[144,640]{1,0:T(8,128)(2,1)S(1)}, u32[]{:S(2)}, u32[]{:S(2)}) collective-permute-start(bf16[144,640]{1,0:T(8,128)(2,1)S(1)} %slice.72), channel_id=1, source_target_pairs={{0,1},{1,0},{2,3},{3,2},{4,5},{5,4},{6,7},{7,6},{8,9},{9,8},{10,11... | collective-permute-start | bytes 552968 | tf_op jit(solution)/shard_map/ppermute | solution.py:19
  50.2 6.7 %collective-permute-done.refs_1_ = bf16[288,640]{1,0:T(8,128)(2,1)S(1)} collective-permute-done((bf16[288,640]{1,0:T(8,128)(2,1)S(1)}, bf16[288,640]{1,0:T(8,128)(2,1)S(1)}, u32[]{:S(2)}, u32[]{:S(2)}) %collective-permute-start) | collective-permute-done | bytes 368672 | tf_op jit(solution)/shard_map/ppermute | solution.py:19
  58.9 4.0 %collective-permute-done.2 = bf16[144,640]{1,0:T(8,128)(2,1)S(1)} collective-permute-done((bf16[144,640]{1,0:T(8,128)(2,1)S(1)}, bf16[144,640]{1,0:T(8,128)(2,1)S(1)}, u32[]{:S(2)}, u32[]{:S(2)}) %collective-permute-start.2) | collective-permute-done | bytes 184352 | tf_op jit(solution)/shard_map/ppermute | solution.py:19
  65.1 4.2 %shard_map.128 = (bf16[4,640,640]{2,1,0:T(8,128)(2,1)S(1)}, bf16[4,576,80]{2,1,0:T(8,128)(2,1)S(1)}) custom-call(s32[5]{0:T(128)S(1)} %stack.23.place, f32[1,640]{1,0:T(1,128)S(1)} %broadcast_in_dim.13.gain, bf16[288,640]{1,0:T(8,128)(2,1)S(1)} %bitcast.33, bf16[288,640]{1,0:T(8,128)(2,1)S(1)} %collective-permute-done.refs_1_, ...), custom_call_target="tpu_custom_call" | custom-call | tf_op jit(solution)/shard_map/pallas_call | solution.py:364
  72.3 1.9 %copy-done.5 = bf16[4,640,640]{2,1,0:T(8,128)(2,1)S(1)} copy-done((bf16[4,640,640]{2,1,0:T(8,128)(2,1)S(1)}, bf16[4,640,640]{2,1,0:T(8,128)(2,1)}, u32[]{:S(2)}) %copy-start.5) | copy-done | bytes 3276824
  74.2 5.1 %shard_map.129 = bf16[32,24,240]{2,1,0:T(8,128)(2,1)} custom-call(s32[5]{0:T(128)S(1)} %stack.23.place, bf16[3,640,240]{2,1,0:T(8,128)(2,1)S(1)} %bitcast.28, bf16[4,640,640]{2,1,0:T(8,128)(2,1)S(1)} %copy-done.5, bf16[4,576,80]{2,1,0:T(8,128)(2,1)S(1)} %get-tuple-element.25.kept), custom_call_target="tpu_custom_call" | custom-call | tf_op jit(solution)/shard_map/pallas_call | solution.py:364
  79.3 6.2 %all-to-all-start.2 = ((bf16[32,24,240]{2,1,0:T(8,128)(2,1)}), bf16[32,24,240]{2,1,0:T(8,128)(2,1)S(1)}, u32[]{:S(2)}, u32[]{:S(2)}) async-start(bf16[32,24,240]{2,1,0:T(8,128)(2,1)} %shard_map.129), calls=%async_computation.2 | async-start | bytes 786432 | tf_op jit(solution)/shard_map/all_to_all | solution.py:461
  85.8 1.7 %collective-permute-start.10 = (bf16[4,40,640]{2,1,0:T(8,128)(2,1)S(1)}, bf16[4,40,640]{2,1,0:T(8,128)(2,1)S(1)}, u32[]{:S(2)}, u32[]{:S(2)}) collective-permute-start(bf16[4,40,640]{2,1,0:T(8,128)(2,1)S(1)} %slice.75), channel_id=1, source_target_pairs={{0,1},{1,0},{2,3},{3,2},{4,5},{5,4},{6,7},{7,6},{8,9},{9,8},{10,11... | collective-permute-start | bytes 614408 | tf_op jit(solution)/shard_map/ppermute | solution.py:19
  89.6 6.4 %collective-permute-done.10.refs_3_ = bf16[4,40,640]{2,1,0:T(8,128)(2,1)S(1)} collective-permute-done((bf16[4,40,640]{2,1,0:T(8,128)(2,1)S(1)}, bf16[4,40,640]{2,1,0:T(8,128)(2,1)S(1)}, u32[]{:S(2)}, u32[]{:S(2)}) %collective-permute-start.10) | collective-permute-done | bytes 204832 | tf_op jit(solution)/shard_map/ppermute | solution.py:19
  102.2 1.9 %copy-done.2 = bf16[4,8,2,40,640]{4,3,2,1,0:T(8,128)(2,1)S(1)} copy-done((bf16[4,8,2,40,640]{4,3,2,1,0:T(8,128)(2,1)S(1)}, bf16[4,8,2,40,640]{4,3,2,1,0:T(8,128)(2,1)}, u32[]{:S(2)}) %copy-start.2) | copy-done | bytes 3276824
  104.1 10.7 %shard_map.131 = (bf16[2,2,4,40,640]{4,3,2,1,0:T(8,128)(2,1)S(1)}, bf16[2,2,4,40,640]{4,3,2,1,0:T(8,128)(2,1)S(1)}, f32[1,128]{1,0:T(1,128)S(1)}, f32[320,128]{1...) custom-call(s32[5]{0:T(128)S(1)} %stack.23.place, ...), custom_call_target="tpu_custom_call" | custom-call | tf_op jit(solution)/shard_map/pallas_call | solution.py:364
  115.0 2.2 %shard_map.132 = (f32[320,640]{1,0:T(8,128)S(1)}, f32[320,640]{1,0:T(8,128)S(1)}) custom-call(f32[320,128]{1,0:T(8,128)S(1)} %get-tuple-element.29.d_raw, f32[320,640]{1,0:T(8,128)S(1)} %get-tuple-element.30.q_hat, f32[320,640]{1,0:T(8,128)S(1)} %get-tuple-element.31.k_hat, f32[1,640]{1,0:T(1,128)S(1)} %broadcast_in_dim_tile.9.qgain, ...), custom_call_target="tpu_custom_call" | custom-call | tf_op jit(solution)/shard_map/pallas_call | solution.py:364
  119.2 4.8 %shard_map.133 = bf16[8,40,640]{2,1,0:T(8,128)(2,1)} custom-call(f32[320,640]{1,0:T(8,128)S(1)} %get-tuple-element.33.d_qn, f32[320,640]{1,0:T(8,128)S(1)} %get-tuple-element.34.d_kn, f32[320,640]{1,0:T(8,128)S(1)} %get-tuple-element.30.q_hat, f32[320,640]{1,0:T(8,128)S(1)} %get-tuple-element.31.k_hat, f32[320,128]{1,0:T(8,128)S(1)} %get-tuple-element.35.q_rstd, ...), custom_call_target="tpu_custom_call" | custom-call | tf_op jit(solution)/shard_map/pallas_call | solution.py:364
  124.0 4.7 %all-to-all-start.3 = ((bf16[8,40,640]{2,1,0:T(8,128)(2,1)}), bf16[8,40,640]{2,1,0:T(8,128)(2,1)S(1)}, u32[]{:S(2)}, u32[]{:S(2)}) async-start(bf16[8,40,640]{2,1,0:T(8,128)(2,1)} %shard_map.133), calls=%async_computation.3 | async-start | bytes 819200 | tf_op jit(solution)/shard_map/all_to_all | solution.py:515
  130.1 6.3 %collective-permute-done.19 = bf16[4,40,640]{2,1,0:T(8,128)(2,1)S(1)} collective-permute-done((bf16[4,40,640]{2,1,0:T(8,128)(2,1)S(1)}, bf16[4,40,640]{2,1,0:T(8,128)(2,1)S(1)}, u32[]{:S(2)}, u32[]{:S(2)}) %collective-permute-start.19) | collective-permute-done | bytes 204832 | tf_op jit(solution)/shard_map/ppermute | solution.py:19
  136.5 2.6 %collective-permute-start.20 = (bf16[2,40,640]{2,1,0:T(8,128)(2,1)S(1)}, bf16[2,40,640]{2,1,0:T(8,128)(2,1)S(1)}, u32[]{:S(2)}, u32[]{:S(2)}) collective-permute-start(bf16[2,40,640]{2,1,0:T(8,128)(2,1)S(1)} %slice.81), channel_id=1, source_target_pairs={{0,8},{2,10},{4,12},{6,14},{8,0},{10,2},{12,4},{14,6},{1,9},{3,11}... | collective-permute-start | bytes 307208 | tf_op jit(solution)/shard_map/ppermute | solution.py:512
  139.1 5.2 %all-to-all-done.3 = bf16[8,40,640]{2,1,0:T(8,128)(2,1)S(1)} async-done(((bf16[8,40,640]{2,1,0:T(8,128)(2,1)}), bf16[8,40,640]{2,1,0:T(8,128)(2,1)S(1)}, u32[]{:S(2)}, u32[]{:S(2)}) %all-to-all-start.3) | async-done | bytes 409632 | tf_op jit(solution)/shard_map/all_to_all | solution.py:515
  149.6 2.1 %collective-permute-done.24 = f32[640]{0:T(1024)S(1)} collective-permute-done((f32[640]{0:T(1024)S(1)}, f32[640]{0:T(1024)S(1)}, u32[]{:S(2)}, u32[]{:S(2)}) %collective-permute-start.24) | collective-permute-done | bytes 2592 | tf_op jit(solution)/shard_map/ppermute | solution.py:19
  155.0 2.9 %collective-permute-done.22 = bf16[40,640]{1,0:T(8,128)(2,1)S(1)} collective-permute-done((bf16[40,640]{1,0:T(8,128)(2,1)S(1)}, bf16[40,640]{1,0:T(8,128)(2,1)S(1)}, u32[]{:S(2)}, u32[]{:S(2)}) %collective-permute-start.22) | collective-permute-done | bytes 51232 | tf_op jit(solution)/shard_map/ppermute | solution.py:19
  (111 shorter events, 35.6 us)
Async XLA Ops:
  4.2 28.0 %all-to-all-start = ((bf16[8,76,640]{2,1,0:T(8,128)(2,1)}), bf16[8,76,640]{2,1,0:T(8,128)(2,1)S(1)}, u32[]{:S(2)}, u32[]{:S(2)}) async-start(bf16[8,76,640]{2,1,0:T(8,128)(2,1)} %shard_map.127), calls=%async_computation | async-start | bytes 1638400 | tf_op jit(solution)/shard_map/all_to_all | solution.py:406
  33.3 37.7 %all-to-all-start.1 = ((bf16[16,3,40,240]{3,2,1,0:T(8,128)(2,1)}), bf16[16,3,40,240]{3,2,1,0:T(8,128)(2,1)}, u32[]{:S(2)}, u32[]{:S(2)}) async-start(bf16[16,3,40,240]{3,2,1,0:T(8,128)(2,1)} %bitcast.6), calls=%async_computation.1 | async-start | bytes 1966080 | tf_op jit(solution)/shard_map/all_to_all | solution.py:424
  37.6 10.8 %collective-permute-start.1 = (bf16[288,640]{1,0:T(8,128)(2,1)S(1)}, bf16[288,640]{1,0:T(8,128)(2,1)S(1)}, u32[]{:S(2)}, u32[]{:S(2)}) collective-permute-start(bf16[288,640]{1,0:T(8,128)(2,1)S(1)} %bitcast.30), channel_id=1, source_target_pairs={{0,16},{16,0},{1,17},{17,1},{2,18},{18,2},{3,19},{19,3},{4,20},{20... | collective-permute-start | bytes 1105928 | tf_op jit(solution)/shard_map/ppermute | solution.py:19
  39.2 17.6 %collective-permute-start = (bf16[288,640]{1,0:T(8,128)(2,1)S(1)}, bf16[288,640]{1,0:T(8,128)(2,1)S(1)}, u32[]{:S(2)}, u32[]{:S(2)}) collective-permute-start(bf16[288,640]{1,0:T(8,128)(2,1)S(1)} %bitcast.31), channel_id=1, source_target_pairs={{0,1},{1,0},{2,3},{3,2},{4,5},{5,4},{6,7},{7,6},{8,9},{9,8},{10,11... | collective-permute-start | bytes 1105928 | tf_op jit(solution)/shard_map/ppermute | solution.py:19
  48.5 14.5 %collective-permute-start.2 = (bf16[144,640]{1,0:T(8,128)(2,1)S(1)}, bf16[144,640]{1,0:T(8,128)(2,1)S(1)}, u32[]{:S(2)}, u32[]{:S(2)}) collective-permute-start(bf16[144,640]{1,0:T(8,128)(2,1)S(1)} %slice.72), channel_id=1, source_target_pairs={{0,1},{1,0},{2,3},{3,2},{4,5},{5,4},{6,7},{7,6},{8,9},{9,8},{10,11... | collective-permute-start | bytes 552968 | tf_op jit(solution)/shard_map/ppermute | solution.py:19
  56.9 6.1 %collective-permute-start.3 = (bf16[144,640]{1,0:T(8,128)(2,1)S(1)}, bf16[144,640]{1,0:T(8,128)(2,1)S(1)}, u32[]{:S(2)}, u32[]{:S(2)}) collective-permute-start(bf16[144,640]{1,0:T(8,128)(2,1)S(1)} %slice.73), channel_id=1, source_target_pairs={{0,16},{16,0},{1,17},{17,1},{2,18},{18,2},{3,19},{19,3},{4,20},{20... | collective-permute-start | bytes 552968 | tf_op jit(solution)/shard_map/ppermute | solution.py:19
  58.4 6.3 %collective-permute-start.4 = (bf16[288,640]{1,0:T(8,128)(2,1)S(1)}, bf16[288,640]{1,0:T(8,128)(2,1)S(1)}, u32[]{:S(2)}, u32[]{:S(2)}) collective-permute-start(bf16[288,640]{1,0:T(8,128)(2,1)S(1)} %bitcast.32), channel_id=1, source_target_pairs={{0,2},{2,0},{4,6},{6,4},{8,10},{10,8},{12,14},{14,12},{1,3},{3,1},... | collective-permute-start | bytes 1105928 | tf_op jit(solution)/shard_map/ppermute | solution.py:19
  58.4 6.7 %collective-permute-start.5 = (bf16[288,640]{1,0:T(8,128)(2,1)S(1)}, bf16[288,640]{1,0:T(8,128)(2,1)S(1)}, u32[]{:S(2)}, u32[]{:S(2)}) collective-permute-start(bf16[288,640]{1,0:T(8,128)(2,1)S(1)} %collective-permute-done.refs_1_), channel_id=1, source_target_pairs={{0,2},{2,0},{4,6},{6,4},{8,10},{10,8},{12,14},{14,12},{1,3},{3,1},... | collective-permute-start | bytes 1105928 | tf_op jit(solution)/shard_map/ppermute | solution.py:19
  58.9 6.2 %collective-permute-start.6 = (bf16[288,640]{1,0:T(8,128)(2,1)S(1)}, bf16[288,640]{1,0:T(8,128)(2,1)S(1)}, u32[]{:S(2)}, u32[]{:S(2)}) collective-permute-start(bf16[288,640]{1,0:T(8,128)(2,1)S(1)} %collective-permute-done.1.refs_2_), channel_id=1, source_target_pairs={{0,2},{2,0},{4,6},{6,4},{8,10},{10,8},{12,14},{14,12},{1,3},{3,1},... | collective-permute-start | bytes 1105928 | tf_op jit(solution)/shard_map/ppermute | solution.py:19
  63.1 22.6 %collective-permute-start.9 = (bf16[8,40,640]{2,1,0:T(8,128)(2,1)S(1)}, bf16[8,40,640]{2,1,0:T(8,128)(2,1)S(1)}, u32[]{:S(2)}, u32[]{:S(2)}) collective-permute-start(bf16[8,40,640]{2,1,0:T(8,128)(2,1)S(1)} %slice.74.refs_0_), channel_id=1, source_target_pairs={{0,16},{16,0},{1,17},{17,1},{2,18},{18,2},{3,19},{19,3},{4,20},{20... | collective-permute-start | bytes 1228808 | tf_op jit(solution)/shard_map/ppermute | solution.py:19
  64.7 22.8 %collective-permute-start.8 = (bf16[8,40,640]{2,1,0:T(8,128)(2,1)S(1)}, bf16[8,40,640]{2,1,0:T(8,128)(2,1)S(1)}, u32[]{:S(2)}, u32[]{:S(2)}) collective-permute-start(bf16[8,40,640]{2,1,0:T(8,128)(2,1)S(1)} %slice.74.refs_0_), channel_id=1, source_target_pairs={{0,1},{1,0},{2,3},{3,2},{4,5},{5,4},{6,7},{7,6},{8,9},{9,8},{10,11... | collective-permute-start | bytes 1228808 | tf_op jit(solution)/shard_map/ppermute | solution.py:19
  79.3 22.9 %all-to-all-start.2 = ((bf16[32,24,240]{2,1,0:T(8,128)(2,1)}), bf16[32,24,240]{2,1,0:T(8,128)(2,1)S(1)}, u32[]{:S(2)}, u32[]{:S(2)}) async-start(bf16[32,24,240]{2,1,0:T(8,128)(2,1)} %shard_map.129), calls=%async_computation.2 | async-start | bytes 786432 | tf_op jit(solution)/shard_map/all_to_all | solution.py:461
  85.4 11.9 %collective-permute-start.12 = (bf16[8,40,640]{2,1,0:T(8,128)(2,1)S(1)}, bf16[8,40,640]{2,1,0:T(8,128)(2,1)S(1)}, u32[]{:S(2)}, u32[]{:S(2)}) collective-permute-start(bf16[8,40,640]{2,1,0:T(8,128)(2,1)S(1)} %slice.74.refs_0_), channel_id=1, source_target_pairs={{0,2},{2,0},{4,6},{6,4},{8,10},{10,8},{12,14},{14,12},{1,3},{3,1},... | collective-permute-start | bytes 1228808 | tf_op jit(solution)/shard_map/ppermute | solution.py:19
  85.8 10.2 %collective-permute-start.10 = (bf16[4,40,640]{2,1,0:T(8,128)(2,1)S(1)}, bf16[4,40,640]{2,1,0:T(8,128)(2,1)S(1)}, u32[]{:S(2)}, u32[]{:S(2)}) collective-permute-start(bf16[4,40,640]{2,1,0:T(8,128)(2,1)S(1)} %slice.75), channel_id=1, source_target_pairs={{0,1},{1,0},{2,3},{3,2},{4,5},{5,4},{6,7},{7,6},{8,9},{9,8},{10,11... | collective-permute-start | bytes 614408 | tf_op jit(solution)/shard_map/ppermute | solution.py:19
  87.6 9.8 %collective-permute-start.13 = (bf16[8,40,640]{2,1,0:T(8,128)(2,1)S(1)}, bf16[8,40,640]{2,1,0:T(8,128)(2,1)}, u32[]{:S(2)}, u32[]{:S(2)}) collective-permute-start(bf16[8,40,640]{2,1,0:T(8,128)(2,1)S(1)} %collective-permute-done.8.refs_1_), channel_id=1, source_target_pairs={{0,2},{2,0},{4,6},{6,4},{8,10},{10,8},{12,14},{14,12},{1,3},{3,1},... | collective-permute-start | bytes 1228808 | tf_op jit(solution)/shard_map/ppermute | solution.py:19
  87.7 9.7 %collective-permute-start.14 = (bf16[8,40,640]{2,1,0:T(8,128)(2,1)S(1)}, bf16[8,40,640]{2,1,0:T(8,128)(2,1)}, u32[]{:S(2)}, u32[]{:S(2)}) collective-permute-start(bf16[8,40,640]{2,1,0:T(8,128)(2,1)S(1)} %collective-permute-done.9.refs_2_), channel_id=1, source_target_pairs={{0,2},{2,0},{4,6},{6,4},{8,10},{10,8},{12,14},{14,12},{1,3},{3,1},... | collective-permute-start | bytes 1228808 | tf_op jit(solution)/shard_map/ppermute | solution.py:19
  88.1 9.0 %collective-permute-start.11 = (bf16[4,40,640]{2,1,0:T(8,128)(2,1)S(1)}, bf16[4,40,640]{2,1,0:T(8,128)(2,1)}, u32[]{:S(2)}, u32[]{:S(2)}) collective-permute-start(bf16[4,40,640]{2,1,0:T(8,128)(2,1)S(1)} %slice.76), channel_id=1, source_target_pairs={{0,16},{16,0},{1,17},{17,1},{2,18},{18,2},{3,19},{19,3},{4,20},{20... | collective-permute-start | bytes 614408 | tf_op jit(solution)/shard_map/ppermute | solution.py:19
  117.5 11.9 %collective-permute-start.18 = (bf16[2,4,40,640]{3,2,1,0:T(8,128)(2,1)S(1)}, bf16[2,4,40,640]{3,2,1,0:T(8,128)(2,1)S(1)}, u32[]{:S(2)}, u32[]{:S(2)}) collective-permute-start(bf16[2,4,40,640]{3,2,1,0:T(8,128)(2,1)S(1)} %slice_bitcast_fusion), channel_id=1, source_target_pairs={{0,16},{16,0},{1,17},{17,1},{2,18},{18,2},{3,19},{19,3},{4,20},{20... | collective-permute-start | bytes 1228808 | tf_op jit(solution)/shard_map/ppermute | solution.py:19
  124.0 20.3 %all-to-all-start.3 = ((bf16[8,40,640]{2,1,0:T(8,128)(2,1)}), bf16[8,40,640]{2,1,0:T(8,128)(2,1)S(1)}, u32[]{:S(2)}, u32[]{:S(2)}) async-start(bf16[8,40,640]{2,1,0:T(8,128)(2,1)} %shard_map.133), calls=%async_computation.3 | async-start | bytes 819200 | tf_op jit(solution)/shard_map/all_to_all | solution.py:515
  129.5 6.9 %collective-permute-start.19 = (bf16[4,40,640]{2,1,0:T(8,128)(2,1)S(1)}, bf16[4,40,640]{2,1,0:T(8,128)(2,1)S(1)}, u32[]{:S(2)}, u32[]{:S(2)}) collective-permute-start(bf16[4,40,640]{2,1,0:T(8,128)(2,1)S(1)} %slice_bitcast_fusion.1), channel_id=1, source_target_pairs={{0,1},{1,0},{2,3},{3,2},{4,5},{5,4},{6,7},{7,6},{8,9},{9,8},{10,11... | collective-permute-start | bytes 614408 | tf_op jit(solution)/shard_map/ppermute | solution.py:19
  136.5 13.0 %collective-permute-start.20 = (bf16[2,40,640]{2,1,0:T(8,128)(2,1)S(1)}, bf16[2,40,640]{2,1,0:T(8,128)(2,1)S(1)}, u32[]{:S(2)}, u32[]{:S(2)}) collective-permute-start(bf16[2,40,640]{2,1,0:T(8,128)(2,1)S(1)} %slice.81), channel_id=1, source_target_pairs={{0,8},{2,10},{4,12},{6,14},{8,0},{10,2},{12,4},{14,6},{1,9},{3,11}... | collective-permute-start | bytes 307208 | tf_op jit(solution)/shard_map/ppermute | solution.py:512
  144.5 3.7 %collective-permute-start.23 = (f32[640]{0:T(1024)S(1)}, f32[640]{0:T(1024)S(1)}, u32[]{:S(2)}, u32[]{:S(2)}) collective-permute-start(f32[640]{0:T(1024)S(1)} %convert_reduce_fusion), channel_id=1, source_target_pairs={{0,1},{1,0},{2,3},{3,2},{4,5},{5,4},{6,7},{7,6},{8,9},{9,8},{10,11... | collective-permute-start | bytes 7688 | tf_op jit(solution)/shard_map/ppermute | solution.py:19
  149.5 4.2 %collective-permute-start.21 = (bf16[1,40,640]{2,1,0:T(8,128)(2,1)S(1)}, bf16[1,40,640]{2,1,0:T(8,128)(2,1)S(1)}, u32[]{:S(2)}, u32[]{:S(2)}) collective-permute-start(bf16[1,40,640]{2,1,0:T(8,128)(2,1)S(1)} %slice.83), channel_id=1, source_target_pairs={{0,4},{2,6},{4,0},{6,2},{8,12},{10,14},{12,8},{14,10},{1,5},{3,7},... | collective-permute-start | bytes 153608 | tf_op jit(solution)/shard_map/ppermute | solution.py:512
  153.7 4.2 %collective-permute-start.22 = (bf16[40,640]{1,0:T(8,128)(2,1)S(1)}, bf16[40,640]{1,0:T(8,128)(2,1)S(1)}, u32[]{:S(2)}, u32[]{:S(2)}) collective-permute-start(bf16[40,640]{1,0:T(8,128)(2,1)S(1)} %fusion.4), channel_id=1, source_target_pairs={{0,16},{16,0},{1,17},{17,1},{2,18},{18,2},{3,19},{19,3},{4,20},{20... | collective-permute-start | bytes 153608 | tf_op jit(solution)/shard_map/ppermute | solution.py:19
  (20 other events, 186.8 us)

commit v6 on v4

--- a/solution.py
+++ b/solution.py
@@ -76,6 +76,33 @@
     else:
         for i in range(number):
             body(i)
+
+
+def taps_kernel(place, mine, theirs, out):
+    odd = place[4] % 2
+    share = out.shape[2]
+    for owner in range(mine.shape[0]):
+        first = jnp.where(odd == 0, mine[owner], theirs[owner])
+        second = jnp.where(odd == 0, theirs[owner], mine[owner])
+        block = jnp.concatenate([first, second], axis=0)
+        for row in range(3):
+            out[row, owner] = block[row * share : (row + 1) * share]
+
+
+def join_kernel(place, *refs):
+    pieces, out = (refs[:-1], refs[-1])
+    x, core, tile = (place[0], place[1], place[2])
+    frames = out.shape[1]
+    for dc in (0, 1):
+        own, by_tile, by_clip, low, high = pieces[5 * dc : 5 * dc + 5]
+        own_kind = 2 * x + (core ^ dc)
+        other_kind = 2 * (x ^ 1) + (core ^ dc)
+        for f in range(frames):
+            out[own_kind, f, tile] = own[f]
+            out[own_kind, f, tile ^ 1] = by_tile[f]
+            out[other_kind, f, tile] = by_clip[f]
+            part, index = (low, f) if f < frames // 2 else (high, f - frames // 2)
+            out[other_kind, f, tile ^ 1] = part[index]
 
 
 def act_kernel(place, gain, *refs, cols, part):
@@ -194,20 +221,20 @@
         rstd = lax.rsqrt(var + EPS)
         return cent * spread(rstd, both), rstd
 
-    hat, rstd = stats(dot(mid, weights[:, pl.ds(0, width)]))
+    hat, rstd = stats(dot(mid, weights[0]))
     q_hat[...] = hat
     q_rstd[...] = rstd
     q_norm = hat * qgain[...]
-    hat, rstd = stats(dot(mid, weights[:, pl.ds(width, width)]))
+    hat, rstd = stats(dot(mid, weights[1]))
     k_hat[...] = hat
     k_rstd[...] = rstd
     hat = hat * kgain[...]
     doubled[pl.ds(0, total), :] = hat
     doubled[pl.ds(total, total), :] = hat
-    value = dot(mid, weights[:, pl.ds(2 * width, width)]).astype(BF).astype(F32)
+    value = dot(mid, weights[2]).astype(BF).astype(F32)
     doubled_v[pl.ds(0, total), :] = value
     doubled_v[pl.ds(total, total), :] = value
-    d_mixed = dot_t(cot, weights[:, pl.ds(3 * width, width)]).astype(BF).astype(F32)
+    d_mixed = dot_t(cot, weights[3]).astype(BF).astype(F32)
     raw_s[...] = jnp.zeros_like(raw_s)
     probs_s[...] = jnp.zeros_like(probs_s)
 
@@ -299,9 +326,9 @@
 
     d_query = back(d_qn[...] * qgain[...], q_hat[...], q_rstd[...])
     d_key = back(d_kn[...] * kgain[...], k_hat[...], k_rstd[...])
-    out = dot_t(d_query, weights[:, pl.ds(0, width)])
-    out += dot_t(d_key, weights[:, pl.ds(width, width)])
-    out += dot_t(d_value[...], weights[:, pl.ds(2 * width, width)])
+    out = dot_t(d_query, weights[0])
+    out += dot_t(d_key, weights[1])
+    out += dot_t(d_value[...], weights[2])
 
     row = lax.broadcasted_iota(jnp.int32, (width, 128), 0)
     col = lax.broadcasted_iota(jnp.int32, (width, 128), 1)
@@ -363,19 +390,27 @@
     place = jnp.stack([x, core, tile, 4 * x + 2 * core + tile, plane]).astype(jnp.int32)
     flat = source.reshape(tokens, width)
 
+    lines = 3 * share // 2
     mine = lax.dynamic_slice_in_dim(conv_weight, x * (width // 2), width // 2, axis=2)
     mine = mine.reshape(3, 3, share, 4, part).transpose(3, 0, 2, 1, 4)
-    mine = mine.reshape(4, 3, share, 3 * part)
-    spread_out = jnp.broadcast_to(mine[None], (frames // 2,) + mine.shape)
-    conv_in = lax.all_to_all(spread_out.reshape((ranks,) + mine.shape[1:]), square, 0, 0, tiled=True)
-    cot_blocks, conv_in = lax.optimization_barrier((cot.reshape(frames, count, width), conv_in))
-    cot_blocks = lax.all_to_all(cot_blocks, "frame", 0, 0, tiled=True)
-    conv_full = conv_in.transpose(1, 0, 2, 3).reshape(3, width, 3 * part)
-    attn_full = lax.all_gather(attn_weight, square, axis=0, tiled=True)
-
-    half = tokens // 2
+    mine = mine.reshape(4, 2, lines, 3 * part).transpose(1, 0, 2, 3)
+    mine = jnp.broadcast_to(mine[None], (frames // 4,) + mine.shape)
+    mine = mine.reshape(ranks, lines, 3 * part)
+    conv_half = lax.all_to_all(mine, square, 0, 0, tiled=True)
+
     along_x = swap(flat, "dp")
     along_y = swap(flat, "tile")
+
+    kinds = lax.dynamic_slice_in_dim(attn_weight, x * 2 * width, 2 * width, axis=1)
+    kinds = kinds.reshape(share, 2, width).transpose(1, 0, 2)
+    kinds = jnp.broadcast_to(kinds[None], (frames // 2,) + kinds.shape).reshape(frames, share, width)
+    kinds, conv_half, along_x, along_y = lax.optimization_barrier(
+        (kinds, conv_half, along_x, along_y)
+    )
+    own = lax.all_to_all(kinds, "frame", 0, 0, tiled=True)
+    conv_other = lax.ppermute(conv_half, "frame", [(i, i ^ 2) for i in range(frames)])
+
+    half = tokens // 2
     across = jnp.concatenate([swap(along_x[:half], "tile"), swap(along_y[half:], "dp")])
     pieces = [flat, along_y, along_x, across]
     pieces += [swap(piece, "frame") for piece in pieces]
@@ -389,6 +424,18 @@
         *pieces,
     )
 
+    cot_blocks = cot.reshape(frames, count, width)
+    cot_blocks, own, acts, kept, conv_half, conv_other = lax.optimization_barrier(
+        (cot_blocks, own, acts, kept, conv_half, conv_other)
+    )
+    cot_blocks = lax.all_to_all(cot_blocks, "frame", 0, 0, tiled=True)
+    by_tile = swap(own, "tile")
+    by_clip = swap(own, "dp")
+
+    (conv_full,) = call(
+        taps_kernel, 12, [((3, ranks, share, 3 * part), BF)], [], place, conv_half, conv_other
+    )
+    conv_full = conv_full.reshape(3, width, 3 * part)
     blocked = (2 * ranks, 2 * third, 3 * part)
     plain = (2, 2, tiles * tokens, part)
     (mid,) = call(
@@ -404,11 +451,21 @@
     if frames > 8:
         mid = mid.reshape(2, 2, tiles, frames, 3, third, part).transpose(0, 3, 2, 1, 5, 4, 6)
         mid = mid.reshape(blocked)
+    mid, cot_blocks, by_tile, by_clip = lax.optimization_barrier(
+        (mid, cot_blocks, by_tile, by_clip)
+    )
     groups = None
     if clips > 2:
         groups = [[2 * ranks * g + i for i in range(2 * ranks)] for g in range(clips // 2)]
-    mid, cot_blocks = lax.optimization_barrier((mid, cot_blocks))
     mid = lax.all_to_all(mid, ("dp",) + square, 0, 0, axis_index_groups=groups, tiled=True)
+
+    middle = frames // 2
+    parts = [own, by_tile, by_clip, swap(by_clip[:middle], "tile"), swap(by_tile[middle:], "dp")]
+    parts += [swap(piece, "frame") for piece in parts]
+    (attn_full,) = call(
+        join_kernel, 16, [((4, frames, tiles, share, width), BF)], [], place, *parts
+    )
+    attn_full = attn_full.reshape(4, width, width)
 
     lanes = frames * SLOT
     padded = round_up(count + 3, 8)

time: 153 us -> 151 us (0.987)
  between operations: 14.4 us -> 1.04 us
  starting transfers between devices: 36.6 us -> 48.8 us
  waiting for transfers between devices: 60.7 us -> 49.6 us
  local copies, waits for them, and re-layouts: 10.3 us -> 16.8 us
  Pallas kernels: 27.4 us -> 30.5 us
    all_to_all x1, waiting for transfers between devices: 12.6 us -> 0.01 us  [local(): lax.all_to_all(mid, ('dp',) + square, 0, 0, axis_index_groups=groups, til...]
    ppermute x14 -> x23, waiting for transfers between devices: 28.4 us -> 40.1 us  [swap(): lax.ppermute(x, axis, [(i, i ^ 1) for i in range(lax.axis_size(axis))])]
    unnamed x25 -> x33, local copies, waits for them, and re-layouts: 4.63 us -> 11.6 us
    all_to_all x1 -> x2, waiting for transfers between devices: 6.55 us -> 0.01 us  [the longest x1 0.01 us: local(): conv_half = lax.all_to_all(mine, square, 0, 0, tiled=True)]
    all_to_all x1, waiting for transfers between devices: 6.06 us -> 0.01 us  [local(): cot_blocks = lax.all_to_all(cot_blocks, 'frame', 0, 0, tiled=True)]
    ppermute x14 -> x23, starting transfers between devices: 14.1 us -> 18.7 us  [swap(): lax.ppermute(x, axis, [(i, i ^ 1) for i in range(lax.axis_size(axis))])]
    all_to_all x1 -> x2, starting transfers between devices: 7.52 us -> 12.1 us  [the longest x1 7.39 us: local(): conv_half = lax.all_to_all(mine, square, 0, 0, tiled=True)]
    pallas_call x5 -> x7, Pallas kernels: 27.4 us -> 30.5 us  [call(): pl.pallas_call(kernel, out_shape=[jax.ShapeDtypeStruct(shape, dtype) for...]
  transfers between devices with their start and end apart: 21 -> 31, of which waited for: 14 -> 16; matrix products, arithmetic and copies ran while one was open for 6% -> 3% of each run, Pallas kernels for 11% -> 13%
where the time goes in v6:
time: 151 us; the launch traced here: 150 us
  waiting for transfers between devices  49.6 us (33%)
  starting transfers between devices  48.8 us (32%)
  Pallas kernels  30.5 us (20%)
  local copies, waits for them, and re-layouts  16.8 us (11%)
  other arithmetic  3.08 us (2%)
    ppermute x23, waiting for transfers between devices, swap(): lax.ppermute(x, axis, [(i, i ^ 1) for i in range(lax.axis_size(axis))])  40.1 us
    pallas_call x7, Pallas kernels, call(): pl.pallas_call(kernel, out_shape=[jax.ShapeDtypeStruct(shape, dtype) for...  30.5 us
    ppermute x23, starting transfers between devices, swap(): lax.ppermute(x, axis, [(i, i ^ 1) for i in range(lax.axis_size(axis))])  18.7 us
    unnamed x33, local copies, waits for them, and re-layouts  11.6 us
    all_to_all x1, starting transfers between devices, local(): conv_half = lax.all_to_all(mine, square, 0, 0, tiled=True)  7.39 us
    all_to_all x1, waiting for transfers between devices, local(): d_back = lax.all_to_all(d_mid, 'frame', 0, 0, tiled=True)  5.16 us
    all_to_all x1, starting transfers between devices, local(): lax.all_to_all(mid, ('dp',) + square, 0, 0, axis_index_groups=groups, til...  4.91 us
    all_to_all x1, starting transfers between devices, local(): d_back = lax.all_to_all(d_mid, 'frame', 0, 0, tiled=True)  4.77 us
  transfers between devices with their start and end apart: 31, of which 16 were waited for; matrix products, arithmetic and copies ran while one was open for 3% of the time, Pallas kernels for 13%

profile of v6, /device:TPU:0, one launch (start us, length us, event | category | flops | bytes accessed | tf_op | source)
XLA Modules:
  0.0 149.7 jit_solution(17583550721822511204)
XLA Ops:
  3.7 7.4 %all-to-all-start = ((bf16[16,60,240]{2,1,0:T(8,128)(2,1)}), bf16[16,60,240]{2,1,0:T(8,128)(2,1)S(1)}, u32[]{:S(2)}, u32[]{:S(2)}) async-start(bf16[16,60,240]{2,1,0:T(8,128)(2,1)} %bitcast.9), calls=%async_computation | async-start | bytes 1048576 | tf_op jit(solution)/shard_map/all_to_all | solution.py:399
  11.1 2.0 %collective-permute-start.1 = (bf16[288,640]{1,0:T(8,128)(2,1)S(1)}, bf16[288,640]{1,0:T(8,128)(2,1)S(1)}, u32[]{:S(2)}, u32[]{:S(2)}) collective-permute-start(bf16[288,640]{1,0:T(8,128)(2,1)S(1)} %bitcast.34), channel_id=1, source_target_pairs={{0,1},{1,0},{2,3},{3,2},{4,5},{5,4},{6,7},{7,6},{8,9},{9,8},{10,11... | collective-permute-start | bytes 1105928 | tf_op jit(solution)/shard_map/ppermute | solution.py:19
  14.6 13.1 %collective-permute-done.1.refs_1_ = bf16[288,640]{1,0:T(8,128)(2,1)S(1)} collective-permute-done((bf16[288,640]{1,0:T(8,128)(2,1)S(1)}, bf16[288,640]{1,0:T(8,128)(2,1)S(1)}, u32[]{:S(2)}, u32[]{:S(2)}) %collective-permute-start.1) | collective-permute-done | bytes 368672 | tf_op jit(solution)/shard_map/ppermute | solution.py:19
  29.0 4.7 %all-to-all-start.1 = ((bf16[8,40,640]{2,1,0:T(8,128)(2,1)}), bf16[8,40,640]{2,1,0:T(8,128)(2,1)S(1)}, u32[]{:S(2)}, u32[]{:S(2)}) async-start(bf16[8,40,640]{2,1,0:T(8,128)(2,1)} %bitcast.6), calls=%async_computation.1 | async-start | bytes 819200 | tf_op jit(solution)/shard_map/all_to_all | solution.py:410
  36.0 1.8 %collective-permute-start.8 = (bf16[16,60,240]{2,1,0:T(8,128)(2,1)S(1)}, bf16[16,60,240]{2,1,0:T(8,128)(2,1)}, u32[]{:S(2)}, u32[]{:S(2)}) collective-permute-start(bf16[16,60,240]{2,1,0:T(8,128)(2,1)S(1)} %all-to-all-done.mine), channel_id=1, source_target_pairs={{0,4},{2,6},{4,0},{6,2},{8,12},{10,14},{12,8},{14,10},{1,5},{3,7},... | collective-permute-start | bytes 1382408 | tf_op jit(solution)/shard_map/ppermute | solution.py:411
  37.8 3.0 %collective-permute-done.3 = bf16[144,640]{1,0:T(8,128)(2,1)S(1)} collective-permute-done((bf16[144,640]{1,0:T(8,128)(2,1)S(1)}, bf16[144,640]{1,0:T(8,128)(2,1)S(1)}, u32[]{:S(2)}, u32[]{:S(2)}) %collective-permute-start.3) | collective-permute-done | bytes 184352 | tf_op jit(solution)/shard_map/ppermute | solution.py:19
  41.0 1.8 %reshape_squeeze.6 = bf16[8,36,640]{2,1,0:T(8,128)(2,1)} reshape(bf16[1,1,9,32,640]{4,3,2,1,0:T(8,128)(2,1)} %param.9) | data formatting | bytes 737280 | tf_op jit(solution)/shard_map/reshape;squeeze | solution.py:427
  45.6 4.8 %shard_map.127 = (bf16[4,640,640]{2,1,0:T(8,128)(2,1)S(1)}, bf16[4,576,80]{2,1,0:T(8,128)(2,1)S(1)}) custom-call(s32[5]{0:T(128)S(1)} %stack.23.place, f32[1,640]{1,0:T(1,128)S(1)} %broadcast_in_dim.8.gain, bf16[288,640]{1,0:T(8,128)(2,1)S(1)} %bitcast.37, bf16[288,640]{1,0:T(8,128)(2,1)S(1)} %collective-permute-done.1.refs_1_, ...), custom_call_target="tpu_custom_call" | custom-call | tf_op jit(solution)/shard_map/pallas_call | solution.py:360
  52.1 2.7 %collective-permute-done.8.theirs = bf16[16,60,240]{2,1,0:T(8,128)(2,1)} collective-permute-done((bf16[16,60,240]{2,1,0:T(8,128)(2,1)S(1)}, bf16[16,60,240]{2,1,0:T(8,128)(2,1)}, u32[]{:S(2)}, u32[]{:S(2)}) %collective-permute-start.8) | collective-permute-done | bytes 460832 | tf_op jit(solution)/shard_map/ppermute | solution.py:411
  54.9 3.8 %all-to-all-start.2 = ((bf16[8,36,640]{2,1,0:T(8,128)(2,1)}), bf16[8,36,640]{2,1,0:T(8,128)(2,1)S(1)}, u32[]{:S(2)}, u32[]{:S(2)}) async-start(bf16[8,36,640]{2,1,0:T(8,128)(2,1)} %reshape_squeeze.6), calls=%async_computation.2 | async-start | bytes 819200 | tf_op jit(solution)/shard_map/all_to_all | solution.py:431
  62.8 1.9 %copy-done.5 = bf16[4,640,640]{2,1,0:T(8,128)(2,1)S(1)} copy-done((bf16[4,640,640]{2,1,0:T(8,128)(2,1)S(1)}, bf16[4,640,640]{2,1,0:T(8,128)(2,1)}, u32[]{:S(2)}) %copy-start.5) | copy-done | bytes 3276824
  64.7 5.1 %shard_map.129 = bf16[32,24,240]{2,1,0:T(8,128)(2,1)} custom-call(s32[5]{0:T(128)S(1)} %stack.23.place, bf16[3,640,240]{2,1,0:T(8,128)(2,1)S(1)} %bitcast.33, bf16[4,640,640]{2,1,0:T(8,128)(2,1)S(1)} %copy-done.5, bf16[4,576,80]{2,1,0:T(8,128)(2,1)S(1)} %get-tuple-element.44.kept), custom_call_target="tpu_custom_call" | custom-call | tf_op jit(solution)/shard_map/pallas_call | solution.py:360
  71.7 4.9 %all-to-all-start.3 = ((bf16[32,24,240]{2,1,0:T(8,128)(2,1)}), bf16[32,24,240]{2,1,0:T(8,128)(2,1)S(1)}, u32[]{:S(2)}, u32[]{:S(2)}) async-start(bf16[32,24,240]{2,1,0:T(8,128)(2,1)} %shard_map.129), calls=%async_computation.3 | async-start | bytes 786432 | tf_op jit(solution)/shard_map/all_to_all | solution.py:460
  80.8 6.5 %collective-permute-done.11.refs_3_ = bf16[4,40,640]{2,1,0:T(8,128)(2,1)} collective-permute-done((bf16[4,40,640]{2,1,0:T(8,128)(2,1)S(1)}, bf16[4,40,640]{2,1,0:T(8,128)(2,1)}, u32[]{:S(2)}, u32[]{:S(2)}) %collective-permute-start.11) | collective-permute-done | bytes 204832 | tf_op jit(solution)/shard_map/ppermute | solution.py:19
  93.2 1.9 %copy-done.2 = bf16[4,8,2,40,640]{4,3,2,1,0:T(8,128)(2,1)S(1)} copy-done((bf16[4,8,2,40,640]{4,3,2,1,0:T(8,128)(2,1)S(1)}, bf16[4,8,2,40,640]{4,3,2,1,0:T(8,128)(2,1)}, u32[]{:S(2)}) %copy-start.2) | copy-done | bytes 3276824
  95.2 10.6 %shard_map.131 = (bf16[2,2,4,40,640]{4,3,2,1,0:T(8,128)(2,1)S(1)}, bf16[2,2,4,40,640]{4,3,2,1,0:T(8,128)(2,1)S(1)}, f32[1,128]{1,0:T(1,128)S(1)}, f32[320,128]{1...) custom-call(s32[5]{0:T(128)S(1)} %stack.23.place, ...), custom_call_target="tpu_custom_call" | custom-call | tf_op jit(solution)/shard_map/pallas_call | solution.py:360
  106.0 2.2 %shard_map.132 = (f32[320,640]{1,0:T(8,128)S(1)}, f32[320,640]{1,0:T(8,128)S(1)}) custom-call(f32[320,128]{1,0:T(8,128)S(1)} %get-tuple-element.53.d_raw, f32[320,640]{1,0:T(8,128)S(1)} %get-tuple-element.54.q_hat, f32[320,640]{1,0:T(8,128)S(1)} %get-tuple-element.55.k_hat, f32[1,640]{1,0:T(1,128)S(1)} %broadcast_in_dim_tile.9.qgain, ...), custom_call_target="tpu_custom_call" | custom-call | tf_op jit(solution)/shard_map/pallas_call | solution.py:360
  110.2 4.9 %shard_map.133 = bf16[8,40,640]{2,1,0:T(8,128)(2,1)} custom-call(f32[320,640]{1,0:T(8,128)S(1)} %get-tuple-element.57.d_qn, f32[320,640]{1,0:T(8,128)S(1)} %get-tuple-element.58.d_kn, f32[320,640]{1,0:T(8,128)S(1)} %get-tuple-element.54.q_hat, f32[320,640]{1,0:T(8,128)S(1)} %get-tuple-element.55.k_hat, f32[320,128]{1,0:T(8,128)S(1)} %get-tuple-element.59.q_rstd, ...), custom_call_target="tpu_custom_call" | custom-call | tf_op jit(solution)/shard_map/pallas_call | solution.py:360
  115.1 4.8 %all-to-all-start.4 = ((bf16[8,40,640]{2,1,0:T(8,128)(2,1)}), bf16[8,40,640]{2,1,0:T(8,128)(2,1)S(1)}, u32[]{:S(2)}, u32[]{:S(2)}) async-start(bf16[8,40,640]{2,1,0:T(8,128)(2,1)} %shard_map.133), calls=%async_computation.4 | async-start | bytes 819200 | tf_op jit(solution)/shard_map/all_to_all | solution.py:522
  121.3 6.2 %collective-permute-done.20 = bf16[4,40,640]{2,1,0:T(8,128)(2,1)S(1)} collective-permute-done((bf16[4,40,640]{2,1,0:T(8,128)(2,1)S(1)}, bf16[4,40,640]{2,1,0:T(8,128)(2,1)S(1)}, u32[]{:S(2)}, u32[]{:S(2)}) %collective-permute-start.20) | collective-permute-done | bytes 204832 | tf_op jit(solution)/shard_map/ppermute | solution.py:19
  127.6 2.6 %collective-permute-start.21 = (bf16[2,40,640]{2,1,0:T(8,128)(2,1)S(1)}, bf16[2,40,640]{2,1,0:T(8,128)(2,1)S(1)}, u32[]{:S(2)}, u32[]{:S(2)}) collective-permute-start(bf16[2,40,640]{2,1,0:T(8,128)(2,1)S(1)} %slice.72), channel_id=1, source_target_pairs={{0,8},{2,10},{4,12},{6,14},{8,0},{10,2},{12,4},{14,6},{1,9},{3,11}... | collective-permute-start | bytes 307208 | tf_op jit(solution)/shard_map/ppermute | solution.py:519
  130.2 5.2 %all-to-all-done.4 = bf16[8,40,640]{2,1,0:T(8,128)(2,1)S(1)} async-done(((bf16[8,40,640]{2,1,0:T(8,128)(2,1)}), bf16[8,40,640]{2,1,0:T(8,128)(2,1)S(1)}, u32[]{:S(2)}, u32[]{:S(2)}) %all-to-all-start.4) | async-done | bytes 409632 | tf_op jit(solution)/shard_map/all_to_all | solution.py:522
  140.7 2.0 %collective-permute-done.25 = f32[640]{0:T(1024)S(1)} collective-permute-done((f32[640]{0:T(1024)S(1)}, f32[640]{0:T(1024)S(1)}, u32[]{:S(2)}, u32[]{:S(2)}) %collective-permute-start.25) | collective-permute-done | bytes 2592 | tf_op jit(solution)/shard_map/ppermute | solution.py:19
  146.0 3.1 %collective-permute-done.23 = bf16[40,640]{1,0:T(8,128)(2,1)S(1)} collective-permute-done((bf16[40,640]{1,0:T(8,128)(2,1)S(1)}, bf16[40,640]{1,0:T(8,128)(2,1)S(1)}, u32[]{:S(2)}, u32[]{:S(2)}) %collective-permute-start.23) | collective-permute-done | bytes 51232 | tf_op jit(solution)/shard_map/ppermute | solution.py:19
  (121 shorter events, 41.7 us)
Async XLA Ops:
  3.7 24.0 %all-to-all-start = ((bf16[16,60,240]{2,1,0:T(8,128)(2,1)}), bf16[16,60,240]{2,1,0:T(8,128)(2,1)S(1)}, u32[]{:S(2)}, u32[]{:S(2)}) async-start(bf16[16,60,240]{2,1,0:T(8,128)(2,1)} %bitcast.9), calls=%async_computation | async-start | bytes 1048576 | tf_op jit(solution)/shard_map/all_to_all | solution.py:399
  11.1 16.6 %collective-permute-start.1 = (bf16[288,640]{1,0:T(8,128)(2,1)S(1)}, bf16[288,640]{1,0:T(8,128)(2,1)S(1)}, u32[]{:S(2)}, u32[]{:S(2)}) collective-permute-start(bf16[288,640]{1,0:T(8,128)(2,1)S(1)} %bitcast.34), channel_id=1, source_target_pairs={{0,1},{1,0},{2,3},{3,2},{4,5},{5,4},{6,7},{7,6},{8,9},{9,8},{10,11... | collective-permute-start | bytes 1105928 | tf_op jit(solution)/shard_map/ppermute | solution.py:19
  13.0 14.7 %collective-permute-start = (bf16[288,640]{1,0:T(8,128)(2,1)S(1)}, bf16[288,640]{1,0:T(8,128)(2,1)S(1)}, u32[]{:S(2)}, u32[]{:S(2)}) collective-permute-start(bf16[288,640]{1,0:T(8,128)(2,1)S(1)} %bitcast.35), channel_id=1, source_target_pairs={{0,16},{16,0},{1,17},{17,1},{2,18},{18,2},{3,19},{19,3},{4,20},{20... | collective-permute-start | bytes 1105928 | tf_op jit(solution)/shard_map/ppermute | solution.py:19
  28.5 7.5 %collective-permute-start.2 = (bf16[144,640]{1,0:T(8,128)(2,1)S(1)}, bf16[144,640]{1,0:T(8,128)(2,1)S(1)}, u32[]{:S(2)}, u32[]{:S(2)}) collective-permute-start(bf16[144,640]{1,0:T(8,128)(2,1)S(1)} %slice.51), channel_id=1, source_target_pairs={{0,1},{1,0},{2,3},{3,2},{4,5},{5,4},{6,7},{7,6},{8,9},{9,8},{10,11... | collective-permute-start | bytes 552968 | tf_op jit(solution)/shard_map/ppermute | solution.py:19
  29.0 25.9 %all-to-all-start.1 = ((bf16[8,40,640]{2,1,0:T(8,128)(2,1)}), bf16[8,40,640]{2,1,0:T(8,128)(2,1)S(1)}, u32[]{:S(2)}, u32[]{:S(2)}) async-start(bf16[8,40,640]{2,1,0:T(8,128)(2,1)} %bitcast.6), calls=%async_computation.1 | async-start | bytes 819200 | tf_op jit(solution)/shard_map/all_to_all | solution.py:410
  33.7 7.1 %collective-permute-start.3 = (bf16[144,640]{1,0:T(8,128)(2,1)S(1)}, bf16[144,640]{1,0:T(8,128)(2,1)S(1)}, u32[]{:S(2)}, u32[]{:S(2)}) collective-permute-start(bf16[144,640]{1,0:T(8,128)(2,1)S(1)} %slice.52), channel_id=1, source_target_pairs={{0,16},{16,0},{1,17},{17,1},{2,18},{18,2},{3,19},{19,3},{4,20},{20... | collective-permute-start | bytes 552968 | tf_op jit(solution)/shard_map/ppermute | solution.py:19
  35.3 7.6 %collective-permute-start.4 = (bf16[288,640]{1,0:T(8,128)(2,1)S(1)}, bf16[288,640]{1,0:T(8,128)(2,1)S(1)}, u32[]{:S(2)}, u32[]{:S(2)}) collective-permute-start(bf16[288,640]{1,0:T(8,128)(2,1)S(1)} %bitcast.36), channel_id=1, source_target_pairs={{0,2},{2,0},{4,6},{6,4},{8,10},{10,8},{12,14},{14,12},{1,3},{3,1},... | collective-permute-start | bytes 1105928 | tf_op jit(solution)/shard_map/ppermute | solution.py:19
  35.5 8.1 %collective-permute-start.5 = (bf16[288,640]{1,0:T(8,128)(2,1)S(1)}, bf16[288,640]{1,0:T(8,128)(2,1)}, u32[]{:S(2)}, u32[]{:S(2)}) collective-permute-start(bf16[288,640]{1,0:T(8,128)(2,1)S(1)} %collective-permute-done.1.refs_1_), channel_id=1, source_target_pairs={{0,2},{2,0},{4,6},{6,4},{8,10},{10,8},{12,14},{14,12},{1,3},{3,1},... | collective-permute-start | bytes 1105928 | tf_op jit(solution)/shard_map/ppermute | solution.py:19
  35.8 7.9 %collective-permute-start.6 = (bf16[288,640]{1,0:T(8,128)(2,1)S(1)}, bf16[288,640]{1,0:T(8,128)(2,1)}, u32[]{:S(2)}, u32[]{:S(2)}) collective-permute-start(bf16[288,640]{1,0:T(8,128)(2,1)S(1)} %collective-permute-done.refs_2_), channel_id=1, source_target_pairs={{0,2},{2,0},{4,6},{6,4},{8,10},{10,8},{12,14},{14,12},{1,3},{3,1},... | collective-permute-start | bytes 1105928 | tf_op jit(solution)/shard_map/ppermute | solution.py:19
  36.0 18.8 %collective-permute-start.8 = (bf16[16,60,240]{2,1,0:T(8,128)(2,1)S(1)}, bf16[16,60,240]{2,1,0:T(8,128)(2,1)}, u32[]{:S(2)}, u32[]{:S(2)}) collective-permute-start(bf16[16,60,240]{2,1,0:T(8,128)(2,1)S(1)} %all-to-all-done.mine), channel_id=1, source_target_pairs={{0,4},{2,6},{4,0},{6,2},{8,12},{10,14},{12,8},{14,10},{1,5},{3,7},... | collective-permute-start | bytes 1382408 | tf_op jit(solution)/shard_map/ppermute | solution.py:411
  54.9 16.9 %all-to-all-start.2 = ((bf16[8,36,640]{2,1,0:T(8,128)(2,1)}), bf16[8,36,640]{2,1,0:T(8,128)(2,1)S(1)}, u32[]{:S(2)}, u32[]{:S(2)}) async-start(bf16[8,36,640]{2,1,0:T(8,128)(2,1)} %reshape_squeeze.6), calls=%async_computation.2 | async-start | bytes 819200 | tf_op jit(solution)/shard_map/all_to_all | solution.py:431
  58.6 11.9 %collective-permute-start.10 = (bf16[8,40,640]{2,1,0:T(8,128)(2,1)S(1)}, bf16[8,40,640]{2,1,0:T(8,128)(2,1)S(1)}, u32[]{:S(2)}, u32[]{:S(2)}) collective-permute-start(bf16[8,40,640]{2,1,0:T(8,128)(2,1)S(1)} %all-to-all-done.1.refs_0_), channel_id=1, source_target_pairs={{0,16},{16,0},{1,17},{17,1},{2,18},{18,2},{3,19},{19,3},{4,20},{20... | collective-permute-start | bytes 1228808 | tf_op jit(solution)/shard_map/ppermute | solution.py:19
  60.1 11.6 %collective-permute-start.9 = (bf16[8,40,640]{2,1,0:T(8,128)(2,1)S(1)}, bf16[8,40,640]{2,1,0:T(8,128)(2,1)S(1)}, u32[]{:S(2)}, u32[]{:S(2)}) collective-permute-start(bf16[8,40,640]{2,1,0:T(8,128)(2,1)S(1)} %all-to-all-done.1.refs_0_), channel_id=1, source_target_pairs={{0,1},{1,0},{2,3},{3,2},{4,5},{5,4},{6,7},{7,6},{8,9},{9,8},{10,11... | collective-permute-start | bytes 1228808 | tf_op jit(solution)/shard_map/ppermute | solution.py:19
  71.7 21.5 %all-to-all-start.3 = ((bf16[32,24,240]{2,1,0:T(8,128)(2,1)}), bf16[32,24,240]{2,1,0:T(8,128)(2,1)S(1)}, u32[]{:S(2)}, u32[]{:S(2)}) async-start(bf16[32,24,240]{2,1,0:T(8,128)(2,1)} %shard_map.129), calls=%async_computation.3 | async-start | bytes 786432 | tf_op jit(solution)/shard_map/all_to_all | solution.py:460
  76.6 11.8 %collective-permute-start.13 = (bf16[8,40,640]{2,1,0:T(8,128)(2,1)S(1)}, bf16[8,40,640]{2,1,0:T(8,128)(2,1)S(1)}, u32[]{:S(2)}, u32[]{:S(2)}) collective-permute-start(bf16[8,40,640]{2,1,0:T(8,128)(2,1)S(1)} %all-to-all-done.1.refs_0_), channel_id=1, source_target_pairs={{0,2},{2,0},{4,6},{6,4},{8,10},{10,8},{12,14},{14,12},{1,3},{3,1},... | collective-permute-start | bytes 1228808 | tf_op jit(solution)/shard_map/ppermute | solution.py:19
  77.0 10.3 %collective-permute-start.11 = (bf16[4,40,640]{2,1,0:T(8,128)(2,1)S(1)}, bf16[4,40,640]{2,1,0:T(8,128)(2,1)}, u32[]{:S(2)}, u32[]{:S(2)}) collective-permute-start(bf16[4,40,640]{2,1,0:T(8,128)(2,1)S(1)} %slice.53), channel_id=1, source_target_pairs={{0,1},{1,0},{2,3},{3,2},{4,5},{5,4},{6,7},{7,6},{8,9},{9,8},{10,11... | collective-permute-start | bytes 614408 | tf_op jit(solution)/shard_map/ppermute | solution.py:19
  78.7 9.4 %collective-permute-start.12 = (bf16[4,40,640]{2,1,0:T(8,128)(2,1)S(1)}, bf16[4,40,640]{2,1,0:T(8,128)(2,1)}, u32[]{:S(2)}, u32[]{:S(2)}) collective-permute-start(bf16[4,40,640]{2,1,0:T(8,128)(2,1)S(1)} %slice.54), channel_id=1, source_target_pairs={{0,16},{16,0},{1,17},{17,1},{2,18},{18,2},{3,19},{19,3},{4,20},{20... | collective-permute-start | bytes 614408 | tf_op jit(solution)/shard_map/ppermute | solution.py:19
  80.3 9.7 %collective-permute-start.14 = (bf16[8,40,640]{2,1,0:T(8,128)(2,1)S(1)}, bf16[8,40,640]{2,1,0:T(8,128)(2,1)S(1)}, u32[]{:S(2)}, u32[]{:S(2)}) collective-permute-start(bf16[8,40,640]{2,1,0:T(8,128)(2,1)S(1)} %collective-permute-done.9.refs_1_), channel_id=1, source_target_pairs={{0,2},{2,0},{4,6},{6,4},{8,10},{10,8},{12,14},{14,12},{1,3},{3,1},... | collective-permute-start | bytes 1228808 | tf_op jit(solution)/shard_map/ppermute | solution.py:19
  80.3 9.7 %collective-permute-start.15 = (bf16[8,40,640]{2,1,0:T(8,128)(2,1)S(1)}, bf16[8,40,640]{2,1,0:T(8,128)(2,1)}, u32[]{:S(2)}, u32[]{:S(2)}) collective-permute-start(bf16[8,40,640]{2,1,0:T(8,128)(2,1)S(1)} %collective-permute-done.10.refs_2_), channel_id=1, source_target_pairs={{0,2},{2,0},{4,6},{6,4},{8,10},{10,8},{12,14},{14,12},{1,3},{3,1},... | collective-permute-start | bytes 1228808 | tf_op jit(solution)/shard_map/ppermute | solution.py:19
  108.5 11.8 %collective-permute-start.19 = (bf16[2,4,40,640]{3,2,1,0:T(8,128)(2,1)S(1)}, bf16[2,4,40,640]{3,2,1,0:T(8,128)(2,1)S(1)}, u32[]{:S(2)}, u32[]{:S(2)}) collective-permute-start(bf16[2,4,40,640]{3,2,1,0:T(8,128)(2,1)S(1)} %slice_bitcast_fusion), channel_id=1, source_target_pairs={{0,16},{16,0},{1,17},{17,1},{2,18},{18,2},{3,19},{19,3},{4,20},{20... | collective-permute-start | bytes 1228808 | tf_op jit(solution)/shard_map/ppermute | solution.py:19
  115.1 20.3 %all-to-all-start.4 = ((bf16[8,40,640]{2,1,0:T(8,128)(2,1)}), bf16[8,40,640]{2,1,0:T(8,128)(2,1)S(1)}, u32[]{:S(2)}, u32[]{:S(2)}) async-start(bf16[8,40,640]{2,1,0:T(8,128)(2,1)} %shard_map.133), calls=%async_computation.4 | async-start | bytes 819200 | tf_op jit(solution)/shard_map/all_to_all | solution.py:522
  120.5 7.0 %collective-permute-start.20 = (bf16[4,40,640]{2,1,0:T(8,128)(2,1)S(1)}, bf16[4,40,640]{2,1,0:T(8,128)(2,1)S(1)}, u32[]{:S(2)}, u32[]{:S(2)}) collective-permute-start(bf16[4,40,640]{2,1,0:T(8,128)(2,1)S(1)} %slice_bitcast_fusion.1), channel_id=1, source_target_pairs={{0,1},{1,0},{2,3},{3,2},{4,5},{5,4},{6,7},{7,6},{8,9},{9,8},{10,11... | collective-permute-start | bytes 614408 | tf_op jit(solution)/shard_map/ppermute | solution.py:19
  127.6 13.0 %collective-permute-start.21 = (bf16[2,40,640]{2,1,0:T(8,128)(2,1)S(1)}, bf16[2,40,640]{2,1,0:T(8,128)(2,1)S(1)}, u32[]{:S(2)}, u32[]{:S(2)}) collective-permute-start(bf16[2,40,640]{2,1,0:T(8,128)(2,1)S(1)} %slice.72), channel_id=1, source_target_pairs={{0,8},{2,10},{4,12},{6,14},{8,0},{10,2},{12,4},{14,6},{1,9},{3,11}... | collective-permute-start | bytes 307208 | tf_op jit(solution)/shard_map/ppermute | solution.py:519
  140.7 4.2 %collective-permute-start.22 = (bf16[1,40,640]{2,1,0:T(8,128)(2,1)S(1)}, bf16[1,40,640]{2,1,0:T(8,128)(2,1)S(1)}, u32[]{:S(2)}, u32[]{:S(2)}) collective-permute-start(bf16[1,40,640]{2,1,0:T(8,128)(2,1)S(1)} %slice.74), channel_id=1, source_target_pairs={{0,4},{2,6},{4,0},{6,2},{8,12},{10,14},{12,8},{14,10},{1,5},{3,7},... | collective-permute-start | bytes 153608 | tf_op jit(solution)/shard_map/ppermute | solution.py:519
  (23 other events, 160.1 us)

commit v7 on v6

--- a/solution.py
+++ b/solution.py
@@ -390,30 +390,31 @@
     place = jnp.stack([x, core, tile, 4 * x + 2 * core + tile, plane]).astype(jnp.int32)
     flat = source.reshape(tokens, width)
 
+    kinds = lax.dynamic_slice_in_dim(attn_weight, x * 2 * width, 2 * width, axis=1)
+    kinds = kinds.reshape(share, 2, width).transpose(1, 0, 2)
+    kinds = jnp.broadcast_to(kinds[None], (frames // 2,) + kinds.shape).reshape(frames, share, width)
+    own = lax.all_to_all(kinds, "frame", 0, 0, tiled=True)
+
+    along_x = swap(flat, "dp")
+    along_y = swap(flat, "tile")
+
     lines = 3 * share // 2
     mine = lax.dynamic_slice_in_dim(conv_weight, x * (width // 2), width // 2, axis=2)
     mine = mine.reshape(3, 3, share, 4, part).transpose(3, 0, 2, 1, 4)
     mine = mine.reshape(4, 2, lines, 3 * part).transpose(1, 0, 2, 3)
     mine = jnp.broadcast_to(mine[None], (frames // 4,) + mine.shape)
     mine = mine.reshape(ranks, lines, 3 * part)
+    mine, own, along_x, along_y = lax.optimization_barrier((mine, own, along_x, along_y))
     conv_half = lax.all_to_all(mine, square, 0, 0, tiled=True)
-
-    along_x = swap(flat, "dp")
-    along_y = swap(flat, "tile")
-
-    kinds = lax.dynamic_slice_in_dim(attn_weight, x * 2 * width, 2 * width, axis=1)
-    kinds = kinds.reshape(share, 2, width).transpose(1, 0, 2)
-    kinds = jnp.broadcast_to(kinds[None], (frames // 2,) + kinds.shape).reshape(frames, share, width)
-    kinds, conv_half, along_x, along_y = lax.optimization_barrier(
-        (kinds, conv_half, along_x, along_y)
-    )
-    own = lax.all_to_all(kinds, "frame", 0, 0, tiled=True)
-    conv_other = lax.ppermute(conv_half, "frame", [(i, i ^ 2) for i in range(frames)])
 
     half = tokens // 2
     across = jnp.concatenate([swap(along_x[:half], "tile"), swap(along_y[half:], "dp")])
     pieces = [flat, along_y, along_x, across]
     pieces += [swap(piece, "frame") for piece in pieces]
+    cot_blocks = cot.reshape(frames, count, width)
+    cot_blocks, conv_half, pieces = lax.optimization_barrier((cot_blocks, conv_half, pieces))
+    cot_blocks = lax.all_to_all(cot_blocks, "frame", 0, 0, tiled=True)
+    conv_other = lax.ppermute(conv_half, "frame", [(i, i ^ 2) for i in range(frames)])
     acts, kept = call(
         functools.partial(act_kernel, cols=cols, part=part),
         20,
@@ -423,15 +424,8 @@
         norm_gain[None],
         *pieces,
     )
-
-    cot_blocks = cot.reshape(frames, count, width)
-    cot_blocks, own, acts, kept, conv_half, conv_other = lax.optimization_barrier(
-        (cot_blocks, own, acts, kept, conv_half, conv_other)
-    )
-    cot_blocks = lax.all_to_all(cot_blocks, "frame", 0, 0, tiled=True)
     by_tile = swap(own, "tile")
     by_clip = swap(own, "dp")
-
     (conv_full,) = call(
         taps_kernel, 12, [((3, ranks, share, 3 * part), BF)], [], place, conv_half, conv_other
     )
@@ -462,6 +456,7 @@
     middle = frames // 2
     parts = [own, by_tile, by_clip, swap(by_clip[:middle], "tile"), swap(by_tile[middle:], "dp")]
     parts += [swap(piece, "frame") for piece in parts]
+    parts, mid = lax.optimization_barrier((parts, mid))
     (attn_full,) = call(
         join_kernel, 16, [((4, frames, tiles, share, width), BF)], [], place, *parts
     )
@@ -511,15 +506,17 @@
         [],
         d_qn, d_kn, q_hat, k_hat, q_rstd, k_rstd, d_value, attn_full, qgain, kgain, scale_sums,
     )
+    d_back = lax.all_to_all(d_mid, "frame", 0, 0, tiled=True)
     shares = add(shares[0], swap(shares[1], "dp"))
     shares = add(shares[0], swap(shares[1], "tile"))
     step = frames // 4
     while step > 0:
         pairs = [(i, i ^ (2 * step)) for i in range(frames)]
+        if step == 1:
+            shares, d_back = lax.optimization_barrier((shares, d_back))
         shares = add(shares[:step], lax.ppermute(shares[step:], "frame", pairs))
         step //= 2
     shares = shares[0]
-    d_back = lax.all_to_all(d_mid, "frame", 0, 0, tiled=True)
     small = jnp.sum(d_back[:, count : count + 3].astype(F32), axis=(0, 1))
     d_back = d_back[:, :count].reshape(rows, cols, width)
     mid_grad = (cot.astype(F32) + d_back.astype(F32)).astype(BF)

time: 151 us -> 161 us (1.066)
  waiting for transfers between devices: 49.6 us -> 70.6 us
  local copies, waits for them, and re-layouts: 16.8 us -> 9.25 us
  starting transfers between devices: 48.8 us -> 45.4 us
    ppermute x2, waiting for transfers between devices: 1.59 us -> 16 us  [local(): shares = add(shares[:step], lax.ppermute(shares[step:], 'frame', pairs))]
    unnamed x33 -> x25, local copies, waits for them, and re-layouts: 11.6 us -> 3.03 us
    ppermute x1, waiting for transfers between devices: 2.73 us -> 10.1 us  [local(): lax.ppermute(conv_half, 'frame', [(i, i ^ 2) for i in range(frames)])]
    all_to_all x1, waiting for transfers between devices: 5.16 us -> 0.01 us  [local(): d_back = lax.all_to_all(d_mid, 'frame', 0, 0, tiled=True)]
    all_to_all x1, starting transfers between devices: 7.39 us -> 5.12 us  [local(): conv_half = lax.all_to_all(mine, square, 0, 0, tiled=True)]
    all_to_all x1, starting transfers between devices: 4.91 us -> 3.03 us  [local(): lax.all_to_all(mid, ('dp',) + square, 0, 0, axis_index_groups=groups, til...]
    all_to_all x1, waiting for transfers between devices: 0.01 us -> 1.85 us  [local(): conv_half = lax.all_to_all(mine, square, 0, 0, tiled=True)]
    ppermute x23, waiting for transfers between devices: 40.1 us -> 41.9 us  [swap(): lax.ppermute(x, axis, [(i, i ^ 1) for i in range(lax.axis_size(axis))])]
  transfers between devices with their start and end apart: 31 -> 31, of which waited for: 16 -> 16; matrix products, arithmetic and copies ran while one was open for 3% -> 3% of each run, Pallas kernels for 13% -> 11%
where the time goes in v7:
time: 161 us; the launch traced here: 160 us
  waiting for transfers between devices  70.6 us (44%)
  starting transfers between devices  45.4 us (28%)
  Pallas kernels  30.4 us (19%)
  local copies, waits for them, and re-layouts  9.25 us (6%)
  other arithmetic  3.06 us (2%)
    ppermute x23, waiting for transfers between devices, swap(): lax.ppermute(x, axis, [(i, i ^ 1) for i in range(lax.axis_size(axis))])  41.9 us
    pallas_call x7, Pallas kernels, call(): pl.pallas_call(kernel, out_shape=[jax.ShapeDtypeStruct(shape, dtype) for...  30.4 us
    ppermute x23, starting transfers between devices, swap(): lax.ppermute(x, axis, [(i, i ^ 1) for i in range(lax.axis_size(axis))])  17.1 us
    ppermute x2, waiting for transfers between devices, local(): shares = add(shares[:step], lax.ppermute(shares[step:], 'frame', pairs))  16 us
    ppermute x1, waiting for transfers between devices, local(): lax.ppermute(conv_half, 'frame', [(i, i ^ 2) for i in range(frames)])  10.1 us
    all_to_all x1, starting transfers between devices, local(): own = lax.all_to_all(kinds, 'frame', 0, 0, tiled=True)  6.33 us
    all_to_all x1, starting transfers between devices, local(): conv_half = lax.all_to_all(mine, square, 0, 0, tiled=True)  5.12 us
    all_to_all x1, starting transfers between devices, local(): d_back = lax.all_to_all(d_mid, 'frame', 0, 0, tiled=True)  4.86 us
  transfers between devices with their start and end apart: 31, of which 16 were waited for; matrix products, arithmetic and copies ran while one was open for 3% of the time, Pallas kernels for 11%

profile of v7, /device:TPU:0, one launch (start us, length us, event | category | flops | bytes accessed | tf_op | source)
XLA Modules:
  0.0 159.7 jit_solution(10398123330584271683)
XLA Ops:
  2.5 6.3 %all-to-all-start = ((bf16[8,40,640]{2,1,0:T(8,128)(2,1)}), bf16[8,40,640]{2,1,0:T(8,128)(2,1)S(1)}, u32[]{:S(2)}, u32[]{:S(2)}) async-start(bf16[8,40,640]{2,1,0:T(8,128)(2,1)} %bitcast.9), calls=%async_computation | async-start | bytes 819200 | tf_op jit(solution)/shard_map/all_to_all | solution.py:396
  13.0 6.8 %collective-permute-done.refs_2_ = bf16[288,640]{1,0:T(8,128)(2,1)S(1)} collective-permute-done((bf16[288,640]{1,0:T(8,128)(2,1)S(1)}, bf16[288,640]{1,0:T(8,128)(2,1)S(1)}, u32[]{:S(2)}, u32[]{:S(2)}) %collective-permute-start) | collective-permute-done | bytes 368672 | tf_op jit(solution)/shard_map/ppermute | solution.py:19
  22.6 5.1 %all-to-all-start.1 = ((bf16[16,60,240]{2,1,0:T(8,128)(2,1)}), bf16[16,60,240]{2,1,0:T(8,128)(2,1)S(1)}, u32[]{:S(2)}, u32[]{:S(2)}) async-start(bf16[16,60,240]{2,1,0:T(8,128)(2,1)} %bitcast.38), calls=%async_computation.1 | async-start | bytes 1048576 | tf_op jit(solution)/shard_map/all_to_all | solution.py:408
  27.7 2.0 %collective-permute-start.2 = (bf16[144,640]{1,0:T(8,128)(2,1)S(1)}, bf16[144,640]{1,0:T(8,128)(2,1)S(1)}, u32[]{:S(2)}, u32[]{:S(2)}) collective-permute-start(bf16[144,640]{1,0:T(8,128)(2,1)S(1)} %slice.51), channel_id=1, source_target_pairs={{0,1},{1,0},{2,3},{3,2},{4,5},{5,4},{6,7},{7,6},{8,9},{9,8},{10,11... | collective-permute-start | bytes 552968 | tf_op jit(solution)/shard_map/ppermute | solution.py:19
  30.9 7.5 %collective-permute-done.2 = bf16[144,640]{1,0:T(8,128)(2,1)S(1)} collective-permute-done((bf16[144,640]{1,0:T(8,128)(2,1)S(1)}, bf16[144,640]{1,0:T(8,128)(2,1)S(1)}, u32[]{:S(2)}, u32[]{:S(2)}) %collective-permute-start.2) | collective-permute-done | bytes 184352 | tf_op jit(solution)/shard_map/ppermute | solution.py:19
  38.5 1.9 %reshape_squeeze.7 = bf16[8,36,640]{2,1,0:T(8,128)(2,1)} reshape(bf16[1,1,9,32,640]{4,3,2,1,0:T(8,128)(2,1)} %param.9) | data formatting | bytes 737280 | tf_op jit(solution)/shard_map/reshape;squeeze | solution.py:414
  40.4 1.9 %all-to-all-done.1.mine = bf16[16,60,240]{2,1,0:T(8,128)(2,1)S(1)} async-done(((bf16[16,60,240]{2,1,0:T(8,128)(2,1)}), bf16[16,60,240]{2,1,0:T(8,128)(2,1)S(1)}, u32[]{:S(2)}, u32[]{:S(2)}) %all-to-all-start.1) | async-done | bytes 460832 | tf_op jit(solution)/shard_map/all_to_all | solution.py:408
  42.2 4.0 %all-to-all-start.2 = ((bf16[8,36,640]{2,1,0:T(8,128)(2,1)}), bf16[8,36,640]{2,1,0:T(8,128)(2,1)S(1)}, u32[]{:S(2)}, u32[]{:S(2)}) async-start(bf16[8,36,640]{2,1,0:T(8,128)(2,1)} %reshape_squeeze.7), calls=%async_computation.2 | async-start | bytes 819200 | tf_op jit(solution)/shard_map/all_to_all | solution.py:416
  46.3 2.0 %collective-permute-start.8 = (bf16[16,60,240]{2,1,0:T(8,128)(2,1)S(1)}, bf16[16,60,240]{2,1,0:T(8,128)(2,1)}, u32[]{:S(2)}, u32[]{:S(2)}) collective-permute-start(bf16[16,60,240]{2,1,0:T(8,128)(2,1)S(1)} %all-to-all-done.1.mine), channel_id=1, source_target_pairs={{0,4},{2,6},{4,0},{6,2},{8,12},{10,14},{12,8},{14,10},{1,5},{3,7},... | collective-permute-start | bytes 1382408 | tf_op jit(solution)/shard_map/ppermute | solution.py:417
  52.4 4.8 %shard_map.128 = (bf16[4,640,640]{2,1,0:T(8,128)(2,1)S(1)}, bf16[4,576,80]{2,1,0:T(8,128)(2,1)S(1)}) custom-call(s32[5]{0:T(128)S(1)} %stack.23.place, f32[1,640]{1,0:T(1,128)S(1)} %broadcast_in_dim.8.gain, bf16[288,640]{1,0:T(8,128)(2,1)S(1)} %bitcast.37, bf16[288,640]{1,0:T(8,128)(2,1)S(1)} %collective-permute-done.1.refs_1_, ...), custom_call_target="tpu_custom_call" | custom-call | tf_op jit(solution)/shard_map/pallas_call | solution.py:360
  57.3 10.1 %collective-permute-done.8.theirs = bf16[16,60,240]{2,1,0:T(8,128)(2,1)} collective-permute-done((bf16[16,60,240]{2,1,0:T(8,128)(2,1)S(1)}, bf16[16,60,240]{2,1,0:T(8,128)(2,1)}, u32[]{:S(2)}, u32[]{:S(2)}) %collective-permute-start.8) | collective-permute-done | bytes 460832 | tf_op jit(solution)/shard_map/ppermute | solution.py:417
  68.6 5.1 %shard_map.129 = bf16[32,24,240]{2,1,0:T(8,128)(2,1)} custom-call(s32[5]{0:T(128)S(1)} %stack.23.place, bf16[3,640,240]{2,1,0:T(8,128)(2,1)S(1)} %bitcast.33, bf16[4,640,640]{2,1,0:T(8,128)(2,1)S(1)} %get-tuple-element.65.acts, bf16[4,576,80]{2,1,0:T(8,128)(2,1)S(1)} %get-tuple-element.66.kept), custom_call_target="tpu_custom_call" | custom-call | tf_op jit(solution)/shard_map/pallas_call | solution.py:360
  73.7 3.0 %all-to-all-start.3 = ((bf16[32,24,240]{2,1,0:T(8,128)(2,1)}), bf16[32,24,240]{2,1,0:T(8,128)(2,1)S(1)}, u32[]{:S(2)}, u32[]{:S(2)}) async-start(bf16[32,24,240]{2,1,0:T(8,128)(2,1)} %shard_map.129), calls=%async_computation.3 | async-start | bytes 786432 | tf_op jit(solution)/shard_map/all_to_all | solution.py:454
  77.4 1.8 %collective-permute-start.11 = (bf16[4,40,640]{2,1,0:T(8,128)(2,1)S(1)}, bf16[4,40,640]{2,1,0:T(8,128)(2,1)}, u32[]{:S(2)}, u32[]{:S(2)}) collective-permute-start(bf16[4,40,640]{2,1,0:T(8,128)(2,1)S(1)} %slice.53), channel_id=1, source_target_pairs={{0,1},{1,0},{2,3},{3,2},{4,5},{5,4},{6,7},{7,6},{8,9},{9,8},{10,11... | collective-permute-start | bytes 614408 | tf_op jit(solution)/shard_map/ppermute | solution.py:19
  80.7 6.7 %collective-permute-done.11.refs_3_ = bf16[4,40,640]{2,1,0:T(8,128)(2,1)} collective-permute-done((bf16[4,40,640]{2,1,0:T(8,128)(2,1)S(1)}, bf16[4,40,640]{2,1,0:T(8,128)(2,1)}, u32[]{:S(2)}, u32[]{:S(2)}) %collective-permute-start.11) | collective-permute-done | bytes 204832 | tf_op jit(solution)/shard_map/ppermute | solution.py:19
  91.9 10.7 %shard_map.131 = (bf16[2,2,4,40,640]{4,3,2,1,0:T(8,128)(2,1)S(1)}, bf16[2,2,4,40,640]{4,3,2,1,0:T(8,128)(2,1)S(1)}, f32[1,128]{1,0:T(1,128)S(1)}, f32[320,128]{1...) custom-call(s32[5]{0:T(128)S(1)} %stack.23.place, ...), custom_call_target="tpu_custom_call" | custom-call | tf_op jit(solution)/shard_map/pallas_call | solution.py:360
  102.8 2.2 %shard_map.132 = (f32[320,640]{1,0:T(8,128)S(1)}, f32[320,640]{1,0:T(8,128)S(1)}) custom-call(f32[320,128]{1,0:T(8,128)S(1)} %get-tuple-element.85.d_raw, f32[320,640]{1,0:T(8,128)S(1)} %get-tuple-element.86.q_hat, f32[320,640]{1,0:T(8,128)S(1)} %get-tuple-element.87.k_hat, f32[1,640]{1,0:T(1,128)S(1)} %broadcast_in_dim_tile.9.qgain, ...), custom_call_target="tpu_custom_call" | custom-call | tf_op jit(solution)/shard_map/pallas_call | solution.py:360
  106.9 10.2 %collective-permute-done.19 = bf16[2,4,40,640]{3,2,1,0:T(8,128)(2,1)S(1)} collective-permute-done((bf16[2,4,40,640]{3,2,1,0:T(8,128)(2,1)S(1)}, bf16[2,4,40,640]{3,2,1,0:T(8,128)(2,1)S(1)}, u32[]{:S(2)}, u32[]{:S(2)}) %collective-permute-start.19) | collective-permute-done | bytes 409632 | tf_op jit(solution)/shard_map/ppermute | solution.py:19
  118.2 4.8 %shard_map.133 = bf16[8,40,640]{2,1,0:T(8,128)(2,1)} custom-call(f32[320,640]{1,0:T(8,128)S(1)} %get-tuple-element.90.d_qn, f32[320,640]{1,0:T(8,128)S(1)} %get-tuple-element.91.d_kn, f32[320,640]{1,0:T(8,128)S(1)} %get-tuple-element.86.q_hat, f32[320,640]{1,0:T(8,128)S(1)} %get-tuple-element.87.k_hat, f32[320,128]{1,0:T(8,128)S(1)} %get-tuple-element.92.q_rstd, ...), custom_call_target="tpu_custom_call" | custom-call | tf_op jit(solution)/shard_map/pallas_call | solution.py:360
  123.0 4.9 %all-to-all-start.4 = ((bf16[8,40,640]{2,1,0:T(8,128)(2,1)}), bf16[8,40,640]{2,1,0:T(8,128)(2,1)S(1)}, u32[]{:S(2)}, u32[]{:S(2)}) async-start(bf16[8,40,640]{2,1,0:T(8,128)(2,1)} %shard_map.133), calls=%async_computation.4 | async-start | bytes 819200 | tf_op jit(solution)/shard_map/all_to_all | solution.py:509
  128.0 3.0 %collective-permute-start.21 = (bf16[2,40,640]{2,1,0:T(8,128)(2,1)S(1)}, bf16[2,40,640]{2,1,0:T(8,128)(2,1)S(1)}, u32[]{:S(2)}, u32[]{:S(2)}) collective-permute-start(bf16[2,40,640]{2,1,0:T(8,128)(2,1)S(1)} %slice.71), channel_id=1, source_target_pairs={{0,8},{2,10},{4,12},{6,14},{8,0},{10,2},{12,4},{14,6},{1,9},{3,11}... | collective-permute-start | bytes 307208 | tf_op jit(solution)/shard_map/ppermute | solution.py:517
  131.0 14.2 %collective-permute-done.21 = bf16[2,40,640]{2,1,0:T(8,128)(2,1)S(1)} collective-permute-done((bf16[2,40,640]{2,1,0:T(8,128)(2,1)S(1)}, bf16[2,40,640]{2,1,0:T(8,128)(2,1)S(1)}, u32[]{:S(2)}, u32[]{:S(2)}) %collective-permute-start.21) | collective-permute-done | bytes 102432 | tf_op jit(solution)/shard_map/ppermute | solution.py:517
  146.4 2.6 %collective-permute-done.24 = f32[640]{0:T(1024)S(1)} collective-permute-done((f32[640]{0:T(1024)S(1)}, f32[640]{0:T(1024)S(1)}, u32[]{:S(2)}, u32[]{:S(2)}) %collective-permute-start.24) | collective-permute-done | bytes 2592 | tf_op jit(solution)/shard_map/ppermute | solution.py:19
  156.5 2.5 %collective-permute-done.23 = bf16[40,640]{1,0:T(8,128)(2,1)S(1)} collective-permute-done((bf16[40,640]{1,0:T(8,128)(2,1)S(1)}, bf16[40,640]{1,0:T(8,128)(2,1)S(1)}, u32[]{:S(2)}, u32[]{:S(2)}) %collective-permute-start.23) | collective-permute-done | bytes 51232 | tf_op jit(solution)/shard_map/ppermute | solution.py:19
  (113 shorter events, 34.5 us)
Async XLA Ops:
  2.5 19.2 %all-to-all-start = ((bf16[8,40,640]{2,1,0:T(8,128)(2,1)}), bf16[8,40,640]{2,1,0:T(8,128)(2,1)S(1)}, u32[]{:S(2)}, u32[]{:S(2)}) async-start(bf16[8,40,640]{2,1,0:T(8,128)(2,1)} %bitcast.9), calls=%async_computation | async-start | bytes 819200 | tf_op jit(solution)/shard_map/all_to_all | solution.py:396
  8.8 11.0 %collective-permute-start = (bf16[288,640]{1,0:T(8,128)(2,1)S(1)}, bf16[288,640]{1,0:T(8,128)(2,1)S(1)}, u32[]{:S(2)}, u32[]{:S(2)}) collective-permute-start(bf16[288,640]{1,0:T(8,128)(2,1)S(1)} %bitcast.34), channel_id=1, source_target_pairs={{0,16},{16,0},{1,17},{17,1},{2,18},{18,2},{3,19},{19,3},{4,20},{20... | collective-permute-start | bytes 1105928 | tf_op jit(solution)/shard_map/ppermute | solution.py:19
  10.4 10.7 %collective-permute-start.1 = (bf16[288,640]{1,0:T(8,128)(2,1)S(1)}, bf16[288,640]{1,0:T(8,128)(2,1)S(1)}, u32[]{:S(2)}, u32[]{:S(2)}) collective-permute-start(bf16[288,640]{1,0:T(8,128)(2,1)S(1)} %bitcast.35), channel_id=1, source_target_pairs={{0,1},{1,0},{2,3},{3,2},{4,5},{5,4},{6,7},{7,6},{8,9},{9,8},{10,11... | collective-permute-start | bytes 1105928 | tf_op jit(solution)/shard_map/ppermute | solution.py:19
  22.6 19.7 %all-to-all-start.1 = ((bf16[16,60,240]{2,1,0:T(8,128)(2,1)}), bf16[16,60,240]{2,1,0:T(8,128)(2,1)S(1)}, u32[]{:S(2)}, u32[]{:S(2)}) async-start(bf16[16,60,240]{2,1,0:T(8,128)(2,1)} %bitcast.38), calls=%async_computation.1 | async-start | bytes 1048576 | tf_op jit(solution)/shard_map/all_to_all | solution.py:408
  27.7 10.6 %collective-permute-start.2 = (bf16[144,640]{1,0:T(8,128)(2,1)S(1)}, bf16[144,640]{1,0:T(8,128)(2,1)S(1)}, u32[]{:S(2)}, u32[]{:S(2)}) collective-permute-start(bf16[144,640]{1,0:T(8,128)(2,1)S(1)} %slice.51), channel_id=1, source_target_pairs={{0,1},{1,0},{2,3},{3,2},{4,5},{5,4},{6,7},{7,6},{8,9},{9,8},{10,11... | collective-permute-start | bytes 552968 | tf_op jit(solution)/shard_map/ppermute | solution.py:19
  29.7 8.6 %collective-permute-start.3 = (bf16[144,640]{1,0:T(8,128)(2,1)S(1)}, bf16[144,640]{1,0:T(8,128)(2,1)S(1)}, u32[]{:S(2)}, u32[]{:S(2)}) collective-permute-start(bf16[144,640]{1,0:T(8,128)(2,1)S(1)} %slice.52), channel_id=1, source_target_pairs={{0,16},{16,0},{1,17},{17,1},{2,18},{18,2},{3,19},{19,3},{4,20},{20... | collective-permute-start | bytes 552968 | tf_op jit(solution)/shard_map/ppermute | solution.py:19
  30.3 10.0 %collective-permute-start.4 = (bf16[288,640]{1,0:T(8,128)(2,1)S(1)}, bf16[288,640]{1,0:T(8,128)(2,1)S(1)}, u32[]{:S(2)}, u32[]{:S(2)}) collective-permute-start(bf16[288,640]{1,0:T(8,128)(2,1)S(1)} %bitcast.36), channel_id=1, source_target_pairs={{0,2},{2,0},{4,6},{6,4},{8,10},{10,8},{12,14},{14,12},{1,3},{3,1},... | collective-permute-start | bytes 1105928 | tf_op jit(solution)/shard_map/ppermute | solution.py:19
  30.3 10.0 %collective-permute-start.5 = (bf16[288,640]{1,0:T(8,128)(2,1)S(1)}, bf16[288,640]{1,0:T(8,128)(2,1)}, u32[]{:S(2)}, u32[]{:S(2)}) collective-permute-start(bf16[288,640]{1,0:T(8,128)(2,1)S(1)} %collective-permute-done.1.refs_1_), channel_id=1, source_target_pairs={{0,2},{2,0},{4,6},{6,4},{8,10},{10,8},{12,14},{14,12},{1,3},{3,1},... | collective-permute-start | bytes 1105928 | tf_op jit(solution)/shard_map/ppermute | solution.py:19
  30.9 9.5 %collective-permute-start.6 = (bf16[288,640]{1,0:T(8,128)(2,1)S(1)}, bf16[288,640]{1,0:T(8,128)(2,1)}, u32[]{:S(2)}, u32[]{:S(2)}) collective-permute-start(bf16[288,640]{1,0:T(8,128)(2,1)S(1)} %collective-permute-done.refs_2_), channel_id=1, source_target_pairs={{0,2},{2,0},{4,6},{6,4},{8,10},{10,8},{12,14},{14,12},{1,3},{3,1},... | collective-permute-start | bytes 1105928 | tf_op jit(solution)/shard_map/ppermute | solution.py:19
  42.2 31.4 %all-to-all-start.2 = ((bf16[8,36,640]{2,1,0:T(8,128)(2,1)}), bf16[8,36,640]{2,1,0:T(8,128)(2,1)S(1)}, u32[]{:S(2)}, u32[]{:S(2)}) async-start(bf16[8,36,640]{2,1,0:T(8,128)(2,1)} %reshape_squeeze.7), calls=%async_computation.2 | async-start | bytes 819200 | tf_op jit(solution)/shard_map/all_to_all | solution.py:416
  46.3 21.1 %collective-permute-start.8 = (bf16[16,60,240]{2,1,0:T(8,128)(2,1)S(1)}, bf16[16,60,240]{2,1,0:T(8,128)(2,1)}, u32[]{:S(2)}, u32[]{:S(2)}) collective-permute-start(bf16[16,60,240]{2,1,0:T(8,128)(2,1)S(1)} %all-to-all-done.1.mine), channel_id=1, source_target_pairs={{0,4},{2,6},{4,0},{6,2},{8,12},{10,14},{12,8},{14,10},{1,5},{3,7},... | collective-permute-start | bytes 1382408 | tf_op jit(solution)/shard_map/ppermute | solution.py:417
  48.3 25.4 %collective-permute-start.9 = (bf16[8,40,640]{2,1,0:T(8,128)(2,1)S(1)}, bf16[8,40,640]{2,1,0:T(8,128)(2,1)S(1)}, u32[]{:S(2)}, u32[]{:S(2)}) collective-permute-start(bf16[8,40,640]{2,1,0:T(8,128)(2,1)S(1)} %all-to-all-done.refs_0_), channel_id=1, source_target_pairs={{0,1},{1,0},{2,3},{3,2},{4,5},{5,4},{6,7},{7,6},{8,9},{9,8},{10,11... | collective-permute-start | bytes 1228808 | tf_op jit(solution)/shard_map/ppermute | solution.py:19
  48.8 24.8 %collective-permute-start.10 = (bf16[8,40,640]{2,1,0:T(8,128)(2,1)S(1)}, bf16[8,40,640]{2,1,0:T(8,128)(2,1)S(1)}, u32[]{:S(2)}, u32[]{:S(2)}) collective-permute-start(bf16[8,40,640]{2,1,0:T(8,128)(2,1)S(1)} %all-to-all-done.refs_0_), channel_id=1, source_target_pairs={{0,16},{16,0},{1,17},{17,1},{2,18},{18,2},{3,19},{19,3},{4,20},{20... | collective-permute-start | bytes 1228808 | tf_op jit(solution)/shard_map/ppermute | solution.py:19
  73.7 16.6 %all-to-all-start.3 = ((bf16[32,24,240]{2,1,0:T(8,128)(2,1)}), bf16[32,24,240]{2,1,0:T(8,128)(2,1)S(1)}, u32[]{:S(2)}, u32[]{:S(2)}) async-start(bf16[32,24,240]{2,1,0:T(8,128)(2,1)} %shard_map.129), calls=%async_computation.3 | async-start | bytes 786432 | tf_op jit(solution)/shard_map/all_to_all | solution.py:454
  76.7 12.0 %collective-permute-start.13 = (bf16[8,40,640]{2,1,0:T(8,128)(2,1)S(1)}, bf16[8,40,640]{2,1,0:T(8,128)(2,1)S(1)}, u32[]{:S(2)}, u32[]{:S(2)}) collective-permute-start(bf16[8,40,640]{2,1,0:T(8,128)(2,1)S(1)} %all-to-all-done.refs_0_), channel_id=1, source_target_pairs={{0,2},{2,0},{4,6},{6,4},{8,10},{10,8},{12,14},{14,12},{1,3},{3,1},... | collective-permute-start | bytes 1228808 | tf_op jit(solution)/shard_map/ppermute | solution.py:19
  77.1 11.7 %collective-permute-start.14 = (bf16[8,40,640]{2,1,0:T(8,128)(2,1)S(1)}, bf16[8,40,640]{2,1,0:T(8,128)(2,1)S(1)}, u32[]{:S(2)}, u32[]{:S(2)}) collective-permute-start(bf16[8,40,640]{2,1,0:T(8,128)(2,1)S(1)} %collective-permute-done.9.refs_1_), channel_id=1, source_target_pairs={{0,2},{2,0},{4,6},{6,4},{8,10},{10,8},{12,14},{14,12},{1,3},{3,1},... | collective-permute-start | bytes 1228808 | tf_op jit(solution)/shard_map/ppermute | solution.py:19
  77.4 10.0 %collective-permute-start.11 = (bf16[4,40,640]{2,1,0:T(8,128)(2,1)S(1)}, bf16[4,40,640]{2,1,0:T(8,128)(2,1)}, u32[]{:S(2)}, u32[]{:S(2)}) collective-permute-start(bf16[4,40,640]{2,1,0:T(8,128)(2,1)S(1)} %slice.53), channel_id=1, source_target_pairs={{0,1},{1,0},{2,3},{3,2},{4,5},{5,4},{6,7},{7,6},{8,9},{9,8},{10,11... | collective-permute-start | bytes 614408 | tf_op jit(solution)/shard_map/ppermute | solution.py:19
  79.3 9.5 %collective-permute-start.15 = (bf16[8,40,640]{2,1,0:T(8,128)(2,1)S(1)}, bf16[8,40,640]{2,1,0:T(8,128)(2,1)}, u32[]{:S(2)}, u32[]{:S(2)}) collective-permute-start(bf16[8,40,640]{2,1,0:T(8,128)(2,1)S(1)} %collective-permute-done.10.refs_2_), channel_id=1, source_target_pairs={{0,2},{2,0},{4,6},{6,4},{8,10},{10,8},{12,14},{14,12},{1,3},{3,1},... | collective-permute-start | bytes 1228808 | tf_op jit(solution)/shard_map/ppermute | solution.py:19
  79.3 9.2 %collective-permute-start.12 = (bf16[4,40,640]{2,1,0:T(8,128)(2,1)S(1)}, bf16[4,40,640]{2,1,0:T(8,128)(2,1)}, u32[]{:S(2)}, u32[]{:S(2)}) collective-permute-start(bf16[4,40,640]{2,1,0:T(8,128)(2,1)S(1)} %slice.54), channel_id=1, source_target_pairs={{0,16},{16,0},{1,17},{17,1},{2,18},{18,2},{3,19},{19,3},{4,20},{20... | collective-permute-start | bytes 614408 | tf_op jit(solution)/shard_map/ppermute | solution.py:19
  105.3 11.8 %collective-permute-start.19 = (bf16[2,4,40,640]{3,2,1,0:T(8,128)(2,1)S(1)}, bf16[2,4,40,640]{3,2,1,0:T(8,128)(2,1)S(1)}, u32[]{:S(2)}, u32[]{:S(2)}) collective-permute-start(bf16[2,4,40,640]{3,2,1,0:T(8,128)(2,1)S(1)} %slice_bitcast_fusion), channel_id=1, source_target_pairs={{0,16},{16,0},{1,17},{17,1},{2,18},{18,2},{3,19},{19,3},{4,20},{20... | collective-permute-start | bytes 1228808 | tf_op jit(solution)/shard_map/ppermute | solution.py:19
  117.2 10.6 %collective-permute-start.20 = (bf16[4,40,640]{2,1,0:T(8,128)(2,1)S(1)}, bf16[4,40,640]{2,1,0:T(8,128)(2,1)S(1)}, u32[]{:S(2)}, u32[]{:S(2)}) collective-permute-start(bf16[4,40,640]{2,1,0:T(8,128)(2,1)S(1)} %slice_bitcast_fusion.1), channel_id=1, source_target_pairs={{0,1},{1,0},{2,3},{3,2},{4,5},{5,4},{6,7},{7,6},{8,9},{9,8},{10,11... | collective-permute-start | bytes 614408 | tf_op jit(solution)/shard_map/ppermute | solution.py:19
  123.0 22.2 %all-to-all-start.4 = ((bf16[8,40,640]{2,1,0:T(8,128)(2,1)}), bf16[8,40,640]{2,1,0:T(8,128)(2,1)S(1)}, u32[]{:S(2)}, u32[]{:S(2)}) async-start(bf16[8,40,640]{2,1,0:T(8,128)(2,1)} %shard_map.133), calls=%async_computation.4 | async-start | bytes 819200 | tf_op jit(solution)/shard_map/all_to_all | solution.py:509
  128.0 17.2 %collective-permute-start.21 = (bf16[2,40,640]{2,1,0:T(8,128)(2,1)S(1)}, bf16[2,40,640]{2,1,0:T(8,128)(2,1)S(1)}, u32[]{:S(2)}, u32[]{:S(2)}) collective-permute-start(bf16[2,40,640]{2,1,0:T(8,128)(2,1)S(1)} %slice.71), channel_id=1, source_target_pairs={{0,8},{2,10},{4,12},{6,14},{8,0},{10,2},{12,4},{14,6},{1,9},{3,11}... | collective-permute-start | bytes 307208 | tf_op jit(solution)/shard_map/ppermute | solution.py:517
  154.9 4.2 %collective-permute-start.23 = (bf16[40,640]{1,0:T(8,128)(2,1)S(1)}, bf16[40,640]{1,0:T(8,128)(2,1)S(1)}, u32[]{:S(2)}, u32[]{:S(2)}) collective-permute-start(bf16[40,640]{1,0:T(8,128)(2,1)S(1)} %fusion.4), channel_id=1, source_target_pairs={{0,16},{16,0},{1,17},{17,1},{2,18},{18,2},{3,19},{19,3},{4,20},{20... | collective-permute-start | bytes 153608 | tf_op jit(solution)/shard_map/ppermute | solution.py:19
  (19 other events, 150.1 us)

commit v8 on v7

--- a/solution.py
+++ b/solution.py
@@ -76,17 +76,6 @@
     else:
         for i in range(number):
             body(i)
-
-
-def taps_kernel(place, mine, theirs, out):
-    odd = place[4] % 2
-    share = out.shape[2]
-    for owner in range(mine.shape[0]):
-        first = jnp.where(odd == 0, mine[owner], theirs[owner])
-        second = jnp.where(odd == 0, theirs[owner], mine[owner])
-        block = jnp.concatenate([first, second], axis=0)
-        for row in range(3):
-            out[row, owner] = block[row * share : (row + 1) * share]
 
 
 def join_kernel(place, *refs):
@@ -398,23 +387,21 @@
     along_x = swap(flat, "dp")
     along_y = swap(flat, "tile")
 
-    lines = 3 * share // 2
     mine = lax.dynamic_slice_in_dim(conv_weight, x * (width // 2), width // 2, axis=2)
     mine = mine.reshape(3, 3, share, 4, part).transpose(3, 0, 2, 1, 4)
-    mine = mine.reshape(4, 2, lines, 3 * part).transpose(1, 0, 2, 3)
-    mine = jnp.broadcast_to(mine[None], (frames // 4,) + mine.shape)
-    mine = mine.reshape(ranks, lines, 3 * part)
+    mine = mine.reshape(4, 3, share, 3 * part)
+    mine = jnp.broadcast_to(mine[None], (frames // 2,) + mine.shape)
+    mine = mine.reshape((ranks,) + mine.shape[2:])
     mine, own, along_x, along_y = lax.optimization_barrier((mine, own, along_x, along_y))
-    conv_half = lax.all_to_all(mine, square, 0, 0, tiled=True)
+    conv_in = lax.all_to_all(mine, square, 0, 0, tiled=True)
 
     half = tokens // 2
     across = jnp.concatenate([swap(along_x[:half], "tile"), swap(along_y[half:], "dp")])
     pieces = [flat, along_y, along_x, across]
     pieces += [swap(piece, "frame") for piece in pieces]
     cot_blocks = cot.reshape(frames, count, width)
-    cot_blocks, conv_half, pieces = lax.optimization_barrier((cot_blocks, conv_half, pieces))
+    cot_blocks, conv_in, pieces = lax.optimization_barrier((cot_blocks, conv_in, pieces))
     cot_blocks = lax.all_to_all(cot_blocks, "frame", 0, 0, tiled=True)
-    conv_other = lax.ppermute(conv_half, "frame", [(i, i ^ 2) for i in range(frames)])
     acts, kept = call(
         functools.partial(act_kernel, cols=cols, part=part),
         20,
@@ -426,10 +413,7 @@
     )
     by_tile = swap(own, "tile")
     by_clip = swap(own, "dp")
-    (conv_full,) = call(
-        taps_kernel, 12, [((3, ranks, share, 3 * part), BF)], [], place, conv_half, conv_other
-    )
-    conv_full = conv_full.reshape(3, width, 3 * part)
+    conv_full = conv_in.transpose(1, 0, 2, 3).reshape(3, width, 3 * part)
     blocked = (2 * ranks, 2 * third, 3 * part)
     plain = (2, 2, tiles * tokens, part)
     (mid,) = call(
@@ -513,7 +497,7 @@
     while step > 0:
         pairs = [(i, i ^ (2 * step)) for i in range(frames)]
         if step == 1:
-            shares, d_back = lax.optimization_barrier((shares, d_back))
+            _, d_back = lax.optimization_barrier((shares, d_back))
         shares = add(shares[:step], lax.ppermute(shares[step:], "frame", pairs))
         step //= 2
     shares = shares[0]

time: 161 us -> 158 us (0.981)
  starting transfers between devices: 45.4 us -> 47.8 us
    ppermute x1 -> x0, waiting for transfers between devices: 10.1 us -> none  [local(): lax.ppermute(conv_half, 'frame', [(i, i ^ 2) for i in range(frames)])]
    all_to_all x1, waiting for transfers between devices: 1.85 us -> 10.6 us  [local(): conv_in = lax.all_to_all(mine, square, 0, 0, tiled=True)]
    all_to_all x1, starting transfers between devices: 3.03 us -> 5.88 us  [local(): lax.all_to_all(mid, ('dp',) + square, 0, 0, axis_index_groups=groups, til...]
    unnamed x25, local copies, waits for them, and re-layouts: 3.03 us -> 0.2 us
    ppermute x1 -> x0, starting transfers between devices: 2.02 us -> none  [local(): lax.ppermute(conv_half, 'frame', [(i, i ^ 2) for i in range(frames)])]
    pallas_call x7 -> x6, Pallas kernels: 30.4 us -> 29 us  [call(): pl.pallas_call(kernel, out_shape=[jax.ShapeDtypeStruct(shape, dtype) for...]
  transfers between devices with their start and end apart: 31 -> 30, of which waited for: 16 -> 16; matrix products, arithmetic and copies ran while one was open for 3% -> 4% of each run, Pallas kernels for 11% -> 11%
where the time goes in v8:
time: 158 us
  waiting for transfers between devices  69.1 us (44%)
  starting transfers between devices  47.8 us (30%)
  Pallas kernels  29 us (18%)
  local copies, waits for them, and re-layouts  7.66 us (5%)
  other arithmetic  3.06 us (2%)
    ppermute x23, waiting for transfers between devices, swap(): lax.ppermute(x, axis, [(i, i ^ 1) for i in range(lax.axis_size(axis))])  41.5 us
    pallas_call x6, Pallas kernels, call(): pl.pallas_call(kernel, out_shape=[jax.ShapeDtypeStruct(shape, dtype) for...  29 us
    ppermute x23, starting transfers between devices, swap(): lax.ppermute(x, axis, [(i, i ^ 1) for i in range(lax.axis_size(axis))])  17.1 us
    ppermute x2, waiting for transfers between devices, local(): shares = add(shares[:step], lax.ppermute(shares[step:], 'frame', pairs))  15.9 us
    all_to_all x1, waiting for transfers between devices, local(): conv_in = lax.all_to_all(mine, square, 0, 0, tiled=True)  10.6 us
    all_to_all x1, starting transfers between devices, local(): own = lax.all_to_all(kinds, 'frame', 0, 0, tiled=True)  6.33 us
    all_to_all x1, starting transfers between devices, local(): lax.all_to_all(mid, ('dp',) + square, 0, 0, axis_index_groups=groups, til...  5.88 us
    all_to_all x1, starting transfers between devices, local(): cot_blocks = lax.all_to_all(cot_blocks, 'frame', 0, 0, tiled=True)  5.59 us
  transfers between devices with their start and end apart: 30, of which 16 were waited for; matrix products, arithmetic and copies ran while one was open for 4% of the time, Pallas kernels for 11%

profile of v8, /device:TPU:0, one launch (start us, length us, event | category | flops | bytes accessed | tf_op | source)
XLA Modules:
  0.0 157.7 jit_solution(1641357367626369490)
XLA Ops:
  2.5 6.3 %all-to-all-start = ((bf16[8,40,640]{2,1,0:T(8,128)(2,1)}), bf16[8,40,640]{2,1,0:T(8,128)(2,1)S(1)}, u32[]{:S(2)}, u32[]{:S(2)}) async-start(bf16[8,40,640]{2,1,0:T(8,128)(2,1)} %bitcast.8), calls=%async_computation | async-start | bytes 819200 | tf_op jit(solution)/shard_map/all_to_all | solution.py:385
  12.8 7.0 %collective-permute-done.refs_2_ = bf16[288,640]{1,0:T(8,128)(2,1)S(1)} collective-permute-done((bf16[288,640]{1,0:T(8,128)(2,1)S(1)}, bf16[288,640]{1,0:T(8,128)(2,1)S(1)}, u32[]{:S(2)}, u32[]{:S(2)}) %collective-permute-start) | collective-permute-done | bytes 368672 | tf_op jit(solution)/shard_map/ppermute | solution.py:19
  22.7 5.2 %all-to-all-start.1 = ((bf16[16,3,40,240]{3,2,1,0:T(8,128)(2,1)}), bf16[16,3,40,240]{3,2,1,0:T(8,128)(2,1)}, u32[]{:S(2)}, u32[]{:S(2)}) async-start(bf16[16,3,40,240]{3,2,1,0:T(8,128)(2,1)} %bitcast.36), calls=%async_computation.1 | async-start | bytes 1966080 | tf_op jit(solution)/shard_map/all_to_all | solution.py:396
  27.9 1.9 %collective-permute-start.2 = (bf16[144,640]{1,0:T(8,128)(2,1)S(1)}, bf16[144,640]{1,0:T(8,128)(2,1)S(1)}, u32[]{:S(2)}, u32[]{:S(2)}) collective-permute-start(bf16[144,640]{1,0:T(8,128)(2,1)S(1)} %slice.51), channel_id=1, source_target_pairs={{0,1},{1,0},{2,3},{3,2},{4,5},{5,4},{6,7},{7,6},{8,9},{9,8},{10,11... | collective-permute-start | bytes 552968 | tf_op jit(solution)/shard_map/ppermute | solution.py:19
  31.0 6.9 %collective-permute-done.2 = bf16[144,640]{1,0:T(8,128)(2,1)S(1)} collective-permute-done((bf16[144,640]{1,0:T(8,128)(2,1)S(1)}, bf16[144,640]{1,0:T(8,128)(2,1)S(1)}, u32[]{:S(2)}, u32[]{:S(2)}) %collective-permute-start.2) | collective-permute-done | bytes 184352 | tf_op jit(solution)/shard_map/ppermute | solution.py:19
  38.0 1.8 %reshape_squeeze.7 = bf16[8,36,640]{2,1,0:T(8,128)(2,1)} reshape(bf16[1,1,9,32,640]{4,3,2,1,0:T(8,128)(2,1)} %param.9) | data formatting | bytes 737280 | tf_op jit(solution)/shard_map/reshape;squeeze | solution.py:402
  39.9 10.6 %all-to-all-done.1 = bf16[16,3,40,240]{3,2,1,0:T(8,128)(2,1)} async-done(((bf16[16,3,40,240]{3,2,1,0:T(8,128)(2,1)}), bf16[16,3,40,240]{3,2,1,0:T(8,128)(2,1)}, u32[]{:S(2)}, u32[]{:S(2)}) %all-to-all-start.1) | async-done | bytes 921632 | tf_op jit(solution)/shard_map/all_to_all | solution.py:396
  50.5 5.6 %all-to-all-start.2 = ((bf16[8,36,640]{2,1,0:T(8,128)(2,1)}), bf16[8,36,640]{2,1,0:T(8,128)(2,1)S(1)}, u32[]{:S(2)}, u32[]{:S(2)}) async-start(bf16[8,36,640]{2,1,0:T(8,128)(2,1)} %reshape_squeeze.7), calls=%async_computation.2 | async-start | bytes 819200 | tf_op jit(solution)/shard_map/all_to_all | solution.py:404
  58.8 4.8 %shard_map.127 = (bf16[4,640,640]{2,1,0:T(8,128)(2,1)S(1)}, bf16[4,576,80]{2,1,0:T(8,128)(2,1)S(1)}) custom-call(s32[5]{0:T(128)S(1)} %stack.23.place, f32[1,640]{1,0:T(1,128)S(1)} %broadcast_in_dim.20.gain, bf16[288,640]{1,0:T(8,128)(2,1)S(1)} %bitcast.35, bf16[288,640]{1,0:T(8,128)(2,1)S(1)} %collective-permute-done.1.refs_1_, ...), custom_call_target="tpu_custom_call" | custom-call | tf_op jit(solution)/shard_map/pallas_call | solution.py:349
  63.6 5.1 %shard_map.128 = bf16[32,24,240]{2,1,0:T(8,128)(2,1)} custom-call(s32[5]{0:T(128)S(1)} %stack.23.place, bf16[3,640,240]{2,1,0:T(8,128)(2,1)S(1)} %bitcast.31, bf16[4,640,640]{2,1,0:T(8,128)(2,1)S(1)} %get-tuple-element.64.acts, bf16[4,576,80]{2,1,0:T(8,128)(2,1)S(1)} %get-tuple-element.65.kept), custom_call_target="tpu_custom_call" | custom-call | tf_op jit(solution)/shard_map/pallas_call | solution.py:349
  69.0 5.9 %all-to-all-start.3 = ((bf16[32,24,240]{2,1,0:T(8,128)(2,1)}), bf16[32,24,240]{2,1,0:T(8,128)(2,1)S(1)}, u32[]{:S(2)}, u32[]{:S(2)}) async-start(bf16[32,24,240]{2,1,0:T(8,128)(2,1)} %shard_map.128), calls=%async_computation.3 | async-start | bytes 786432 | tf_op jit(solution)/shard_map/all_to_all | solution.py:438
  75.6 1.8 %collective-permute-start.10 = (bf16[4,40,640]{2,1,0:T(8,128)(2,1)S(1)}, bf16[4,40,640]{2,1,0:T(8,128)(2,1)S(1)}, u32[]{:S(2)}, u32[]{:S(2)}) collective-permute-start(bf16[4,40,640]{2,1,0:T(8,128)(2,1)S(1)} %slice.53), channel_id=1, source_target_pairs={{0,1},{1,0},{2,3},{3,2},{4,5},{5,4},{6,7},{7,6},{8,9},{9,8},{10,11... | collective-permute-start | bytes 614408 | tf_op jit(solution)/shard_map/ppermute | solution.py:19
  78.9 6.6 %collective-permute-done.10.refs_3_ = bf16[4,40,640]{2,1,0:T(8,128)(2,1)S(1)} collective-permute-done((bf16[4,40,640]{2,1,0:T(8,128)(2,1)S(1)}, bf16[4,40,640]{2,1,0:T(8,128)(2,1)S(1)}, u32[]{:S(2)}, u32[]{:S(2)}) %collective-permute-start.10) | collective-permute-done | bytes 204832 | tf_op jit(solution)/shard_map/ppermute | solution.py:19
  90.0 10.6 %shard_map.130 = (bf16[2,2,4,40,640]{4,3,2,1,0:T(8,128)(2,1)S(1)}, bf16[2,2,4,40,640]{4,3,2,1,0:T(8,128)(2,1)S(1)}, f32[1,128]{1,0:T(1,128)S(1)}, f32[320,128]{1...) custom-call(s32[5]{0:T(128)S(1)} %stack.23.place, ...), custom_call_target="tpu_custom_call" | custom-call | tf_op jit(solution)/shard_map/pallas_call | solution.py:349
  100.8 2.2 %shard_map.131 = (f32[320,640]{1,0:T(8,128)S(1)}, f32[320,640]{1,0:T(8,128)S(1)}) custom-call(f32[320,128]{1,0:T(8,128)S(1)} %get-tuple-element.84.d_raw, f32[320,640]{1,0:T(8,128)S(1)} %get-tuple-element.85.q_hat, f32[320,640]{1,0:T(8,128)S(1)} %get-tuple-element.86.k_hat, f32[1,640]{1,0:T(1,128)S(1)} %broadcast_in_dim_tile.9.qgain, ...), custom_call_target="tpu_custom_call" | custom-call | tf_op jit(solution)/shard_map/pallas_call | solution.py:349
  104.9 10.2 %collective-permute-done.18 = bf16[2,4,40,640]{3,2,1,0:T(8,128)(2,1)S(1)} collective-permute-done((bf16[2,4,40,640]{3,2,1,0:T(8,128)(2,1)S(1)}, bf16[2,4,40,640]{3,2,1,0:T(8,128)(2,1)S(1)}, u32[]{:S(2)}, u32[]{:S(2)}) %collective-permute-start.18) | collective-permute-done | bytes 409632 | tf_op jit(solution)/shard_map/ppermute | solution.py:19
  116.2 4.8 %shard_map.132 = bf16[8,40,640]{2,1,0:T(8,128)(2,1)} custom-call(f32[320,640]{1,0:T(8,128)S(1)} %get-tuple-element.89.d_qn, f32[320,640]{1,0:T(8,128)S(1)} %get-tuple-element.90.d_kn, f32[320,640]{1,0:T(8,128)S(1)} %get-tuple-element.85.q_hat, f32[320,640]{1,0:T(8,128)S(1)} %get-tuple-element.86.k_hat, f32[320,128]{1,0:T(8,128)S(1)} %get-tuple-element.91.q_rstd, ...), custom_call_target="tpu_custom_call" | custom-call | tf_op jit(solution)/shard_map/pallas_call | solution.py:349
  121.0 4.9 %all-to-all-start.4 = ((bf16[8,40,640]{2,1,0:T(8,128)(2,1)}), bf16[8,40,640]{2,1,0:T(8,128)(2,1)S(1)}, u32[]{:S(2)}, u32[]{:S(2)}) async-start(bf16[8,40,640]{2,1,0:T(8,128)(2,1)} %shard_map.132), calls=%async_computation.4 | async-start | bytes 819200 | tf_op jit(solution)/shard_map/all_to_all | solution.py:493
  126.0 3.0 %collective-permute-start.20 = (bf16[2,40,640]{2,1,0:T(8,128)(2,1)S(1)}, bf16[2,40,640]{2,1,0:T(8,128)(2,1)S(1)}, u32[]{:S(2)}, u32[]{:S(2)}) collective-permute-start(bf16[2,40,640]{2,1,0:T(8,128)(2,1)S(1)} %slice.71), channel_id=1, source_target_pairs={{0,8},{2,10},{4,12},{6,14},{8,0},{10,2},{12,4},{14,6},{1,9},{3,11}... | collective-permute-start | bytes 307208 | tf_op jit(solution)/shard_map/ppermute | solution.py:501
  129.0 14.2 %collective-permute-done.20 = bf16[2,40,640]{2,1,0:T(8,128)(2,1)S(1)} collective-permute-done((bf16[2,40,640]{2,1,0:T(8,128)(2,1)S(1)}, bf16[2,40,640]{2,1,0:T(8,128)(2,1)S(1)}, u32[]{:S(2)}, u32[]{:S(2)}) %collective-permute-start.20) | collective-permute-done | bytes 102432 | tf_op jit(solution)/shard_map/ppermute | solution.py:501
  144.4 2.6 %collective-permute-done.23 = f32[640]{0:T(1024)S(1)} collective-permute-done((f32[640]{0:T(1024)S(1)}, f32[640]{0:T(1024)S(1)}, u32[]{:S(2)}, u32[]{:S(2)}) %collective-permute-start.23) | collective-permute-done | bytes 2592 | tf_op jit(solution)/shard_map/ppermute | solution.py:19
  148.7 1.9 %collective-permute-done.24 = f32[640]{0:T(1024)S(1)} collective-permute-done((f32[640]{0:T(1024)S(1)}, f32[640]{0:T(1024)S(1)}, u32[]{:S(2)}, u32[]{:S(2)}) %collective-permute-start.24) | collective-permute-done | bytes 2592 | tf_op jit(solution)/shard_map/ppermute | solution.py:19
  151.1 1.7 %collective-permute-done.21 = bf16[1,40,640]{2,1,0:T(8,128)(2,1)S(1)} collective-permute-done((bf16[1,40,640]{2,1,0:T(8,128)(2,1)S(1)}, bf16[1,40,640]{2,1,0:T(8,128)(2,1)S(1)}, u32[]{:S(2)}, u32[]{:S(2)}) %collective-permute-start.21) | collective-permute-done | bytes 51232 | tf_op jit(solution)/shard_map/ppermute | solution.py:501
  154.5 2.5 %collective-permute-done.22 = bf16[40,640]{1,0:T(8,128)(2,1)S(1)} collective-permute-done((bf16[40,640]{1,0:T(8,128)(2,1)S(1)}, bf16[40,640]{1,0:T(8,128)(2,1)S(1)}, u32[]{:S(2)}, u32[]{:S(2)}) %collective-permute-start.22) | collective-permute-done | bytes 51232 | tf_op jit(solution)/shard_map/ppermute | solution.py:19
  (110 shorter events, 28.6 us)
Async XLA Ops:
  2.5 19.2 %all-to-all-start = ((bf16[8,40,640]{2,1,0:T(8,128)(2,1)}), bf16[8,40,640]{2,1,0:T(8,128)(2,1)S(1)}, u32[]{:S(2)}, u32[]{:S(2)}) async-start(bf16[8,40,640]{2,1,0:T(8,128)(2,1)} %bitcast.8), calls=%async_computation | async-start | bytes 819200 | tf_op jit(solution)/shard_map/all_to_all | solution.py:385
  8.8 11.0 %collective-permute-start = (bf16[288,640]{1,0:T(8,128)(2,1)S(1)}, bf16[288,640]{1,0:T(8,128)(2,1)S(1)}, u32[]{:S(2)}, u32[]{:S(2)}) collective-permute-start(bf16[288,640]{1,0:T(8,128)(2,1)S(1)} %bitcast.32), channel_id=1, source_target_pairs={{0,16},{16,0},{1,17},{17,1},{2,18},{18,2},{3,19},{19,3},{4,20},{20... | collective-permute-start | bytes 1105928 | tf_op jit(solution)/shard_map/ppermute | solution.py:19
  10.4 10.7 %collective-permute-start.1 = (bf16[288,640]{1,0:T(8,128)(2,1)S(1)}, bf16[288,640]{1,0:T(8,128)(2,1)S(1)}, u32[]{:S(2)}, u32[]{:S(2)}) collective-permute-start(bf16[288,640]{1,0:T(8,128)(2,1)S(1)} %bitcast.33), channel_id=1, source_target_pairs={{0,1},{1,0},{2,3},{3,2},{4,5},{5,4},{6,7},{7,6},{8,9},{9,8},{10,11... | collective-permute-start | bytes 1105928 | tf_op jit(solution)/shard_map/ppermute | solution.py:19
  22.7 27.8 %all-to-all-start.1 = ((bf16[16,3,40,240]{3,2,1,0:T(8,128)(2,1)}), bf16[16,3,40,240]{3,2,1,0:T(8,128)(2,1)}, u32[]{:S(2)}, u32[]{:S(2)}) async-start(bf16[16,3,40,240]{3,2,1,0:T(8,128)(2,1)} %bitcast.36), calls=%async_computation.1 | async-start | bytes 1966080 | tf_op jit(solution)/shard_map/all_to_all | solution.py:396
  27.9 9.9 %collective-permute-start.2 = (bf16[144,640]{1,0:T(8,128)(2,1)S(1)}, bf16[144,640]{1,0:T(8,128)(2,1)S(1)}, u32[]{:S(2)}, u32[]{:S(2)}) collective-permute-start(bf16[144,640]{1,0:T(8,128)(2,1)S(1)} %slice.51), channel_id=1, source_target_pairs={{0,1},{1,0},{2,3},{3,2},{4,5},{5,4},{6,7},{7,6},{8,9},{9,8},{10,11... | collective-permute-start | bytes 552968 | tf_op jit(solution)/shard_map/ppermute | solution.py:19
  29.9 8.0 %collective-permute-start.3 = (bf16[144,640]{1,0:T(8,128)(2,1)S(1)}, bf16[144,640]{1,0:T(8,128)(2,1)S(1)}, u32[]{:S(2)}, u32[]{:S(2)}) collective-permute-start(bf16[144,640]{1,0:T(8,128)(2,1)S(1)} %slice.52), channel_id=1, source_target_pairs={{0,16},{16,0},{1,17},{17,1},{2,18},{18,2},{3,19},{19,3},{4,20},{20... | collective-permute-start | bytes 552968 | tf_op jit(solution)/shard_map/ppermute | solution.py:19
  30.5 9.3 %collective-permute-start.4 = (bf16[288,640]{1,0:T(8,128)(2,1)S(1)}, bf16[288,640]{1,0:T(8,128)(2,1)S(1)}, u32[]{:S(2)}, u32[]{:S(2)}) collective-permute-start(bf16[288,640]{1,0:T(8,128)(2,1)S(1)} %bitcast.34), channel_id=1, source_target_pairs={{0,2},{2,0},{4,6},{6,4},{8,10},{10,8},{12,14},{14,12},{1,3},{3,1},... | collective-permute-start | bytes 1105928 | tf_op jit(solution)/shard_map/ppermute | solution.py:19
  30.5 9.3 %collective-permute-start.5 = (bf16[288,640]{1,0:T(8,128)(2,1)S(1)}, bf16[288,640]{1,0:T(8,128)(2,1)S(1)}, u32[]{:S(2)}, u32[]{:S(2)}) collective-permute-start(bf16[288,640]{1,0:T(8,128)(2,1)S(1)} %collective-permute-done.1.refs_1_), channel_id=1, source_target_pairs={{0,2},{2,0},{4,6},{6,4},{8,10},{10,8},{12,14},{14,12},{1,3},{3,1},... | collective-permute-start | bytes 1105928 | tf_op jit(solution)/shard_map/ppermute | solution.py:19
  31.0 8.8 %collective-permute-start.6 = (bf16[288,640]{1,0:T(8,128)(2,1)S(1)}, bf16[288,640]{1,0:T(8,128)(2,1)}, u32[]{:S(2)}, u32[]{:S(2)}) collective-permute-start(bf16[288,640]{1,0:T(8,128)(2,1)S(1)} %collective-permute-done.refs_2_), channel_id=1, source_target_pairs={{0,2},{2,0},{4,6},{6,4},{8,10},{10,8},{12,14},{14,12},{1,3},{3,1},... | collective-permute-start | bytes 1105928 | tf_op jit(solution)/shard_map/ppermute | solution.py:19
  50.5 18.5 %all-to-all-start.2 = ((bf16[8,36,640]{2,1,0:T(8,128)(2,1)}), bf16[8,36,640]{2,1,0:T(8,128)(2,1)S(1)}, u32[]{:S(2)}, u32[]{:S(2)}) async-start(bf16[8,36,640]{2,1,0:T(8,128)(2,1)} %reshape_squeeze.7), calls=%async_computation.2 | async-start | bytes 819200 | tf_op jit(solution)/shard_map/all_to_all | solution.py:404
  56.1 12.6 %collective-permute-start.8 = (bf16[8,40,640]{2,1,0:T(8,128)(2,1)S(1)}, bf16[8,40,640]{2,1,0:T(8,128)(2,1)S(1)}, u32[]{:S(2)}, u32[]{:S(2)}) collective-permute-start(bf16[8,40,640]{2,1,0:T(8,128)(2,1)S(1)} %all-to-all-done.refs_0_), channel_id=1, source_target_pairs={{0,1},{1,0},{2,3},{3,2},{4,5},{5,4},{6,7},{7,6},{8,9},{9,8},{10,11... | collective-permute-start | bytes 1228808 | tf_op jit(solution)/shard_map/ppermute | solution.py:19
  56.7 12.0 %collective-permute-start.9 = (bf16[8,40,640]{2,1,0:T(8,128)(2,1)S(1)}, bf16[8,40,640]{2,1,0:T(8,128)(2,1)S(1)}, u32[]{:S(2)}, u32[]{:S(2)}) collective-permute-start(bf16[8,40,640]{2,1,0:T(8,128)(2,1)S(1)} %all-to-all-done.refs_0_), channel_id=1, source_target_pairs={{0,16},{16,0},{1,17},{17,1},{2,18},{18,2},{3,19},{19,3},{4,20},{20... | collective-permute-start | bytes 1228808 | tf_op jit(solution)/shard_map/ppermute | solution.py:19
  69.0 19.4 %all-to-all-start.3 = ((bf16[32,24,240]{2,1,0:T(8,128)(2,1)}), bf16[32,24,240]{2,1,0:T(8,128)(2,1)S(1)}, u32[]{:S(2)}, u32[]{:S(2)}) async-start(bf16[32,24,240]{2,1,0:T(8,128)(2,1)} %shard_map.128), calls=%async_computation.3 | async-start | bytes 786432 | tf_op jit(solution)/shard_map/all_to_all | solution.py:438
  74.9 12.0 %collective-permute-start.12 = (bf16[8,40,640]{2,1,0:T(8,128)(2,1)S(1)}, bf16[8,40,640]{2,1,0:T(8,128)(2,1)S(1)}, u32[]{:S(2)}, u32[]{:S(2)}) collective-permute-start(bf16[8,40,640]{2,1,0:T(8,128)(2,1)S(1)} %all-to-all-done.refs_0_), channel_id=1, source_target_pairs={{0,2},{2,0},{4,6},{6,4},{8,10},{10,8},{12,14},{14,12},{1,3},{3,1},... | collective-permute-start | bytes 1228808 | tf_op jit(solution)/shard_map/ppermute | solution.py:19
  75.2 11.7 %collective-permute-start.13 = (bf16[8,40,640]{2,1,0:T(8,128)(2,1)S(1)}, bf16[8,40,640]{2,1,0:T(8,128)(2,1)S(1)}, u32[]{:S(2)}, u32[]{:S(2)}) collective-permute-start(bf16[8,40,640]{2,1,0:T(8,128)(2,1)S(1)} %collective-permute-done.8.refs_1_), channel_id=1, source_target_pairs={{0,2},{2,0},{4,6},{6,4},{8,10},{10,8},{12,14},{14,12},{1,3},{3,1},... | collective-permute-start | bytes 1228808 | tf_op jit(solution)/shard_map/ppermute | solution.py:19
  75.6 9.9 %collective-permute-start.10 = (bf16[4,40,640]{2,1,0:T(8,128)(2,1)S(1)}, bf16[4,40,640]{2,1,0:T(8,128)(2,1)S(1)}, u32[]{:S(2)}, u32[]{:S(2)}) collective-permute-start(bf16[4,40,640]{2,1,0:T(8,128)(2,1)S(1)} %slice.53), channel_id=1, source_target_pairs={{0,1},{1,0},{2,3},{3,2},{4,5},{5,4},{6,7},{7,6},{8,9},{9,8},{10,11... | collective-permute-start | bytes 614408 | tf_op jit(solution)/shard_map/ppermute | solution.py:19
  77.4 9.5 %collective-permute-start.14 = (bf16[8,40,640]{2,1,0:T(8,128)(2,1)S(1)}, bf16[8,40,640]{2,1,0:T(8,128)(2,1)}, u32[]{:S(2)}, u32[]{:S(2)}) collective-permute-start(bf16[8,40,640]{2,1,0:T(8,128)(2,1)S(1)} %collective-permute-done.9.refs_2_), channel_id=1, source_target_pairs={{0,2},{2,0},{4,6},{6,4},{8,10},{10,8},{12,14},{14,12},{1,3},{3,1},... | collective-permute-start | bytes 1228808 | tf_op jit(solution)/shard_map/ppermute | solution.py:19
  77.4 9.2 %collective-permute-start.11 = (bf16[4,40,640]{2,1,0:T(8,128)(2,1)S(1)}, bf16[4,40,640]{2,1,0:T(8,128)(2,1)}, u32[]{:S(2)}, u32[]{:S(2)}) collective-permute-start(bf16[4,40,640]{2,1,0:T(8,128)(2,1)S(1)} %slice.54), channel_id=1, source_target_pairs={{0,16},{16,0},{1,17},{17,1},{2,18},{18,2},{3,19},{19,3},{4,20},{20... | collective-permute-start | bytes 614408 | tf_op jit(solution)/shard_map/ppermute | solution.py:19
  103.3 11.8 %collective-permute-start.18 = (bf16[2,4,40,640]{3,2,1,0:T(8,128)(2,1)S(1)}, bf16[2,4,40,640]{3,2,1,0:T(8,128)(2,1)S(1)}, u32[]{:S(2)}, u32[]{:S(2)}) collective-permute-start(bf16[2,4,40,640]{3,2,1,0:T(8,128)(2,1)S(1)} %slice_bitcast_fusion), channel_id=1, source_target_pairs={{0,16},{16,0},{1,17},{17,1},{2,18},{18,2},{3,19},{19,3},{4,20},{20... | collective-permute-start | bytes 1228808 | tf_op jit(solution)/shard_map/ppermute | solution.py:19
  115.3 10.6 %collective-permute-start.19 = (bf16[4,40,640]{2,1,0:T(8,128)(2,1)S(1)}, bf16[4,40,640]{2,1,0:T(8,128)(2,1)S(1)}, u32[]{:S(2)}, u32[]{:S(2)}) collective-permute-start(bf16[4,40,640]{2,1,0:T(8,128)(2,1)S(1)} %slice_bitcast_fusion.1), channel_id=1, source_target_pairs={{0,1},{1,0},{2,3},{3,2},{4,5},{5,4},{6,7},{7,6},{8,9},{9,8},{10,11... | collective-permute-start | bytes 614408 | tf_op jit(solution)/shard_map/ppermute | solution.py:19
  121.0 22.2 %all-to-all-start.4 = ((bf16[8,40,640]{2,1,0:T(8,128)(2,1)}), bf16[8,40,640]{2,1,0:T(8,128)(2,1)S(1)}, u32[]{:S(2)}, u32[]{:S(2)}) async-start(bf16[8,40,640]{2,1,0:T(8,128)(2,1)} %shard_map.132), calls=%async_computation.4 | async-start | bytes 819200 | tf_op jit(solution)/shard_map/all_to_all | solution.py:493
  126.0 17.2 %collective-permute-start.20 = (bf16[2,40,640]{2,1,0:T(8,128)(2,1)S(1)}, bf16[2,40,640]{2,1,0:T(8,128)(2,1)S(1)}, u32[]{:S(2)}, u32[]{:S(2)}) collective-permute-start(bf16[2,40,640]{2,1,0:T(8,128)(2,1)S(1)} %slice.71), channel_id=1, source_target_pairs={{0,8},{2,10},{4,12},{6,14},{8,0},{10,2},{12,4},{14,6},{1,9},{3,11}... | collective-permute-start | bytes 307208 | tf_op jit(solution)/shard_map/ppermute | solution.py:501
  148.7 4.1 %collective-permute-start.21 = (bf16[1,40,640]{2,1,0:T(8,128)(2,1)S(1)}, bf16[1,40,640]{2,1,0:T(8,128)(2,1)S(1)}, u32[]{:S(2)}, u32[]{:S(2)}) collective-permute-start(bf16[1,40,640]{2,1,0:T(8,128)(2,1)S(1)} %slice.73), channel_id=1, source_target_pairs={{0,4},{2,6},{4,0},{6,2},{8,12},{10,14},{12,8},{14,10},{1,5},{3,7},... | collective-permute-start | bytes 153608 | tf_op jit(solution)/shard_map/ppermute | solution.py:501
  152.8 4.2 %collective-permute-start.22 = (bf16[40,640]{1,0:T(8,128)(2,1)S(1)}, bf16[40,640]{1,0:T(8,128)(2,1)S(1)}, u32[]{:S(2)}, u32[]{:S(2)}) collective-permute-start(bf16[40,640]{1,0:T(8,128)(2,1)S(1)} %fusion.4), channel_id=1, source_target_pairs={{0,16},{16,0},{1,17},{17,1},{2,18},{18,2},{3,19},{19,3},{4,20},{20... | collective-permute-start | bytes 153608 | tf_op jit(solution)/shard_map/ppermute | solution.py:19
  (18 other events, 175.7 us)

commit v9 on v8

--- a/solution.py
+++ b/solution.py
@@ -491,7 +491,8 @@
         d_qn, d_kn, q_hat, k_hat, q_rstd, k_rstd, d_value, attn_full, qgain, kgain, scale_sums,
     )
     d_back = lax.all_to_all(d_mid, "frame", 0, 0, tiled=True)
-    shares = add(shares[0], swap(shares[1], "dp"))
+    theirs, _ = lax.optimization_barrier((swap(shares[1], "dp"), d_mid))
+    shares = add(shares[0], theirs)
     shares = add(shares[0], swap(shares[1], "tile"))
     step = frames // 4
     while step > 0:

time: 158 us -> 154 us (0.975)
  waiting for transfers between devices: 69.1 us -> 64.4 us
    ppermute x23, waiting for transfers between devices: 41.5 us -> 37.4 us  [swap(): lax.ppermute(x, axis, [(i, i ^ 1) for i in range(lax.axis_size(axis))])]
  transfers between devices with their start and end apart: 30 -> 30, of which waited for: 16 -> 17; matrix products, arithmetic and copies ran while one was open for 4% -> 4% of each run, Pallas kernels for 11% -> 11%
where the time goes in v9:
time: 154 us; the launch traced here: 153 us
  waiting for transfers between devices  64.4 us (42%)
  starting transfers between devices  47.8 us (31%)
  Pallas kernels  29 us (19%)
  local copies, waits for them, and re-layouts  7.66 us (5%)
  other arithmetic  3.06 us (2%)
    ppermute x23, waiting for transfers between devices, swap(): lax.ppermute(x, axis, [(i, i ^ 1) for i in range(lax.axis_size(axis))])  37.4 us
    pallas_call x6, Pallas kernels, call(): pl.pallas_call(kernel, out_shape=[jax.ShapeDtypeStruct(shape, dtype) for...  29 us
    ppermute x23, starting transfers between devices, swap(): lax.ppermute(x, axis, [(i, i ^ 1) for i in range(lax.axis_size(axis))])  17.1 us
    ppermute x2, waiting for transfers between devices, local(): shares = add(shares[:step], lax.ppermute(shares[step:], 'frame', pairs))  15.3 us
    all_to_all x1, waiting for transfers between devices, local(): conv_in = lax.all_to_all(mine, square, 0, 0, tiled=True)  10.6 us
    all_to_all x1, starting transfers between devices, local(): own = lax.all_to_all(kinds, 'frame', 0, 0, tiled=True)  6.33 us
    all_to_all x1, starting transfers between devices, local(): lax.all_to_all(mid, ('dp',) + square, 0, 0, axis_index_groups=groups, til...  5.88 us
    all_to_all x1, starting transfers between devices, local(): cot_blocks = lax.all_to_all(cot_blocks, 'frame', 0, 0, tiled=True)  5.59 us
  transfers between devices with their start and end apart: 30, of which 17 were waited for; matrix products, arithmetic and copies ran while one was open for 4% of the time, Pallas kernels for 11%

profile of v9, /device:TPU:0, one launch (start us, length us, event | category | flops | bytes accessed | tf_op | source)
XLA Modules:
  0.0 152.9 jit_solution(12483248046833756760)
XLA Ops:
  2.5 6.3 %all-to-all-start = ((bf16[8,40,640]{2,1,0:T(8,128)(2,1)}), bf16[8,40,640]{2,1,0:T(8,128)(2,1)S(1)}, u32[]{:S(2)}, u32[]{:S(2)}) async-start(bf16[8,40,640]{2,1,0:T(8,128)(2,1)} %bitcast.8), calls=%async_computation | async-start | bytes 819200 | tf_op jit(solution)/shard_map/all_to_all | solution.py:385
  12.8 7.0 %collective-permute-done.refs_2_ = bf16[288,640]{1,0:T(8,128)(2,1)S(1)} collective-permute-done((bf16[288,640]{1,0:T(8,128)(2,1)S(1)}, bf16[288,640]{1,0:T(8,128)(2,1)S(1)}, u32[]{:S(2)}, u32[]{:S(2)}) %collective-permute-start) | collective-permute-done | bytes 368672 | tf_op jit(solution)/shard_map/ppermute | solution.py:19
  22.7 5.2 %all-to-all-start.1 = ((bf16[16,3,40,240]{3,2,1,0:T(8,128)(2,1)}), bf16[16,3,40,240]{3,2,1,0:T(8,128)(2,1)}, u32[]{:S(2)}, u32[]{:S(2)}) async-start(bf16[16,3,40,240]{3,2,1,0:T(8,128)(2,1)} %bitcast.36), calls=%async_computation.1 | async-start | bytes 1966080 | tf_op jit(solution)/shard_map/all_to_all | solution.py:396
  27.9 1.9 %collective-permute-start.2 = (bf16[144,640]{1,0:T(8,128)(2,1)S(1)}, bf16[144,640]{1,0:T(8,128)(2,1)S(1)}, u32[]{:S(2)}, u32[]{:S(2)}) collective-permute-start(bf16[144,640]{1,0:T(8,128)(2,1)S(1)} %slice.51), channel_id=1, source_target_pairs={{0,1},{1,0},{2,3},{3,2},{4,5},{5,4},{6,7},{7,6},{8,9},{9,8},{10,11... | collective-permute-start | bytes 552968 | tf_op jit(solution)/shard_map/ppermute | solution.py:19
  31.0 6.9 %collective-permute-done.2 = bf16[144,640]{1,0:T(8,128)(2,1)S(1)} collective-permute-done((bf16[144,640]{1,0:T(8,128)(2,1)S(1)}, bf16[144,640]{1,0:T(8,128)(2,1)S(1)}, u32[]{:S(2)}, u32[]{:S(2)}) %collective-permute-start.2) | collective-permute-done | bytes 184352 | tf_op jit(solution)/shard_map/ppermute | solution.py:19
  38.0 1.8 %reshape_squeeze.7 = bf16[8,36,640]{2,1,0:T(8,128)(2,1)} reshape(bf16[1,1,9,32,640]{4,3,2,1,0:T(8,128)(2,1)} %param.9) | data formatting | bytes 737280 | tf_op jit(solution)/shard_map/reshape;squeeze | solution.py:402
  39.9 10.6 %all-to-all-done.1 = bf16[16,3,40,240]{3,2,1,0:T(8,128)(2,1)} async-done(((bf16[16,3,40,240]{3,2,1,0:T(8,128)(2,1)}), bf16[16,3,40,240]{3,2,1,0:T(8,128)(2,1)}, u32[]{:S(2)}, u32[]{:S(2)}) %all-to-all-start.1) | async-done | bytes 921632 | tf_op jit(solution)/shard_map/all_to_all | solution.py:396
  50.5 5.6 %all-to-all-start.2 = ((bf16[8,36,640]{2,1,0:T(8,128)(2,1)}), bf16[8,36,640]{2,1,0:T(8,128)(2,1)S(1)}, u32[]{:S(2)}, u32[]{:S(2)}) async-start(bf16[8,36,640]{2,1,0:T(8,128)(2,1)} %reshape_squeeze.7), calls=%async_computation.2 | async-start | bytes 819200 | tf_op jit(solution)/shard_map/all_to_all | solution.py:404
  58.8 4.8 %shard_map.127 = (bf16[4,640,640]{2,1,0:T(8,128)(2,1)S(1)}, bf16[4,576,80]{2,1,0:T(8,128)(2,1)S(1)}) custom-call(s32[5]{0:T(128)S(1)} %stack.23.place, f32[1,640]{1,0:T(1,128)S(1)} %broadcast_in_dim.20.gain, bf16[288,640]{1,0:T(8,128)(2,1)S(1)} %bitcast.35, bf16[288,640]{1,0:T(8,128)(2,1)S(1)} %collective-permute-done.1.refs_1_, ...), custom_call_target="tpu_custom_call" | custom-call | tf_op jit(solution)/shard_map/pallas_call | solution.py:349
  63.6 5.1 %shard_map.128 = bf16[32,24,240]{2,1,0:T(8,128)(2,1)} custom-call(s32[5]{0:T(128)S(1)} %stack.23.place, bf16[3,640,240]{2,1,0:T(8,128)(2,1)S(1)} %bitcast.31, bf16[4,640,640]{2,1,0:T(8,128)(2,1)S(1)} %get-tuple-element.65.acts, bf16[4,576,80]{2,1,0:T(8,128)(2,1)S(1)} %get-tuple-element.66.kept), custom_call_target="tpu_custom_call" | custom-call | tf_op jit(solution)/shard_map/pallas_call | solution.py:349
  69.0 5.9 %all-to-all-start.3 = ((bf16[32,24,240]{2,1,0:T(8,128)(2,1)}), bf16[32,24,240]{2,1,0:T(8,128)(2,1)S(1)}, u32[]{:S(2)}, u32[]{:S(2)}) async-start(bf16[32,24,240]{2,1,0:T(8,128)(2,1)} %shard_map.128), calls=%async_computation.3 | async-start | bytes 786432 | tf_op jit(solution)/shard_map/all_to_all | solution.py:438
  75.6 1.8 %collective-permute-start.10 = (bf16[4,40,640]{2,1,0:T(8,128)(2,1)S(1)}, bf16[4,40,640]{2,1,0:T(8,128)(2,1)S(1)}, u32[]{:S(2)}, u32[]{:S(2)}) collective-permute-start(bf16[4,40,640]{2,1,0:T(8,128)(2,1)S(1)} %slice.53), channel_id=1, source_target_pairs={{0,1},{1,0},{2,3},{3,2},{4,5},{5,4},{6,7},{7,6},{8,9},{9,8},{10,11... | collective-permute-start | bytes 614408 | tf_op jit(solution)/shard_map/ppermute | solution.py:19
  78.9 6.6 %collective-permute-done.10.refs_3_ = bf16[4,40,640]{2,1,0:T(8,128)(2,1)S(1)} collective-permute-done((bf16[4,40,640]{2,1,0:T(8,128)(2,1)S(1)}, bf16[4,40,640]{2,1,0:T(8,128)(2,1)S(1)}, u32[]{:S(2)}, u32[]{:S(2)}) %collective-permute-start.10) | collective-permute-done | bytes 204832 | tf_op jit(solution)/shard_map/ppermute | solution.py:19
  90.0 10.6 %shard_map.130 = (bf16[2,2,4,40,640]{4,3,2,1,0:T(8,128)(2,1)S(1)}, bf16[2,2,4,40,640]{4,3,2,1,0:T(8,128)(2,1)S(1)}, f32[1,128]{1,0:T(1,128)S(1)}, f32[320,128]{1...) custom-call(s32[5]{0:T(128)S(1)} %stack.23.place, ...), custom_call_target="tpu_custom_call" | custom-call | tf_op jit(solution)/shard_map/pallas_call | solution.py:349
  100.8 2.2 %shard_map.131 = (f32[320,640]{1,0:T(8,128)S(1)}, f32[320,640]{1,0:T(8,128)S(1)}) custom-call(f32[320,128]{1,0:T(8,128)S(1)} %get-tuple-element.85.d_raw, f32[320,640]{1,0:T(8,128)S(1)} %get-tuple-element.86.q_hat, f32[320,640]{1,0:T(8,128)S(1)} %get-tuple-element.87.k_hat, f32[1,640]{1,0:T(1,128)S(1)} %broadcast_in_dim_tile.9.qgain, ...), custom_call_target="tpu_custom_call" | custom-call | tf_op jit(solution)/shard_map/pallas_call | solution.py:349
  104.9 4.8 %shard_map.132 = bf16[8,40,640]{2,1,0:T(8,128)(2,1)} custom-call(f32[320,640]{1,0:T(8,128)S(1)} %get-tuple-element.90.d_qn, f32[320,640]{1,0:T(8,128)S(1)} %get-tuple-element.91.d_kn, f32[320,640]{1,0:T(8,128)S(1)} %get-tuple-element.86.q_hat, f32[320,640]{1,0:T(8,128)S(1)} %get-tuple-element.87.k_hat, f32[320,128]{1,0:T(8,128)S(1)} %get-tuple-element.92.q_rstd, ...), custom_call_target="tpu_custom_call" | custom-call | tf_op jit(solution)/shard_map/pallas_call | solution.py:349
  109.7 5.4 %collective-permute-done.18 = bf16[2,4,40,640]{3,2,1,0:T(8,128)(2,1)S(1)} collective-permute-done((bf16[2,4,40,640]{3,2,1,0:T(8,128)(2,1)S(1)}, bf16[2,4,40,640]{3,2,1,0:T(8,128)(2,1)S(1)}, u32[]{:S(2)}, u32[]{:S(2)}) %collective-permute-start.18) | collective-permute-done | bytes 409632 | tf_op jit(solution)/shard_map/ppermute | solution.py:19
  116.2 4.9 %all-to-all-start.4 = ((bf16[8,40,640]{2,1,0:T(8,128)(2,1)}), bf16[8,40,640]{2,1,0:T(8,128)(2,1)S(1)}, u32[]{:S(2)}, u32[]{:S(2)}) async-start(bf16[8,40,640]{2,1,0:T(8,128)(2,1)} %shard_map.132), calls=%async_computation.4 | async-start | bytes 819200 | tf_op jit(solution)/shard_map/all_to_all | solution.py:493
  121.9 2.9 %collective-permute-start.20 = (bf16[2,40,640]{2,1,0:T(8,128)(2,1)S(1)}, bf16[2,40,640]{2,1,0:T(8,128)(2,1)S(1)}, u32[]{:S(2)}, u32[]{:S(2)}) collective-permute-start(bf16[2,40,640]{2,1,0:T(8,128)(2,1)S(1)} %slice.71), channel_id=1, source_target_pairs={{0,8},{2,10},{4,12},{6,14},{8,0},{10,2},{12,4},{14,6},{1,9},{3,11}... | collective-permute-start | bytes 307208 | tf_op jit(solution)/shard_map/ppermute | solution.py:502
  124.8 13.5 %collective-permute-done.20 = bf16[2,40,640]{2,1,0:T(8,128)(2,1)S(1)} collective-permute-done((bf16[2,40,640]{2,1,0:T(8,128)(2,1)S(1)}, bf16[2,40,640]{2,1,0:T(8,128)(2,1)S(1)}, u32[]{:S(2)}, u32[]{:S(2)}) %collective-permute-start.20) | collective-permute-done | bytes 102432 | tf_op jit(solution)/shard_map/ppermute | solution.py:502
  139.6 2.6 %collective-permute-done.23 = f32[640]{0:T(1024)S(1)} collective-permute-done((f32[640]{0:T(1024)S(1)}, f32[640]{0:T(1024)S(1)}, u32[]{:S(2)}, u32[]{:S(2)}) %collective-permute-start.23) | collective-permute-done | bytes 2592 | tf_op jit(solution)/shard_map/ppermute | solution.py:19
  143.9 1.9 %collective-permute-done.24 = f32[640]{0:T(1024)S(1)} collective-permute-done((f32[640]{0:T(1024)S(1)}, f32[640]{0:T(1024)S(1)}, u32[]{:S(2)}, u32[]{:S(2)}) %collective-permute-start.24) | collective-permute-done | bytes 2592 | tf_op jit(solution)/shard_map/ppermute | solution.py:19
  146.3 1.7 %collective-permute-done.21 = bf16[1,40,640]{2,1,0:T(8,128)(2,1)S(1)} collective-permute-done((bf16[1,40,640]{2,1,0:T(8,128)(2,1)S(1)}, bf16[1,40,640]{2,1,0:T(8,128)(2,1)S(1)}, u32[]{:S(2)}, u32[]{:S(2)}) %collective-permute-start.21) | collective-permute-done | bytes 51232 | tf_op jit(solution)/shard_map/ppermute | solution.py:502
  149.7 2.5 %collective-permute-done.22 = bf16[40,640]{1,0:T(8,128)(2,1)S(1)} collective-permute-done((bf16[40,640]{1,0:T(8,128)(2,1)S(1)}, bf16[40,640]{1,0:T(8,128)(2,1)S(1)}, u32[]{:S(2)}, u32[]{:S(2)}) %collective-permute-start.22) | collective-permute-done | bytes 51232 | tf_op jit(solution)/shard_map/ppermute | solution.py:19
  (110 shorter events, 29.4 us)
Async XLA Ops:
  2.5 19.2 %all-to-all-start = ((bf16[8,40,640]{2,1,0:T(8,128)(2,1)}), bf16[8,40,640]{2,1,0:T(8,128)(2,1)S(1)}, u32[]{:S(2)}, u32[]{:S(2)}) async-start(bf16[8,40,640]{2,1,0:T(8,128)(2,1)} %bitcast.8), calls=%async_computation | async-start | bytes 819200 | tf_op jit(solution)/shard_map/all_to_all | solution.py:385
  8.8 11.0 %collective-permute-start = (bf16[288,640]{1,0:T(8,128)(2,1)S(1)}, bf16[288,640]{1,0:T(8,128)(2,1)S(1)}, u32[]{:S(2)}, u32[]{:S(2)}) collective-permute-start(bf16[288,640]{1,0:T(8,128)(2,1)S(1)} %bitcast.32), channel_id=1, source_target_pairs={{0,16},{16,0},{1,17},{17,1},{2,18},{18,2},{3,19},{19,3},{4,20},{20... | collective-permute-start | bytes 1105928 | tf_op jit(solution)/shard_map/ppermute | solution.py:19
  10.4 10.7 %collective-permute-start.1 = (bf16[288,640]{1,0:T(8,128)(2,1)S(1)}, bf16[288,640]{1,0:T(8,128)(2,1)S(1)}, u32[]{:S(2)}, u32[]{:S(2)}) collective-permute-start(bf16[288,640]{1,0:T(8,128)(2,1)S(1)} %bitcast.33), channel_id=1, source_target_pairs={{0,1},{1,0},{2,3},{3,2},{4,5},{5,4},{6,7},{7,6},{8,9},{9,8},{10,11... | collective-permute-start | bytes 1105928 | tf_op jit(solution)/shard_map/ppermute | solution.py:19
  22.7 27.8 %all-to-all-start.1 = ((bf16[16,3,40,240]{3,2,1,0:T(8,128)(2,1)}), bf16[16,3,40,240]{3,2,1,0:T(8,128)(2,1)}, u32[]{:S(2)}, u32[]{:S(2)}) async-start(bf16[16,3,40,240]{3,2,1,0:T(8,128)(2,1)} %bitcast.36), calls=%async_computation.1 | async-start | bytes 1966080 | tf_op jit(solution)/shard_map/all_to_all | solution.py:396
  27.9 9.9 %collective-permute-start.2 = (bf16[144,640]{1,0:T(8,128)(2,1)S(1)}, bf16[144,640]{1,0:T(8,128)(2,1)S(1)}, u32[]{:S(2)}, u32[]{:S(2)}) collective-permute-start(bf16[144,640]{1,0:T(8,128)(2,1)S(1)} %slice.51), channel_id=1, source_target_pairs={{0,1},{1,0},{2,3},{3,2},{4,5},{5,4},{6,7},{7,6},{8,9},{9,8},{10,11... | collective-permute-start | bytes 552968 | tf_op jit(solution)/shard_map/ppermute | solution.py:19
  29.9 8.0 %collective-permute-start.3 = (bf16[144,640]{1,0:T(8,128)(2,1)S(1)}, bf16[144,640]{1,0:T(8,128)(2,1)S(1)}, u32[]{:S(2)}, u32[]{:S(2)}) collective-permute-start(bf16[144,640]{1,0:T(8,128)(2,1)S(1)} %slice.52), channel_id=1, source_target_pairs={{0,16},{16,0},{1,17},{17,1},{2,18},{18,2},{3,19},{19,3},{4,20},{20... | collective-permute-start | bytes 552968 | tf_op jit(solution)/shard_map/ppermute | solution.py:19
  30.5 9.3 %collective-permute-start.4 = (bf16[288,640]{1,0:T(8,128)(2,1)S(1)}, bf16[288,640]{1,0:T(8,128)(2,1)S(1)}, u32[]{:S(2)}, u32[]{:S(2)}) collective-permute-start(bf16[288,640]{1,0:T(8,128)(2,1)S(1)} %bitcast.34), channel_id=1, source_target_pairs={{0,2},{2,0},{4,6},{6,4},{8,10},{10,8},{12,14},{14,12},{1,3},{3,1},... | collective-permute-start | bytes 1105928 | tf_op jit(solution)/shard_map/ppermute | solution.py:19
  30.5 9.3 %collective-permute-start.5 = (bf16[288,640]{1,0:T(8,128)(2,1)S(1)}, bf16[288,640]{1,0:T(8,128)(2,1)S(1)}, u32[]{:S(2)}, u32[]{:S(2)}) collective-permute-start(bf16[288,640]{1,0:T(8,128)(2,1)S(1)} %collective-permute-done.1.refs_1_), channel_id=1, source_target_pairs={{0,2},{2,0},{4,6},{6,4},{8,10},{10,8},{12,14},{14,12},{1,3},{3,1},... | collective-permute-start | bytes 1105928 | tf_op jit(solution)/shard_map/ppermute | solution.py:19
  31.0 8.8 %collective-permute-start.6 = (bf16[288,640]{1,0:T(8,128)(2,1)S(1)}, bf16[288,640]{1,0:T(8,128)(2,1)}, u32[]{:S(2)}, u32[]{:S(2)}) collective-permute-start(bf16[288,640]{1,0:T(8,128)(2,1)S(1)} %collective-permute-done.refs_2_), channel_id=1, source_target_pairs={{0,2},{2,0},{4,6},{6,4},{8,10},{10,8},{12,14},{14,12},{1,3},{3,1},... | collective-permute-start | bytes 1105928 | tf_op jit(solution)/shard_map/ppermute | solution.py:19
  50.5 18.5 %all-to-all-start.2 = ((bf16[8,36,640]{2,1,0:T(8,128)(2,1)}), bf16[8,36,640]{2,1,0:T(8,128)(2,1)S(1)}, u32[]{:S(2)}, u32[]{:S(2)}) async-start(bf16[8,36,640]{2,1,0:T(8,128)(2,1)} %reshape_squeeze.7), calls=%async_computation.2 | async-start | bytes 819200 | tf_op jit(solution)/shard_map/all_to_all | solution.py:404
  56.1 12.6 %collective-permute-start.8 = (bf16[8,40,640]{2,1,0:T(8,128)(2,1)S(1)}, bf16[8,40,640]{2,1,0:T(8,128)(2,1)S(1)}, u32[]{:S(2)}, u32[]{:S(2)}) collective-permute-start(bf16[8,40,640]{2,1,0:T(8,128)(2,1)S(1)} %all-to-all-done.refs_0_), channel_id=1, source_target_pairs={{0,1},{1,0},{2,3},{3,2},{4,5},{5,4},{6,7},{7,6},{8,9},{9,8},{10,11... | collective-permute-start | bytes 1228808 | tf_op jit(solution)/shard_map/ppermute | solution.py:19
  56.7 12.0 %collective-permute-start.9 = (bf16[8,40,640]{2,1,0:T(8,128)(2,1)S(1)}, bf16[8,40,640]{2,1,0:T(8,128)(2,1)S(1)}, u32[]{:S(2)}, u32[]{:S(2)}) collective-permute-start(bf16[8,40,640]{2,1,0:T(8,128)(2,1)S(1)} %all-to-all-done.refs_0_), channel_id=1, source_target_pairs={{0,16},{16,0},{1,17},{17,1},{2,18},{18,2},{3,19},{19,3},{4,20},{20... | collective-permute-start | bytes 1228808 | tf_op jit(solution)/shard_map/ppermute | solution.py:19
  69.0 19.4 %all-to-all-start.3 = ((bf16[32,24,240]{2,1,0:T(8,128)(2,1)}), bf16[32,24,240]{2,1,0:T(8,128)(2,1)S(1)}, u32[]{:S(2)}, u32[]{:S(2)}) async-start(bf16[32,24,240]{2,1,0:T(8,128)(2,1)} %shard_map.128), calls=%async_computation.3 | async-start | bytes 786432 | tf_op jit(solution)/shard_map/all_to_all | solution.py:438
  74.9 12.0 %collective-permute-start.12 = (bf16[8,40,640]{2,1,0:T(8,128)(2,1)S(1)}, bf16[8,40,640]{2,1,0:T(8,128)(2,1)S(1)}, u32[]{:S(2)}, u32[]{:S(2)}) collective-permute-start(bf16[8,40,640]{2,1,0:T(8,128)(2,1)S(1)} %all-to-all-done.refs_0_), channel_id=1, source_target_pairs={{0,2},{2,0},{4,6},{6,4},{8,10},{10,8},{12,14},{14,12},{1,3},{3,1},... | collective-permute-start | bytes 1228808 | tf_op jit(solution)/shard_map/ppermute | solution.py:19
  75.2 11.7 %collective-permute-start.13 = (bf16[8,40,640]{2,1,0:T(8,128)(2,1)S(1)}, bf16[8,40,640]{2,1,0:T(8,128)(2,1)S(1)}, u32[]{:S(2)}, u32[]{:S(2)}) collective-permute-start(bf16[8,40,640]{2,1,0:T(8,128)(2,1)S(1)} %collective-permute-done.8.refs_1_), channel_id=1, source_target_pairs={{0,2},{2,0},{4,6},{6,4},{8,10},{10,8},{12,14},{14,12},{1,3},{3,1},... | collective-permute-start | bytes 1228808 | tf_op jit(solution)/shard_map/ppermute | solution.py:19
  75.6 9.9 %collective-permute-start.10 = (bf16[4,40,640]{2,1,0:T(8,128)(2,1)S(1)}, bf16[4,40,640]{2,1,0:T(8,128)(2,1)S(1)}, u32[]{:S(2)}, u32[]{:S(2)}) collective-permute-start(bf16[4,40,640]{2,1,0:T(8,128)(2,1)S(1)} %slice.53), channel_id=1, source_target_pairs={{0,1},{1,0},{2,3},{3,2},{4,5},{5,4},{6,7},{7,6},{8,9},{9,8},{10,11... | collective-permute-start | bytes 614408 | tf_op jit(solution)/shard_map/ppermute | solution.py:19
  77.4 9.5 %collective-permute-start.14 = (bf16[8,40,640]{2,1,0:T(8,128)(2,1)S(1)}, bf16[8,40,640]{2,1,0:T(8,128)(2,1)}, u32[]{:S(2)}, u32[]{:S(2)}) collective-permute-start(bf16[8,40,640]{2,1,0:T(8,128)(2,1)S(1)} %collective-permute-done.9.refs_2_), channel_id=1, source_target_pairs={{0,2},{2,0},{4,6},{6,4},{8,10},{10,8},{12,14},{14,12},{1,3},{3,1},... | collective-permute-start | bytes 1228808 | tf_op jit(solution)/shard_map/ppermute | solution.py:19
  77.4 9.2 %collective-permute-start.11 = (bf16[4,40,640]{2,1,0:T(8,128)(2,1)S(1)}, bf16[4,40,640]{2,1,0:T(8,128)(2,1)}, u32[]{:S(2)}, u32[]{:S(2)}) collective-permute-start(bf16[4,40,640]{2,1,0:T(8,128)(2,1)S(1)} %slice.54), channel_id=1, source_target_pairs={{0,16},{16,0},{1,17},{17,1},{2,18},{18,2},{3,19},{19,3},{4,20},{20... | collective-permute-start | bytes 614408 | tf_op jit(solution)/shard_map/ppermute | solution.py:19
  103.3 11.8 %collective-permute-start.18 = (bf16[2,4,40,640]{3,2,1,0:T(8,128)(2,1)S(1)}, bf16[2,4,40,640]{3,2,1,0:T(8,128)(2,1)S(1)}, u32[]{:S(2)}, u32[]{:S(2)}) collective-permute-start(bf16[2,4,40,640]{3,2,1,0:T(8,128)(2,1)S(1)} %slice_bitcast_fusion), channel_id=1, source_target_pairs={{0,16},{16,0},{1,17},{17,1},{2,18},{18,2},{3,19},{19,3},{4,20},{20... | collective-permute-start | bytes 1228808 | tf_op jit(solution)/shard_map/ppermute | solution.py:19
  115.3 6.6 %collective-permute-start.19 = (bf16[4,40,640]{2,1,0:T(8,128)(2,1)S(1)}, bf16[4,40,640]{2,1,0:T(8,128)(2,1)S(1)}, u32[]{:S(2)}, u32[]{:S(2)}) collective-permute-start(bf16[4,40,640]{2,1,0:T(8,128)(2,1)S(1)} %slice_bitcast_fusion.1), channel_id=1, source_target_pairs={{0,1},{1,0},{2,3},{3,2},{4,5},{5,4},{6,7},{7,6},{8,9},{9,8},{10,11... | collective-permute-start | bytes 614408 | tf_op jit(solution)/shard_map/ppermute | solution.py:19
  116.2 22.2 %all-to-all-start.4 = ((bf16[8,40,640]{2,1,0:T(8,128)(2,1)}), bf16[8,40,640]{2,1,0:T(8,128)(2,1)S(1)}, u32[]{:S(2)}, u32[]{:S(2)}) async-start(bf16[8,40,640]{2,1,0:T(8,128)(2,1)} %shard_map.132), calls=%async_computation.4 | async-start | bytes 819200 | tf_op jit(solution)/shard_map/all_to_all | solution.py:493
  121.9 16.4 %collective-permute-start.20 = (bf16[2,40,640]{2,1,0:T(8,128)(2,1)S(1)}, bf16[2,40,640]{2,1,0:T(8,128)(2,1)S(1)}, u32[]{:S(2)}, u32[]{:S(2)}) collective-permute-start(bf16[2,40,640]{2,1,0:T(8,128)(2,1)S(1)} %slice.71), channel_id=1, source_target_pairs={{0,8},{2,10},{4,12},{6,14},{8,0},{10,2},{12,4},{14,6},{1,9},{3,11}... | collective-permute-start | bytes 307208 | tf_op jit(solution)/shard_map/ppermute | solution.py:502
  143.9 4.1 %collective-permute-start.21 = (bf16[1,40,640]{2,1,0:T(8,128)(2,1)S(1)}, bf16[1,40,640]{2,1,0:T(8,128)(2,1)S(1)}, u32[]{:S(2)}, u32[]{:S(2)}) collective-permute-start(bf16[1,40,640]{2,1,0:T(8,128)(2,1)S(1)} %slice.73), channel_id=1, source_target_pairs={{0,4},{2,6},{4,0},{6,2},{8,12},{10,14},{12,8},{14,10},{1,5},{3,7},... | collective-permute-start | bytes 153608 | tf_op jit(solution)/shard_map/ppermute | solution.py:502
  148.0 4.2 %collective-permute-start.22 = (bf16[40,640]{1,0:T(8,128)(2,1)S(1)}, bf16[40,640]{1,0:T(8,128)(2,1)S(1)}, u32[]{:S(2)}, u32[]{:S(2)}) collective-permute-start(bf16[40,640]{1,0:T(8,128)(2,1)S(1)} %fusion.4), channel_id=1, source_target_pairs={{0,16},{16,0},{1,17},{17,1},{2,18},{18,2},{3,19},{19,3},{4,20},{20... | collective-permute-start | bytes 153608 | tf_op jit(solution)/shard_map/ppermute | solution.py:19
  (18 other events, 174.9 us)

commit v10 on v7

--- a/solution.py
+++ b/solution.py
@@ -76,6 +76,31 @@
     else:
         for i in range(number):
             body(i)
+
+
+def pack_kernel(place, weights, cot, out):
+    share, width = (weights.shape[0], cot.shape[1])
+    frames = out.shape[0]
+    count = cot.shape[0] // frames
+    half = share // 2
+    x = place[0]
+    chosen = [
+        jnp.where(x == 0, weights[:, pl.ds(c * width, width)], weights[:, pl.ds((2 + c) * width, width)])
+        for c in (0, 1)
+    ]
+    for f in range(frames):
+        start = (f // 2 % 2) * half
+        rows = [cot[pl.ds(f * count, count), :], chosen[f % 2][start : start + half]]
+        out[f] = jnp.concatenate(rows, axis=0)
+
+
+def merge_kernel(place, mine, theirs, out):
+    odd = place[4] % 2
+    half = mine.shape[1]
+    for owner in range(mine.shape[0]):
+        first = jnp.where(odd == 0, mine[owner], theirs[owner])
+        second = jnp.where(odd == 0, theirs[owner], mine[owner])
+        out[owner] = jnp.concatenate([first, second], axis=0)
 
 
 def taps_kernel(place, mine, theirs, out):
@@ -209,7 +234,7 @@
                 piece = [b[:, j * part : (j + 1) * part] for b in blocks]
                 start = f * padded + j * third
                 mid_s[pl.ds(start, third), :] = jnp.concatenate(piece, axis=1).astype(F32)
-            cot_s[pl.ds(f * padded, count), :] = cot_in[f].astype(F32)
+            cot_s[pl.ds(f * padded, count), :] = cot_in[f, pl.ds(0, count), :].astype(F32)
     mid = mid_s[...].astype(BF)
     cot = cot_s[...].astype(BF)
     pick = picker(width, lanes, depth, 0)
@@ -390,31 +415,36 @@
     place = jnp.stack([x, core, tile, 4 * x + 2 * core + tile, plane]).astype(jnp.int32)
     flat = source.reshape(tokens, width)
 
-    kinds = lax.dynamic_slice_in_dim(attn_weight, x * 2 * width, 2 * width, axis=1)
-    kinds = kinds.reshape(share, 2, width).transpose(1, 0, 2)
-    kinds = jnp.broadcast_to(kinds[None], (frames // 2,) + kinds.shape).reshape(frames, share, width)
-    own = lax.all_to_all(kinds, "frame", 0, 0, tiled=True)
-
+    (packed,) = call(
+        pack_kernel,
+        12,
+        [((frames, count + share // 2, width), BF)],
+        [],
+        place,
+        attn_weight,
+        cot.reshape(tokens, width),
+    )
+    packed = lax.all_to_all(packed, "frame", 0, 0, tiled=True)
+
+    half = tokens // 2
     along_x = swap(flat, "dp")
     along_y = swap(flat, "tile")
-
+    across = jnp.concatenate([swap(along_x[:half], "tile"), swap(along_y[half:], "dp")])
+    pieces = [flat, along_y, along_x, across]
+    pieces += [swap(piece, "frame") for piece in pieces]
+
+    planes = [(i, i ^ 2) for i in range(frames)]
     lines = 3 * share // 2
     mine = lax.dynamic_slice_in_dim(conv_weight, x * (width // 2), width // 2, axis=2)
     mine = mine.reshape(3, 3, share, 4, part).transpose(3, 0, 2, 1, 4)
     mine = mine.reshape(4, 2, lines, 3 * part).transpose(1, 0, 2, 3)
     mine = jnp.broadcast_to(mine[None], (frames // 4,) + mine.shape)
     mine = mine.reshape(ranks, lines, 3 * part)
-    mine, own, along_x, along_y = lax.optimization_barrier((mine, own, along_x, along_y))
+    mine, packed, pieces = lax.optimization_barrier((mine, packed, pieces))
     conv_half = lax.all_to_all(mine, square, 0, 0, tiled=True)
-
-    half = tokens // 2
-    across = jnp.concatenate([swap(along_x[:half], "tile"), swap(along_y[half:], "dp")])
-    pieces = [flat, along_y, along_x, across]
-    pieces += [swap(piece, "frame") for piece in pieces]
-    cot_blocks = cot.reshape(frames, count, width)
-    cot_blocks, conv_half, pieces = lax.optimization_barrier((cot_blocks, conv_half, pieces))
-    cot_blocks = lax.all_to_all(cot_blocks, "frame", 0, 0, tiled=True)
-    conv_other = lax.ppermute(conv_half, "frame", [(i, i ^ 2) for i in range(frames)])
+    own = packed[:, count:]
+    own_other = lax.ppermute(own, "frame", planes)
+    conv_other = lax.ppermute(conv_half, "frame", planes)
     acts, kept = call(
         functools.partial(act_kernel, cols=cols, part=part),
         20,
@@ -424,12 +454,13 @@
         norm_gain[None],
         *pieces,
     )
+    (conv_full,) = call(
+        taps_kernel, 12, [((3, ranks, share, 3 * part), BF)], [], place, conv_half, conv_other
+    )
+    conv_full = conv_full.reshape(3, width, 3 * part)
+    (own,) = call(merge_kernel, 8, [((frames, share, width), BF)], [], place, own, own_other)
     by_tile = swap(own, "tile")
     by_clip = swap(own, "dp")
-    (conv_full,) = call(
-        taps_kernel, 12, [((3, ranks, share, 3 * part), BF)], [], place, conv_half, conv_other
-    )
-    conv_full = conv_full.reshape(3, width, 3 * part)
     blocked = (2 * ranks, 2 * third, 3 * part)
     plain = (2, 2, tiles * tokens, part)
     (mid,) = call(
@@ -445,9 +476,7 @@
     if frames > 8:
         mid = mid.reshape(2, 2, tiles, frames, 3, third, part).transpose(0, 3, 2, 1, 5, 4, 6)
         mid = mid.reshape(blocked)
-    mid, cot_blocks, by_tile, by_clip = lax.optimization_barrier(
-        (mid, cot_blocks, by_tile, by_clip)
-    )
+    mid, by_tile, by_clip = lax.optimization_barrier((mid, by_tile, by_clip))
     groups = None
     if clips > 2:
         groups = [[2 * ranks * g + i for i in range(2 * ranks)] for g in range(clips // 2)]
@@ -484,7 +513,7 @@
             (full, F32), (full, F32), (double, F32), (double, F32), (full, F32),
             (narrow, F32), (narrow, F32),
         ],
-        place, mid, cot_blocks, attn_full, qgain, kgain, scale,
+        place, mid, packed, attn_full, qgain, kgain, scale,
     )
     d_qn, d_kn = call(
         functools.partial(slope_kernel, heads=heads, padded=padded),
@@ -507,13 +536,13 @@
         d_qn, d_kn, q_hat, k_hat, q_rstd, k_rstd, d_value, attn_full, qgain, kgain, scale_sums,
     )
     d_back = lax.all_to_all(d_mid, "frame", 0, 0, tiled=True)
-    shares = add(shares[0], swap(shares[1], "dp"))
+    theirs, _ = lax.optimization_barrier((swap(shares[1], "dp"), d_mid))
+    shares = add(shares[0], theirs)
     shares = add(shares[0], swap(shares[1], "tile"))
+    shares, d_back = lax.optimization_barrier((shares, d_back))
     step = frames // 4
     while step > 0:
         pairs = [(i, i ^ (2 * step)) for i in range(frames)]
-        if step == 1:
-            shares, d_back = lax.optimization_barrier((shares, d_back))
         shares = add(shares[:step], lax.ppermute(shares[step:], "frame", pairs))
         step //= 2
     shares = shares[0]

time: 161 us -> 142 us (0.88)
  waiting for transfers between devices: 70.6 us -> 52.4 us
  starting transfers between devices: 45.4 us -> 39.7 us
  local copies, waits for them, and re-layouts: 9.25 us -> 13.8 us
    ppermute x23, waiting for transfers between devices: 41.9 us -> 27.7 us  [swap(): lax.ppermute(x, axis, [(i, i ^ 1) for i in range(lax.axis_size(axis))])]
    ppermute x2, waiting for transfers between devices: 16 us -> 3.68 us  [local(): shares = add(shares[:step], lax.ppermute(shares[step:], 'frame', pairs))]
    all_to_all x1, waiting for transfers between devices: 1.85 us -> 12.5 us  [local(): conv_half = lax.all_to_all(mine, square, 0, 0, tiled=True)]
    ppermute x1 -> x2, waiting for transfers between devices: 10.1 us -> 1.09 us  [the longest x1 0.67 us: local(): conv_other = lax.ppermute(conv_half, 'frame', planes)]
    all_to_all x2 -> x1, starting transfers between devices: 10.3 us -> 4.88 us  [local(): packed = lax.all_to_all(packed, 'frame', 0, 0, tiled=True)]
    all_to_all x1, waiting for transfers between devices: 0.01 us -> 5.15 us  [local(): d_back = lax.all_to_all(d_mid, 'frame', 0, 0, tiled=True)]
    unnamed x25 -> x33, local copies, waits for them, and re-layouts: 3.03 us -> 5.94 us
    ppermute x2, starting transfers between devices: 2.98 us -> 0.14 us  [local(): shares = add(shares[:step], lax.ppermute(shares[step:], 'frame', pairs))]
  transfers between devices with their start and end apart: 31 -> 31, of which waited for: 16 -> 19; matrix products, arithmetic and copies ran while one was open for 3% -> 6% of each run, Pallas kernels for 11% -> 14%
where the time goes in v10:
time: 142 us
  waiting for transfers between devices  52.4 us (37%)
  starting transfers between devices  39.7 us (28%)
  Pallas kernels  31.6 us (22%)
  local copies, waits for them, and re-layouts  13.8 us (10%)
  other arithmetic  3.06 us (2%)
    pallas_call x9, Pallas kernels, call(): pl.pallas_call(kernel, out_shape=[jax.ShapeDtypeStruct(shape, dtype) for...  31.6 us
    ppermute x23, waiting for transfers between devices, swap(): lax.ppermute(x, axis, [(i, i ^ 1) for i in range(lax.axis_size(axis))])  27.7 us
    ppermute x23, starting transfers between devices, swap(): lax.ppermute(x, axis, [(i, i ^ 1) for i in range(lax.axis_size(axis))])  19.1 us
    all_to_all x1, waiting for transfers between devices, local(): conv_half = lax.all_to_all(mine, square, 0, 0, tiled=True)  12.5 us
    unnamed x33, local copies, waits for them, and re-layouts  5.94 us
    all_to_all x1, waiting for transfers between devices, local(): d_back = lax.all_to_all(d_mid, 'frame', 0, 0, tiled=True)  5.15 us
    all_to_all x1, starting transfers between devices, local(): packed = lax.all_to_all(packed, 'frame', 0, 0, tiled=True)  4.88 us
    all_to_all x1, starting transfers between devices, local(): d_back = lax.all_to_all(d_mid, 'frame', 0, 0, tiled=True)  4.33 us
  transfers between devices with their start and end apart: 31, of which 19 were waited for; matrix products, arithmetic and copies ran while one was open for 6% of the time, Pallas kernels for 14%

profile of v10, /device:TPU:0, one launch (start us, length us, event | category | flops | bytes accessed | tf_op | source)
XLA Modules:
  0.0 141.5 jit_solution(16157093848409904437)
XLA Ops:
  0.6 3.0 %collective-permute-start.1 = (bf16[288,640]{1,0:T(8,128)(2,1)}, bf16[288,640]{1,0:T(8,128)(2,1)S(1)}, u32[]{:S(2)}, u32[]{:S(2)}) collective-permute-start(bf16[288,640]{1,0:T(8,128)(2,1)} %bitcast.32), channel_id=1, source_target_pairs={{0,16},{16,0},{1,17},{17,1},{2,18},{18,2},{3,19},{19,3},{4,20},{20... | collective-permute-start | bytes 1105928 | tf_op jit(solution)/shard_map/ppermute | solution.py:19
  8.6 4.9 %all-to-all-start = ((bf16[8,56,640]{2,1,0:T(8,128)(2,1)}), bf16[8,56,640]{2,1,0:T(8,128)(2,1)S(1)}, u32[]{:S(2)}, u32[]{:S(2)}) async-start(bf16[8,56,640]{2,1,0:T(8,128)(2,1)} %shard_map.127), calls=%async_computation | async-start | bytes 1146880 | tf_op jit(solution)/shard_map/all_to_all | solution.py:427
  16.4 4.2 %collective-permute-done.2 = bf16[144,640]{1,0:T(8,128)(2,1)S(1)} collective-permute-done((bf16[144,640]{1,0:T(8,128)(2,1)S(1)}, bf16[144,640]{1,0:T(8,128)(2,1)S(1)}, u32[]{:S(2)}, u32[]{:S(2)}) %collective-permute-start.2) | collective-permute-done | bytes 184352 | tf_op jit(solution)/shard_map/ppermute | solution.py:19
  22.2 2.1 %copy.15 = bf16[4,3,40,3,80]{4,3,0,2,1:T(4,128)(2,1)} copy(bf16[4,3,40,3,80]{4,0,2,3,1:T(4,128)(2,1)} %bitcast.37) | data formatting | bytes 460800 | tf_op jit(solution)/shard_map/transpose | solution.py:439
  24.4 2.1 %reshape.49 = bf16[4,2,60,240]{3,0,2,1:T(4,128)(2,1)} reshape(bf16[4,3,40,3,80]{4,3,0,2,1:T(4,128)(2,1)} %copy.15) | data formatting | bytes 460800 | tf_op jit(solution)/shard_map/reshape | solution.py:440
  27.6 2.3 %all-to-all-done.cot_in = bf16[8,56,640]{2,1,0:T(8,128)(2,1)S(1)} async-done(((bf16[8,56,640]{2,1,0:T(8,128)(2,1)}), bf16[8,56,640]{2,1,0:T(8,128)(2,1)S(1)}, u32[]{:S(2)}, u32[]{:S(2)}) %all-to-all-start) | async-done | bytes 573472 | tf_op jit(solution)/shard_map/all_to_all | solution.py:427
  30.7 3.7 %all-to-all-start.1 = ((bf16[16,60,240]{2,1,0:T(8,128)(2,1)}), bf16[16,60,240]{2,1,0:T(8,128)(2,1)S(1)}, u32[]{:S(2)}, u32[]{:S(2)}) async-start(bf16[16,60,240]{2,1,0:T(8,128)(2,1)} %bitcast.36), calls=%async_computation.1 | async-start | bytes 1048576 | tf_op jit(solution)/shard_map/all_to_all | solution.py:444
  34.5 2.0 %collective-permute-start.8 = (bf16[8,20,640]{2,1,0:T(8,128)(2,1)S(1)}, bf16[8,20,640]{2,1,0:T(8,128)(2,1)S(1)}, u32[]{:S(2)}, u32[]{:S(2)}) collective-permute-start(bf16[8,20,640]{2,1,0:T(8,128)(2,1)S(1)} %slice.56.mine), channel_id=1, source_target_pairs={{0,4},{2,6},{4,0},{6,2},{8,12},{10,14},{12,8},{14,10},{1,5},{3,7},... | collective-permute-start | bytes 614408 | tf_op jit(solution)/shard_map/ppermute | solution.py:446
  36.5 12.5 %all-to-all-done.1.mine = bf16[16,60,240]{2,1,0:T(8,128)(2,1)S(1)} async-done(((bf16[16,60,240]{2,1,0:T(8,128)(2,1)}), bf16[16,60,240]{2,1,0:T(8,128)(2,1)S(1)}, u32[]{:S(2)}, u32[]{:S(2)}) %all-to-all-start.1) | async-done | bytes 460832 | tf_op jit(solution)/shard_map/all_to_all | solution.py:444
  49.0 1.8 %collective-permute-start.9 = (bf16[16,60,240]{2,1,0:T(8,128)(2,1)S(1)}, bf16[16,60,240]{2,1,0:T(8,128)(2,1)S(1)}, u32[]{:S(2)}, u32[]{:S(2)}) collective-permute-start(bf16[16,60,240]{2,1,0:T(8,128)(2,1)S(1)} %all-to-all-done.1.mine), channel_id=1, source_target_pairs={{0,4},{2,6},{4,0},{6,2},{8,12},{10,14},{12,8},{14,10},{1,5},{3,7},... | collective-permute-start | bytes 1382408 | tf_op jit(solution)/shard_map/ppermute | solution.py:447
  57.9 4.7 %shard_map.130 = (bf16[4,640,640]{2,1,0:T(8,128)(2,1)S(1)}, bf16[4,576,80]{2,1,0:T(8,128)(2,1)S(1)}) custom-call(s32[5]{0:T(128)S(1)} %stack.23.place, f32[1,640]{1,0:T(1,128)S(1)} %broadcast_in_dim.5.gain, bf16[288,640]{1,0:T(8,128)(2,1)S(1)} %bitcast.35, bf16[288,640]{1,0:T(8,128)(2,1)S(1)} %collective-permute-done.refs_1_, ...), custom_call_target="tpu_custom_call" | custom-call | tf_op jit(solution)/shard_map/pallas_call | solution.py:385
  64.0 5.1 %shard_map.131 = bf16[32,24,240]{2,1,0:T(8,128)(2,1)} custom-call(s32[5]{0:T(128)S(1)} %stack.23.place, bf16[3,640,240]{2,1,0:T(8,128)(2,1)S(1)} %bitcast.30, bf16[4,640,640]{2,1,0:T(8,128)(2,1)S(1)} %get-tuple-element.58.acts, bf16[4,576,80]{2,1,0:T(8,128)(2,1)S(1)} %get-tuple-element.59.kept), custom_call_target="tpu_custom_call" | custom-call | tf_op jit(solution)/shard_map/pallas_call | solution.py:385
  69.1 3.7 %all-to-all-start.2 = ((bf16[32,24,240]{2,1,0:T(8,128)(2,1)}), bf16[32,24,240]{2,1,0:T(8,128)(2,1)S(1)}, u32[]{:S(2)}, u32[]{:S(2)}) async-start(bf16[32,24,240]{2,1,0:T(8,128)(2,1)} %shard_map.131), calls=%async_computation.2 | async-start | bytes 786432 | tf_op jit(solution)/shard_map/all_to_all | solution.py:483
  76.9 6.6 %collective-permute-done.12.refs_3_ = bf16[4,40,640]{2,1,0:T(8,128)(2,1)S(1)} collective-permute-done((bf16[4,40,640]{2,1,0:T(8,128)(2,1)S(1)}, bf16[4,40,640]{2,1,0:T(8,128)(2,1)S(1)}, u32[]{:S(2)}, u32[]{:S(2)}) %collective-permute-start.12) | collective-permute-done | bytes 204832 | tf_op jit(solution)/shard_map/ppermute | solution.py:19
  88.1 10.6 %shard_map.133 = (bf16[2,2,4,40,640]{4,3,2,1,0:T(8,128)(2,1)S(1)}, bf16[2,2,4,40,640]{4,3,2,1,0:T(8,128)(2,1)S(1)}, f32[1,128]{1,0:T(1,128)S(1)}, f32[320,128]{1...) custom-call(s32[5]{0:T(128)S(1)} %stack.23.place, ...), custom_call_target="tpu_custom_call" | custom-call | tf_op jit(solution)/shard_map/pallas_call | solution.py:385
  98.9 1.9 %shard_map.134 = (f32[320,640]{1,0:T(8,128)S(1)}, f32[320,640]{1,0:T(8,128)S(1)}) custom-call(f32[320,128]{1,0:T(8,128)S(1)} %get-tuple-element.76.d_raw, f32[320,640]{1,0:T(8,128)S(1)} %get-tuple-element.77.q_hat, f32[320,640]{1,0:T(8,128)S(1)} %get-tuple-element.78.k_hat, f32[1,640]{1,0:T(1,128)S(1)} %broadcast_in_dim_tile.9.qgain, ...), custom_call_target="tpu_custom_call" | custom-call | tf_op jit(solution)/shard_map/pallas_call | solution.py:385
  102.9 4.8 %shard_map.135 = bf16[8,40,640]{2,1,0:T(8,128)(2,1)} custom-call(f32[320,640]{1,0:T(8,128)S(1)} %get-tuple-element.81.d_qn, f32[320,640]{1,0:T(8,128)S(1)} %get-tuple-element.82.d_kn, f32[320,640]{1,0:T(8,128)S(1)} %get-tuple-element.77.q_hat, f32[320,640]{1,0:T(8,128)S(1)} %get-tuple-element.78.k_hat, f32[320,128]{1,0:T(8,128)S(1)} %get-tuple-element.83.q_rstd, ...), custom_call_target="tpu_custom_call" | custom-call | tf_op jit(solution)/shard_map/pallas_call | solution.py:385
  107.7 4.3 %all-to-all-start.3 = ((bf16[8,40,640]{2,1,0:T(8,128)(2,1)}), bf16[8,40,640]{2,1,0:T(8,128)(2,1)S(1)}, u32[]{:S(2)}, u32[]{:S(2)}) async-start(bf16[8,40,640]{2,1,0:T(8,128)(2,1)} %shard_map.135), calls=%async_computation.3 | async-start | bytes 819200 | tf_op jit(solution)/shard_map/all_to_all | solution.py:538
  114.0 5.8 %collective-permute-done.21 = bf16[4,40,640]{2,1,0:T(8,128)(2,1)S(1)} collective-permute-done((bf16[4,40,640]{2,1,0:T(8,128)(2,1)S(1)}, bf16[4,40,640]{2,1,0:T(8,128)(2,1)S(1)}, u32[]{:S(2)}, u32[]{:S(2)}) %collective-permute-start.21) | collective-permute-done | bytes 204832 | tf_op jit(solution)/shard_map/ppermute | solution.py:19
  119.8 5.2 %all-to-all-done.3 = bf16[8,40,640]{2,1,0:T(8,128)(2,1)S(1)} async-done(((bf16[8,40,640]{2,1,0:T(8,128)(2,1)}), bf16[8,40,640]{2,1,0:T(8,128)(2,1)S(1)}, u32[]{:S(2)}, u32[]{:S(2)}) %all-to-all-start.3) | async-done | bytes 409632 | tf_op jit(solution)/shard_map/all_to_all | solution.py:538
  126.1 2.6 %collective-permute-done.25 = f32[640]{0:T(1024)S(1)} collective-permute-done((f32[640]{0:T(1024)S(1)}, f32[640]{0:T(1024)S(1)}, u32[]{:S(2)}, u32[]{:S(2)}) %collective-permute-start.25) | collective-permute-done | bytes 2592 | tf_op jit(solution)/shard_map/ppermute | solution.py:19
  130.3 2.0 %collective-permute-done.26 = f32[640]{0:T(1024)S(1)} collective-permute-done((f32[640]{0:T(1024)S(1)}, f32[640]{0:T(1024)S(1)}, u32[]{:S(2)}, u32[]{:S(2)}) %collective-permute-start.26) | collective-permute-done | bytes 2592 | tf_op jit(solution)/shard_map/ppermute | solution.py:19
  133.1 3.6 %collective-permute-done.23 = bf16[1,40,640]{2,1,0:T(8,128)(2,1)S(1)} collective-permute-done((bf16[1,40,640]{2,1,0:T(8,128)(2,1)S(1)}, bf16[1,40,640]{2,1,0:T(8,128)(2,1)S(1)}, u32[]{:S(2)}, u32[]{:S(2)}) %collective-permute-start.23) | collective-permute-done | bytes 51232 | tf_op jit(solution)/shard_map/ppermute | solution.py:546
  138.4 2.5 %collective-permute-done.24 = bf16[40,640]{1,0:T(8,128)(2,1)S(1)} collective-permute-done((bf16[40,640]{1,0:T(8,128)(2,1)S(1)}, bf16[40,640]{1,0:T(8,128)(2,1)S(1)}, u32[]{:S(2)}, u32[]{:S(2)}) %collective-permute-start.24) | collective-permute-done | bytes 51232 | tf_op jit(solution)/shard_map/ppermute | solution.py:19
  (119 shorter events, 38.4 us)
Async XLA Ops:
  0.6 12.8 %collective-permute-start.1 = (bf16[288,640]{1,0:T(8,128)(2,1)}, bf16[288,640]{1,0:T(8,128)(2,1)S(1)}, u32[]{:S(2)}, u32[]{:S(2)}) collective-permute-start(bf16[288,640]{1,0:T(8,128)(2,1)} %bitcast.32), channel_id=1, source_target_pairs={{0,16},{16,0},{1,17},{17,1},{2,18},{18,2},{3,19},{19,3},{4,20},{20... | collective-permute-start | bytes 1105928 | tf_op jit(solution)/shard_map/ppermute | solution.py:19
  3.7 10.7 %collective-permute-start = (bf16[288,640]{1,0:T(8,128)(2,1)}, bf16[288,640]{1,0:T(8,128)(2,1)S(1)}, u32[]{:S(2)}, u32[]{:S(2)}) collective-permute-start(bf16[288,640]{1,0:T(8,128)(2,1)} %bitcast.33), channel_id=1, source_target_pairs={{0,1},{1,0},{2,3},{3,2},{4,5},{5,4},{6,7},{7,6},{8,9},{9,8},{10,11... | collective-permute-start | bytes 1105928 | tf_op jit(solution)/shard_map/ppermute | solution.py:19
  8.6 21.3 %all-to-all-start = ((bf16[8,56,640]{2,1,0:T(8,128)(2,1)}), bf16[8,56,640]{2,1,0:T(8,128)(2,1)S(1)}, u32[]{:S(2)}, u32[]{:S(2)}) async-start(bf16[8,56,640]{2,1,0:T(8,128)(2,1)} %shard_map.127), calls=%async_computation | async-start | bytes 1146880 | tf_op jit(solution)/shard_map/all_to_all | solution.py:427
  13.5 7.1 %collective-permute-start.2 = (bf16[144,640]{1,0:T(8,128)(2,1)S(1)}, bf16[144,640]{1,0:T(8,128)(2,1)S(1)}, u32[]{:S(2)}, u32[]{:S(2)}) collective-permute-start(bf16[144,640]{1,0:T(8,128)(2,1)S(1)} %slice.72), channel_id=1, source_target_pairs={{0,1},{1,0},{2,3},{3,2},{4,5},{5,4},{6,7},{7,6},{8,9},{9,8},{10,11... | collective-permute-start | bytes 552968 | tf_op jit(solution)/shard_map/ppermute | solution.py:19
  14.3 6.6 %collective-permute-start.3 = (bf16[144,640]{1,0:T(8,128)(2,1)S(1)}, bf16[144,640]{1,0:T(8,128)(2,1)S(1)}, u32[]{:S(2)}, u32[]{:S(2)}) collective-permute-start(bf16[144,640]{1,0:T(8,128)(2,1)S(1)} %slice.73), channel_id=1, source_target_pairs={{0,16},{16,0},{1,17},{17,1},{2,18},{18,2},{3,19},{19,3},{4,20},{20... | collective-permute-start | bytes 552968 | tf_op jit(solution)/shard_map/ppermute | solution.py:19
  15.9 11.6 %collective-permute-start.4 = (bf16[288,640]{1,0:T(8,128)(2,1)S(1)}, bf16[288,640]{1,0:T(8,128)(2,1)S(1)}, u32[]{:S(2)}, u32[]{:S(2)}) collective-permute-start(bf16[288,640]{1,0:T(8,128)(2,1)S(1)} %bitcast.34), channel_id=1, source_target_pairs={{0,2},{2,0},{4,6},{6,4},{8,10},{10,8},{12,14},{14,12},{1,3},{3,1},... | collective-permute-start | bytes 1105928 | tf_op jit(solution)/shard_map/ppermute | solution.py:19
  15.9 11.6 %collective-permute-start.5 = (bf16[288,640]{1,0:T(8,128)(2,1)S(1)}, bf16[288,640]{1,0:T(8,128)(2,1)S(1)}, u32[]{:S(2)}, u32[]{:S(2)}) collective-permute-start(bf16[288,640]{1,0:T(8,128)(2,1)S(1)} %collective-permute-done.refs_1_), channel_id=1, source_target_pairs={{0,2},{2,0},{4,6},{6,4},{8,10},{10,8},{12,14},{14,12},{1,3},{3,1},... | collective-permute-start | bytes 1105928 | tf_op jit(solution)/shard_map/ppermute | solution.py:19
  16.4 11.1 %collective-permute-start.6 = (bf16[288,640]{1,0:T(8,128)(2,1)S(1)}, bf16[288,640]{1,0:T(8,128)(2,1)}, u32[]{:S(2)}, u32[]{:S(2)}) collective-permute-start(bf16[288,640]{1,0:T(8,128)(2,1)S(1)} %collective-permute-done.1.refs_2_), channel_id=1, source_target_pairs={{0,2},{2,0},{4,6},{6,4},{8,10},{10,8},{12,14},{14,12},{1,3},{3,1},... | collective-permute-start | bytes 1105928 | tf_op jit(solution)/shard_map/ppermute | solution.py:19
  21.0 6.6 %collective-permute-start.7 = (bf16[288,640]{1,0:T(8,128)(2,1)S(1)}, bf16[288,640]{1,0:T(8,128)(2,1)}, u32[]{:S(2)}, u32[]{:S(2)}) collective-permute-start(bf16[288,640]{1,0:T(8,128)(2,1)S(1)} %constant_dynamic-update-slice_fusion.refs_3_), channel_id=1, source_target_pairs={{0,2},{2,0},{4,6},{6,4},{8,10},{10,8},{12,14},{14,12},{1,3},{3,1},... | collective-permute-start | bytes 1105928 | tf_op jit(solution)/shard_map/ppermute | solution.py:19
  30.7 18.3 %all-to-all-start.1 = ((bf16[16,60,240]{2,1,0:T(8,128)(2,1)}), bf16[16,60,240]{2,1,0:T(8,128)(2,1)S(1)}, u32[]{:S(2)}, u32[]{:S(2)}) async-start(bf16[16,60,240]{2,1,0:T(8,128)(2,1)} %bitcast.36), calls=%async_computation.1 | async-start | bytes 1048576 | tf_op jit(solution)/shard_map/all_to_all | solution.py:444
  34.5 16.8 %collective-permute-start.8 = (bf16[8,20,640]{2,1,0:T(8,128)(2,1)S(1)}, bf16[8,20,640]{2,1,0:T(8,128)(2,1)S(1)}, u32[]{:S(2)}, u32[]{:S(2)}) collective-permute-start(bf16[8,20,640]{2,1,0:T(8,128)(2,1)S(1)} %slice.56.mine), channel_id=1, source_target_pairs={{0,4},{2,6},{4,0},{6,2},{8,12},{10,14},{12,8},{14,10},{1,5},{3,7},... | collective-permute-start | bytes 614408 | tf_op jit(solution)/shard_map/ppermute | solution.py:446
  49.0 14.4 %collective-permute-start.9 = (bf16[16,60,240]{2,1,0:T(8,128)(2,1)S(1)}, bf16[16,60,240]{2,1,0:T(8,128)(2,1)S(1)}, u32[]{:S(2)}, u32[]{:S(2)}) collective-permute-start(bf16[16,60,240]{2,1,0:T(8,128)(2,1)S(1)} %all-to-all-done.1.mine), channel_id=1, source_target_pairs={{0,4},{2,6},{4,0},{6,2},{8,12},{10,14},{12,8},{14,10},{1,5},{3,7},... | collective-permute-start | bytes 1382408 | tf_op jit(solution)/shard_map/ppermute | solution.py:447
  51.9 17.2 %collective-permute-start.10 = (bf16[8,40,640]{2,1,0:T(8,128)(2,1)S(1)}, bf16[8,40,640]{2,1,0:T(8,128)(2,1)S(1)}, u32[]{:S(2)}, u32[]{:S(2)}) collective-permute-start(bf16[8,40,640]{2,1,0:T(8,128)(2,1)S(1)} %shard_map.128.refs_0_), channel_id=1, source_target_pairs={{0,1},{1,0},{2,3},{3,2},{4,5},{5,4},{6,7},{7,6},{8,9},{9,8},{10,11... | collective-permute-start | bytes 1228808 | tf_op jit(solution)/shard_map/ppermute | solution.py:19
  53.4 15.7 %collective-permute-start.11 = (bf16[8,40,640]{2,1,0:T(8,128)(2,1)S(1)}, bf16[8,40,640]{2,1,0:T(8,128)(2,1)S(1)}, u32[]{:S(2)}, u32[]{:S(2)}) collective-permute-start(bf16[8,40,640]{2,1,0:T(8,128)(2,1)S(1)} %shard_map.128.refs_0_), channel_id=1, source_target_pairs={{0,16},{16,0},{1,17},{17,1},{2,18},{18,2},{3,19},{19,3},{4,20},{20... | collective-permute-start | bytes 1228808 | tf_op jit(solution)/shard_map/ppermute | solution.py:19
  69.1 17.3 %all-to-all-start.2 = ((bf16[32,24,240]{2,1,0:T(8,128)(2,1)}), bf16[32,24,240]{2,1,0:T(8,128)(2,1)S(1)}, u32[]{:S(2)}, u32[]{:S(2)}) async-start(bf16[32,24,240]{2,1,0:T(8,128)(2,1)} %shard_map.131), calls=%async_computation.2 | async-start | bytes 786432 | tf_op jit(solution)/shard_map/all_to_all | solution.py:483
  72.9 12.0 %collective-permute-start.14 = (bf16[8,40,640]{2,1,0:T(8,128)(2,1)S(1)}, bf16[8,40,640]{2,1,0:T(8,128)(2,1)S(1)}, u32[]{:S(2)}, u32[]{:S(2)}) collective-permute-start(bf16[8,40,640]{2,1,0:T(8,128)(2,1)S(1)} %shard_map.128.refs_0_), channel_id=1, source_target_pairs={{0,2},{2,0},{4,6},{6,4},{8,10},{10,8},{12,14},{14,12},{1,3},{3,1},... | collective-permute-start | bytes 1228808 | tf_op jit(solution)/shard_map/ppermute | solution.py:19
  73.2 11.7 %collective-permute-start.15 = (bf16[8,40,640]{2,1,0:T(8,128)(2,1)S(1)}, bf16[8,40,640]{2,1,0:T(8,128)(2,1)}, u32[]{:S(2)}, u32[]{:S(2)}) collective-permute-start(bf16[8,40,640]{2,1,0:T(8,128)(2,1)S(1)} %collective-permute-done.10.refs_1_), channel_id=1, source_target_pairs={{0,2},{2,0},{4,6},{6,4},{8,10},{10,8},{12,14},{14,12},{1,3},{3,1},... | collective-permute-start | bytes 1228808 | tf_op jit(solution)/shard_map/ppermute | solution.py:19
  73.6 9.9 %collective-permute-start.12 = (bf16[4,40,640]{2,1,0:T(8,128)(2,1)S(1)}, bf16[4,40,640]{2,1,0:T(8,128)(2,1)S(1)}, u32[]{:S(2)}, u32[]{:S(2)}) collective-permute-start(bf16[4,40,640]{2,1,0:T(8,128)(2,1)S(1)} %slice.57), channel_id=1, source_target_pairs={{0,1},{1,0},{2,3},{3,2},{4,5},{5,4},{6,7},{7,6},{8,9},{9,8},{10,11... | collective-permute-start | bytes 614408 | tf_op jit(solution)/shard_map/ppermute | solution.py:19
  75.4 9.5 %collective-permute-start.16 = (bf16[8,40,640]{2,1,0:T(8,128)(2,1)S(1)}, bf16[8,40,640]{2,1,0:T(8,128)(2,1)}, u32[]{:S(2)}, u32[]{:S(2)}) collective-permute-start(bf16[8,40,640]{2,1,0:T(8,128)(2,1)S(1)} %collective-permute-done.11.refs_2_), channel_id=1, source_target_pairs={{0,2},{2,0},{4,6},{6,4},{8,10},{10,8},{12,14},{14,12},{1,3},{3,1},... | collective-permute-start | bytes 1228808 | tf_op jit(solution)/shard_map/ppermute | solution.py:19
  75.4 9.2 %collective-permute-start.13 = (bf16[4,40,640]{2,1,0:T(8,128)(2,1)S(1)}, bf16[4,40,640]{2,1,0:T(8,128)(2,1)}, u32[]{:S(2)}, u32[]{:S(2)}) collective-permute-start(bf16[4,40,640]{2,1,0:T(8,128)(2,1)S(1)} %slice.58), channel_id=1, source_target_pairs={{0,16},{16,0},{1,17},{17,1},{2,18},{18,2},{3,19},{19,3},{4,20},{20... | collective-permute-start | bytes 614408 | tf_op jit(solution)/shard_map/ppermute | solution.py:19
  101.3 11.6 %collective-permute-start.20 = (bf16[2,4,40,640]{3,2,1,0:T(8,128)(2,1)S(1)}, bf16[2,4,40,640]{3,2,1,0:T(8,128)(2,1)S(1)}, u32[]{:S(2)}, u32[]{:S(2)}) collective-permute-start(bf16[2,4,40,640]{3,2,1,0:T(8,128)(2,1)S(1)} %slice_bitcast_fusion), channel_id=1, source_target_pairs={{0,16},{16,0},{1,17},{17,1},{2,18},{18,2},{3,19},{19,3},{4,20},{20... | collective-permute-start | bytes 1228808 | tf_op jit(solution)/shard_map/ppermute | solution.py:19
  107.7 17.2 %all-to-all-start.3 = ((bf16[8,40,640]{2,1,0:T(8,128)(2,1)}), bf16[8,40,640]{2,1,0:T(8,128)(2,1)S(1)}, u32[]{:S(2)}, u32[]{:S(2)}) async-start(bf16[8,40,640]{2,1,0:T(8,128)(2,1)} %shard_map.135), calls=%async_computation.3 | async-start | bytes 819200 | tf_op jit(solution)/shard_map/all_to_all | solution.py:538
  113.1 6.7 %collective-permute-start.21 = (bf16[4,40,640]{2,1,0:T(8,128)(2,1)S(1)}, bf16[4,40,640]{2,1,0:T(8,128)(2,1)S(1)}, u32[]{:S(2)}, u32[]{:S(2)}) collective-permute-start(bf16[4,40,640]{2,1,0:T(8,128)(2,1)S(1)} %slice_bitcast_fusion.1), channel_id=1, source_target_pairs={{0,1},{1,0},{2,3},{3,2},{4,5},{5,4},{6,7},{7,6},{8,9},{9,8},{10,11... | collective-permute-start | bytes 614408 | tf_op jit(solution)/shard_map/ppermute | solution.py:19
  126.1 6.4 %collective-permute-start.22 = (bf16[2,40,640]{2,1,0:T(8,128)(2,1)S(1)}, bf16[2,40,640]{2,1,0:T(8,128)(2,1)S(1)}, u32[]{:S(2)}, u32[]{:S(2)}) collective-permute-start(bf16[2,40,640]{2,1,0:T(8,128)(2,1)S(1)} %slice.65), channel_id=1, source_target_pairs={{0,8},{2,10},{4,12},{6,14},{8,0},{10,2},{12,4},{14,6},{1,9},{3,11}... | collective-permute-start | bytes 307208 | tf_op jit(solution)/shard_map/ppermute | solution.py:546
  (23 other events, 162.5 us)

commit v11 on v10

--- a/solution.py
+++ b/solution.py
@@ -17,6 +17,16 @@
 
 def swap(x, axis):
     return lax.ppermute(x, axis, [(i, i ^ 1) for i in range(lax.axis_size(axis))])
+
+
+def swap_both(x, axis, bit):
+    sizes = (lax.axis_size("dp"), lax.axis_size(axis))
+    pairs = [
+        (i * sizes[1] + j, (i ^ 1) * sizes[1] + (j ^ bit))
+        for i in range(sizes[0])
+        for j in range(sizes[1])
+    ]
+    return lax.ppermute(x, ("dp", axis), pairs)
 
 
 def round_up(value, unit):
@@ -101,17 +111,6 @@
         first = jnp.where(odd == 0, mine[owner], theirs[owner])
         second = jnp.where(odd == 0, theirs[owner], mine[owner])
         out[owner] = jnp.concatenate([first, second], axis=0)
-
-
-def taps_kernel(place, mine, theirs, out):
-    odd = place[4] % 2
-    share = out.shape[2]
-    for owner in range(mine.shape[0]):
-        first = jnp.where(odd == 0, mine[owner], theirs[owner])
-        second = jnp.where(odd == 0, theirs[owner], mine[owner])
-        block = jnp.concatenate([first, second], axis=0)
-        for row in range(3):
-            out[row, owner] = block[row * share : (row + 1) * share]
 
 
 def join_kernel(place, *refs):
@@ -424,6 +423,7 @@
         attn_weight,
         cot.reshape(tokens, width),
     )
+    flat, packed = lax.optimization_barrier((flat, packed))
     packed = lax.all_to_all(packed, "frame", 0, 0, tiled=True)
 
     half = tokens // 2
@@ -433,18 +433,15 @@
     pieces = [flat, along_y, along_x, across]
     pieces += [swap(piece, "frame") for piece in pieces]
 
-    planes = [(i, i ^ 2) for i in range(frames)]
-    lines = 3 * share // 2
     mine = lax.dynamic_slice_in_dim(conv_weight, x * (width // 2), width // 2, axis=2)
     mine = mine.reshape(3, 3, share, 4, part).transpose(3, 0, 2, 1, 4)
-    mine = mine.reshape(4, 2, lines, 3 * part).transpose(1, 0, 2, 3)
-    mine = jnp.broadcast_to(mine[None], (frames // 4,) + mine.shape)
-    mine = mine.reshape(ranks, lines, 3 * part)
+    mine = mine.reshape(4, 3, share, 3 * part)
+    mine = jnp.broadcast_to(mine[None], (frames // 2,) + mine.shape)
+    mine = mine.reshape((ranks,) + mine.shape[2:])
     mine, packed, pieces = lax.optimization_barrier((mine, packed, pieces))
-    conv_half = lax.all_to_all(mine, square, 0, 0, tiled=True)
+    conv_in = lax.all_to_all(mine, square, 0, 0, tiled=True)
     own = packed[:, count:]
-    own_other = lax.ppermute(own, "frame", planes)
-    conv_other = lax.ppermute(conv_half, "frame", planes)
+    own_other = lax.ppermute(own, "frame", [(i, i ^ 2) for i in range(frames)])
     acts, kept = call(
         functools.partial(act_kernel, cols=cols, part=part),
         20,
@@ -454,10 +451,8 @@
         norm_gain[None],
         *pieces,
     )
-    (conv_full,) = call(
-        taps_kernel, 12, [((3, ranks, share, 3 * part), BF)], [], place, conv_half, conv_other
-    )
-    conv_full = conv_full.reshape(3, width, 3 * part)
+    conv_in, acts, kept = lax.optimization_barrier((conv_in, acts, kept))
+    conv_full = conv_in.transpose(1, 0, 2, 3).reshape(3, width, 3 * part)
     (own,) = call(merge_kernel, 8, [((frames, share, width), BF)], [], place, own, own_other)
     by_tile = swap(own, "tile")
     by_clip = swap(own, "dp")
@@ -541,24 +536,26 @@
     shares = add(shares[0], swap(shares[1], "tile"))
     shares, d_back = lax.optimization_barrier((shares, d_back))
     step = frames // 4
-    while step > 0:
+    while step > 1:
         pairs = [(i, i ^ (2 * step)) for i in range(frames)]
         shares = add(shares[:step], lax.ppermute(shares[step:], "frame", pairs))
         step //= 2
-    shares = shares[0]
+    by_plane = lax.ppermute(shares[1], "frame", [(i, i ^ 2) for i in range(frames)])
+    by_clip = swap(shares[0], "dp")
+    by_both = swap_both(shares[1], "frame", 2)
+    shares = shares[0].astype(F32) + by_plane.astype(F32)
+    theirs = by_clip.astype(F32) + by_both.astype(F32)
     small = jnp.sum(d_back[:, count : count + 3].astype(F32), axis=(0, 1))
     d_back = d_back[:, :count].reshape(rows, cols, width)
     mid_grad = (cot.astype(F32) + d_back.astype(F32)).astype(BF)
 
-    small = small + swap(small, "tile")
-    if clips == 2:
-        small = small + swap(small, "dp")
-    else:
-        small = lax.psum(small, "dp")
+    by_tile = swap(small, "tile")
+    small = (small + by_tile) + (swap(small, "dp") + swap_both(small, "tile", 1))
+    if clips > 2:
         same_clip = [[i for i in range(clips) if i % 2 == c] for c in (0, 1)]
-        shares = lax.psum(shares, "dp", axis_index_groups=same_clip)
-    theirs = swap(shares, "dp").astype(F32)
-    shares = shares.astype(F32)
+        small, shares, theirs = lax.psum(
+            (small, shares, theirs), "dp", axis_index_groups=same_clip
+        )
     factor = 1.0 / math.sqrt(clips * frames * tiles * tokens)
     value_grad = jnp.where(x == 0, shares, theirs) * factor
     out_proj_grad = jnp.where(x == 0, theirs, shares) * factor

time: 142 us -> 158 us (1.11)
  starting transfers between devices: 39.7 us -> 45.4 us
  local copies, waits for them, and re-layouts: 13.8 us -> 19.4 us
  waiting for transfers between devices: 52.4 us -> 56.5 us
    ppermute x2 -> x4, waiting for transfers between devices: 1.09 us -> 23.8 us  [the longest x1 22.1 us: local(): own_other = lax.ppermute(own, 'frame', [(i, i ^ 2) for i in range(frames)])]
    all_to_all x1, waiting for transfers between devices: 12.5 us -> 0.01 us  [local(): conv_in = lax.all_to_all(mine, square, 0, 0, tiled=True)]
    ppermute x23, waiting for transfers between devices: 27.7 us -> 23.6 us  [swap(): lax.ppermute(x, axis, [(i, i ^ 1) for i in range(lax.axis_size(axis))])]
    broadcast_in_dim x1 -> x2, local copies, waits for them, and re-layouts: 0.84 us -> 4.21 us  [local(): mine = jnp.broadcast_to(mine[None], (frames // 2,) + mine.shape)]
    unnamed x33 -> x37, local copies, waits for them, and re-layouts: 5.94 us -> 8.41 us
    all_to_all x1, waiting for transfers between devices: 2.33 us -> 0.01 us  [local(): packed = lax.all_to_all(packed, 'frame', 0, 0, tiled=True)]
    reshape x1 -> x0, local copies, waits for them, and re-layouts: 2.13 us -> none  [local(): mine = mine.reshape(4, 2, lines, 3 * part).transpose(1, 0, 2, 3)]
    all_to_all x1, starting transfers between devices: 3.69 us -> 5.8 us  [local(): conv_in = lax.all_to_all(mine, square, 0, 0, tiled=True)]
  transfers between devices with their start and end apart: 31 -> 32, of which waited for: 19 -> 17; matrix products, arithmetic and copies ran while one was open for 6% -> 7% of each run, Pallas kernels for 14% -> 11%
where the time goes in v11:
time: 158 us; the launch traced here: 157 us
  waiting for transfers between devices  56.5 us (36%)
  starting transfers between devices  45.4 us (29%)
  Pallas kernels  31.3 us (20%)
  local copies, waits for them, and re-layouts  19.4 us (12%)
  other arithmetic  3.08 us (2%)
    pallas_call x8, Pallas kernels, call(): pl.pallas_call(kernel, out_shape=[jax.ShapeDtypeStruct(shape, dtype) for...  31.3 us
    ppermute x23, waiting for transfers between devices, swap(): lax.ppermute(x, axis, [(i, i ^ 1) for i in range(lax.axis_size(axis))])  23.6 us
    ppermute x1, waiting for transfers between devices, local(): own_other = lax.ppermute(own, 'frame', [(i, i ^ 2) for i in range(frames)])  22.1 us
    ppermute x23, starting transfers between devices, swap(): lax.ppermute(x, axis, [(i, i ^ 1) for i in range(lax.axis_size(axis))])  20.9 us
    unnamed x37, local copies, waits for them, and re-layouts  8.41 us
    all_to_all x1, starting transfers between devices, local(): conv_in = lax.all_to_all(mine, square, 0, 0, tiled=True)  5.8 us
    all_to_all x1, waiting for transfers between devices, local(): d_back = lax.all_to_all(d_mid, 'frame', 0, 0, tiled=True)  5.16 us
    all_to_all x1, starting transfers between devices, local(): packed = lax.all_to_all(packed, 'frame', 0, 0, tiled=True)  4.88 us
  transfers between devices with their start and end apart: 32, of which 17 were waited for; matrix products, arithmetic and copies ran while one was open for 7% of the time, Pallas kernels for 11%

profile of v11, /device:TPU:0, one launch (start us, length us, event | category | flops | bytes accessed | tf_op | source)
XLA Modules:
  0.0 156.7 jit_solution(86402317654473979)
XLA Ops:
  4.2 2.9 %collective-permute-start.1 = (bf16[288,640]{1,0:T(8,128)(2,1)}, bf16[288,640]{1,0:T(8,128)(2,1)S(1)}, u32[]{:S(2)}, u32[]{:S(2)}) collective-permute-start(bf16[288,640]{1,0:T(8,128)(2,1)} %bitcast.36), channel_id=1, source_target_pairs={{0,16},{16,0},{1,17},{17,1},{2,18},{18,2},{3,19},{19,3},{4,20},{20... | collective-permute-start | bytes 1105928 | tf_op jit(solution)/shard_map/ppermute | solution.py:19
  8.6 4.9 %all-to-all-start = ((bf16[8,56,640]{2,1,0:T(8,128)(2,1)}), bf16[8,56,640]{2,1,0:T(8,128)(2,1)S(1)}, u32[]{:S(2)}, u32[]{:S(2)}) async-start(bf16[8,56,640]{2,1,0:T(8,128)(2,1)} %shard_map.127), calls=%async_computation | async-start | bytes 1146880 | tf_op jit(solution)/shard_map/all_to_all | solution.py:427
  13.5 2.4 %collective-permute-done.1.refs_2_ = bf16[288,640]{1,0:T(8,128)(2,1)S(1)} collective-permute-done((bf16[288,640]{1,0:T(8,128)(2,1)}, bf16[288,640]{1,0:T(8,128)(2,1)S(1)}, u32[]{:S(2)}, u32[]{:S(2)}) %collective-permute-start.1) | collective-permute-done | bytes 368672 | tf_op jit(solution)/shard_map/ppermute | solution.py:19
  19.8 2.0 %collective-permute-done.2 = bf16[144,640]{1,0:T(8,128)(2,1)S(1)} collective-permute-done((bf16[144,640]{1,0:T(8,128)(2,1)S(1)}, bf16[144,640]{1,0:T(8,128)(2,1)S(1)}, u32[]{:S(2)}, u32[]{:S(2)}) %collective-permute-start.2) | collective-permute-done | bytes 184352 | tf_op jit(solution)/shard_map/ppermute | solution.py:19
  24.4 1.9 %reshape.45 = bf16[3,3,40,4,80]{4,3,2,1,0:T(4,128)(2,1)} reshape(bf16[9,40,320]{2,1,0:T(8,128)(2,1)} %constant_dynamic-slice_fusion) | data formatting | bytes 460800 | tf_op jit(solution)/shard_map/reshape | solution.py:437
  26.3 2.0 %copy.17 = bf16[4,3,40,3,80]{4,3,2,1,0:T(4,128)(2,1)} copy(bf16[4,3,40,3,80]{4,0,2,3,1:T(4,128)(2,1)} %bitcast.41) | data formatting | bytes 460800 | tf_op jit(solution)/shard_map/transpose | solution.py:437
  28.3 2.0 %broadcast_in_dim.11 = bf16[4,3,40,240]{3,2,1,0:T(8,128)(2,1)} reshape(bf16[4,3,40,3,80]{4,3,2,1,0:T(4,128)(2,1)} %copy.17) | data formatting | bytes 460800 | tf_op jit(solution)/shard_map/broadcast_in_dim | solution.py:439
  30.4 2.2 %broadcast_in_dim.12 = bf16[4,4,3,40,240]{4,3,2,1,0:T(8,128)(2,1)} broadcast(bf16[4,3,40,240]{3,2,1,0:T(8,128)(2,1)} %broadcast_in_dim.11), dimensions={1,2,3,4} | broadcast | bytes 1152000 | tf_op jit(solution)/shard_map/broadcast_in_dim | solution.py:439
  32.6 5.8 %all-to-all-start.1 = ((bf16[16,3,40,240]{3,2,1,0:T(8,128)(2,1)}), bf16[16,3,40,240]{3,2,1,0:T(8,128)(2,1)}, u32[]{:S(2)}, u32[]{:S(2)}) async-start(bf16[16,3,40,240]{3,2,1,0:T(8,128)(2,1)} %bitcast.40), calls=%async_computation.1 | async-start | bytes 1966080 | tf_op jit(solution)/shard_map/all_to_all | solution.py:442
  38.5 1.9 %collective-permute-start.8 = (bf16[8,20,640]{2,1,0:T(8,128)(2,1)S(1)}, bf16[8,20,640]{2,1,0:T(8,128)(2,1)S(1)}, u32[]{:S(2)}, u32[]{:S(2)}) collective-permute-start(bf16[8,20,640]{2,1,0:T(8,128)(2,1)S(1)} %slice.58.mine), channel_id=1, source_target_pairs={{0,4},{2,6},{4,0},{6,2},{8,12},{10,14},{12,8},{14,10},{1,5},{3,7},... | collective-permute-start | bytes 614408 | tf_op jit(solution)/shard_map/ppermute | solution.py:444
  40.4 22.1 %collective-permute-done.8.theirs = bf16[8,20,640]{2,1,0:T(8,128)(2,1)S(1)} collective-permute-done((bf16[8,20,640]{2,1,0:T(8,128)(2,1)S(1)}, bf16[8,20,640]{2,1,0:T(8,128)(2,1)S(1)}, u32[]{:S(2)}, u32[]{:S(2)}) %collective-permute-start.8) | collective-permute-done | bytes 204832 | tf_op jit(solution)/shard_map/ppermute | solution.py:444
  67.6 4.8 %shard_map.129 = (bf16[4,640,640]{2,1,0:T(8,128)(2,1)S(1)}, bf16[4,576,80]{2,1,0:T(8,128)(2,1)S(1)}) custom-call(s32[5]{0:T(128)S(1)} %stack.23.place, f32[1,640]{1,0:T(1,128)S(1)} %broadcast_in_dim.13.gain, bf16[288,640]{1,0:T(8,128)(2,1)S(1)} %bitcast.39, bf16[288,640]{1,0:T(8,128)(2,1)S(1)} %collective-permute-done.refs_1_, ...), custom_call_target="tpu_custom_call" | custom-call | tf_op jit(solution)/shard_map/pallas_call | solution.py:384
  76.3 1.9 %copy-done.2 = bf16[4,640,640]{2,1,0:T(8,128)(2,1)S(1)} copy-done((bf16[4,640,640]{2,1,0:T(8,128)(2,1)S(1)}, bf16[4,640,640]{2,1,0:T(8,128)(2,1)}, u32[]{:S(2)}) %copy-start.2) | copy-done | bytes 3276824
  78.2 5.1 %shard_map.130 = bf16[32,24,240]{2,1,0:T(8,128)(2,1)} custom-call(s32[5]{0:T(128)S(1)} %stack.23.place, bf16[3,640,240]{2,1,0:T(8,128)(2,1)S(1)} %bitcast.34, bf16[4,640,640]{2,1,0:T(8,128)(2,1)S(1)} %copy-done.2, bf16[4,576,80]{2,1,0:T(8,128)(2,1)S(1)} %copy-done.6), custom_call_target="tpu_custom_call" | custom-call | tf_op jit(solution)/shard_map/pallas_call | solution.py:384
  83.3 3.5 %all-to-all-start.2 = ((bf16[32,24,240]{2,1,0:T(8,128)(2,1)}), bf16[32,24,240]{2,1,0:T(8,128)(2,1)S(1)}, u32[]{:S(2)}, u32[]{:S(2)}) async-start(bf16[32,24,240]{2,1,0:T(8,128)(2,1)} %shard_map.130), calls=%async_computation.2 | async-start | bytes 786432 | tf_op jit(solution)/shard_map/all_to_all | solution.py:478
  90.8 6.7 %collective-permute-done.11.refs_3_ = bf16[4,40,640]{2,1,0:T(8,128)(2,1)} collective-permute-done((bf16[4,40,640]{2,1,0:T(8,128)(2,1)S(1)}, bf16[4,40,640]{2,1,0:T(8,128)(2,1)}, u32[]{:S(2)}, u32[]{:S(2)}) %collective-permute-start.11) | collective-permute-done | bytes 204832 | tf_op jit(solution)/shard_map/ppermute | solution.py:19
  102.1 10.7 %shard_map.132 = (bf16[2,2,4,40,640]{4,3,2,1,0:T(8,128)(2,1)S(1)}, bf16[2,2,4,40,640]{4,3,2,1,0:T(8,128)(2,1)S(1)}, f32[1,128]{1,0:T(1,128)S(1)}, f32[320,128]{1...) custom-call(s32[5]{0:T(128)S(1)} %stack.23.place, ...), custom_call_target="tpu_custom_call" | custom-call | tf_op jit(solution)/shard_map/pallas_call | solution.py:384
  112.9 2.2 %shard_map.133 = (f32[320,640]{1,0:T(8,128)S(1)}, f32[320,640]{1,0:T(8,128)S(1)}) custom-call(f32[320,128]{1,0:T(8,128)S(1)} %get-tuple-element.86.d_raw, f32[320,640]{1,0:T(8,128)S(1)} %get-tuple-element.87.q_hat, f32[320,640]{1,0:T(8,128)S(1)} %get-tuple-element.88.k_hat, f32[1,640]{1,0:T(1,128)S(1)} %broadcast_in_dim_tile.9.qgain, ...), custom_call_target="tpu_custom_call" | custom-call | tf_op jit(solution)/shard_map/pallas_call | solution.py:384
  117.0 4.8 %shard_map.134 = bf16[8,40,640]{2,1,0:T(8,128)(2,1)} custom-call(f32[320,640]{1,0:T(8,128)S(1)} %get-tuple-element.91.d_qn, f32[320,640]{1,0:T(8,128)S(1)} %get-tuple-element.92.d_kn, f32[320,640]{1,0:T(8,128)S(1)} %get-tuple-element.87.q_hat, f32[320,640]{1,0:T(8,128)S(1)} %get-tuple-element.88.k_hat, f32[320,128]{1,0:T(8,128)S(1)} %get-tuple-element.93.q_rstd, ...), custom_call_target="tpu_custom_call" | custom-call | tf_op jit(solution)/shard_map/pallas_call | solution.py:384
  121.8 4.5 %all-to-all-start.3 = ((bf16[8,40,640]{2,1,0:T(8,128)(2,1)}), bf16[8,40,640]{2,1,0:T(8,128)(2,1)S(1)}, u32[]{:S(2)}, u32[]{:S(2)}) async-start(bf16[8,40,640]{2,1,0:T(8,128)(2,1)} %shard_map.134), calls=%async_computation.3 | async-start | bytes 819200 | tf_op jit(solution)/shard_map/all_to_all | solution.py:533
  128.3 5.7 %collective-permute-done.20 = bf16[4,40,640]{2,1,0:T(8,128)(2,1)S(1)} collective-permute-done((bf16[4,40,640]{2,1,0:T(8,128)(2,1)S(1)}, bf16[4,40,640]{2,1,0:T(8,128)(2,1)S(1)}, u32[]{:S(2)}, u32[]{:S(2)}) %collective-permute-start.20) | collective-permute-done | bytes 204832 | tf_op jit(solution)/shard_map/ppermute | solution.py:19
  134.1 5.2 %all-to-all-done.3 = bf16[8,40,640]{2,1,0:T(8,128)(2,1)S(1)} async-done(((bf16[8,40,640]{2,1,0:T(8,128)(2,1)}), bf16[8,40,640]{2,1,0:T(8,128)(2,1)S(1)}, u32[]{:S(2)}, u32[]{:S(2)}) %all-to-all-start.3) | async-done | bytes 409632 | tf_op jit(solution)/shard_map/all_to_all | solution.py:533
  145.8 3.8 %collective-permute-done.21 = bf16[2,40,640]{2,1,0:T(8,128)(2,1)S(1)} collective-permute-done((bf16[2,40,640]{2,1,0:T(8,128)(2,1)S(1)}, bf16[2,40,640]{2,1,0:T(8,128)(2,1)S(1)}, u32[]{:S(2)}, u32[]{:S(2)}) %collective-permute-start.21) | collective-permute-done | bytes 102432 | tf_op jit(solution)/shard_map/ppermute | solution.py:541
  149.8 2.1 %collective-permute-start.24 = (bf16[40,640]{1,0:T(8,128)(2,1)S(1)}, bf16[40,640]{1,0:T(8,128)(2,1)S(1)}, u32[]{:S(2)}, u32[]{:S(2)}) collective-permute-start(bf16[40,640]{1,0:T(8,128)(2,1)S(1)} %get-tuple-element.103), channel_id=1, source_target_pairs={{0,20},{2,22},{4,16},{6,18},{8,28},{10,30},{12,24},{14,26},{16,4},... | collective-permute-start | bytes 153608 | tf_op jit(solution)/shard_map/ppermute | solution.py:29
  (122 shorter events, 44.3 us)
Async XLA Ops:
  4.2 11.7 %collective-permute-start.1 = (bf16[288,640]{1,0:T(8,128)(2,1)}, bf16[288,640]{1,0:T(8,128)(2,1)S(1)}, u32[]{:S(2)}, u32[]{:S(2)}) collective-permute-start(bf16[288,640]{1,0:T(8,128)(2,1)} %bitcast.36), channel_id=1, source_target_pairs={{0,16},{16,0},{1,17},{17,1},{2,18},{18,2},{3,19},{19,3},{4,20},{20... | collective-permute-start | bytes 1105928 | tf_op jit(solution)/shard_map/ppermute | solution.py:19
  7.1 10.7 %collective-permute-start = (bf16[288,640]{1,0:T(8,128)(2,1)}, bf16[288,640]{1,0:T(8,128)(2,1)S(1)}, u32[]{:S(2)}, u32[]{:S(2)}) collective-permute-start(bf16[288,640]{1,0:T(8,128)(2,1)} %bitcast.37), channel_id=1, source_target_pairs={{0,1},{1,0},{2,3},{3,2},{4,5},{5,4},{6,7},{7,6},{8,9},{9,8},{10,11... | collective-permute-start | bytes 1105928 | tf_op jit(solution)/shard_map/ppermute | solution.py:19
  8.6 21.8 %all-to-all-start = ((bf16[8,56,640]{2,1,0:T(8,128)(2,1)}), bf16[8,56,640]{2,1,0:T(8,128)(2,1)S(1)}, u32[]{:S(2)}, u32[]{:S(2)}) async-start(bf16[8,56,640]{2,1,0:T(8,128)(2,1)} %shard_map.127), calls=%async_computation | async-start | bytes 1146880 | tf_op jit(solution)/shard_map/all_to_all | solution.py:427
  15.9 5.9 %collective-permute-start.2 = (bf16[144,640]{1,0:T(8,128)(2,1)S(1)}, bf16[144,640]{1,0:T(8,128)(2,1)S(1)}, u32[]{:S(2)}, u32[]{:S(2)}) collective-permute-start(bf16[144,640]{1,0:T(8,128)(2,1)S(1)} %slice.74), channel_id=1, source_target_pairs={{0,1},{1,0},{2,3},{3,2},{4,5},{5,4},{6,7},{7,6},{8,9},{9,8},{10,11... | collective-permute-start | bytes 552968 | tf_op jit(solution)/shard_map/ppermute | solution.py:19
  17.8 5.6 %collective-permute-start.3 = (bf16[144,640]{1,0:T(8,128)(2,1)S(1)}, bf16[144,640]{1,0:T(8,128)(2,1)S(1)}, u32[]{:S(2)}, u32[]{:S(2)}) collective-permute-start(bf16[144,640]{1,0:T(8,128)(2,1)S(1)} %slice.75), channel_id=1, source_target_pairs={{0,16},{16,0},{1,17},{17,1},{2,18},{18,2},{3,19},{19,3},{4,20},{20... | collective-permute-start | bytes 552968 | tf_op jit(solution)/shard_map/ppermute | solution.py:19
  19.3 11.0 %collective-permute-start.4 = (bf16[288,640]{1,0:T(8,128)(2,1)S(1)}, bf16[288,640]{1,0:T(8,128)(2,1)S(1)}, u32[]{:S(2)}, u32[]{:S(2)}) collective-permute-start(bf16[288,640]{1,0:T(8,128)(2,1)S(1)} %bitcast.38), channel_id=1, source_target_pairs={{0,2},{2,0},{4,6},{6,4},{8,10},{10,8},{12,14},{14,12},{1,3},{3,1},... | collective-permute-start | bytes 1105928 | tf_op jit(solution)/shard_map/ppermute | solution.py:19
  19.3 11.0 %collective-permute-start.5 = (bf16[288,640]{1,0:T(8,128)(2,1)S(1)}, bf16[288,640]{1,0:T(8,128)(2,1)S(1)}, u32[]{:S(2)}, u32[]{:S(2)}) collective-permute-start(bf16[288,640]{1,0:T(8,128)(2,1)S(1)} %collective-permute-done.refs_1_), channel_id=1, source_target_pairs={{0,2},{2,0},{4,6},{6,4},{8,10},{10,8},{12,14},{14,12},{1,3},{3,1},... | collective-permute-start | bytes 1105928 | tf_op jit(solution)/shard_map/ppermute | solution.py:19
  19.8 10.5 %collective-permute-start.6 = (bf16[288,640]{1,0:T(8,128)(2,1)S(1)}, bf16[288,640]{1,0:T(8,128)(2,1)}, u32[]{:S(2)}, u32[]{:S(2)}) collective-permute-start(bf16[288,640]{1,0:T(8,128)(2,1)S(1)} %collective-permute-done.1.refs_2_), channel_id=1, source_target_pairs={{0,2},{2,0},{4,6},{6,4},{8,10},{10,8},{12,14},{14,12},{1,3},{3,1},... | collective-permute-start | bytes 1105928 | tf_op jit(solution)/shard_map/ppermute | solution.py:19
  23.4 7.0 %collective-permute-start.7 = (bf16[288,640]{1,0:T(8,128)(2,1)S(1)}, bf16[288,640]{1,0:T(8,128)(2,1)}, u32[]{:S(2)}, u32[]{:S(2)}) collective-permute-start(bf16[288,640]{1,0:T(8,128)(2,1)S(1)} %constant_dynamic-update-slice_fusion.refs_3_), channel_id=1, source_target_pairs={{0,2},{2,0},{4,6},{6,4},{8,10},{10,8},{12,14},{14,12},{1,3},{3,1},... | collective-permute-start | bytes 1105928 | tf_op jit(solution)/shard_map/ppermute | solution.py:19
  32.6 42.3 %all-to-all-start.1 = ((bf16[16,3,40,240]{3,2,1,0:T(8,128)(2,1)}), bf16[16,3,40,240]{3,2,1,0:T(8,128)(2,1)}, u32[]{:S(2)}, u32[]{:S(2)}) async-start(bf16[16,3,40,240]{3,2,1,0:T(8,128)(2,1)} %bitcast.40), calls=%async_computation.1 | async-start | bytes 1966080 | tf_op jit(solution)/shard_map/all_to_all | solution.py:442
  38.5 24.0 %collective-permute-start.8 = (bf16[8,20,640]{2,1,0:T(8,128)(2,1)S(1)}, bf16[8,20,640]{2,1,0:T(8,128)(2,1)S(1)}, u32[]{:S(2)}, u32[]{:S(2)}) collective-permute-start(bf16[8,20,640]{2,1,0:T(8,128)(2,1)S(1)} %slice.58.mine), channel_id=1, source_target_pairs={{0,4},{2,6},{4,0},{6,2},{8,12},{10,14},{12,8},{14,10},{1,5},{3,7},... | collective-permute-start | bytes 614408 | tf_op jit(solution)/shard_map/ppermute | solution.py:444
  63.2 20.1 %collective-permute-start.9 = (bf16[8,40,640]{2,1,0:T(8,128)(2,1)S(1)}, bf16[8,40,640]{2,1,0:T(8,128)(2,1)S(1)}, u32[]{:S(2)}, u32[]{:S(2)}) collective-permute-start(bf16[8,40,640]{2,1,0:T(8,128)(2,1)S(1)} %shard_map.128.refs_0_), channel_id=1, source_target_pairs={{0,1},{1,0},{2,3},{3,2},{4,5},{5,4},{6,7},{7,6},{8,9},{9,8},{10,11... | collective-permute-start | bytes 1228808 | tf_op jit(solution)/shard_map/ppermute | solution.py:19
  64.7 18.6 %collective-permute-start.10 = (bf16[8,40,640]{2,1,0:T(8,128)(2,1)S(1)}, bf16[8,40,640]{2,1,0:T(8,128)(2,1)S(1)}, u32[]{:S(2)}, u32[]{:S(2)}) collective-permute-start(bf16[8,40,640]{2,1,0:T(8,128)(2,1)S(1)} %shard_map.128.refs_0_), channel_id=1, source_target_pairs={{0,16},{16,0},{1,17},{17,1},{2,18},{18,2},{3,19},{19,3},{4,20},{20... | collective-permute-start | bytes 1228808 | tf_op jit(solution)/shard_map/ppermute | solution.py:19
  83.3 17.1 %all-to-all-start.2 = ((bf16[32,24,240]{2,1,0:T(8,128)(2,1)}), bf16[32,24,240]{2,1,0:T(8,128)(2,1)S(1)}, u32[]{:S(2)}, u32[]{:S(2)}) async-start(bf16[32,24,240]{2,1,0:T(8,128)(2,1)} %shard_map.130), calls=%async_computation.2 | async-start | bytes 786432 | tf_op jit(solution)/shard_map/all_to_all | solution.py:478
  86.9 12.0 %collective-permute-start.13 = (bf16[8,40,640]{2,1,0:T(8,128)(2,1)S(1)}, bf16[8,40,640]{2,1,0:T(8,128)(2,1)S(1)}, u32[]{:S(2)}, u32[]{:S(2)}) collective-permute-start(bf16[8,40,640]{2,1,0:T(8,128)(2,1)S(1)} %shard_map.128.refs_0_), channel_id=1, source_target_pairs={{0,2},{2,0},{4,6},{6,4},{8,10},{10,8},{12,14},{14,12},{1,3},{3,1},... | collective-permute-start | bytes 1228808 | tf_op jit(solution)/shard_map/ppermute | solution.py:19
  87.2 11.7 %collective-permute-start.14 = (bf16[8,40,640]{2,1,0:T(8,128)(2,1)S(1)}, bf16[8,40,640]{2,1,0:T(8,128)(2,1)S(1)}, u32[]{:S(2)}, u32[]{:S(2)}) collective-permute-start(bf16[8,40,640]{2,1,0:T(8,128)(2,1)S(1)} %collective-permute-done.9.refs_1_), channel_id=1, source_target_pairs={{0,2},{2,0},{4,6},{6,4},{8,10},{10,8},{12,14},{14,12},{1,3},{3,1},... | collective-permute-start | bytes 1228808 | tf_op jit(solution)/shard_map/ppermute | solution.py:19
  87.5 10.0 %collective-permute-start.11 = (bf16[4,40,640]{2,1,0:T(8,128)(2,1)S(1)}, bf16[4,40,640]{2,1,0:T(8,128)(2,1)}, u32[]{:S(2)}, u32[]{:S(2)}) collective-permute-start(bf16[4,40,640]{2,1,0:T(8,128)(2,1)S(1)} %slice.59), channel_id=1, source_target_pairs={{0,1},{1,0},{2,3},{3,2},{4,5},{5,4},{6,7},{7,6},{8,9},{9,8},{10,11... | collective-permute-start | bytes 614408 | tf_op jit(solution)/shard_map/ppermute | solution.py:19
  89.4 9.5 %collective-permute-start.15 = (bf16[8,40,640]{2,1,0:T(8,128)(2,1)S(1)}, bf16[8,40,640]{2,1,0:T(8,128)(2,1)}, u32[]{:S(2)}, u32[]{:S(2)}) collective-permute-start(bf16[8,40,640]{2,1,0:T(8,128)(2,1)S(1)} %collective-permute-done.10.refs_2_), channel_id=1, source_target_pairs={{0,2},{2,0},{4,6},{6,4},{8,10},{10,8},{12,14},{14,12},{1,3},{3,1},... | collective-permute-start | bytes 1228808 | tf_op jit(solution)/shard_map/ppermute | solution.py:19
  89.4 9.2 %collective-permute-start.12 = (bf16[4,40,640]{2,1,0:T(8,128)(2,1)S(1)}, bf16[4,40,640]{2,1,0:T(8,128)(2,1)}, u32[]{:S(2)}, u32[]{:S(2)}) collective-permute-start(bf16[4,40,640]{2,1,0:T(8,128)(2,1)S(1)} %slice.60), channel_id=1, source_target_pairs={{0,16},{16,0},{1,17},{17,1},{2,18},{18,2},{3,19},{19,3},{4,20},{20... | collective-permute-start | bytes 614408 | tf_op jit(solution)/shard_map/ppermute | solution.py:19
  115.4 11.8 %collective-permute-start.19 = (bf16[2,4,40,640]{3,2,1,0:T(8,128)(2,1)S(1)}, bf16[2,4,40,640]{3,2,1,0:T(8,128)(2,1)S(1)}, u32[]{:S(2)}, u32[]{:S(2)}) collective-permute-start(bf16[2,4,40,640]{3,2,1,0:T(8,128)(2,1)S(1)} %slice_bitcast_fusion), channel_id=1, source_target_pairs={{0,16},{16,0},{1,17},{17,1},{2,18},{18,2},{3,19},{19,3},{4,20},{20... | collective-permute-start | bytes 1228808 | tf_op jit(solution)/shard_map/ppermute | solution.py:19
  121.8 17.4 %all-to-all-start.3 = ((bf16[8,40,640]{2,1,0:T(8,128)(2,1)}), bf16[8,40,640]{2,1,0:T(8,128)(2,1)S(1)}, u32[]{:S(2)}, u32[]{:S(2)}) async-start(bf16[8,40,640]{2,1,0:T(8,128)(2,1)} %shard_map.134), calls=%async_computation.3 | async-start | bytes 819200 | tf_op jit(solution)/shard_map/all_to_all | solution.py:533
  127.4 6.7 %collective-permute-start.20 = (bf16[4,40,640]{2,1,0:T(8,128)(2,1)S(1)}, bf16[4,40,640]{2,1,0:T(8,128)(2,1)S(1)}, u32[]{:S(2)}, u32[]{:S(2)}) collective-permute-start(bf16[4,40,640]{2,1,0:T(8,128)(2,1)S(1)} %slice_bitcast_fusion.1), channel_id=1, source_target_pairs={{0,1},{1,0},{2,3},{3,2},{4,5},{5,4},{6,7},{7,6},{8,9},{9,8},{10,11... | collective-permute-start | bytes 614408 | tf_op jit(solution)/shard_map/ppermute | solution.py:19
  143.9 5.8 %collective-permute-start.21 = (bf16[2,40,640]{2,1,0:T(8,128)(2,1)S(1)}, bf16[2,40,640]{2,1,0:T(8,128)(2,1)S(1)}, u32[]{:S(2)}, u32[]{:S(2)}) collective-permute-start(bf16[2,40,640]{2,1,0:T(8,128)(2,1)S(1)} %slice.67), channel_id=1, source_target_pairs={{0,8},{2,10},{4,12},{6,14},{8,0},{10,2},{12,4},{14,6},{1,9},{3,11}... | collective-permute-start | bytes 307208 | tf_op jit(solution)/shard_map/ppermute | solution.py:541
  149.8 5.1 %collective-permute-start.24 = (bf16[40,640]{1,0:T(8,128)(2,1)S(1)}, bf16[40,640]{1,0:T(8,128)(2,1)S(1)}, u32[]{:S(2)}, u32[]{:S(2)}) collective-permute-start(bf16[40,640]{1,0:T(8,128)(2,1)S(1)} %get-tuple-element.103), channel_id=1, source_target_pairs={{0,20},{2,22},{4,16},{6,18},{8,28},{10,30},{12,24},{14,26},{16,4},... | collective-permute-start | bytes 153608 | tf_op jit(solution)/shard_map/ppermute | solution.py:29
  (26 other events, 223.8 us)

commit v12 on v10

--- a/solution.py
+++ b/solution.py
@@ -17,6 +17,16 @@
 
 def swap(x, axis):
     return lax.ppermute(x, axis, [(i, i ^ 1) for i in range(lax.axis_size(axis))])
+
+
+def swap_both(x, axis, bit):
+    sizes = (lax.axis_size("dp"), lax.axis_size(axis))
+    pairs = [
+        (i * sizes[1] + j, (i ^ 1) * sizes[1] + (j ^ bit))
+        for i in range(sizes[0])
+        for j in range(sizes[1])
+    ]
+    return lax.ppermute(x, ("dp", axis), pairs)
 
 
 def round_up(value, unit):
@@ -539,26 +549,27 @@
     theirs, _ = lax.optimization_barrier((swap(shares[1], "dp"), d_mid))
     shares = add(shares[0], theirs)
     shares = add(shares[0], swap(shares[1], "tile"))
-    shares, d_back = lax.optimization_barrier((shares, d_back))
     step = frames // 4
-    while step > 0:
+    while step > 1:
         pairs = [(i, i ^ (2 * step)) for i in range(frames)]
         shares = add(shares[:step], lax.ppermute(shares[step:], "frame", pairs))
         step //= 2
-    shares = shares[0]
+    by_plane = lax.ppermute(shares[1], "frame", planes)
+    by_clip = swap(shares[0], "dp")
+    by_both = swap_both(shares[1], "frame", 2)
+    shares = shares[0].astype(F32) + by_plane.astype(F32)
+    theirs = by_clip.astype(F32) + by_both.astype(F32)
     small = jnp.sum(d_back[:, count : count + 3].astype(F32), axis=(0, 1))
     d_back = d_back[:, :count].reshape(rows, cols, width)
     mid_grad = (cot.astype(F32) + d_back.astype(F32)).astype(BF)
 
     small = small + swap(small, "tile")
-    if clips == 2:
-        small = small + swap(small, "dp")
-    else:
-        small = lax.psum(small, "dp")
+    small = small + swap(small, "dp")
+    if clips > 2:
         same_clip = [[i for i in range(clips) if i % 2 == c] for c in (0, 1)]
-        shares = lax.psum(shares, "dp", axis_index_groups=same_clip)
-    theirs = swap(shares, "dp").astype(F32)
-    shares = shares.astype(F32)
+        small, shares, theirs = lax.psum(
+            (small, shares, theirs), "dp", axis_index_groups=same_clip
+        )
     factor = 1.0 / math.sqrt(clips * frames * tiles * tokens)
     value_grad = jnp.where(x == 0, shares, theirs) * factor
     out_proj_grad = jnp.where(x == 0, theirs, shares) * factor

time: 142 us -> 150 us (1.056)
  starting transfers between devices: 39.7 us -> 45.9 us
    ppermute x2 -> x1, waiting for transfers between devices: 3.68 us -> 13.8 us  [local(): shares = add(shares[:step], lax.ppermute(shares[step:], 'frame', pairs))]
    all_to_all x1, waiting for transfers between devices: 5.15 us -> 0.01 us  [local(): d_back = lax.all_to_all(d_mid, 'frame', 0, 0, tiled=True)]
    ppermute x23, waiting for transfers between devices: 27.7 us -> 24.1 us  [swap(): lax.ppermute(x, axis, [(i, i ^ 1) for i in range(lax.axis_size(axis))])]
    ppermute x2 -> x1, starting transfers between devices: 0.14 us -> 2.88 us  [local(): shares = add(shares[:step], lax.ppermute(shares[step:], 'frame', pairs))]
    ppermute x0 -> x2, starting transfers between devices: none -> 2.45 us  [the longest x1 2.38 us: swap_both(): return lax.ppermute(x, ('dp', axis), pairs)]
  transfers between devices with their start and end apart: 31 -> 32, of which waited for: 19 -> 17; matrix products, arithmetic and copies ran while one was open for 6% -> 6% of each run, Pallas kernels for 14% -> 13%
where the time goes in v12:
time: 150 us; the launch traced here: 149 us
  waiting for transfers between devices  53.8 us (36%)
  starting transfers between devices  45.9 us (31%)
  Pallas kernels  31.6 us (21%)
  local copies, waits for them, and re-layouts  13.8 us (9%)
  other arithmetic  3.07 us (2%)
    pallas_call x9, Pallas kernels, call(): pl.pallas_call(kernel, out_shape=[jax.ShapeDtypeStruct(shape, dtype) for...  31.6 us
    ppermute x23, waiting for transfers between devices, swap(): lax.ppermute(x, axis, [(i, i ^ 1) for i in range(lax.axis_size(axis))])  24.1 us
    ppermute x23, starting transfers between devices, swap(): lax.ppermute(x, axis, [(i, i ^ 1) for i in range(lax.axis_size(axis))])  19.5 us
    ppermute x1, waiting for transfers between devices, local(): shares = add(shares[:step], lax.ppermute(shares[step:], 'frame', pairs))  13.8 us
    all_to_all x1, waiting for transfers between devices, local(): conv_half = lax.all_to_all(mine, square, 0, 0, tiled=True)  12.5 us
    unnamed x33, local copies, waits for them, and re-layouts  5.94 us
    all_to_all x1, starting transfers between devices, local(): d_back = lax.all_to_all(d_mid, 'frame', 0, 0, tiled=True)  4.89 us
    all_to_all x1, starting transfers between devices, local(): packed = lax.all_to_all(packed, 'frame', 0, 0, tiled=True)  4.88 us
  transfers between devices with their start and end apart: 32, of which 17 were waited for; matrix products, arithmetic and copies ran while one was open for 6% of the time, Pallas kernels for 13%

profile of v12, /device:TPU:0, one launch (start us, length us, event | category | flops | bytes accessed | tf_op | source)
XLA Modules:
  0.0 149.1 jit_solution(7137634563476256383)
XLA Ops:
  0.6 3.0 %collective-permute-start.1 = (bf16[288,640]{1,0:T(8,128)(2,1)}, bf16[288,640]{1,0:T(8,128)(2,1)S(1)}, u32[]{:S(2)}, u32[]{:S(2)}) collective-permute-start(bf16[288,640]{1,0:T(8,128)(2,1)} %bitcast.38), channel_id=1, source_target_pairs={{0,16},{16,0},{1,17},{17,1},{2,18},{18,2},{3,19},{19,3},{4,20},{20... | collective-permute-start | bytes 1105928 | tf_op jit(solution)/shard_map/ppermute | solution.py:19
  8.6 4.9 %all-to-all-start = ((bf16[8,56,640]{2,1,0:T(8,128)(2,1)}), bf16[8,56,640]{2,1,0:T(8,128)(2,1)S(1)}, u32[]{:S(2)}, u32[]{:S(2)}) async-start(bf16[8,56,640]{2,1,0:T(8,128)(2,1)} %shard_map.127), calls=%async_computation | async-start | bytes 1146880 | tf_op jit(solution)/shard_map/all_to_all | solution.py:437
  16.4 4.2 %collective-permute-done.2 = bf16[144,640]{1,0:T(8,128)(2,1)S(1)} collective-permute-done((bf16[144,640]{1,0:T(8,128)(2,1)S(1)}, bf16[144,640]{1,0:T(8,128)(2,1)S(1)}, u32[]{:S(2)}, u32[]{:S(2)}) %collective-permute-start.2) | collective-permute-done | bytes 184352 | tf_op jit(solution)/shard_map/ppermute | solution.py:19
  22.2 2.2 %copy.15 = bf16[4,3,40,3,80]{4,3,0,2,1:T(4,128)(2,1)} copy(bf16[4,3,40,3,80]{4,0,2,3,1:T(4,128)(2,1)} %bitcast.43) | data formatting | bytes 460800 | tf_op jit(solution)/shard_map/transpose | solution.py:449
  24.4 2.1 %reshape.49 = bf16[4,2,60,240]{3,0,2,1:T(4,128)(2,1)} reshape(bf16[4,3,40,3,80]{4,3,0,2,1:T(4,128)(2,1)} %copy.15) | data formatting | bytes 460800 | tf_op jit(solution)/shard_map/reshape | solution.py:450
  27.6 2.3 %all-to-all-done.cot_in = bf16[8,56,640]{2,1,0:T(8,128)(2,1)S(1)} async-done(((bf16[8,56,640]{2,1,0:T(8,128)(2,1)}), bf16[8,56,640]{2,1,0:T(8,128)(2,1)S(1)}, u32[]{:S(2)}, u32[]{:S(2)}) %all-to-all-start) | async-done | bytes 573472 | tf_op jit(solution)/shard_map/all_to_all | solution.py:437
  30.7 3.7 %all-to-all-start.1 = ((bf16[16,60,240]{2,1,0:T(8,128)(2,1)}), bf16[16,60,240]{2,1,0:T(8,128)(2,1)S(1)}, u32[]{:S(2)}, u32[]{:S(2)}) async-start(bf16[16,60,240]{2,1,0:T(8,128)(2,1)} %bitcast.42), calls=%async_computation.1 | async-start | bytes 1048576 | tf_op jit(solution)/shard_map/all_to_all | solution.py:454
  34.5 2.0 %collective-permute-start.8 = (bf16[8,20,640]{2,1,0:T(8,128)(2,1)S(1)}, bf16[8,20,640]{2,1,0:T(8,128)(2,1)S(1)}, u32[]{:S(2)}, u32[]{:S(2)}) collective-permute-start(bf16[8,20,640]{2,1,0:T(8,128)(2,1)S(1)} %slice.58.mine), channel_id=1, source_target_pairs={{0,4},{2,6},{4,0},{6,2},{8,12},{10,14},{12,8},{14,10},{1,5},{3,7},... | collective-permute-start | bytes 614408 | tf_op jit(solution)/shard_map/ppermute | solution.py:456
  36.5 12.5 %all-to-all-done.1.mine = bf16[16,60,240]{2,1,0:T(8,128)(2,1)S(1)} async-done(((bf16[16,60,240]{2,1,0:T(8,128)(2,1)}), bf16[16,60,240]{2,1,0:T(8,128)(2,1)S(1)}, u32[]{:S(2)}, u32[]{:S(2)}) %all-to-all-start.1) | async-done | bytes 460832 | tf_op jit(solution)/shard_map/all_to_all | solution.py:454
  49.0 1.8 %collective-permute-start.9 = (bf16[16,60,240]{2,1,0:T(8,128)(2,1)S(1)}, bf16[16,60,240]{2,1,0:T(8,128)(2,1)S(1)}, u32[]{:S(2)}, u32[]{:S(2)}) collective-permute-start(bf16[16,60,240]{2,1,0:T(8,128)(2,1)S(1)} %all-to-all-done.1.mine), channel_id=1, source_target_pairs={{0,4},{2,6},{4,0},{6,2},{8,12},{10,14},{12,8},{14,10},{1,5},{3,7},... | collective-permute-start | bytes 1382408 | tf_op jit(solution)/shard_map/ppermute | solution.py:457
  57.9 4.7 %shard_map.130 = (bf16[4,640,640]{2,1,0:T(8,128)(2,1)S(1)}, bf16[4,576,80]{2,1,0:T(8,128)(2,1)S(1)}) custom-call(s32[5]{0:T(128)S(1)} %stack.23.place, f32[1,640]{1,0:T(1,128)S(1)} %broadcast_in_dim.5.gain, bf16[288,640]{1,0:T(8,128)(2,1)S(1)} %bitcast.41, bf16[288,640]{1,0:T(8,128)(2,1)S(1)} %collective-permute-done.refs_1_, ...), custom_call_target="tpu_custom_call" | custom-call | tf_op jit(solution)/shard_map/pallas_call | solution.py:395
  64.0 5.1 %shard_map.131 = bf16[32,24,240]{2,1,0:T(8,128)(2,1)} custom-call(s32[5]{0:T(128)S(1)} %stack.23.place, bf16[3,640,240]{2,1,0:T(8,128)(2,1)S(1)} %bitcast.36, bf16[4,640,640]{2,1,0:T(8,128)(2,1)S(1)} %get-tuple-element.56.acts, bf16[4,576,80]{2,1,0:T(8,128)(2,1)S(1)} %get-tuple-element.57.kept), custom_call_target="tpu_custom_call" | custom-call | tf_op jit(solution)/shard_map/pallas_call | solution.py:395
  69.1 3.7 %all-to-all-start.2 = ((bf16[32,24,240]{2,1,0:T(8,128)(2,1)}), bf16[32,24,240]{2,1,0:T(8,128)(2,1)S(1)}, u32[]{:S(2)}, u32[]{:S(2)}) async-start(bf16[32,24,240]{2,1,0:T(8,128)(2,1)} %shard_map.131), calls=%async_computation.2 | async-start | bytes 786432 | tf_op jit(solution)/shard_map/all_to_all | solution.py:493
  73.6 1.8 %collective-permute-start.12 = (bf16[4,40,640]{2,1,0:T(8,128)(2,1)S(1)}, bf16[4,40,640]{2,1,0:T(8,128)(2,1)S(1)}, u32[]{:S(2)}, u32[]{:S(2)}) collective-permute-start(bf16[4,40,640]{2,1,0:T(8,128)(2,1)S(1)} %slice.59), channel_id=1, source_target_pairs={{0,1},{1,0},{2,3},{3,2},{4,5},{5,4},{6,7},{7,6},{8,9},{9,8},{10,11... | collective-permute-start | bytes 614408 | tf_op jit(solution)/shard_map/ppermute | solution.py:19
  76.9 6.6 %collective-permute-done.12.refs_3_ = bf16[4,40,640]{2,1,0:T(8,128)(2,1)S(1)} collective-permute-done((bf16[4,40,640]{2,1,0:T(8,128)(2,1)S(1)}, bf16[4,40,640]{2,1,0:T(8,128)(2,1)S(1)}, u32[]{:S(2)}, u32[]{:S(2)}) %collective-permute-start.12) | collective-permute-done | bytes 204832 | tf_op jit(solution)/shard_map/ppermute | solution.py:19
  88.0 10.6 %shard_map.133 = (bf16[2,2,4,40,640]{4,3,2,1,0:T(8,128)(2,1)S(1)}, bf16[2,2,4,40,640]{4,3,2,1,0:T(8,128)(2,1)S(1)}, f32[1,128]{1,0:T(1,128)S(1)}, f32[320,128]{1...) custom-call(s32[5]{0:T(128)S(1)} %stack.23.place, ...), custom_call_target="tpu_custom_call" | custom-call | tf_op jit(solution)/shard_map/pallas_call | solution.py:395
  98.9 1.9 %shard_map.134 = (f32[320,640]{1,0:T(8,128)S(1)}, f32[320,640]{1,0:T(8,128)S(1)}) custom-call(f32[320,128]{1,0:T(8,128)S(1)} %get-tuple-element.74.d_raw, f32[320,640]{1,0:T(8,128)S(1)} %get-tuple-element.75.q_hat, f32[320,640]{1,0:T(8,128)S(1)} %get-tuple-element.76.k_hat, f32[1,640]{1,0:T(1,128)S(1)} %broadcast_in_dim_tile.9.qgain, ...), custom_call_target="tpu_custom_call" | custom-call | tf_op jit(solution)/shard_map/pallas_call | solution.py:395
  102.9 4.8 %shard_map.135 = bf16[8,40,640]{2,1,0:T(8,128)(2,1)} custom-call(f32[320,640]{1,0:T(8,128)S(1)} %get-tuple-element.78.d_qn, f32[320,640]{1,0:T(8,128)S(1)} %get-tuple-element.79.d_kn, f32[320,640]{1,0:T(8,128)S(1)} %get-tuple-element.75.q_hat, f32[320,640]{1,0:T(8,128)S(1)} %get-tuple-element.76.k_hat, f32[320,128]{1,0:T(8,128)S(1)} %get-tuple-element.80.q_rstd, ...), custom_call_target="tpu_custom_call" | custom-call | tf_op jit(solution)/shard_map/pallas_call | solution.py:395
  107.7 5.2 %collective-permute-done.20 = bf16[2,4,40,640]{3,2,1,0:T(8,128)(2,1)S(1)} collective-permute-done((bf16[2,4,40,640]{3,2,1,0:T(8,128)(2,1)S(1)}, bf16[2,4,40,640]{3,2,1,0:T(8,128)(2,1)S(1)}, u32[]{:S(2)}, u32[]{:S(2)}) %collective-permute-start.20) | collective-permute-done | bytes 409632 | tf_op jit(solution)/shard_map/ppermute | solution.py:19
  114.0 4.9 %all-to-all-start.3 = ((bf16[8,40,640]{2,1,0:T(8,128)(2,1)}), bf16[8,40,640]{2,1,0:T(8,128)(2,1)S(1)}, u32[]{:S(2)}, u32[]{:S(2)}) async-start(bf16[8,40,640]{2,1,0:T(8,128)(2,1)} %shard_map.135), calls=%async_computation.3 | async-start | bytes 819200 | tf_op jit(solution)/shard_map/all_to_all | solution.py:548
  119.5 2.9 %collective-permute-start.22 = (bf16[2,40,640]{2,1,0:T(8,128)(2,1)S(1)}, bf16[2,40,640]{2,1,0:T(8,128)(2,1)S(1)}, u32[]{:S(2)}, u32[]{:S(2)}) collective-permute-start(bf16[2,40,640]{2,1,0:T(8,128)(2,1)S(1)} %slice.80), channel_id=1, source_target_pairs={{0,8},{2,10},{4,12},{6,14},{8,0},{10,2},{12,4},{14,6},{1,9},{3,11}... | collective-permute-start | bytes 307208 | tf_op jit(solution)/shard_map/ppermute | solution.py:555
  122.4 13.8 %collective-permute-done.22 = bf16[2,40,640]{2,1,0:T(8,128)(2,1)S(1)} collective-permute-done((bf16[2,40,640]{2,1,0:T(8,128)(2,1)S(1)}, bf16[2,40,640]{2,1,0:T(8,128)(2,1)S(1)}, u32[]{:S(2)}, u32[]{:S(2)}) %collective-permute-start.22) | collective-permute-done | bytes 102432 | tf_op jit(solution)/shard_map/ppermute | solution.py:555
  136.3 2.4 %collective-permute-start.25 = (bf16[40,640]{1,0:T(8,128)(2,1)S(1)}, bf16[40,640]{1,0:T(8,128)(2,1)S(1)}, u32[]{:S(2)}, u32[]{:S(2)}) collective-permute-start(bf16[40,640]{1,0:T(8,128)(2,1)S(1)} %get-tuple-element.89), channel_id=1, source_target_pairs={{0,20},{2,22},{4,16},{6,18},{8,28},{10,30},{12,24},{14,26},{16,4},... | collective-permute-start | bytes 153608 | tf_op jit(solution)/shard_map/ppermute | solution.py:29
  140.2 2.2 %collective-permute-done.26 = f32[640]{0:T(1024)S(1)} collective-permute-done((f32[640]{0:T(1024)S(1)}, f32[640]{0:T(1024)S(1)}, u32[]{:S(2)}, u32[]{:S(2)}) %collective-permute-start.26) | collective-permute-done | bytes 2592 | tf_op jit(solution)/shard_map/ppermute | solution.py:19
  (120 shorter events, 38.7 us)
Async XLA Ops:
  0.6 12.8 %collective-permute-start.1 = (bf16[288,640]{1,0:T(8,128)(2,1)}, bf16[288,640]{1,0:T(8,128)(2,1)S(1)}, u32[]{:S(2)}, u32[]{:S(2)}) collective-permute-start(bf16[288,640]{1,0:T(8,128)(2,1)} %bitcast.38), channel_id=1, source_target_pairs={{0,16},{16,0},{1,17},{17,1},{2,18},{18,2},{3,19},{19,3},{4,20},{20... | collective-permute-start | bytes 1105928 | tf_op jit(solution)/shard_map/ppermute | solution.py:19
  3.7 10.7 %collective-permute-start = (bf16[288,640]{1,0:T(8,128)(2,1)}, bf16[288,640]{1,0:T(8,128)(2,1)S(1)}, u32[]{:S(2)}, u32[]{:S(2)}) collective-permute-start(bf16[288,640]{1,0:T(8,128)(2,1)} %bitcast.39), channel_id=1, source_target_pairs={{0,1},{1,0},{2,3},{3,2},{4,5},{5,4},{6,7},{7,6},{8,9},{9,8},{10,11... | collective-permute-start | bytes 1105928 | tf_op jit(solution)/shard_map/ppermute | solution.py:19
  8.6 21.3 %all-to-all-start = ((bf16[8,56,640]{2,1,0:T(8,128)(2,1)}), bf16[8,56,640]{2,1,0:T(8,128)(2,1)S(1)}, u32[]{:S(2)}, u32[]{:S(2)}) async-start(bf16[8,56,640]{2,1,0:T(8,128)(2,1)} %shard_map.127), calls=%async_computation | async-start | bytes 1146880 | tf_op jit(solution)/shard_map/all_to_all | solution.py:437
  13.5 7.1 %collective-permute-start.2 = (bf16[144,640]{1,0:T(8,128)(2,1)S(1)}, bf16[144,640]{1,0:T(8,128)(2,1)S(1)}, u32[]{:S(2)}, u32[]{:S(2)}) collective-permute-start(bf16[144,640]{1,0:T(8,128)(2,1)S(1)} %slice.74), channel_id=1, source_target_pairs={{0,1},{1,0},{2,3},{3,2},{4,5},{5,4},{6,7},{7,6},{8,9},{9,8},{10,11... | collective-permute-start | bytes 552968 | tf_op jit(solution)/shard_map/ppermute | solution.py:19
  14.3 6.6 %collective-permute-start.3 = (bf16[144,640]{1,0:T(8,128)(2,1)S(1)}, bf16[144,640]{1,0:T(8,128)(2,1)S(1)}, u32[]{:S(2)}, u32[]{:S(2)}) collective-permute-start(bf16[144,640]{1,0:T(8,128)(2,1)S(1)} %slice.75), channel_id=1, source_target_pairs={{0,16},{16,0},{1,17},{17,1},{2,18},{18,2},{3,19},{19,3},{4,20},{20... | collective-permute-start | bytes 552968 | tf_op jit(solution)/shard_map/ppermute | solution.py:19
  15.9 11.6 %collective-permute-start.4 = (bf16[288,640]{1,0:T(8,128)(2,1)S(1)}, bf16[288,640]{1,0:T(8,128)(2,1)S(1)}, u32[]{:S(2)}, u32[]{:S(2)}) collective-permute-start(bf16[288,640]{1,0:T(8,128)(2,1)S(1)} %bitcast.40), channel_id=1, source_target_pairs={{0,2},{2,0},{4,6},{6,4},{8,10},{10,8},{12,14},{14,12},{1,3},{3,1},... | collective-permute-start | bytes 1105928 | tf_op jit(solution)/shard_map/ppermute | solution.py:19
  15.9 11.6 %collective-permute-start.5 = (bf16[288,640]{1,0:T(8,128)(2,1)S(1)}, bf16[288,640]{1,0:T(8,128)(2,1)S(1)}, u32[]{:S(2)}, u32[]{:S(2)}) collective-permute-start(bf16[288,640]{1,0:T(8,128)(2,1)S(1)} %collective-permute-done.refs_1_), channel_id=1, source_target_pairs={{0,2},{2,0},{4,6},{6,4},{8,10},{10,8},{12,14},{14,12},{1,3},{3,1},... | collective-permute-start | bytes 1105928 | tf_op jit(solution)/shard_map/ppermute | solution.py:19
  16.4 11.1 %collective-permute-start.6 = (bf16[288,640]{1,0:T(8,128)(2,1)S(1)}, bf16[288,640]{1,0:T(8,128)(2,1)}, u32[]{:S(2)}, u32[]{:S(2)}) collective-permute-start(bf16[288,640]{1,0:T(8,128)(2,1)S(1)} %collective-permute-done.1.refs_2_), channel_id=1, source_target_pairs={{0,2},{2,0},{4,6},{6,4},{8,10},{10,8},{12,14},{14,12},{1,3},{3,1},... | collective-permute-start | bytes 1105928 | tf_op jit(solution)/shard_map/ppermute | solution.py:19
  30.7 18.2 %all-to-all-start.1 = ((bf16[16,60,240]{2,1,0:T(8,128)(2,1)}), bf16[16,60,240]{2,1,0:T(8,128)(2,1)S(1)}, u32[]{:S(2)}, u32[]{:S(2)}) async-start(bf16[16,60,240]{2,1,0:T(8,128)(2,1)} %bitcast.42), calls=%async_computation.1 | async-start | bytes 1048576 | tf_op jit(solution)/shard_map/all_to_all | solution.py:454
  34.5 16.8 %collective-permute-start.8 = (bf16[8,20,640]{2,1,0:T(8,128)(2,1)S(1)}, bf16[8,20,640]{2,1,0:T(8,128)(2,1)S(1)}, u32[]{:S(2)}, u32[]{:S(2)}) collective-permute-start(bf16[8,20,640]{2,1,0:T(8,128)(2,1)S(1)} %slice.58.mine), channel_id=1, source_target_pairs={{0,4},{2,6},{4,0},{6,2},{8,12},{10,14},{12,8},{14,10},{1,5},{3,7},... | collective-permute-start | bytes 614408 | tf_op jit(solution)/shard_map/ppermute | solution.py:456
  49.0 14.4 %collective-permute-start.9 = (bf16[16,60,240]{2,1,0:T(8,128)(2,1)S(1)}, bf16[16,60,240]{2,1,0:T(8,128)(2,1)S(1)}, u32[]{:S(2)}, u32[]{:S(2)}) collective-permute-start(bf16[16,60,240]{2,1,0:T(8,128)(2,1)S(1)} %all-to-all-done.1.mine), channel_id=1, source_target_pairs={{0,4},{2,6},{4,0},{6,2},{8,12},{10,14},{12,8},{14,10},{1,5},{3,7},... | collective-permute-start | bytes 1382408 | tf_op jit(solution)/shard_map/ppermute | solution.py:457
  51.9 17.2 %collective-permute-start.10 = (bf16[8,40,640]{2,1,0:T(8,128)(2,1)S(1)}, bf16[8,40,640]{2,1,0:T(8,128)(2,1)S(1)}, u32[]{:S(2)}, u32[]{:S(2)}) collective-permute-start(bf16[8,40,640]{2,1,0:T(8,128)(2,1)S(1)} %shard_map.128.refs_0_), channel_id=1, source_target_pairs={{0,1},{1,0},{2,3},{3,2},{4,5},{5,4},{6,7},{7,6},{8,9},{9,8},{10,11... | collective-permute-start | bytes 1228808 | tf_op jit(solution)/shard_map/ppermute | solution.py:19
  53.4 15.7 %collective-permute-start.11 = (bf16[8,40,640]{2,1,0:T(8,128)(2,1)S(1)}, bf16[8,40,640]{2,1,0:T(8,128)(2,1)S(1)}, u32[]{:S(2)}, u32[]{:S(2)}) collective-permute-start(bf16[8,40,640]{2,1,0:T(8,128)(2,1)S(1)} %shard_map.128.refs_0_), channel_id=1, source_target_pairs={{0,16},{16,0},{1,17},{17,1},{2,18},{18,2},{3,19},{19,3},{4,20},{20... | collective-permute-start | bytes 1228808 | tf_op jit(solution)/shard_map/ppermute | solution.py:19
  69.1 17.3 %all-to-all-start.2 = ((bf16[32,24,240]{2,1,0:T(8,128)(2,1)}), bf16[32,24,240]{2,1,0:T(8,128)(2,1)S(1)}, u32[]{:S(2)}, u32[]{:S(2)}) async-start(bf16[32,24,240]{2,1,0:T(8,128)(2,1)} %shard_map.131), calls=%async_computation.2 | async-start | bytes 786432 | tf_op jit(solution)/shard_map/all_to_all | solution.py:493
  72.9 12.0 %collective-permute-start.14 = (bf16[8,40,640]{2,1,0:T(8,128)(2,1)S(1)}, bf16[8,40,640]{2,1,0:T(8,128)(2,1)S(1)}, u32[]{:S(2)}, u32[]{:S(2)}) collective-permute-start(bf16[8,40,640]{2,1,0:T(8,128)(2,1)S(1)} %shard_map.128.refs_0_), channel_id=1, source_target_pairs={{0,2},{2,0},{4,6},{6,4},{8,10},{10,8},{12,14},{14,12},{1,3},{3,1},... | collective-permute-start | bytes 1228808 | tf_op jit(solution)/shard_map/ppermute | solution.py:19
  73.2 11.7 %collective-permute-start.15 = (bf16[8,40,640]{2,1,0:T(8,128)(2,1)S(1)}, bf16[8,40,640]{2,1,0:T(8,128)(2,1)}, u32[]{:S(2)}, u32[]{:S(2)}) collective-permute-start(bf16[8,40,640]{2,1,0:T(8,128)(2,1)S(1)} %collective-permute-done.10.refs_1_), channel_id=1, source_target_pairs={{0,2},{2,0},{4,6},{6,4},{8,10},{10,8},{12,14},{14,12},{1,3},{3,1},... | collective-permute-start | bytes 1228808 | tf_op jit(solution)/shard_map/ppermute | solution.py:19
  73.6 9.9 %collective-permute-start.12 = (bf16[4,40,640]{2,1,0:T(8,128)(2,1)S(1)}, bf16[4,40,640]{2,1,0:T(8,128)(2,1)S(1)}, u32[]{:S(2)}, u32[]{:S(2)}) collective-permute-start(bf16[4,40,640]{2,1,0:T(8,128)(2,1)S(1)} %slice.59), channel_id=1, source_target_pairs={{0,1},{1,0},{2,3},{3,2},{4,5},{5,4},{6,7},{7,6},{8,9},{9,8},{10,11... | collective-permute-start | bytes 614408 | tf_op jit(solution)/shard_map/ppermute | solution.py:19
  75.4 9.5 %collective-permute-start.16 = (bf16[8,40,640]{2,1,0:T(8,128)(2,1)S(1)}, bf16[8,40,640]{2,1,0:T(8,128)(2,1)}, u32[]{:S(2)}, u32[]{:S(2)}) collective-permute-start(bf16[8,40,640]{2,1,0:T(8,128)(2,1)S(1)} %collective-permute-done.11.refs_2_), channel_id=1, source_target_pairs={{0,2},{2,0},{4,6},{6,4},{8,10},{10,8},{12,14},{14,12},{1,3},{3,1},... | collective-permute-start | bytes 1228808 | tf_op jit(solution)/shard_map/ppermute | solution.py:19
  75.4 9.2 %collective-permute-start.13 = (bf16[4,40,640]{2,1,0:T(8,128)(2,1)S(1)}, bf16[4,40,640]{2,1,0:T(8,128)(2,1)}, u32[]{:S(2)}, u32[]{:S(2)}) collective-permute-start(bf16[4,40,640]{2,1,0:T(8,128)(2,1)S(1)} %slice.60), channel_id=1, source_target_pairs={{0,16},{16,0},{1,17},{17,1},{2,18},{18,2},{3,19},{19,3},{4,20},{20... | collective-permute-start | bytes 614408 | tf_op jit(solution)/shard_map/ppermute | solution.py:19
  101.3 11.6 %collective-permute-start.20 = (bf16[2,4,40,640]{3,2,1,0:T(8,128)(2,1)S(1)}, bf16[2,4,40,640]{3,2,1,0:T(8,128)(2,1)S(1)}, u32[]{:S(2)}, u32[]{:S(2)}) collective-permute-start(bf16[2,4,40,640]{3,2,1,0:T(8,128)(2,1)S(1)} %slice_bitcast_fusion), channel_id=1, source_target_pairs={{0,16},{16,0},{1,17},{17,1},{2,18},{18,2},{3,19},{19,3},{4,20},{20... | collective-permute-start | bytes 1228808 | tf_op jit(solution)/shard_map/ppermute | solution.py:19
  114.0 24.7 %all-to-all-start.3 = ((bf16[8,40,640]{2,1,0:T(8,128)(2,1)}), bf16[8,40,640]{2,1,0:T(8,128)(2,1)S(1)}, u32[]{:S(2)}, u32[]{:S(2)}) async-start(bf16[8,40,640]{2,1,0:T(8,128)(2,1)} %shard_map.135), calls=%async_computation.3 | async-start | bytes 819200 | tf_op jit(solution)/shard_map/all_to_all | solution.py:548
  119.5 16.7 %collective-permute-start.22 = (bf16[2,40,640]{2,1,0:T(8,128)(2,1)S(1)}, bf16[2,40,640]{2,1,0:T(8,128)(2,1)S(1)}, u32[]{:S(2)}, u32[]{:S(2)}) collective-permute-start(bf16[2,40,640]{2,1,0:T(8,128)(2,1)S(1)} %slice.80), channel_id=1, source_target_pairs={{0,8},{2,10},{4,12},{6,14},{8,0},{10,2},{12,4},{14,6},{1,9},{3,11}... | collective-permute-start | bytes 307208 | tf_op jit(solution)/shard_map/ppermute | solution.py:555
  136.2 10.8 %collective-permute-start.23 = (bf16[40,640]{1,0:T(8,128)(2,1)S(1)}, bf16[40,640]{1,0:T(8,128)(2,1)S(1)}, u32[]{:S(2)}, u32[]{:S(2)}) collective-permute-start(bf16[40,640]{1,0:T(8,128)(2,1)S(1)} %get-tuple-element.89), channel_id=1, source_target_pairs={{0,4},{2,6},{4,0},{6,2},{8,12},{10,14},{12,8},{14,10},{1,5},{3,7},... | collective-permute-start | bytes 153608 | tf_op jit(solution)/shard_map/ppermute | solution.py:557
  136.3 10.8 %collective-permute-start.25 = (bf16[40,640]{1,0:T(8,128)(2,1)S(1)}, bf16[40,640]{1,0:T(8,128)(2,1)S(1)}, u32[]{:S(2)}, u32[]{:S(2)}) collective-permute-start(bf16[40,640]{1,0:T(8,128)(2,1)S(1)} %get-tuple-element.89), channel_id=1, source_target_pairs={{0,20},{2,22},{4,16},{6,18},{8,28},{10,30},{12,24},{14,26},{16,4},... | collective-permute-start | bytes 153608 | tf_op jit(solution)/shard_map/ppermute | solution.py:29
  (24 other events, 182.6 us)

commit v13 on v12

--- a/solution.py
+++ b/solution.py
@@ -549,6 +549,7 @@
     theirs, _ = lax.optimization_barrier((swap(shares[1], "dp"), d_mid))
     shares = add(shares[0], theirs)
     shares = add(shares[0], swap(shares[1], "tile"))
+    shares, d_back = lax.optimization_barrier((shares, d_back))
     step = frames // 4
     while step > 1:
         pairs = [(i, i ^ (2 * step)) for i in range(frames)]

time: 150 us -> 144 us (0.960)
  starting transfers between devices: 45.9 us -> 41.9 us
  waiting for transfers between devices: 53.8 us -> 52.3 us
    ppermute x1, waiting for transfers between devices: 13.8 us -> 3.13 us  [local(): shares = add(shares[:step], lax.ppermute(shares[step:], 'frame', pairs))]
    all_to_all x1, waiting for transfers between devices: 0.01 us -> 5.16 us  [local(): d_back = lax.all_to_all(d_mid, 'frame', 0, 0, tiled=True)]
    ppermute x1, starting transfers between devices: 2.88 us -> 0.07 us  [local(): shares = add(shares[:step], lax.ppermute(shares[step:], 'frame', pairs))]
    ppermute x23, waiting for transfers between devices: 24.1 us -> 26.7 us  [swap(): lax.ppermute(x, axis, [(i, i ^ 1) for i in range(lax.axis_size(axis))])]
  transfers between devices with their start and end apart: 32 -> 32, of which waited for: 17 -> 20; matrix products, arithmetic and copies ran while one was open for 6% -> 6% of each run, Pallas kernels for 13% -> 13%
where the time goes in v13:
time: 144 us
  waiting for transfers between devices  52.3 us (36%)
  starting transfers between devices  41.9 us (29%)
  Pallas kernels  31.6 us (22%)
  local copies, waits for them, and re-layouts  13.8 us (10%)
  other arithmetic  3.07 us (2%)
    pallas_call x9, Pallas kernels, call(): pl.pallas_call(kernel, out_shape=[jax.ShapeDtypeStruct(shape, dtype) for...  31.6 us
    ppermute x23, waiting for transfers between devices, swap(): lax.ppermute(x, axis, [(i, i ^ 1) for i in range(lax.axis_size(axis))])  26.7 us
    ppermute x23, starting transfers between devices, swap(): lax.ppermute(x, axis, [(i, i ^ 1) for i in range(lax.axis_size(axis))])  18.6 us
    all_to_all x1, waiting for transfers between devices, local(): conv_half = lax.all_to_all(mine, square, 0, 0, tiled=True)  12.5 us
    unnamed x33, local copies, waits for them, and re-layouts  5.94 us
    all_to_all x1, waiting for transfers between devices, local(): d_back = lax.all_to_all(d_mid, 'frame', 0, 0, tiled=True)  5.16 us
    all_to_all x1, starting transfers between devices, local(): packed = lax.all_to_all(packed, 'frame', 0, 0, tiled=True)  4.88 us
    all_to_all x1, starting transfers between devices, local(): d_back = lax.all_to_all(d_mid, 'frame', 0, 0, tiled=True)  4.35 us
  transfers between devices with their start and end apart: 32, of which 20 were waited for; matrix products, arithmetic and copies ran while one was open for 6% of the time, Pallas kernels for 13%

profile of v13, /device:TPU:0, one launch (start us, length us, event | category | flops | bytes accessed | tf_op | source)
XLA Modules:
  0.0 143.6 jit_solution(5170075103024617682)
XLA Ops:
  0.6 3.0 %collective-permute-start.1 = (bf16[288,640]{1,0:T(8,128)(2,1)}, bf16[288,640]{1,0:T(8,128)(2,1)S(1)}, u32[]{:S(2)}, u32[]{:S(2)}) collective-permute-start(bf16[288,640]{1,0:T(8,128)(2,1)} %bitcast.38), channel_id=1, source_target_pairs={{0,16},{16,0},{1,17},{17,1},{2,18},{18,2},{3,19},{19,3},{4,20},{20... | collective-permute-start | bytes 1105928 | tf_op jit(solution)/shard_map/ppermute | solution.py:19
  8.6 4.9 %all-to-all-start = ((bf16[8,56,640]{2,1,0:T(8,128)(2,1)}), bf16[8,56,640]{2,1,0:T(8,128)(2,1)S(1)}, u32[]{:S(2)}, u32[]{:S(2)}) async-start(bf16[8,56,640]{2,1,0:T(8,128)(2,1)} %shard_map.127), calls=%async_computation | async-start | bytes 1146880 | tf_op jit(solution)/shard_map/all_to_all | solution.py:437
  16.4 4.2 %collective-permute-done.2 = bf16[144,640]{1,0:T(8,128)(2,1)S(1)} collective-permute-done((bf16[144,640]{1,0:T(8,128)(2,1)S(1)}, bf16[144,640]{1,0:T(8,128)(2,1)S(1)}, u32[]{:S(2)}, u32[]{:S(2)}) %collective-permute-start.2) | collective-permute-done | bytes 184352 | tf_op jit(solution)/shard_map/ppermute | solution.py:19
  22.2 2.2 %copy.15 = bf16[4,3,40,3,80]{4,3,0,2,1:T(4,128)(2,1)} copy(bf16[4,3,40,3,80]{4,0,2,3,1:T(4,128)(2,1)} %bitcast.43) | data formatting | bytes 460800 | tf_op jit(solution)/shard_map/transpose | solution.py:449
  24.4 2.1 %reshape.49 = bf16[4,2,60,240]{3,0,2,1:T(4,128)(2,1)} reshape(bf16[4,3,40,3,80]{4,3,0,2,1:T(4,128)(2,1)} %copy.15) | data formatting | bytes 460800 | tf_op jit(solution)/shard_map/reshape | solution.py:450
  27.6 2.3 %all-to-all-done.cot_in = bf16[8,56,640]{2,1,0:T(8,128)(2,1)S(1)} async-done(((bf16[8,56,640]{2,1,0:T(8,128)(2,1)}), bf16[8,56,640]{2,1,0:T(8,128)(2,1)S(1)}, u32[]{:S(2)}, u32[]{:S(2)}) %all-to-all-start) | async-done | bytes 573472 | tf_op jit(solution)/shard_map/all_to_all | solution.py:437
  30.7 3.7 %all-to-all-start.1 = ((bf16[16,60,240]{2,1,0:T(8,128)(2,1)}), bf16[16,60,240]{2,1,0:T(8,128)(2,1)S(1)}, u32[]{:S(2)}, u32[]{:S(2)}) async-start(bf16[16,60,240]{2,1,0:T(8,128)(2,1)} %bitcast.42), calls=%async_computation.1 | async-start | bytes 1048576 | tf_op jit(solution)/shard_map/all_to_all | solution.py:454
  34.5 2.0 %collective-permute-start.8 = (bf16[8,20,640]{2,1,0:T(8,128)(2,1)S(1)}, bf16[8,20,640]{2,1,0:T(8,128)(2,1)S(1)}, u32[]{:S(2)}, u32[]{:S(2)}) collective-permute-start(bf16[8,20,640]{2,1,0:T(8,128)(2,1)S(1)} %slice.58.mine), channel_id=1, source_target_pairs={{0,4},{2,6},{4,0},{6,2},{8,12},{10,14},{12,8},{14,10},{1,5},{3,7},... | collective-permute-start | bytes 614408 | tf_op jit(solution)/shard_map/ppermute | solution.py:456
  36.5 12.5 %all-to-all-done.1.mine = bf16[16,60,240]{2,1,0:T(8,128)(2,1)S(1)} async-done(((bf16[16,60,240]{2,1,0:T(8,128)(2,1)}), bf16[16,60,240]{2,1,0:T(8,128)(2,1)S(1)}, u32[]{:S(2)}, u32[]{:S(2)}) %all-to-all-start.1) | async-done | bytes 460832 | tf_op jit(solution)/shard_map/all_to_all | solution.py:454
  49.0 1.8 %collective-permute-start.9 = (bf16[16,60,240]{2,1,0:T(8,128)(2,1)S(1)}, bf16[16,60,240]{2,1,0:T(8,128)(2,1)S(1)}, u32[]{:S(2)}, u32[]{:S(2)}) collective-permute-start(bf16[16,60,240]{2,1,0:T(8,128)(2,1)S(1)} %all-to-all-done.1.mine), channel_id=1, source_target_pairs={{0,4},{2,6},{4,0},{6,2},{8,12},{10,14},{12,8},{14,10},{1,5},{3,7},... | collective-permute-start | bytes 1382408 | tf_op jit(solution)/shard_map/ppermute | solution.py:457
  57.9 4.7 %shard_map.130 = (bf16[4,640,640]{2,1,0:T(8,128)(2,1)S(1)}, bf16[4,576,80]{2,1,0:T(8,128)(2,1)S(1)}) custom-call(s32[5]{0:T(128)S(1)} %stack.23.place, f32[1,640]{1,0:T(1,128)S(1)} %broadcast_in_dim.5.gain, bf16[288,640]{1,0:T(8,128)(2,1)S(1)} %bitcast.41, bf16[288,640]{1,0:T(8,128)(2,1)S(1)} %collective-permute-done.refs_1_, ...), custom_call_target="tpu_custom_call" | custom-call | tf_op jit(solution)/shard_map/pallas_call | solution.py:395
  64.0 5.1 %shard_map.131 = bf16[32,24,240]{2,1,0:T(8,128)(2,1)} custom-call(s32[5]{0:T(128)S(1)} %stack.23.place, bf16[3,640,240]{2,1,0:T(8,128)(2,1)S(1)} %bitcast.36, bf16[4,640,640]{2,1,0:T(8,128)(2,1)S(1)} %get-tuple-element.58.acts, bf16[4,576,80]{2,1,0:T(8,128)(2,1)S(1)} %get-tuple-element.59.kept), custom_call_target="tpu_custom_call" | custom-call | tf_op jit(solution)/shard_map/pallas_call | solution.py:395
  69.1 3.7 %all-to-all-start.2 = ((bf16[32,24,240]{2,1,0:T(8,128)(2,1)}), bf16[32,24,240]{2,1,0:T(8,128)(2,1)S(1)}, u32[]{:S(2)}, u32[]{:S(2)}) async-start(bf16[32,24,240]{2,1,0:T(8,128)(2,1)} %shard_map.131), calls=%async_computation.2 | async-start | bytes 786432 | tf_op jit(solution)/shard_map/all_to_all | solution.py:493
  76.9 6.6 %collective-permute-done.12.refs_3_ = bf16[4,40,640]{2,1,0:T(8,128)(2,1)S(1)} collective-permute-done((bf16[4,40,640]{2,1,0:T(8,128)(2,1)S(1)}, bf16[4,40,640]{2,1,0:T(8,128)(2,1)S(1)}, u32[]{:S(2)}, u32[]{:S(2)}) %collective-permute-start.12) | collective-permute-done | bytes 204832 | tf_op jit(solution)/shard_map/ppermute | solution.py:19
  88.0 10.6 %shard_map.133 = (bf16[2,2,4,40,640]{4,3,2,1,0:T(8,128)(2,1)S(1)}, bf16[2,2,4,40,640]{4,3,2,1,0:T(8,128)(2,1)S(1)}, f32[1,128]{1,0:T(1,128)S(1)}, f32[320,128]{1...) custom-call(s32[5]{0:T(128)S(1)} %stack.23.place, ...), custom_call_target="tpu_custom_call" | custom-call | tf_op jit(solution)/shard_map/pallas_call | solution.py:395
  98.9 1.9 %shard_map.134 = (f32[320,640]{1,0:T(8,128)S(1)}, f32[320,640]{1,0:T(8,128)S(1)}) custom-call(f32[320,128]{1,0:T(8,128)S(1)} %get-tuple-element.76.d_raw, f32[320,640]{1,0:T(8,128)S(1)} %get-tuple-element.77.q_hat, f32[320,640]{1,0:T(8,128)S(1)} %get-tuple-element.78.k_hat, f32[1,640]{1,0:T(1,128)S(1)} %broadcast_in_dim_tile.9.qgain, ...), custom_call_target="tpu_custom_call" | custom-call | tf_op jit(solution)/shard_map/pallas_call | solution.py:395
  102.9 4.8 %shard_map.135 = bf16[8,40,640]{2,1,0:T(8,128)(2,1)} custom-call(f32[320,640]{1,0:T(8,128)S(1)} %get-tuple-element.81.d_qn, f32[320,640]{1,0:T(8,128)S(1)} %get-tuple-element.82.d_kn, f32[320,640]{1,0:T(8,128)S(1)} %get-tuple-element.77.q_hat, f32[320,640]{1,0:T(8,128)S(1)} %get-tuple-element.78.k_hat, f32[320,128]{1,0:T(8,128)S(1)} %get-tuple-element.83.q_rstd, ...), custom_call_target="tpu_custom_call" | custom-call | tf_op jit(solution)/shard_map/pallas_call | solution.py:395
  107.7 4.4 %all-to-all-start.3 = ((bf16[8,40,640]{2,1,0:T(8,128)(2,1)}), bf16[8,40,640]{2,1,0:T(8,128)(2,1)S(1)}, u32[]{:S(2)}, u32[]{:S(2)}) async-start(bf16[8,40,640]{2,1,0:T(8,128)(2,1)} %shard_map.135), calls=%async_computation.3 | async-start | bytes 819200 | tf_op jit(solution)/shard_map/all_to_all | solution.py:548
  114.0 5.8 %collective-permute-done.21 = bf16[4,40,640]{2,1,0:T(8,128)(2,1)S(1)} collective-permute-done((bf16[4,40,640]{2,1,0:T(8,128)(2,1)S(1)}, bf16[4,40,640]{2,1,0:T(8,128)(2,1)S(1)}, u32[]{:S(2)}, u32[]{:S(2)}) %collective-permute-start.21) | collective-permute-done | bytes 204832 | tf_op jit(solution)/shard_map/ppermute | solution.py:19
  119.8 5.2 %all-to-all-done.3 = bf16[8,40,640]{2,1,0:T(8,128)(2,1)S(1)} async-done(((bf16[8,40,640]{2,1,0:T(8,128)(2,1)}), bf16[8,40,640]{2,1,0:T(8,128)(2,1)S(1)}, u32[]{:S(2)}, u32[]{:S(2)}) %all-to-all-start.3) | async-done | bytes 409632 | tf_op jit(solution)/shard_map/all_to_all | solution.py:548
  126.0 2.7 %collective-permute-done.26 = f32[640]{0:T(1024)S(1)} collective-permute-done((f32[640]{0:T(1024)S(1)}, f32[640]{0:T(1024)S(1)}, u32[]{:S(2)}, u32[]{:S(2)}) %collective-permute-start.26) | collective-permute-done | bytes 2592 | tf_op jit(solution)/shard_map/ppermute | solution.py:19
  130.4 1.9 %collective-permute-done.27 = f32[640]{0:T(1024)S(1)} collective-permute-done((f32[640]{0:T(1024)S(1)}, f32[640]{0:T(1024)S(1)}, u32[]{:S(2)}, u32[]{:S(2)}) %collective-permute-start.27) | collective-permute-done | bytes 2592 | tf_op jit(solution)/shard_map/ppermute | solution.py:19
  132.8 3.1 %collective-permute-done.22 = bf16[2,40,640]{2,1,0:T(8,128)(2,1)S(1)} collective-permute-done((bf16[2,40,640]{2,1,0:T(8,128)(2,1)S(1)}, bf16[2,40,640]{2,1,0:T(8,128)(2,1)S(1)}, u32[]{:S(2)}, u32[]{:S(2)}) %collective-permute-start.22) | collective-permute-done | bytes 102432 | tf_op jit(solution)/shard_map/ppermute | solution.py:556
  136.1 2.7 %collective-permute-start.25 = (bf16[40,640]{1,0:T(8,128)(2,1)S(1)}, bf16[40,640]{1,0:T(8,128)(2,1)S(1)}, u32[]{:S(2)}, u32[]{:S(2)}) collective-permute-start(bf16[40,640]{1,0:T(8,128)(2,1)S(1)} %get-tuple-element.93), channel_id=1, source_target_pairs={{0,20},{2,22},{4,16},{6,18},{8,28},{10,30},{12,24},{14,26},{16,4},... | collective-permute-start | bytes 153608 | tf_op jit(solution)/shard_map/ppermute | solution.py:29
  (120 shorter events, 40.6 us)
Async XLA Ops:
  0.6 12.8 %collective-permute-start.1 = (bf16[288,640]{1,0:T(8,128)(2,1)}, bf16[288,640]{1,0:T(8,128)(2,1)S(1)}, u32[]{:S(2)}, u32[]{:S(2)}) collective-permute-start(bf16[288,640]{1,0:T(8,128)(2,1)} %bitcast.38), channel_id=1, source_target_pairs={{0,16},{16,0},{1,17},{17,1},{2,18},{18,2},{3,19},{19,3},{4,20},{20... | collective-permute-start | bytes 1105928 | tf_op jit(solution)/shard_map/ppermute | solution.py:19
  3.7 10.7 %collective-permute-start = (bf16[288,640]{1,0:T(8,128)(2,1)}, bf16[288,640]{1,0:T(8,128)(2,1)S(1)}, u32[]{:S(2)}, u32[]{:S(2)}) collective-permute-start(bf16[288,640]{1,0:T(8,128)(2,1)} %bitcast.39), channel_id=1, source_target_pairs={{0,1},{1,0},{2,3},{3,2},{4,5},{5,4},{6,7},{7,6},{8,9},{9,8},{10,11... | collective-permute-start | bytes 1105928 | tf_op jit(solution)/shard_map/ppermute | solution.py:19
  8.6 21.3 %all-to-all-start = ((bf16[8,56,640]{2,1,0:T(8,128)(2,1)}), bf16[8,56,640]{2,1,0:T(8,128)(2,1)S(1)}, u32[]{:S(2)}, u32[]{:S(2)}) async-start(bf16[8,56,640]{2,1,0:T(8,128)(2,1)} %shard_map.127), calls=%async_computation | async-start | bytes 1146880 | tf_op jit(solution)/shard_map/all_to_all | solution.py:437
  13.5 7.1 %collective-permute-start.2 = (bf16[144,640]{1,0:T(8,128)(2,1)S(1)}, bf16[144,640]{1,0:T(8,128)(2,1)S(1)}, u32[]{:S(2)}, u32[]{:S(2)}) collective-permute-start(bf16[144,640]{1,0:T(8,128)(2,1)S(1)} %slice.74), channel_id=1, source_target_pairs={{0,1},{1,0},{2,3},{3,2},{4,5},{5,4},{6,7},{7,6},{8,9},{9,8},{10,11... | collective-permute-start | bytes 552968 | tf_op jit(solution)/shard_map/ppermute | solution.py:19
  14.3 6.6 %collective-permute-start.3 = (bf16[144,640]{1,0:T(8,128)(2,1)S(1)}, bf16[144,640]{1,0:T(8,128)(2,1)S(1)}, u32[]{:S(2)}, u32[]{:S(2)}) collective-permute-start(bf16[144,640]{1,0:T(8,128)(2,1)S(1)} %slice.75), channel_id=1, source_target_pairs={{0,16},{16,0},{1,17},{17,1},{2,18},{18,2},{3,19},{19,3},{4,20},{20... | collective-permute-start | bytes 552968 | tf_op jit(solution)/shard_map/ppermute | solution.py:19
  15.9 11.6 %collective-permute-start.4 = (bf16[288,640]{1,0:T(8,128)(2,1)S(1)}, bf16[288,640]{1,0:T(8,128)(2,1)S(1)}, u32[]{:S(2)}, u32[]{:S(2)}) collective-permute-start(bf16[288,640]{1,0:T(8,128)(2,1)S(1)} %bitcast.40), channel_id=1, source_target_pairs={{0,2},{2,0},{4,6},{6,4},{8,10},{10,8},{12,14},{14,12},{1,3},{3,1},... | collective-permute-start | bytes 1105928 | tf_op jit(solution)/shard_map/ppermute | solution.py:19
  15.9 11.6 %collective-permute-start.5 = (bf16[288,640]{1,0:T(8,128)(2,1)S(1)}, bf16[288,640]{1,0:T(8,128)(2,1)S(1)}, u32[]{:S(2)}, u32[]{:S(2)}) collective-permute-start(bf16[288,640]{1,0:T(8,128)(2,1)S(1)} %collective-permute-done.refs_1_), channel_id=1, source_target_pairs={{0,2},{2,0},{4,6},{6,4},{8,10},{10,8},{12,14},{14,12},{1,3},{3,1},... | collective-permute-start | bytes 1105928 | tf_op jit(solution)/shard_map/ppermute | solution.py:19
  16.4 11.1 %collective-permute-start.6 = (bf16[288,640]{1,0:T(8,128)(2,1)S(1)}, bf16[288,640]{1,0:T(8,128)(2,1)}, u32[]{:S(2)}, u32[]{:S(2)}) collective-permute-start(bf16[288,640]{1,0:T(8,128)(2,1)S(1)} %collective-permute-done.1.refs_2_), channel_id=1, source_target_pairs={{0,2},{2,0},{4,6},{6,4},{8,10},{10,8},{12,14},{14,12},{1,3},{3,1},... | collective-permute-start | bytes 1105928 | tf_op jit(solution)/shard_map/ppermute | solution.py:19
  21.0 6.6 %collective-permute-start.7 = (bf16[288,640]{1,0:T(8,128)(2,1)S(1)}, bf16[288,640]{1,0:T(8,128)(2,1)}, u32[]{:S(2)}, u32[]{:S(2)}) collective-permute-start(bf16[288,640]{1,0:T(8,128)(2,1)S(1)} %constant_dynamic-update-slice_fusion.refs_3_), channel_id=1, source_target_pairs={{0,2},{2,0},{4,6},{6,4},{8,10},{10,8},{12,14},{14,12},{1,3},{3,1},... | collective-permute-start | bytes 1105928 | tf_op jit(solution)/shard_map/ppermute | solution.py:19
  30.7 18.2 %all-to-all-start.1 = ((bf16[16,60,240]{2,1,0:T(8,128)(2,1)}), bf16[16,60,240]{2,1,0:T(8,128)(2,1)S(1)}, u32[]{:S(2)}, u32[]{:S(2)}) async-start(bf16[16,60,240]{2,1,0:T(8,128)(2,1)} %bitcast.42), calls=%async_computation.1 | async-start | bytes 1048576 | tf_op jit(solution)/shard_map/all_to_all | solution.py:454
  34.5 16.8 %collective-permute-start.8 = (bf16[8,20,640]{2,1,0:T(8,128)(2,1)S(1)}, bf16[8,20,640]{2,1,0:T(8,128)(2,1)S(1)}, u32[]{:S(2)}, u32[]{:S(2)}) collective-permute-start(bf16[8,20,640]{2,1,0:T(8,128)(2,1)S(1)} %slice.58.mine), channel_id=1, source_target_pairs={{0,4},{2,6},{4,0},{6,2},{8,12},{10,14},{12,8},{14,10},{1,5},{3,7},... | collective-permute-start | bytes 614408 | tf_op jit(solution)/shard_map/ppermute | solution.py:456
  49.0 14.4 %collective-permute-start.9 = (bf16[16,60,240]{2,1,0:T(8,128)(2,1)S(1)}, bf16[16,60,240]{2,1,0:T(8,128)(2,1)S(1)}, u32[]{:S(2)}, u32[]{:S(2)}) collective-permute-start(bf16[16,60,240]{2,1,0:T(8,128)(2,1)S(1)} %all-to-all-done.1.mine), channel_id=1, source_target_pairs={{0,4},{2,6},{4,0},{6,2},{8,12},{10,14},{12,8},{14,10},{1,5},{3,7},... | collective-permute-start | bytes 1382408 | tf_op jit(solution)/shard_map/ppermute | solution.py:457
  51.9 17.2 %collective-permute-start.10 = (bf16[8,40,640]{2,1,0:T(8,128)(2,1)S(1)}, bf16[8,40,640]{2,1,0:T(8,128)(2,1)S(1)}, u32[]{:S(2)}, u32[]{:S(2)}) collective-permute-start(bf16[8,40,640]{2,1,0:T(8,128)(2,1)S(1)} %shard_map.128.refs_0_), channel_id=1, source_target_pairs={{0,1},{1,0},{2,3},{3,2},{4,5},{5,4},{6,7},{7,6},{8,9},{9,8},{10,11... | collective-permute-start | bytes 1228808 | tf_op jit(solution)/shard_map/ppermute | solution.py:19
  53.4 15.7 %collective-permute-start.11 = (bf16[8,40,640]{2,1,0:T(8,128)(2,1)S(1)}, bf16[8,40,640]{2,1,0:T(8,128)(2,1)S(1)}, u32[]{:S(2)}, u32[]{:S(2)}) collective-permute-start(bf16[8,40,640]{2,1,0:T(8,128)(2,1)S(1)} %shard_map.128.refs_0_), channel_id=1, source_target_pairs={{0,16},{16,0},{1,17},{17,1},{2,18},{18,2},{3,19},{19,3},{4,20},{20... | collective-permute-start | bytes 1228808 | tf_op jit(solution)/shard_map/ppermute | solution.py:19
  69.1 17.3 %all-to-all-start.2 = ((bf16[32,24,240]{2,1,0:T(8,128)(2,1)}), bf16[32,24,240]{2,1,0:T(8,128)(2,1)S(1)}, u32[]{:S(2)}, u32[]{:S(2)}) async-start(bf16[32,24,240]{2,1,0:T(8,128)(2,1)} %shard_map.131), calls=%async_computation.2 | async-start | bytes 786432 | tf_op jit(solution)/shard_map/all_to_all | solution.py:493
  72.9 12.0 %collective-permute-start.14 = (bf16[8,40,640]{2,1,0:T(8,128)(2,1)S(1)}, bf16[8,40,640]{2,1,0:T(8,128)(2,1)S(1)}, u32[]{:S(2)}, u32[]{:S(2)}) collective-permute-start(bf16[8,40,640]{2,1,0:T(8,128)(2,1)S(1)} %shard_map.128.refs_0_), channel_id=1, source_target_pairs={{0,2},{2,0},{4,6},{6,4},{8,10},{10,8},{12,14},{14,12},{1,3},{3,1},... | collective-permute-start | bytes 1228808 | tf_op jit(solution)/shard_map/ppermute | solution.py:19
  73.2 11.7 %collective-permute-start.15 = (bf16[8,40,640]{2,1,0:T(8,128)(2,1)S(1)}, bf16[8,40,640]{2,1,0:T(8,128)(2,1)}, u32[]{:S(2)}, u32[]{:S(2)}) collective-permute-start(bf16[8,40,640]{2,1,0:T(8,128)(2,1)S(1)} %collective-permute-done.10.refs_1_), channel_id=1, source_target_pairs={{0,2},{2,0},{4,6},{6,4},{8,10},{10,8},{12,14},{14,12},{1,3},{3,1},... | collective-permute-start | bytes 1228808 | tf_op jit(solution)/shard_map/ppermute | solution.py:19
  73.6 9.9 %collective-permute-start.12 = (bf16[4,40,640]{2,1,0:T(8,128)(2,1)S(1)}, bf16[4,40,640]{2,1,0:T(8,128)(2,1)S(1)}, u32[]{:S(2)}, u32[]{:S(2)}) collective-permute-start(bf16[4,40,640]{2,1,0:T(8,128)(2,1)S(1)} %slice.59), channel_id=1, source_target_pairs={{0,1},{1,0},{2,3},{3,2},{4,5},{5,4},{6,7},{7,6},{8,9},{9,8},{10,11... | collective-permute-start | bytes 614408 | tf_op jit(solution)/shard_map/ppermute | solution.py:19
  75.4 9.5 %collective-permute-start.16 = (bf16[8,40,640]{2,1,0:T(8,128)(2,1)S(1)}, bf16[8,40,640]{2,1,0:T(8,128)(2,1)}, u32[]{:S(2)}, u32[]{:S(2)}) collective-permute-start(bf16[8,40,640]{2,1,0:T(8,128)(2,1)S(1)} %collective-permute-done.11.refs_2_), channel_id=1, source_target_pairs={{0,2},{2,0},{4,6},{6,4},{8,10},{10,8},{12,14},{14,12},{1,3},{3,1},... | collective-permute-start | bytes 1228808 | tf_op jit(solution)/shard_map/ppermute | solution.py:19
  75.4 9.2 %collective-permute-start.13 = (bf16[4,40,640]{2,1,0:T(8,128)(2,1)S(1)}, bf16[4,40,640]{2,1,0:T(8,128)(2,1)}, u32[]{:S(2)}, u32[]{:S(2)}) collective-permute-start(bf16[4,40,640]{2,1,0:T(8,128)(2,1)S(1)} %slice.60), channel_id=1, source_target_pairs={{0,16},{16,0},{1,17},{17,1},{2,18},{18,2},{3,19},{19,3},{4,20},{20... | collective-permute-start | bytes 614408 | tf_op jit(solution)/shard_map/ppermute | solution.py:19
  101.3 11.6 %collective-permute-start.20 = (bf16[2,4,40,640]{3,2,1,0:T(8,128)(2,1)S(1)}, bf16[2,4,40,640]{3,2,1,0:T(8,128)(2,1)S(1)}, u32[]{:S(2)}, u32[]{:S(2)}) collective-permute-start(bf16[2,4,40,640]{3,2,1,0:T(8,128)(2,1)S(1)} %slice_bitcast_fusion), channel_id=1, source_target_pairs={{0,16},{16,0},{1,17},{17,1},{2,18},{18,2},{3,19},{19,3},{4,20},{20... | collective-permute-start | bytes 1228808 | tf_op jit(solution)/shard_map/ppermute | solution.py:19
  107.7 17.3 %all-to-all-start.3 = ((bf16[8,40,640]{2,1,0:T(8,128)(2,1)}), bf16[8,40,640]{2,1,0:T(8,128)(2,1)S(1)}, u32[]{:S(2)}, u32[]{:S(2)}) async-start(bf16[8,40,640]{2,1,0:T(8,128)(2,1)} %shard_map.135), calls=%async_computation.3 | async-start | bytes 819200 | tf_op jit(solution)/shard_map/all_to_all | solution.py:548
  113.0 6.7 %collective-permute-start.21 = (bf16[4,40,640]{2,1,0:T(8,128)(2,1)S(1)}, bf16[4,40,640]{2,1,0:T(8,128)(2,1)S(1)}, u32[]{:S(2)}, u32[]{:S(2)}) collective-permute-start(bf16[4,40,640]{2,1,0:T(8,128)(2,1)S(1)} %slice_bitcast_fusion.1), channel_id=1, source_target_pairs={{0,1},{1,0},{2,3},{3,2},{4,5},{5,4},{6,7},{7,6},{8,9},{9,8},{10,11... | collective-permute-start | bytes 614408 | tf_op jit(solution)/shard_map/ppermute | solution.py:19
  130.3 5.6 %collective-permute-start.22 = (bf16[2,40,640]{2,1,0:T(8,128)(2,1)S(1)}, bf16[2,40,640]{2,1,0:T(8,128)(2,1)S(1)}, u32[]{:S(2)}, u32[]{:S(2)}) collective-permute-start(bf16[2,40,640]{2,1,0:T(8,128)(2,1)S(1)} %slice.67), channel_id=1, source_target_pairs={{0,8},{2,10},{4,12},{6,14},{8,0},{10,2},{12,4},{14,6},{1,9},{3,11}... | collective-permute-start | bytes 307208 | tf_op jit(solution)/shard_map/ppermute | solution.py:556
  (24 other events, 173.6 us)

commit v14 on v13

--- a/solution.py
+++ b/solution.py
@@ -555,15 +555,16 @@
         pairs = [(i, i ^ (2 * step)) for i in range(frames)]
         shares = add(shares[:step], lax.ppermute(shares[step:], "frame", pairs))
         step //= 2
+    small = jnp.sum(d_back[:, count : count + 3].astype(F32), axis=(0, 1))
+    d_back = d_back[:, :count].reshape(rows, cols, width)
+    mid_grad = (cot.astype(F32) + d_back.astype(F32)).astype(BF)
+
+    small, _ = lax.optimization_barrier((small, shares))
     by_plane = lax.ppermute(shares[1], "frame", planes)
     by_clip = swap(shares[0], "dp")
     by_both = swap_both(shares[1], "frame", 2)
     shares = shares[0].astype(F32) + by_plane.astype(F32)
     theirs = by_clip.astype(F32) + by_both.astype(F32)
-    small = jnp.sum(d_back[:, count : count + 3].astype(F32), axis=(0, 1))
-    d_back = d_back[:, :count].reshape(rows, cols, width)
-    mid_grad = (cot.astype(F32) + d_back.astype(F32)).astype(BF)
-
     small = small + swap(small, "tile")
     small = small + swap(small, "dp")
     if clips > 2:

time: 144 us -> 145 us (level)
    ppermute x1, waiting for transfers between devices: 3.13 us -> 6.51 us  [local(): shares = add(shares[:step], lax.ppermute(shares[step:], 'frame', pairs))]
    ppermute x23, waiting for transfers between devices: 26.7 us -> 24.1 us  [swap(): lax.ppermute(x, axis, [(i, i ^ 1) for i in range(lax.axis_size(axis))])]
  transfers between devices with their start and end apart: 32 -> 32, of which waited for: 20 -> 18; matrix products, arithmetic and copies ran while one was open for 6% -> 6% of each run, Pallas kernels for 13% -> 13%
where the time goes in v14:
time: 145 us; the launch traced here: 144 us
  waiting for transfers between devices  52.5 us (36%)
  starting transfers between devices  41.9 us (29%)
  Pallas kernels  31.6 us (22%)
  local copies, waits for them, and re-layouts  13.8 us (10%)
  other arithmetic  3.07 us (2%)
    pallas_call x9, Pallas kernels, call(): pl.pallas_call(kernel, out_shape=[jax.ShapeDtypeStruct(shape, dtype) for...  31.6 us
    ppermute x23, waiting for transfers between devices, swap(): lax.ppermute(x, axis, [(i, i ^ 1) for i in range(lax.axis_size(axis))])  24.1 us
    ppermute x23, starting transfers between devices, swap(): lax.ppermute(x, axis, [(i, i ^ 1) for i in range(lax.axis_size(axis))])  18.6 us
    all_to_all x1, waiting for transfers between devices, local(): conv_half = lax.all_to_all(mine, square, 0, 0, tiled=True)  12.5 us
    ppermute x1, waiting for transfers between devices, local(): shares = add(shares[:step], lax.ppermute(shares[step:], 'frame', pairs))  6.51 us
    unnamed x33, local copies, waits for them, and re-layouts  5.94 us
    all_to_all x1, waiting for transfers between devices, local(): d_back = lax.all_to_all(d_mid, 'frame', 0, 0, tiled=True)  5.15 us
    all_to_all x1, starting transfers between devices, local(): packed = lax.all_to_all(packed, 'frame', 0, 0, tiled=True)  4.88 us
  transfers between devices with their start and end apart: 32, of which 18 were waited for; matrix products, arithmetic and copies ran while one was open for 6% of the time, Pallas kernels for 13%

profile of v14, /device:TPU:0, one launch (start us, length us, event | category | flops | bytes accessed | tf_op | source)
XLA Modules:
  0.0 143.9 jit_solution(4938163776686361647)
XLA Ops:
  0.6 3.0 %collective-permute-start.1 = (bf16[288,640]{1,0:T(8,128)(2,1)}, bf16[288,640]{1,0:T(8,128)(2,1)S(1)}, u32[]{:S(2)}, u32[]{:S(2)}) collective-permute-start(bf16[288,640]{1,0:T(8,128)(2,1)} %bitcast.38), channel_id=1, source_target_pairs={{0,16},{16,0},{1,17},{17,1},{2,18},{18,2},{3,19},{19,3},{4,20},{20... | collective-permute-start | bytes 1105928 | tf_op jit(solution)/shard_map/ppermute | solution.py:19
  8.6 4.9 %all-to-all-start = ((bf16[8,56,640]{2,1,0:T(8,128)(2,1)}), bf16[8,56,640]{2,1,0:T(8,128)(2,1)S(1)}, u32[]{:S(2)}, u32[]{:S(2)}) async-start(bf16[8,56,640]{2,1,0:T(8,128)(2,1)} %shard_map.127), calls=%async_computation | async-start | bytes 1146880 | tf_op jit(solution)/shard_map/all_to_all | solution.py:437
  16.4 4.2 %collective-permute-done.2 = bf16[144,640]{1,0:T(8,128)(2,1)S(1)} collective-permute-done((bf16[144,640]{1,0:T(8,128)(2,1)S(1)}, bf16[144,640]{1,0:T(8,128)(2,1)S(1)}, u32[]{:S(2)}, u32[]{:S(2)}) %collective-permute-start.2) | collective-permute-done | bytes 184352 | tf_op jit(solution)/shard_map/ppermute | solution.py:19
  22.2 2.2 %copy.15 = bf16[4,3,40,3,80]{4,3,0,2,1:T(4,128)(2,1)} copy(bf16[4,3,40,3,80]{4,0,2,3,1:T(4,128)(2,1)} %bitcast.43) | data formatting | bytes 460800 | tf_op jit(solution)/shard_map/transpose | solution.py:449
  24.4 2.1 %reshape.49 = bf16[4,2,60,240]{3,0,2,1:T(4,128)(2,1)} reshape(bf16[4,3,40,3,80]{4,3,0,2,1:T(4,128)(2,1)} %copy.15) | data formatting | bytes 460800 | tf_op jit(solution)/shard_map/reshape | solution.py:450
  27.6 2.3 %all-to-all-done.cot_in = bf16[8,56,640]{2,1,0:T(8,128)(2,1)S(1)} async-done(((bf16[8,56,640]{2,1,0:T(8,128)(2,1)}), bf16[8,56,640]{2,1,0:T(8,128)(2,1)S(1)}, u32[]{:S(2)}, u32[]{:S(2)}) %all-to-all-start) | async-done | bytes 573472 | tf_op jit(solution)/shard_map/all_to_all | solution.py:437
  30.7 3.7 %all-to-all-start.1 = ((bf16[16,60,240]{2,1,0:T(8,128)(2,1)}), bf16[16,60,240]{2,1,0:T(8,128)(2,1)S(1)}, u32[]{:S(2)}, u32[]{:S(2)}) async-start(bf16[16,60,240]{2,1,0:T(8,128)(2,1)} %bitcast.42), calls=%async_computation.1 | async-start | bytes 1048576 | tf_op jit(solution)/shard_map/all_to_all | solution.py:454
  34.5 2.0 %collective-permute-start.8 = (bf16[8,20,640]{2,1,0:T(8,128)(2,1)S(1)}, bf16[8,20,640]{2,1,0:T(8,128)(2,1)S(1)}, u32[]{:S(2)}, u32[]{:S(2)}) collective-permute-start(bf16[8,20,640]{2,1,0:T(8,128)(2,1)S(1)} %slice.58.mine), channel_id=1, source_target_pairs={{0,4},{2,6},{4,0},{6,2},{8,12},{10,14},{12,8},{14,10},{1,5},{3,7},... | collective-permute-start | bytes 614408 | tf_op jit(solution)/shard_map/ppermute | solution.py:456
  36.5 12.5 %all-to-all-done.1.mine = bf16[16,60,240]{2,1,0:T(8,128)(2,1)S(1)} async-done(((bf16[16,60,240]{2,1,0:T(8,128)(2,1)}), bf16[16,60,240]{2,1,0:T(8,128)(2,1)S(1)}, u32[]{:S(2)}, u32[]{:S(2)}) %all-to-all-start.1) | async-done | bytes 460832 | tf_op jit(solution)/shard_map/all_to_all | solution.py:454
  49.0 1.8 %collective-permute-start.9 = (bf16[16,60,240]{2,1,0:T(8,128)(2,1)S(1)}, bf16[16,60,240]{2,1,0:T(8,128)(2,1)S(1)}, u32[]{:S(2)}, u32[]{:S(2)}) collective-permute-start(bf16[16,60,240]{2,1,0:T(8,128)(2,1)S(1)} %all-to-all-done.1.mine), channel_id=1, source_target_pairs={{0,4},{2,6},{4,0},{6,2},{8,12},{10,14},{12,8},{14,10},{1,5},{3,7},... | collective-permute-start | bytes 1382408 | tf_op jit(solution)/shard_map/ppermute | solution.py:457
  57.9 4.7 %shard_map.130 = (bf16[4,640,640]{2,1,0:T(8,128)(2,1)S(1)}, bf16[4,576,80]{2,1,0:T(8,128)(2,1)S(1)}) custom-call(s32[5]{0:T(128)S(1)} %stack.23.place, f32[1,640]{1,0:T(1,128)S(1)} %broadcast_in_dim.5.gain, bf16[288,640]{1,0:T(8,128)(2,1)S(1)} %bitcast.41, bf16[288,640]{1,0:T(8,128)(2,1)S(1)} %collective-permute-done.refs_1_, ...), custom_call_target="tpu_custom_call" | custom-call | tf_op jit(solution)/shard_map/pallas_call | solution.py:395
  64.0 5.1 %shard_map.131 = bf16[32,24,240]{2,1,0:T(8,128)(2,1)} custom-call(s32[5]{0:T(128)S(1)} %stack.23.place, bf16[3,640,240]{2,1,0:T(8,128)(2,1)S(1)} %bitcast.36, bf16[4,640,640]{2,1,0:T(8,128)(2,1)S(1)} %get-tuple-element.59.acts, bf16[4,576,80]{2,1,0:T(8,128)(2,1)S(1)} %get-tuple-element.60.kept), custom_call_target="tpu_custom_call" | custom-call | tf_op jit(solution)/shard_map/pallas_call | solution.py:395
  69.1 3.7 %all-to-all-start.2 = ((bf16[32,24,240]{2,1,0:T(8,128)(2,1)}), bf16[32,24,240]{2,1,0:T(8,128)(2,1)S(1)}, u32[]{:S(2)}, u32[]{:S(2)}) async-start(bf16[32,24,240]{2,1,0:T(8,128)(2,1)} %shard_map.131), calls=%async_computation.2 | async-start | bytes 786432 | tf_op jit(solution)/shard_map/all_to_all | solution.py:493
  73.6 1.8 %collective-permute-start.12 = (bf16[4,40,640]{2,1,0:T(8,128)(2,1)S(1)}, bf16[4,40,640]{2,1,0:T(8,128)(2,1)S(1)}, u32[]{:S(2)}, u32[]{:S(2)}) collective-permute-start(bf16[4,40,640]{2,1,0:T(8,128)(2,1)S(1)} %slice.59), channel_id=1, source_target_pairs={{0,1},{1,0},{2,3},{3,2},{4,5},{5,4},{6,7},{7,6},{8,9},{9,8},{10,11... | collective-permute-start | bytes 614408 | tf_op jit(solution)/shard_map/ppermute | solution.py:19
  76.9 6.6 %collective-permute-done.12.refs_3_ = bf16[4,40,640]{2,1,0:T(8,128)(2,1)S(1)} collective-permute-done((bf16[4,40,640]{2,1,0:T(8,128)(2,1)S(1)}, bf16[4,40,640]{2,1,0:T(8,128)(2,1)S(1)}, u32[]{:S(2)}, u32[]{:S(2)}) %collective-permute-start.12) | collective-permute-done | bytes 204832 | tf_op jit(solution)/shard_map/ppermute | solution.py:19
  88.0 10.6 %shard_map.133 = (bf16[2,2,4,40,640]{4,3,2,1,0:T(8,128)(2,1)S(1)}, bf16[2,2,4,40,640]{4,3,2,1,0:T(8,128)(2,1)S(1)}, f32[1,128]{1,0:T(1,128)S(1)}, f32[320,128]{1...) custom-call(s32[5]{0:T(128)S(1)} %stack.23.place, ...), custom_call_target="tpu_custom_call" | custom-call | tf_op jit(solution)/shard_map/pallas_call | solution.py:395
  98.9 1.9 %shard_map.134 = (f32[320,640]{1,0:T(8,128)S(1)}, f32[320,640]{1,0:T(8,128)S(1)}) custom-call(f32[320,128]{1,0:T(8,128)S(1)} %get-tuple-element.77.d_raw, f32[320,640]{1,0:T(8,128)S(1)} %get-tuple-element.78.q_hat, f32[320,640]{1,0:T(8,128)S(1)} %get-tuple-element.79.k_hat, f32[1,640]{1,0:T(1,128)S(1)} %broadcast_in_dim_tile.9.qgain, ...), custom_call_target="tpu_custom_call" | custom-call | tf_op jit(solution)/shard_map/pallas_call | solution.py:395
  102.9 4.8 %shard_map.135 = bf16[8,40,640]{2,1,0:T(8,128)(2,1)} custom-call(f32[320,640]{1,0:T(8,128)S(1)} %get-tuple-element.82.d_qn, f32[320,640]{1,0:T(8,128)S(1)} %get-tuple-element.83.d_kn, f32[320,640]{1,0:T(8,128)S(1)} %get-tuple-element.78.q_hat, f32[320,640]{1,0:T(8,128)S(1)} %get-tuple-element.79.k_hat, f32[320,128]{1,0:T(8,128)S(1)} %get-tuple-element.84.q_rstd, ...), custom_call_target="tpu_custom_call" | custom-call | tf_op jit(solution)/shard_map/pallas_call | solution.py:395
  107.7 4.4 %all-to-all-start.3 = ((bf16[8,40,640]{2,1,0:T(8,128)(2,1)}), bf16[8,40,640]{2,1,0:T(8,128)(2,1)S(1)}, u32[]{:S(2)}, u32[]{:S(2)}) async-start(bf16[8,40,640]{2,1,0:T(8,128)(2,1)} %shard_map.135), calls=%async_computation.3 | async-start | bytes 819200 | tf_op jit(solution)/shard_map/all_to_all | solution.py:548
  114.0 5.8 %collective-permute-done.21 = bf16[4,40,640]{2,1,0:T(8,128)(2,1)S(1)} collective-permute-done((bf16[4,40,640]{2,1,0:T(8,128)(2,1)S(1)}, bf16[4,40,640]{2,1,0:T(8,128)(2,1)S(1)}, u32[]{:S(2)}, u32[]{:S(2)}) %collective-permute-start.21) | collective-permute-done | bytes 204832 | tf_op jit(solution)/shard_map/ppermute | solution.py:19
  119.8 5.2 %all-to-all-done.3 = bf16[8,40,640]{2,1,0:T(8,128)(2,1)S(1)} async-done(((bf16[8,40,640]{2,1,0:T(8,128)(2,1)}), bf16[8,40,640]{2,1,0:T(8,128)(2,1)S(1)}, u32[]{:S(2)}, u32[]{:S(2)}) %all-to-all-start.3) | async-done | bytes 409632 | tf_op jit(solution)/shard_map/all_to_all | solution.py:548
  125.3 6.5 %collective-permute-done.22 = bf16[2,40,640]{2,1,0:T(8,128)(2,1)S(1)} collective-permute-done((bf16[2,40,640]{2,1,0:T(8,128)(2,1)S(1)}, bf16[2,40,640]{2,1,0:T(8,128)(2,1)S(1)}, u32[]{:S(2)}, u32[]{:S(2)}) %collective-permute-start.22) | collective-permute-done | bytes 102432 | tf_op jit(solution)/shard_map/ppermute | solution.py:556
  133.5 2.0 %collective-permute-done.26 = f32[640]{0:T(1024)S(1)} collective-permute-done((f32[640]{0:T(1024)S(1)}, f32[640]{0:T(1024)S(1)}, u32[]{:S(2)}, u32[]{:S(2)}) %collective-permute-start.26) | collective-permute-done | bytes 2592 | tf_op jit(solution)/shard_map/ppermute | solution.py:19
  136.4 2.7 %collective-permute-start.25 = (bf16[40,640]{1,0:T(8,128)(2,1)S(1)}, bf16[40,640]{1,0:T(8,128)(2,1)S(1)}, u32[]{:S(2)}, u32[]{:S(2)}) collective-permute-start(bf16[40,640]{1,0:T(8,128)(2,1)S(1)} %get-tuple-element.95), channel_id=1, source_target_pairs={{0,20},{2,22},{4,16},{6,18},{8,28},{10,30},{12,24},{14,26},{16,4},... | collective-permute-start | bytes 153608 | tf_op jit(solution)/shard_map/ppermute | solution.py:29
  (120 shorter events, 38.3 us)
Async XLA Ops:
  0.6 12.8 %collective-permute-start.1 = (bf16[288,640]{1,0:T(8,128)(2,1)}, bf16[288,640]{1,0:T(8,128)(2,1)S(1)}, u32[]{:S(2)}, u32[]{:S(2)}) collective-permute-start(bf16[288,640]{1,0:T(8,128)(2,1)} %bitcast.38), channel_id=1, source_target_pairs={{0,16},{16,0},{1,17},{17,1},{2,18},{18,2},{3,19},{19,3},{4,20},{20... | collective-permute-start | bytes 1105928 | tf_op jit(solution)/shard_map/ppermute | solution.py:19
  3.7 10.7 %collective-permute-start = (bf16[288,640]{1,0:T(8,128)(2,1)}, bf16[288,640]{1,0:T(8,128)(2,1)S(1)}, u32[]{:S(2)}, u32[]{:S(2)}) collective-permute-start(bf16[288,640]{1,0:T(8,128)(2,1)} %bitcast.39), channel_id=1, source_target_pairs={{0,1},{1,0},{2,3},{3,2},{4,5},{5,4},{6,7},{7,6},{8,9},{9,8},{10,11... | collective-permute-start | bytes 1105928 | tf_op jit(solution)/shard_map/ppermute | solution.py:19
  8.6 21.3 %all-to-all-start = ((bf16[8,56,640]{2,1,0:T(8,128)(2,1)}), bf16[8,56,640]{2,1,0:T(8,128)(2,1)S(1)}, u32[]{:S(2)}, u32[]{:S(2)}) async-start(bf16[8,56,640]{2,1,0:T(8,128)(2,1)} %shard_map.127), calls=%async_computation | async-start | bytes 1146880 | tf_op jit(solution)/shard_map/all_to_all | solution.py:437
  13.5 7.1 %collective-permute-start.2 = (bf16[144,640]{1,0:T(8,128)(2,1)S(1)}, bf16[144,640]{1,0:T(8,128)(2,1)S(1)}, u32[]{:S(2)}, u32[]{:S(2)}) collective-permute-start(bf16[144,640]{1,0:T(8,128)(2,1)S(1)} %slice.74), channel_id=1, source_target_pairs={{0,1},{1,0},{2,3},{3,2},{4,5},{5,4},{6,7},{7,6},{8,9},{9,8},{10,11... | collective-permute-start | bytes 552968 | tf_op jit(solution)/shard_map/ppermute | solution.py:19
  14.3 6.6 %collective-permute-start.3 = (bf16[144,640]{1,0:T(8,128)(2,1)S(1)}, bf16[144,640]{1,0:T(8,128)(2,1)S(1)}, u32[]{:S(2)}, u32[]{:S(2)}) collective-permute-start(bf16[144,640]{1,0:T(8,128)(2,1)S(1)} %slice.75), channel_id=1, source_target_pairs={{0,16},{16,0},{1,17},{17,1},{2,18},{18,2},{3,19},{19,3},{4,20},{20... | collective-permute-start | bytes 552968 | tf_op jit(solution)/shard_map/ppermute | solution.py:19
  15.9 11.6 %collective-permute-start.4 = (bf16[288,640]{1,0:T(8,128)(2,1)S(1)}, bf16[288,640]{1,0:T(8,128)(2,1)S(1)}, u32[]{:S(2)}, u32[]{:S(2)}) collective-permute-start(bf16[288,640]{1,0:T(8,128)(2,1)S(1)} %bitcast.40), channel_id=1, source_target_pairs={{0,2},{2,0},{4,6},{6,4},{8,10},{10,8},{12,14},{14,12},{1,3},{3,1},... | collective-permute-start | bytes 1105928 | tf_op jit(solution)/shard_map/ppermute | solution.py:19
  15.9 11.6 %collective-permute-start.5 = (bf16[288,640]{1,0:T(8,128)(2,1)S(1)}, bf16[288,640]{1,0:T(8,128)(2,1)S(1)}, u32[]{:S(2)}, u32[]{:S(2)}) collective-permute-start(bf16[288,640]{1,0:T(8,128)(2,1)S(1)} %collective-permute-done.refs_1_), channel_id=1, source_target_pairs={{0,2},{2,0},{4,6},{6,4},{8,10},{10,8},{12,14},{14,12},{1,3},{3,1},... | collective-permute-start | bytes 1105928 | tf_op jit(solution)/shard_map/ppermute | solution.py:19
  16.4 11.1 %collective-permute-start.6 = (bf16[288,640]{1,0:T(8,128)(2,1)S(1)}, bf16[288,640]{1,0:T(8,128)(2,1)}, u32[]{:S(2)}, u32[]{:S(2)}) collective-permute-start(bf16[288,640]{1,0:T(8,128)(2,1)S(1)} %collective-permute-done.1.refs_2_), channel_id=1, source_target_pairs={{0,2},{2,0},{4,6},{6,4},{8,10},{10,8},{12,14},{14,12},{1,3},{3,1},... | collective-permute-start | bytes 1105928 | tf_op jit(solution)/shard_map/ppermute | solution.py:19
  21.0 6.6 %collective-permute-start.7 = (bf16[288,640]{1,0:T(8,128)(2,1)S(1)}, bf16[288,640]{1,0:T(8,128)(2,1)}, u32[]{:S(2)}, u32[]{:S(2)}) collective-permute-start(bf16[288,640]{1,0:T(8,128)(2,1)S(1)} %constant_dynamic-update-slice_fusion.refs_3_), channel_id=1, source_target_pairs={{0,2},{2,0},{4,6},{6,4},{8,10},{10,8},{12,14},{14,12},{1,3},{3,1},... | collective-permute-start | bytes 1105928 | tf_op jit(solution)/shard_map/ppermute | solution.py:19
  30.7 18.2 %all-to-all-start.1 = ((bf16[16,60,240]{2,1,0:T(8,128)(2,1)}), bf16[16,60,240]{2,1,0:T(8,128)(2,1)S(1)}, u32[]{:S(2)}, u32[]{:S(2)}) async-start(bf16[16,60,240]{2,1,0:T(8,128)(2,1)} %bitcast.42), calls=%async_computation.1 | async-start | bytes 1048576 | tf_op jit(solution)/shard_map/all_to_all | solution.py:454
  34.5 16.8 %collective-permute-start.8 = (bf16[8,20,640]{2,1,0:T(8,128)(2,1)S(1)}, bf16[8,20,640]{2,1,0:T(8,128)(2,1)S(1)}, u32[]{:S(2)}, u32[]{:S(2)}) collective-permute-start(bf16[8,20,640]{2,1,0:T(8,128)(2,1)S(1)} %slice.58.mine), channel_id=1, source_target_pairs={{0,4},{2,6},{4,0},{6,2},{8,12},{10,14},{12,8},{14,10},{1,5},{3,7},... | collective-permute-start | bytes 614408 | tf_op jit(solution)/shard_map/ppermute | solution.py:456
  49.0 14.4 %collective-permute-start.9 = (bf16[16,60,240]{2,1,0:T(8,128)(2,1)S(1)}, bf16[16,60,240]{2,1,0:T(8,128)(2,1)S(1)}, u32[]{:S(2)}, u32[]{:S(2)}) collective-permute-start(bf16[16,60,240]{2,1,0:T(8,128)(2,1)S(1)} %all-to-all-done.1.mine), channel_id=1, source_target_pairs={{0,4},{2,6},{4,0},{6,2},{8,12},{10,14},{12,8},{14,10},{1,5},{3,7},... | collective-permute-start | bytes 1382408 | tf_op jit(solution)/shard_map/ppermute | solution.py:457
  51.9 17.2 %collective-permute-start.10 = (bf16[8,40,640]{2,1,0:T(8,128)(2,1)S(1)}, bf16[8,40,640]{2,1,0:T(8,128)(2,1)S(1)}, u32[]{:S(2)}, u32[]{:S(2)}) collective-permute-start(bf16[8,40,640]{2,1,0:T(8,128)(2,1)S(1)} %shard_map.128.refs_0_), channel_id=1, source_target_pairs={{0,1},{1,0},{2,3},{3,2},{4,5},{5,4},{6,7},{7,6},{8,9},{9,8},{10,11... | collective-permute-start | bytes 1228808 | tf_op jit(solution)/shard_map/ppermute | solution.py:19
  53.4 15.7 %collective-permute-start.11 = (bf16[8,40,640]{2,1,0:T(8,128)(2,1)S(1)}, bf16[8,40,640]{2,1,0:T(8,128)(2,1)S(1)}, u32[]{:S(2)}, u32[]{:S(2)}) collective-permute-start(bf16[8,40,640]{2,1,0:T(8,128)(2,1)S(1)} %shard_map.128.refs_0_), channel_id=1, source_target_pairs={{0,16},{16,0},{1,17},{17,1},{2,18},{18,2},{3,19},{19,3},{4,20},{20... | collective-permute-start | bytes 1228808 | tf_op jit(solution)/shard_map/ppermute | solution.py:19
  69.1 17.3 %all-to-all-start.2 = ((bf16[32,24,240]{2,1,0:T(8,128)(2,1)}), bf16[32,24,240]{2,1,0:T(8,128)(2,1)S(1)}, u32[]{:S(2)}, u32[]{:S(2)}) async-start(bf16[32,24,240]{2,1,0:T(8,128)(2,1)} %shard_map.131), calls=%async_computation.2 | async-start | bytes 786432 | tf_op jit(solution)/shard_map/all_to_all | solution.py:493
  72.9 12.0 %collective-permute-start.14 = (bf16[8,40,640]{2,1,0:T(8,128)(2,1)S(1)}, bf16[8,40,640]{2,1,0:T(8,128)(2,1)S(1)}, u32[]{:S(2)}, u32[]{:S(2)}) collective-permute-start(bf16[8,40,640]{2,1,0:T(8,128)(2,1)S(1)} %shard_map.128.refs_0_), channel_id=1, source_target_pairs={{0,2},{2,0},{4,6},{6,4},{8,10},{10,8},{12,14},{14,12},{1,3},{3,1},... | collective-permute-start | bytes 1228808 | tf_op jit(solution)/shard_map/ppermute | solution.py:19
  73.2 11.7 %collective-permute-start.15 = (bf16[8,40,640]{2,1,0:T(8,128)(2,1)S(1)}, bf16[8,40,640]{2,1,0:T(8,128)(2,1)}, u32[]{:S(2)}, u32[]{:S(2)}) collective-permute-start(bf16[8,40,640]{2,1,0:T(8,128)(2,1)S(1)} %collective-permute-done.10.refs_1_), channel_id=1, source_target_pairs={{0,2},{2,0},{4,6},{6,4},{8,10},{10,8},{12,14},{14,12},{1,3},{3,1},... | collective-permute-start | bytes 1228808 | tf_op jit(solution)/shard_map/ppermute | solution.py:19
  73.6 9.9 %collective-permute-start.12 = (bf16[4,40,640]{2,1,0:T(8,128)(2,1)S(1)}, bf16[4,40,640]{2,1,0:T(8,128)(2,1)S(1)}, u32[]{:S(2)}, u32[]{:S(2)}) collective-permute-start(bf16[4,40,640]{2,1,0:T(8,128)(2,1)S(1)} %slice.59), channel_id=1, source_target_pairs={{0,1},{1,0},{2,3},{3,2},{4,5},{5,4},{6,7},{7,6},{8,9},{9,8},{10,11... | collective-permute-start | bytes 614408 | tf_op jit(solution)/shard_map/ppermute | solution.py:19
  75.4 9.5 %collective-permute-start.16 = (bf16[8,40,640]{2,1,0:T(8,128)(2,1)S(1)}, bf16[8,40,640]{2,1,0:T(8,128)(2,1)}, u32[]{:S(2)}, u32[]{:S(2)}) collective-permute-start(bf16[8,40,640]{2,1,0:T(8,128)(2,1)S(1)} %collective-permute-done.11.refs_2_), channel_id=1, source_target_pairs={{0,2},{2,0},{4,6},{6,4},{8,10},{10,8},{12,14},{14,12},{1,3},{3,1},... | collective-permute-start | bytes 1228808 | tf_op jit(solution)/shard_map/ppermute | solution.py:19
  75.4 9.2 %collective-permute-start.13 = (bf16[4,40,640]{2,1,0:T(8,128)(2,1)S(1)}, bf16[4,40,640]{2,1,0:T(8,128)(2,1)}, u32[]{:S(2)}, u32[]{:S(2)}) collective-permute-start(bf16[4,40,640]{2,1,0:T(8,128)(2,1)S(1)} %slice.60), channel_id=1, source_target_pairs={{0,16},{16,0},{1,17},{17,1},{2,18},{18,2},{3,19},{19,3},{4,20},{20... | collective-permute-start | bytes 614408 | tf_op jit(solution)/shard_map/ppermute | solution.py:19
  101.3 11.6 %collective-permute-start.20 = (bf16[2,4,40,640]{3,2,1,0:T(8,128)(2,1)S(1)}, bf16[2,4,40,640]{3,2,1,0:T(8,128)(2,1)S(1)}, u32[]{:S(2)}, u32[]{:S(2)}) collective-permute-start(bf16[2,4,40,640]{3,2,1,0:T(8,128)(2,1)S(1)} %slice_bitcast_fusion), channel_id=1, source_target_pairs={{0,16},{16,0},{1,17},{17,1},{2,18},{18,2},{3,19},{19,3},{4,20},{20... | collective-permute-start | bytes 1228808 | tf_op jit(solution)/shard_map/ppermute | solution.py:19
  107.7 17.3 %all-to-all-start.3 = ((bf16[8,40,640]{2,1,0:T(8,128)(2,1)}), bf16[8,40,640]{2,1,0:T(8,128)(2,1)S(1)}, u32[]{:S(2)}, u32[]{:S(2)}) async-start(bf16[8,40,640]{2,1,0:T(8,128)(2,1)} %shard_map.135), calls=%async_computation.3 | async-start | bytes 819200 | tf_op jit(solution)/shard_map/all_to_all | solution.py:548
  113.0 6.7 %collective-permute-start.21 = (bf16[4,40,640]{2,1,0:T(8,128)(2,1)S(1)}, bf16[4,40,640]{2,1,0:T(8,128)(2,1)S(1)}, u32[]{:S(2)}, u32[]{:S(2)}) collective-permute-start(bf16[4,40,640]{2,1,0:T(8,128)(2,1)S(1)} %slice_bitcast_fusion.1), channel_id=1, source_target_pairs={{0,1},{1,0},{2,3},{3,2},{4,5},{5,4},{6,7},{7,6},{8,9},{9,8},{10,11... | collective-permute-start | bytes 614408 | tf_op jit(solution)/shard_map/ppermute | solution.py:19
  125.1 6.6 %collective-permute-start.22 = (bf16[2,40,640]{2,1,0:T(8,128)(2,1)S(1)}, bf16[2,40,640]{2,1,0:T(8,128)(2,1)S(1)}, u32[]{:S(2)}, u32[]{:S(2)}) collective-permute-start(bf16[2,40,640]{2,1,0:T(8,128)(2,1)S(1)} %slice.67), channel_id=1, source_target_pairs={{0,8},{2,10},{4,12},{6,14},{8,0},{10,2},{12,4},{14,6},{1,9},{3,11}... | collective-permute-start | bytes 307208 | tf_op jit(solution)/shard_map/ppermute | solution.py:556
  (24 other events, 172.1 us)

commit v15 on v14

--- a/solution.py
+++ b/solution.py
@@ -559,13 +559,13 @@
     d_back = d_back[:, :count].reshape(rows, cols, width)
     mid_grad = (cot.astype(F32) + d_back.astype(F32)).astype(BF)
 
+    small = small + swap(small, "tile")
     small, _ = lax.optimization_barrier((small, shares))
     by_plane = lax.ppermute(shares[1], "frame", planes)
     by_clip = swap(shares[0], "dp")
     by_both = swap_both(shares[1], "frame", 2)
     shares = shares[0].astype(F32) + by_plane.astype(F32)
     theirs = by_clip.astype(F32) + by_both.astype(F32)
-    small = small + swap(small, "tile")
     small = small + swap(small, "dp")
     if clips > 2:
         same_clip = [[i for i in range(clips) if i % 2 == c] for c in (0, 1)]

time: 145 us -> 141 us (0.972)
  waiting for transfers between devices: 52.5 us -> 48.9 us
    ppermute x1, waiting for transfers between devices: 6.51 us -> 2.88 us  [local(): shares = add(shares[:step], lax.ppermute(shares[step:], 'frame', pairs))]
  transfers between devices with their start and end apart: 32 -> 32, of which waited for: 18 -> 18; matrix products, arithmetic and copies ran while one was open for 6% -> 6% of each run, Pallas kernels for 13% -> 14%
where the time goes in v15:
time: 141 us; the launch traced here: 140 us
  waiting for transfers between devices  48.9 us (35%)
  starting transfers between devices  42 us (30%)
  Pallas kernels  31.6 us (22%)
  local copies, waits for them, and re-layouts  13.8 us (10%)
  other arithmetic  3.07 us (2%)
    pallas_call x9, Pallas kernels, call(): pl.pallas_call(kernel, out_shape=[jax.ShapeDtypeStruct(shape, dtype) for...  31.6 us
    ppermute x23, waiting for transfers between devices, swap(): lax.ppermute(x, axis, [(i, i ^ 1) for i in range(lax.axis_size(axis))])  24 us
    ppermute x23, starting transfers between devices, swap(): lax.ppermute(x, axis, [(i, i ^ 1) for i in range(lax.axis_size(axis))])  18.7 us
    all_to_all x1, waiting for transfers between devices, local(): conv_half = lax.all_to_all(mine, square, 0, 0, tiled=True)  12.5 us
    unnamed x33, local copies, waits for them, and re-layouts  5.94 us
    all_to_all x1, waiting for transfers between devices, local(): d_back = lax.all_to_all(d_mid, 'frame', 0, 0, tiled=True)  5.15 us
    all_to_all x1, starting transfers between devices, local(): packed = lax.all_to_all(packed, 'frame', 0, 0, tiled=True)  4.88 us
    all_to_all x1, starting transfers between devices, local(): d_back = lax.all_to_all(d_mid, 'frame', 0, 0, tiled=True)  4.35 us
  transfers between devices with their start and end apart: 32, of which 18 were waited for; matrix products, arithmetic and copies ran while one was open for 6% of the time, Pallas kernels for 14%

profile of v15, /device:TPU:0, one launch (start us, length us, event | category | flops | bytes accessed | tf_op | source)
XLA Modules:
  0.0 140.3 jit_solution(9353596712738701754)
XLA Ops:
  0.6 3.0 %collective-permute-start.1 = (bf16[288,640]{1,0:T(8,128)(2,1)}, bf16[288,640]{1,0:T(8,128)(2,1)S(1)}, u32[]{:S(2)}, u32[]{:S(2)}) collective-permute-start(bf16[288,640]{1,0:T(8,128)(2,1)} %bitcast.38), channel_id=1, source_target_pairs={{0,16},{16,0},{1,17},{17,1},{2,18},{18,2},{3,19},{19,3},{4,20},{20... | collective-permute-start | bytes 1105928 | tf_op jit(solution)/shard_map/ppermute | solution.py:19
  8.6 4.9 %all-to-all-start = ((bf16[8,56,640]{2,1,0:T(8,128)(2,1)}), bf16[8,56,640]{2,1,0:T(8,128)(2,1)S(1)}, u32[]{:S(2)}, u32[]{:S(2)}) async-start(bf16[8,56,640]{2,1,0:T(8,128)(2,1)} %shard_map.127), calls=%async_computation | async-start | bytes 1146880 | tf_op jit(solution)/shard_map/all_to_all | solution.py:437
  16.4 4.2 %collective-permute-done.2 = bf16[144,640]{1,0:T(8,128)(2,1)S(1)} collective-permute-done((bf16[144,640]{1,0:T(8,128)(2,1)S(1)}, bf16[144,640]{1,0:T(8,128)(2,1)S(1)}, u32[]{:S(2)}, u32[]{:S(2)}) %collective-permute-start.2) | collective-permute-done | bytes 184352 | tf_op jit(solution)/shard_map/ppermute | solution.py:19
  22.2 2.2 %copy.15 = bf16[4,3,40,3,80]{4,3,0,2,1:T(4,128)(2,1)} copy(bf16[4,3,40,3,80]{4,0,2,3,1:T(4,128)(2,1)} %bitcast.43) | data formatting | bytes 460800 | tf_op jit(solution)/shard_map/transpose | solution.py:449
  24.4 2.1 %reshape.49 = bf16[4,2,60,240]{3,0,2,1:T(4,128)(2,1)} reshape(bf16[4,3,40,3,80]{4,3,0,2,1:T(4,128)(2,1)} %copy.15) | data formatting | bytes 460800 | tf_op jit(solution)/shard_map/reshape | solution.py:450
  27.6 2.3 %all-to-all-done.cot_in = bf16[8,56,640]{2,1,0:T(8,128)(2,1)S(1)} async-done(((bf16[8,56,640]{2,1,0:T(8,128)(2,1)}), bf16[8,56,640]{2,1,0:T(8,128)(2,1)S(1)}, u32[]{:S(2)}, u32[]{:S(2)}) %all-to-all-start) | async-done | bytes 573472 | tf_op jit(solution)/shard_map/all_to_all | solution.py:437
  30.7 3.7 %all-to-all-start.1 = ((bf16[16,60,240]{2,1,0:T(8,128)(2,1)}), bf16[16,60,240]{2,1,0:T(8,128)(2,1)S(1)}, u32[]{:S(2)}, u32[]{:S(2)}) async-start(bf16[16,60,240]{2,1,0:T(8,128)(2,1)} %bitcast.42), calls=%async_computation.1 | async-start | bytes 1048576 | tf_op jit(solution)/shard_map/all_to_all | solution.py:454
  34.5 2.0 %collective-permute-start.8 = (bf16[8,20,640]{2,1,0:T(8,128)(2,1)S(1)}, bf16[8,20,640]{2,1,0:T(8,128)(2,1)S(1)}, u32[]{:S(2)}, u32[]{:S(2)}) collective-permute-start(bf16[8,20,640]{2,1,0:T(8,128)(2,1)S(1)} %slice.58.mine), channel_id=1, source_target_pairs={{0,4},{2,6},{4,0},{6,2},{8,12},{10,14},{12,8},{14,10},{1,5},{3,7},... | collective-permute-start | bytes 614408 | tf_op jit(solution)/shard_map/ppermute | solution.py:456
  36.5 12.5 %all-to-all-done.1.mine = bf16[16,60,240]{2,1,0:T(8,128)(2,1)S(1)} async-done(((bf16[16,60,240]{2,1,0:T(8,128)(2,1)}), bf16[16,60,240]{2,1,0:T(8,128)(2,1)S(1)}, u32[]{:S(2)}, u32[]{:S(2)}) %all-to-all-start.1) | async-done | bytes 460832 | tf_op jit(solution)/shard_map/all_to_all | solution.py:454
  49.0 1.8 %collective-permute-start.9 = (bf16[16,60,240]{2,1,0:T(8,128)(2,1)S(1)}, bf16[16,60,240]{2,1,0:T(8,128)(2,1)S(1)}, u32[]{:S(2)}, u32[]{:S(2)}) collective-permute-start(bf16[16,60,240]{2,1,0:T(8,128)(2,1)S(1)} %all-to-all-done.1.mine), channel_id=1, source_target_pairs={{0,4},{2,6},{4,0},{6,2},{8,12},{10,14},{12,8},{14,10},{1,5},{3,7},... | collective-permute-start | bytes 1382408 | tf_op jit(solution)/shard_map/ppermute | solution.py:457
  57.9 4.7 %shard_map.130 = (bf16[4,640,640]{2,1,0:T(8,128)(2,1)S(1)}, bf16[4,576,80]{2,1,0:T(8,128)(2,1)S(1)}) custom-call(s32[5]{0:T(128)S(1)} %stack.23.place, f32[1,640]{1,0:T(1,128)S(1)} %broadcast_in_dim.5.gain, bf16[288,640]{1,0:T(8,128)(2,1)S(1)} %bitcast.41, bf16[288,640]{1,0:T(8,128)(2,1)S(1)} %collective-permute-done.refs_1_, ...), custom_call_target="tpu_custom_call" | custom-call | tf_op jit(solution)/shard_map/pallas_call | solution.py:395
  64.0 5.1 %shard_map.131 = bf16[32,24,240]{2,1,0:T(8,128)(2,1)} custom-call(s32[5]{0:T(128)S(1)} %stack.23.place, bf16[3,640,240]{2,1,0:T(8,128)(2,1)S(1)} %bitcast.36, bf16[4,640,640]{2,1,0:T(8,128)(2,1)S(1)} %get-tuple-element.59.acts, bf16[4,576,80]{2,1,0:T(8,128)(2,1)S(1)} %get-tuple-element.60.kept), custom_call_target="tpu_custom_call" | custom-call | tf_op jit(solution)/shard_map/pallas_call | solution.py:395
  69.1 3.7 %all-to-all-start.2 = ((bf16[32,24,240]{2,1,0:T(8,128)(2,1)}), bf16[32,24,240]{2,1,0:T(8,128)(2,1)S(1)}, u32[]{:S(2)}, u32[]{:S(2)}) async-start(bf16[32,24,240]{2,1,0:T(8,128)(2,1)} %shard_map.131), calls=%async_computation.2 | async-start | bytes 786432 | tf_op jit(solution)/shard_map/all_to_all | solution.py:493
  73.6 1.8 %collective-permute-start.12 = (bf16[4,40,640]{2,1,0:T(8,128)(2,1)S(1)}, bf16[4,40,640]{2,1,0:T(8,128)(2,1)S(1)}, u32[]{:S(2)}, u32[]{:S(2)}) collective-permute-start(bf16[4,40,640]{2,1,0:T(8,128)(2,1)S(1)} %slice.59), channel_id=1, source_target_pairs={{0,1},{1,0},{2,3},{3,2},{4,5},{5,4},{6,7},{7,6},{8,9},{9,8},{10,11... | collective-permute-start | bytes 614408 | tf_op jit(solution)/shard_map/ppermute | solution.py:19
  76.9 6.6 %collective-permute-done.12.refs_3_ = bf16[4,40,640]{2,1,0:T(8,128)(2,1)S(1)} collective-permute-done((bf16[4,40,640]{2,1,0:T(8,128)(2,1)S(1)}, bf16[4,40,640]{2,1,0:T(8,128)(2,1)S(1)}, u32[]{:S(2)}, u32[]{:S(2)}) %collective-permute-start.12) | collective-permute-done | bytes 204832 | tf_op jit(solution)/shard_map/ppermute | solution.py:19
  88.0 10.6 %shard_map.133 = (bf16[2,2,4,40,640]{4,3,2,1,0:T(8,128)(2,1)S(1)}, bf16[2,2,4,40,640]{4,3,2,1,0:T(8,128)(2,1)S(1)}, f32[1,128]{1,0:T(1,128)S(1)}, f32[320,128]{1...) custom-call(s32[5]{0:T(128)S(1)} %stack.23.place, ...), custom_call_target="tpu_custom_call" | custom-call | tf_op jit(solution)/shard_map/pallas_call | solution.py:395
  98.9 1.9 %shard_map.134 = (f32[320,640]{1,0:T(8,128)S(1)}, f32[320,640]{1,0:T(8,128)S(1)}) custom-call(f32[320,128]{1,0:T(8,128)S(1)} %get-tuple-element.77.d_raw, f32[320,640]{1,0:T(8,128)S(1)} %get-tuple-element.78.q_hat, f32[320,640]{1,0:T(8,128)S(1)} %get-tuple-element.79.k_hat, f32[1,640]{1,0:T(1,128)S(1)} %broadcast_in_dim_tile.9.qgain, ...), custom_call_target="tpu_custom_call" | custom-call | tf_op jit(solution)/shard_map/pallas_call | solution.py:395
  102.9 4.8 %shard_map.135 = bf16[8,40,640]{2,1,0:T(8,128)(2,1)} custom-call(f32[320,640]{1,0:T(8,128)S(1)} %get-tuple-element.82.d_qn, f32[320,640]{1,0:T(8,128)S(1)} %get-tuple-element.83.d_kn, f32[320,640]{1,0:T(8,128)S(1)} %get-tuple-element.78.q_hat, f32[320,640]{1,0:T(8,128)S(1)} %get-tuple-element.79.k_hat, f32[320,128]{1,0:T(8,128)S(1)} %get-tuple-element.84.q_rstd, ...), custom_call_target="tpu_custom_call" | custom-call | tf_op jit(solution)/shard_map/pallas_call | solution.py:395
  107.7 4.4 %all-to-all-start.3 = ((bf16[8,40,640]{2,1,0:T(8,128)(2,1)}), bf16[8,40,640]{2,1,0:T(8,128)(2,1)S(1)}, u32[]{:S(2)}, u32[]{:S(2)}) async-start(bf16[8,40,640]{2,1,0:T(8,128)(2,1)} %shard_map.135), calls=%async_computation.3 | async-start | bytes 819200 | tf_op jit(solution)/shard_map/all_to_all | solution.py:548
  114.0 5.8 %collective-permute-done.21 = bf16[4,40,640]{2,1,0:T(8,128)(2,1)S(1)} collective-permute-done((bf16[4,40,640]{2,1,0:T(8,128)(2,1)S(1)}, bf16[4,40,640]{2,1,0:T(8,128)(2,1)S(1)}, u32[]{:S(2)}, u32[]{:S(2)}) %collective-permute-start.21) | collective-permute-done | bytes 204832 | tf_op jit(solution)/shard_map/ppermute | solution.py:19
  119.8 5.2 %all-to-all-done.3 = bf16[8,40,640]{2,1,0:T(8,128)(2,1)S(1)} async-done(((bf16[8,40,640]{2,1,0:T(8,128)(2,1)}), bf16[8,40,640]{2,1,0:T(8,128)(2,1)S(1)}, u32[]{:S(2)}, u32[]{:S(2)}) %all-to-all-start.3) | async-done | bytes 409632 | tf_op jit(solution)/shard_map/all_to_all | solution.py:548
  127.0 2.0 %collective-permute-done.26 = f32[640]{0:T(1024)S(1)} collective-permute-done((f32[640]{0:T(1024)S(1)}, f32[640]{0:T(1024)S(1)}, u32[]{:S(2)}, u32[]{:S(2)}) %collective-permute-start.26) | collective-permute-done | bytes 2592 | tf_op jit(solution)/shard_map/ppermute | solution.py:19
  128.9 2.9 %collective-permute-done.22 = bf16[2,40,640]{2,1,0:T(8,128)(2,1)S(1)} collective-permute-done((bf16[2,40,640]{2,1,0:T(8,128)(2,1)S(1)}, bf16[2,40,640]{2,1,0:T(8,128)(2,1)S(1)}, u32[]{:S(2)}, u32[]{:S(2)}) %collective-permute-start.22) | collective-permute-done | bytes 102432 | tf_op jit(solution)/shard_map/ppermute | solution.py:556
  132.8 2.7 %collective-permute-start.25 = (bf16[40,640]{1,0:T(8,128)(2,1)S(1)}, bf16[40,640]{1,0:T(8,128)(2,1)S(1)}, u32[]{:S(2)}, u32[]{:S(2)}) collective-permute-start(bf16[40,640]{1,0:T(8,128)(2,1)S(1)} %get-tuple-element.95), channel_id=1, source_target_pairs={{0,20},{2,22},{4,16},{6,18},{8,28},{10,30},{12,24},{14,26},{16,4},... | collective-permute-start | bytes 153608 | tf_op jit(solution)/shard_map/ppermute | solution.py:29
  (120 shorter events, 38.3 us)
Async XLA Ops:
  0.6 12.8 %collective-permute-start.1 = (bf16[288,640]{1,0:T(8,128)(2,1)}, bf16[288,640]{1,0:T(8,128)(2,1)S(1)}, u32[]{:S(2)}, u32[]{:S(2)}) collective-permute-start(bf16[288,640]{1,0:T(8,128)(2,1)} %bitcast.38), channel_id=1, source_target_pairs={{0,16},{16,0},{1,17},{17,1},{2,18},{18,2},{3,19},{19,3},{4,20},{20... | collective-permute-start | bytes 1105928 | tf_op jit(solution)/shard_map/ppermute | solution.py:19
  3.7 10.7 %collective-permute-start = (bf16[288,640]{1,0:T(8,128)(2,1)}, bf16[288,640]{1,0:T(8,128)(2,1)S(1)}, u32[]{:S(2)}, u32[]{:S(2)}) collective-permute-start(bf16[288,640]{1,0:T(8,128)(2,1)} %bitcast.39), channel_id=1, source_target_pairs={{0,1},{1,0},{2,3},{3,2},{4,5},{5,4},{6,7},{7,6},{8,9},{9,8},{10,11... | collective-permute-start | bytes 1105928 | tf_op jit(solution)/shard_map/ppermute | solution.py:19
  8.6 21.3 %all-to-all-start = ((bf16[8,56,640]{2,1,0:T(8,128)(2,1)}), bf16[8,56,640]{2,1,0:T(8,128)(2,1)S(1)}, u32[]{:S(2)}, u32[]{:S(2)}) async-start(bf16[8,56,640]{2,1,0:T(8,128)(2,1)} %shard_map.127), calls=%async_computation | async-start | bytes 1146880 | tf_op jit(solution)/shard_map/all_to_all | solution.py:437
  13.5 7.1 %collective-permute-start.2 = (bf16[144,640]{1,0:T(8,128)(2,1)S(1)}, bf16[144,640]{1,0:T(8,128)(2,1)S(1)}, u32[]{:S(2)}, u32[]{:S(2)}) collective-permute-start(bf16[144,640]{1,0:T(8,128)(2,1)S(1)} %slice.74), channel_id=1, source_target_pairs={{0,1},{1,0},{2,3},{3,2},{4,5},{5,4},{6,7},{7,6},{8,9},{9,8},{10,11... | collective-permute-start | bytes 552968 | tf_op jit(solution)/shard_map/ppermute | solution.py:19
  14.3 6.6 %collective-permute-start.3 = (bf16[144,640]{1,0:T(8,128)(2,1)S(1)}, bf16[144,640]{1,0:T(8,128)(2,1)S(1)}, u32[]{:S(2)}, u32[]{:S(2)}) collective-permute-start(bf16[144,640]{1,0:T(8,128)(2,1)S(1)} %slice.75), channel_id=1, source_target_pairs={{0,16},{16,0},{1,17},{17,1},{2,18},{18,2},{3,19},{19,3},{4,20},{20... | collective-permute-start | bytes 552968 | tf_op jit(solution)/shard_map/ppermute | solution.py:19
  15.9 11.6 %collective-permute-start.4 = (bf16[288,640]{1,0:T(8,128)(2,1)S(1)}, bf16[288,640]{1,0:T(8,128)(2,1)S(1)}, u32[]{:S(2)}, u32[]{:S(2)}) collective-permute-start(bf16[288,640]{1,0:T(8,128)(2,1)S(1)} %bitcast.40), channel_id=1, source_target_pairs={{0,2},{2,0},{4,6},{6,4},{8,10},{10,8},{12,14},{14,12},{1,3},{3,1},... | collective-permute-start | bytes 1105928 | tf_op jit(solution)/shard_map/ppermute | solution.py:19
  15.9 11.6 %collective-permute-start.5 = (bf16[288,640]{1,0:T(8,128)(2,1)S(1)}, bf16[288,640]{1,0:T(8,128)(2,1)S(1)}, u32[]{:S(2)}, u32[]{:S(2)}) collective-permute-start(bf16[288,640]{1,0:T(8,128)(2,1)S(1)} %collective-permute-done.refs_1_), channel_id=1, source_target_pairs={{0,2},{2,0},{4,6},{6,4},{8,10},{10,8},{12,14},{14,12},{1,3},{3,1},... | collective-permute-start | bytes 1105928 | tf_op jit(solution)/shard_map/ppermute | solution.py:19
  16.4 11.1 %collective-permute-start.6 = (bf16[288,640]{1,0:T(8,128)(2,1)S(1)}, bf16[288,640]{1,0:T(8,128)(2,1)}, u32[]{:S(2)}, u32[]{:S(2)}) collective-permute-start(bf16[288,640]{1,0:T(8,128)(2,1)S(1)} %collective-permute-done.1.refs_2_), channel_id=1, source_target_pairs={{0,2},{2,0},{4,6},{6,4},{8,10},{10,8},{12,14},{14,12},{1,3},{3,1},... | collective-permute-start | bytes 1105928 | tf_op jit(solution)/shard_map/ppermute | solution.py:19
  21.0 6.6 %collective-permute-start.7 = (bf16[288,640]{1,0:T(8,128)(2,1)S(1)}, bf16[288,640]{1,0:T(8,128)(2,1)}, u32[]{:S(2)}, u32[]{:S(2)}) collective-permute-start(bf16[288,640]{1,0:T(8,128)(2,1)S(1)} %constant_dynamic-update-slice_fusion.refs_3_), channel_id=1, source_target_pairs={{0,2},{2,0},{4,6},{6,4},{8,10},{10,8},{12,14},{14,12},{1,3},{3,1},... | collective-permute-start | bytes 1105928 | tf_op jit(solution)/shard_map/ppermute | solution.py:19
  30.7 18.2 %all-to-all-start.1 = ((bf16[16,60,240]{2,1,0:T(8,128)(2,1)}), bf16[16,60,240]{2,1,0:T(8,128)(2,1)S(1)}, u32[]{:S(2)}, u32[]{:S(2)}) async-start(bf16[16,60,240]{2,1,0:T(8,128)(2,1)} %bitcast.42), calls=%async_computation.1 | async-start | bytes 1048576 | tf_op jit(solution)/shard_map/all_to_all | solution.py:454
  34.5 16.8 %collective-permute-start.8 = (bf16[8,20,640]{2,1,0:T(8,128)(2,1)S(1)}, bf16[8,20,640]{2,1,0:T(8,128)(2,1)S(1)}, u32[]{:S(2)}, u32[]{:S(2)}) collective-permute-start(bf16[8,20,640]{2,1,0:T(8,128)(2,1)S(1)} %slice.58.mine), channel_id=1, source_target_pairs={{0,4},{2,6},{4,0},{6,2},{8,12},{10,14},{12,8},{14,10},{1,5},{3,7},... | collective-permute-start | bytes 614408 | tf_op jit(solution)/shard_map/ppermute | solution.py:456
  49.0 14.4 %collective-permute-start.9 = (bf16[16,60,240]{2,1,0:T(8,128)(2,1)S(1)}, bf16[16,60,240]{2,1,0:T(8,128)(2,1)S(1)}, u32[]{:S(2)}, u32[]{:S(2)}) collective-permute-start(bf16[16,60,240]{2,1,0:T(8,128)(2,1)S(1)} %all-to-all-done.1.mine), channel_id=1, source_target_pairs={{0,4},{2,6},{4,0},{6,2},{8,12},{10,14},{12,8},{14,10},{1,5},{3,7},... | collective-permute-start | bytes 1382408 | tf_op jit(solution)/shard_map/ppermute | solution.py:457
  51.9 17.2 %collective-permute-start.10 = (bf16[8,40,640]{2,1,0:T(8,128)(2,1)S(1)}, bf16[8,40,640]{2,1,0:T(8,128)(2,1)S(1)}, u32[]{:S(2)}, u32[]{:S(2)}) collective-permute-start(bf16[8,40,640]{2,1,0:T(8,128)(2,1)S(1)} %shard_map.128.refs_0_), channel_id=1, source_target_pairs={{0,1},{1,0},{2,3},{3,2},{4,5},{5,4},{6,7},{7,6},{8,9},{9,8},{10,11... | collective-permute-start | bytes 1228808 | tf_op jit(solution)/shard_map/ppermute | solution.py:19
  53.4 15.7 %collective-permute-start.11 = (bf16[8,40,640]{2,1,0:T(8,128)(2,1)S(1)}, bf16[8,40,640]{2,1,0:T(8,128)(2,1)S(1)}, u32[]{:S(2)}, u32[]{:S(2)}) collective-permute-start(bf16[8,40,640]{2,1,0:T(8,128)(2,1)S(1)} %shard_map.128.refs_0_), channel_id=1, source_target_pairs={{0,16},{16,0},{1,17},{17,1},{2,18},{18,2},{3,19},{19,3},{4,20},{20... | collective-permute-start | bytes 1228808 | tf_op jit(solution)/shard_map/ppermute | solution.py:19
  69.1 17.3 %all-to-all-start.2 = ((bf16[32,24,240]{2,1,0:T(8,128)(2,1)}), bf16[32,24,240]{2,1,0:T(8,128)(2,1)S(1)}, u32[]{:S(2)}, u32[]{:S(2)}) async-start(bf16[32,24,240]{2,1,0:T(8,128)(2,1)} %shard_map.131), calls=%async_computation.2 | async-start | bytes 786432 | tf_op jit(solution)/shard_map/all_to_all | solution.py:493
  72.9 12.0 %collective-permute-start.14 = (bf16[8,40,640]{2,1,0:T(8,128)(2,1)S(1)}, bf16[8,40,640]{2,1,0:T(8,128)(2,1)S(1)}, u32[]{:S(2)}, u32[]{:S(2)}) collective-permute-start(bf16[8,40,640]{2,1,0:T(8,128)(2,1)S(1)} %shard_map.128.refs_0_), channel_id=1, source_target_pairs={{0,2},{2,0},{4,6},{6,4},{8,10},{10,8},{12,14},{14,12},{1,3},{3,1},... | collective-permute-start | bytes 1228808 | tf_op jit(solution)/shard_map/ppermute | solution.py:19
  73.2 11.7 %collective-permute-start.15 = (bf16[8,40,640]{2,1,0:T(8,128)(2,1)S(1)}, bf16[8,40,640]{2,1,0:T(8,128)(2,1)}, u32[]{:S(2)}, u32[]{:S(2)}) collective-permute-start(bf16[8,40,640]{2,1,0:T(8,128)(2,1)S(1)} %collective-permute-done.10.refs_1_), channel_id=1, source_target_pairs={{0,2},{2,0},{4,6},{6,4},{8,10},{10,8},{12,14},{14,12},{1,3},{3,1},... | collective-permute-start | bytes 1228808 | tf_op jit(solution)/shard_map/ppermute | solution.py:19
  73.6 9.9 %collective-permute-start.12 = (bf16[4,40,640]{2,1,0:T(8,128)(2,1)S(1)}, bf16[4,40,640]{2,1,0:T(8,128)(2,1)S(1)}, u32[]{:S(2)}, u32[]{:S(2)}) collective-permute-start(bf16[4,40,640]{2,1,0:T(8,128)(2,1)S(1)} %slice.59), channel_id=1, source_target_pairs={{0,1},{1,0},{2,3},{3,2},{4,5},{5,4},{6,7},{7,6},{8,9},{9,8},{10,11... | collective-permute-start | bytes 614408 | tf_op jit(solution)/shard_map/ppermute | solution.py:19
  75.4 9.5 %collective-permute-start.16 = (bf16[8,40,640]{2,1,0:T(8,128)(2,1)S(1)}, bf16[8,40,640]{2,1,0:T(8,128)(2,1)}, u32[]{:S(2)}, u32[]{:S(2)}) collective-permute-start(bf16[8,40,640]{2,1,0:T(8,128)(2,1)S(1)} %collective-permute-done.11.refs_2_), channel_id=1, source_target_pairs={{0,2},{2,0},{4,6},{6,4},{8,10},{10,8},{12,14},{14,12},{1,3},{3,1},... | collective-permute-start | bytes 1228808 | tf_op jit(solution)/shard_map/ppermute | solution.py:19
  75.4 9.2 %collective-permute-start.13 = (bf16[4,40,640]{2,1,0:T(8,128)(2,1)S(1)}, bf16[4,40,640]{2,1,0:T(8,128)(2,1)}, u32[]{:S(2)}, u32[]{:S(2)}) collective-permute-start(bf16[4,40,640]{2,1,0:T(8,128)(2,1)S(1)} %slice.60), channel_id=1, source_target_pairs={{0,16},{16,0},{1,17},{17,1},{2,18},{18,2},{3,19},{19,3},{4,20},{20... | collective-permute-start | bytes 614408 | tf_op jit(solution)/shard_map/ppermute | solution.py:19
  101.3 11.6 %collective-permute-start.20 = (bf16[2,4,40,640]{3,2,1,0:T(8,128)(2,1)S(1)}, bf16[2,4,40,640]{3,2,1,0:T(8,128)(2,1)S(1)}, u32[]{:S(2)}, u32[]{:S(2)}) collective-permute-start(bf16[2,4,40,640]{3,2,1,0:T(8,128)(2,1)S(1)} %slice_bitcast_fusion), channel_id=1, source_target_pairs={{0,16},{16,0},{1,17},{17,1},{2,18},{18,2},{3,19},{19,3},{4,20},{20... | collective-permute-start | bytes 1228808 | tf_op jit(solution)/shard_map/ppermute | solution.py:19
  107.7 17.3 %all-to-all-start.3 = ((bf16[8,40,640]{2,1,0:T(8,128)(2,1)}), bf16[8,40,640]{2,1,0:T(8,128)(2,1)S(1)}, u32[]{:S(2)}, u32[]{:S(2)}) async-start(bf16[8,40,640]{2,1,0:T(8,128)(2,1)} %shard_map.135), calls=%async_computation.3 | async-start | bytes 819200 | tf_op jit(solution)/shard_map/all_to_all | solution.py:548
  113.0 6.7 %collective-permute-start.21 = (bf16[4,40,640]{2,1,0:T(8,128)(2,1)S(1)}, bf16[4,40,640]{2,1,0:T(8,128)(2,1)S(1)}, u32[]{:S(2)}, u32[]{:S(2)}) collective-permute-start(bf16[4,40,640]{2,1,0:T(8,128)(2,1)S(1)} %slice_bitcast_fusion.1), channel_id=1, source_target_pairs={{0,1},{1,0},{2,3},{3,2},{4,5},{5,4},{6,7},{7,6},{8,9},{9,8},{10,11... | collective-permute-start | bytes 614408 | tf_op jit(solution)/shard_map/ppermute | solution.py:19
  125.2 6.6 %collective-permute-start.22 = (bf16[2,40,640]{2,1,0:T(8,128)(2,1)S(1)}, bf16[2,40,640]{2,1,0:T(8,128)(2,1)S(1)}, u32[]{:S(2)}, u32[]{:S(2)}) collective-permute-start(bf16[2,40,640]{2,1,0:T(8,128)(2,1)S(1)} %slice.67), channel_id=1, source_target_pairs={{0,8},{2,10},{4,12},{6,14},{8,0},{10,2},{12,4},{14,6},{1,9},{3,11}... | collective-permute-start | bytes 307208 | tf_op jit(solution)/shard_map/ppermute | solution.py:556
  (24 other events, 165.7 us)

commit v16 on v15

--- a/solution.py
+++ b/solution.py
@@ -125,19 +125,28 @@
 
 
 def join_kernel(place, *refs):
-    pieces, out = (refs[:-1], refs[-1])
+    pieces, out, sems = (refs[:-2], refs[-2], refs[-1])
     x, core, tile = (place[0], place[1], place[2])
     frames = out.shape[1]
+    middle = frames // 2
+    copies = []
     for dc in (0, 1):
-        own, by_tile, by_clip, low, high = pieces[5 * dc : 5 * dc + 5]
         own_kind = 2 * x + (core ^ dc)
         other_kind = 2 * (x ^ 1) + (core ^ dc)
-        for f in range(frames):
-            out[own_kind, f, tile] = own[f]
-            out[own_kind, f, tile ^ 1] = by_tile[f]
-            out[other_kind, f, tile] = by_clip[f]
-            part, index = (low, f) if f < frames // 2 else (high, f - frames // 2)
-            out[other_kind, f, tile ^ 1] = part[index]
+        targets = [
+            out.at[own_kind, :, tile],
+            out.at[own_kind, :, tile ^ 1],
+            out.at[other_kind, :, tile],
+            out.at[other_kind, pl.ds(0, middle), tile ^ 1],
+            out.at[other_kind, pl.ds(middle, middle), tile ^ 1],
+        ]
+        for n, target in enumerate(targets):
+            index = 5 * dc + n
+            copies.append(pltpu.make_async_copy(pieces[index], target, sems.at[index]))
+    for copy in copies:
+        copy.start()
+    for copy in copies:
+        copy.wait()
 
 
 def act_kernel(place, gain, *refs, cols, part):
@@ -218,9 +227,9 @@
 
 
 def attend_kernel(
-    place, mid_in, cot_in, weights, qgain, kgain, scale,
+    place, mid_in, cot_in, weights_in, qgain, kgain, scale,
     kept, sent, sums, d_raw, q_hat, k_hat, q_rstd, k_rstd, d_value,
-    mid_s, cot_s, doubled, doubled_v, mixed_s, raw_s, probs_s,
+    mid_s, cot_s, doubled, doubled_v, mixed_s, raw_s, probs_s, weights, sems,
     *, heads, count, padded, part,
 ):
     total, width = mid_s.shape
@@ -229,6 +238,11 @@
     lanes = scale.shape[-1]
     third = count // 3
     x, core, tile, plane = (place[0], place[1], place[2], place[4])
+    copies = [
+        pltpu.make_async_copy(weights_in.at[n], weights.at[n], sems.at[n]) for n in range(4)
+    ]
+    for copy in copies:
+        copy.start()
     mid_s[...] = jnp.zeros_like(mid_s)
     cot_s[...] = jnp.zeros_like(cot_s)
     for z in range(frames // 2):
@@ -256,16 +270,20 @@
         rstd = lax.rsqrt(var + EPS)
         return cent * spread(rstd, both), rstd
 
+    copies[0].wait()
     hat, rstd = stats(dot(mid, weights[0]))
     q_hat[...] = hat
     q_rstd[...] = rstd
     q_norm = hat * qgain[...]
+    copies[1].wait()
     hat, rstd = stats(dot(mid, weights[1]))
     k_hat[...] = hat
     k_rstd[...] = rstd
     hat = hat * kgain[...]
     doubled[pl.ds(0, total), :] = hat
     doubled[pl.ds(total, total), :] = hat
+    copies[2].wait()
+    copies[3].wait()
     value = dot(mid, weights[2]).astype(BF).astype(F32)
     doubled_v[pl.ds(0, total), :] = value
     doubled_v[pl.ds(total, total), :] = value
@@ -343,14 +361,20 @@
 
 
 def back_kernel(
-    d_qn, d_kn, q_hat, k_hat, q_rstd, k_rstd, d_value, weights, qgain, kgain, scale_sums,
+    d_qn, d_kn, q_hat, k_hat, q_rstd, k_rstd, d_value, weights_in, qgain, kgain, scale_sums,
     d_mid,
+    weights, sems,
     *, heads, count, padded,
 ):
     total, width = q_hat.shape
     depth = width // heads
     frames = total // padded
     lanes = scale_sums.shape[-1]
+    copies = [
+        pltpu.make_async_copy(weights_in.at[n], weights.at[n], sems.at[n]) for n in range(3)
+    ]
+    for copy in copies:
+        copy.start()
     pick = picker(width, lanes, depth, 0)
     both = jnp.concatenate([spreader(lanes, width, depth, 0)] * 2, axis=0)
 
@@ -361,6 +385,8 @@
 
     d_query = back(d_qn[...] * qgain[...], q_hat[...], q_rstd[...])
     d_key = back(d_kn[...] * kgain[...], k_hat[...], k_rstd[...])
+    for copy in copies:
+        copy.wait()
     out = dot_t(d_query, weights[0])
     out += dot_t(d_key, weights[1])
     out += dot_t(d_value[...], weights[2])
@@ -389,15 +415,22 @@
         d_mid[f] = jnp.concatenate([tokens, spare], axis=0).astype(BF)
 
 
-def call(kernel, mebibytes, outs, scratch, *args):
+def call(kernel, mebibytes, outs, scratch, *args, apart=(), outs_apart=False, sems=0):
     smem = pl.BlockSpec(memory_space=pltpu.SMEM)
     vmem = pl.BlockSpec(memory_space=pltpu.VMEM)
+    apart_spec = pl.BlockSpec(memory_space=pl.ANY)
+    in_specs = [smem if arg.dtype == jnp.int32 else vmem for arg in args]
+    for index in apart:
+        in_specs[index] = apart_spec
+    shapes = [pltpu.VMEM(shape, dtype) for shape, dtype in scratch]
+    if sems > 0:
+        shapes.append(pltpu.SemaphoreType.DMA((sems,)))
     return pl.pallas_call(
         kernel,
         out_shape=[jax.ShapeDtypeStruct(shape, dtype) for shape, dtype in outs],
-        in_specs=[smem if arg.dtype == jnp.int32 else vmem for arg in args],
-        out_specs=[vmem] * len(outs),
-        scratch_shapes=[pltpu.VMEM(shape, dtype) for shape, dtype in scratch],
+        in_specs=in_specs,
+        out_specs=[apart_spec if outs_apart else vmem] * len(outs),
+        scratch_shapes=shapes,
         compiler_params=pltpu.CompilerParams(vmem_limit_bytes=mebibytes << 20),
     )(*args)
 
@@ -495,9 +528,16 @@
     middle = frames // 2
     parts = [own, by_tile, by_clip, swap(by_clip[:middle], "tile"), swap(by_tile[middle:], "dp")]
     parts += [swap(piece, "frame") for piece in parts]
-    parts, mid = lax.optimization_barrier((parts, mid))
     (attn_full,) = call(
-        join_kernel, 16, [((4, frames, tiles, share, width), BF)], [], place, *parts
+        join_kernel,
+        8,
+        [((4, frames, tiles, share, width), BF)],
+        [],
+        place,
+        *parts,
+        apart=range(1, 11),
+        outs_apart=True,
+        sems=10,
     )
     attn_full = attn_full.reshape(4, width, width)
 
@@ -512,7 +552,7 @@
     narrow = (total, lanes)
     kept, sent, scale_sums, d_raw, q_hat, k_hat, q_rstd, k_rstd, d_value = call(
         functools.partial(attend_kernel, heads=heads, count=count, padded=padded, part=part),
-        20,
+        32,
         [
             ((2, 2, frames // 2, share, width), BF),
             ((2, 2, frames // 2, share, width), BF),
@@ -521,9 +561,10 @@
         ],
         [
             (full, F32), (full, F32), (double, F32), (double, F32), (full, F32),
-            (narrow, F32), (narrow, F32),
+            (narrow, F32), (narrow, F32), ((4, width, width), BF),
         ],
         place, mid, packed, attn_full, qgain, kgain, scale,
+        apart=(3,), sems=4,
     )
     d_qn, d_kn = call(
         functools.partial(slope_kernel, heads=heads, padded=padded),
@@ -542,8 +583,9 @@
         functools.partial(back_kernel, heads=heads, count=count, padded=padded),
         16,
         [((frames, padded, width), BF)],
-        [],
+        [((3, width, width), BF)],
         d_qn, d_kn, q_hat, k_hat, q_rstd, k_rstd, d_value, attn_full, qgain, kgain, scale_sums,
+        apart=(7,), sems=3,
     )
     d_back = lax.all_to_all(d_mid, "frame", 0, 0, tiled=True)
     theirs, _ = lax.optimization_barrier((swap(shares[1], "dp"), d_mid))

time: 141 us -> 147 us (1.043)
  local copies, waits for them, and re-layouts: 13.8 us -> 17.4 us
  Pallas kernels: 31.6 us -> 33.9 us
    unnamed x33 -> x37, local copies, waits for them, and re-layouts: 5.94 us -> 9.52 us
    pallas_call x9, Pallas kernels: 31.6 us -> 33.9 us  [call(): pl.pallas_call(kernel, out_shape=[jax.ShapeDtypeStruct(shape, dtype) for...]
  transfers between devices with their start and end apart: 32 -> 32, of which waited for: 18 -> 18; matrix products, arithmetic and copies ran while one was open for 6% -> 6% of each run, Pallas kernels for 14% -> 15%
where the time goes in v16:
time: 147 us; the launch traced here: 146 us
  waiting for transfers between devices  49.5 us (34%)
  starting transfers between devices  41.5 us (28%)
  Pallas kernels  33.9 us (23%)
  local copies, waits for them, and re-layouts  17.4 us (12%)
  other arithmetic  3.07 us (2%)
    pallas_call x9, Pallas kernels, call(): pl.pallas_call(kernel, out_shape=[jax.ShapeDtypeStruct(shape, dtype) for...  33.9 us
    ppermute x23, waiting for transfers between devices, swap(): lax.ppermute(x, axis, [(i, i ^ 1) for i in range(lax.axis_size(axis))])  24.7 us
    ppermute x23, starting transfers between devices, swap(): lax.ppermute(x, axis, [(i, i ^ 1) for i in range(lax.axis_size(axis))])  18 us
    all_to_all x1, waiting for transfers between devices, local(): conv_half = lax.all_to_all(mine, square, 0, 0, tiled=True)  12.5 us
    unnamed x37, local copies, waits for them, and re-layouts  9.52 us
    all_to_all x1, waiting for transfers between devices, local(): d_back = lax.all_to_all(d_mid, 'frame', 0, 0, tiled=True)  5.15 us
    all_to_all x1, starting transfers between devices, local(): packed = lax.all_to_all(packed, 'frame', 0, 0, tiled=True)  4.88 us
    all_to_all x1, starting transfers between devices, local(): d_back = lax.all_to_all(d_mid, 'frame', 0, 0, tiled=True)  4.69 us
  transfers between devices with their start and end apart: 32, of which 18 were waited for; matrix products, arithmetic and copies ran while one was open for 6% of the time, Pallas kernels for 15%

profile of v16, /device:TPU:0, one launch (start us, length us, event | category | flops | bytes accessed | tf_op | source)
XLA Modules:
  0.0 146.4 jit_solution(9489211980780297666)
XLA Ops:
  0.6 3.0 %collective-permute-start.1 = (bf16[288,640]{1,0:T(8,128)(2,1)}, bf16[288,640]{1,0:T(8,128)(2,1)S(1)}, u32[]{:S(2)}, u32[]{:S(2)}) collective-permute-start(bf16[288,640]{1,0:T(8,128)(2,1)} %bitcast.38), channel_id=1, source_target_pairs={{0,16},{16,0},{1,17},{17,1},{2,18},{18,2},{3,19},{19,3},{4,20},{20... | collective-permute-start | bytes 1105928 | tf_op jit(solution)/shard_map/ppermute | solution.py:19
  8.6 4.9 %all-to-all-start = ((bf16[8,56,640]{2,1,0:T(8,128)(2,1)}), bf16[8,56,640]{2,1,0:T(8,128)(2,1)S(1)}, u32[]{:S(2)}, u32[]{:S(2)}) async-start(bf16[8,56,640]{2,1,0:T(8,128)(2,1)} %shard_map.127), calls=%async_computation | async-start | bytes 1146880 | tf_op jit(solution)/shard_map/all_to_all | solution.py:470
  16.4 4.2 %collective-permute-done.2 = bf16[144,640]{1,0:T(8,128)(2,1)S(1)} collective-permute-done((bf16[144,640]{1,0:T(8,128)(2,1)S(1)}, bf16[144,640]{1,0:T(8,128)(2,1)S(1)}, u32[]{:S(2)}, u32[]{:S(2)}) %collective-permute-start.2) | collective-permute-done | bytes 184352 | tf_op jit(solution)/shard_map/ppermute | solution.py:19
  22.2 2.2 %copy.15 = bf16[4,3,40,3,80]{4,3,0,2,1:T(4,128)(2,1)} copy(bf16[4,3,40,3,80]{4,0,2,3,1:T(4,128)(2,1)} %bitcast.43) | data formatting | bytes 460800 | tf_op jit(solution)/shard_map/transpose | solution.py:482
  24.4 2.1 %reshape.49 = bf16[4,2,60,240]{3,0,2,1:T(4,128)(2,1)} reshape(bf16[4,3,40,3,80]{4,3,0,2,1:T(4,128)(2,1)} %copy.15) | data formatting | bytes 460800 | tf_op jit(solution)/shard_map/reshape | solution.py:483
  27.6 2.3 %all-to-all-done.cot_in = bf16[8,56,640]{2,1,0:T(8,128)(2,1)S(1)} async-done(((bf16[8,56,640]{2,1,0:T(8,128)(2,1)}), bf16[8,56,640]{2,1,0:T(8,128)(2,1)S(1)}, u32[]{:S(2)}, u32[]{:S(2)}) %all-to-all-start) | async-done | bytes 573472 | tf_op jit(solution)/shard_map/all_to_all | solution.py:470
  30.8 3.7 %all-to-all-start.1 = ((bf16[16,60,240]{2,1,0:T(8,128)(2,1)}), bf16[16,60,240]{2,1,0:T(8,128)(2,1)S(1)}, u32[]{:S(2)}, u32[]{:S(2)}) async-start(bf16[16,60,240]{2,1,0:T(8,128)(2,1)} %bitcast.42), calls=%async_computation.1 | async-start | bytes 1048576 | tf_op jit(solution)/shard_map/all_to_all | solution.py:487
  34.5 2.0 %collective-permute-start.9 = (bf16[8,20,640]{2,1,0:T(8,128)(2,1)S(1)}, bf16[8,20,640]{2,1,0:T(8,128)(2,1)S(1)}, u32[]{:S(2)}, u32[]{:S(2)}) collective-permute-start(bf16[8,20,640]{2,1,0:T(8,128)(2,1)S(1)} %slice.58.mine), channel_id=1, source_target_pairs={{0,4},{2,6},{4,0},{6,2},{8,12},{10,14},{12,8},{14,10},{1,5},{3,7},... | collective-permute-start | bytes 614408 | tf_op jit(solution)/shard_map/ppermute | solution.py:489
  36.5 12.5 %all-to-all-done.1.mine = bf16[16,60,240]{2,1,0:T(8,128)(2,1)S(1)} async-done(((bf16[16,60,240]{2,1,0:T(8,128)(2,1)}), bf16[16,60,240]{2,1,0:T(8,128)(2,1)S(1)}, u32[]{:S(2)}, u32[]{:S(2)}) %all-to-all-start.1) | async-done | bytes 460832 | tf_op jit(solution)/shard_map/all_to_all | solution.py:487
  49.0 1.8 %collective-permute-start.8 = (bf16[16,60,240]{2,1,0:T(8,128)(2,1)S(1)}, bf16[16,60,240]{2,1,0:T(8,128)(2,1)S(1)}, u32[]{:S(2)}, u32[]{:S(2)}) collective-permute-start(bf16[16,60,240]{2,1,0:T(8,128)(2,1)S(1)} %all-to-all-done.1.mine), channel_id=1, source_target_pairs={{0,4},{2,6},{4,0},{6,2},{8,12},{10,14},{12,8},{14,10},{1,5},{3,7},... | collective-permute-start | bytes 1382408 | tf_op jit(solution)/shard_map/ppermute | solution.py:490
  57.9 4.7 %shard_map.129 = (bf16[4,640,640]{2,1,0:T(8,128)(2,1)S(1)}, bf16[4,576,80]{2,1,0:T(8,128)(2,1)S(1)}) custom-call(s32[5]{0:T(128)S(1)} %stack.23.place, f32[1,640]{1,0:T(1,128)S(1)} %broadcast_in_dim.5.gain, bf16[288,640]{1,0:T(8,128)(2,1)S(1)} %bitcast.41, bf16[288,640]{1,0:T(8,128)(2,1)S(1)} %collective-permute-done.refs_1_, ...), custom_call_target="tpu_custom_call" | custom-call | tf_op jit(solution)/shard_map/pallas_call | solution.py:428
  64.1 5.1 %shard_map.130 = bf16[32,24,240]{2,1,0:T(8,128)(2,1)} custom-call(s32[5]{0:T(128)S(1)} %stack.23.place, bf16[3,640,240]{2,1,0:T(8,128)(2,1)S(1)} %bitcast.36, bf16[4,640,640]{2,1,0:T(8,128)(2,1)S(1)} %get-tuple-element.47.acts, bf16[4,576,80]{2,1,0:T(8,128)(2,1)S(1)} %get-tuple-element.48.kept), custom_call_target="tpu_custom_call" | custom-call | tf_op jit(solution)/shard_map/pallas_call | solution.py:428
  69.1 3.5 %all-to-all-start.2 = ((bf16[32,24,240]{2,1,0:T(8,128)(2,1)}), bf16[32,24,240]{2,1,0:T(8,128)(2,1)S(1)}, u32[]{:S(2)}, u32[]{:S(2)}) async-start(bf16[32,24,240]{2,1,0:T(8,128)(2,1)} %shard_map.130), calls=%async_computation.2 | async-start | bytes 786432 | tf_op jit(solution)/shard_map/all_to_all | solution.py:526
  76.7 6.7 %collective-permute-done.12.refs_3_ = bf16[4,40,640]{2,1,0:T(8,128)(2,1)S(1)} collective-permute-done((bf16[4,40,640]{2,1,0:T(8,128)(2,1)S(1)}, bf16[4,40,640]{2,1,0:T(8,128)(2,1)S(1)}, u32[]{:S(2)}, u32[]{:S(2)}) %collective-permute-start.12) | collective-permute-done | bytes 204832 | tf_op jit(solution)/shard_map/ppermute | solution.py:19
  86.3 2.2 %shard_map.132 = bf16[4,8,2,40,640]{4,3,2,1,0:T(8,128)(2,1)S(1)} custom-call(s32[5]{0:T(128)S(1)} %stack.23.place, bf16[8,40,640]{2,1,0:T(8,128)(2,1)S(1)} %shard_map.131.refs_0_, bf16[8,40,640]{2,1,0:T(8,128)(2,1)S(1)} %collective-permute-done.10.refs_1_, bf16[8,40,640]{2,1,0:T(8,128)(2,1)S(1)} %collective-permute-done.11.refs_2_, ...), custom_call_target="tpu_custom_call" | custom-call | tf_op jit(solution)/shard_map/pallas_call | solution.py:428
  90.2 1.9 %copy-done.2 = bf16[4,8,2,40,640]{4,3,2,1,0:T(8,128)(2,1)S(1)} copy-done((bf16[4,8,2,40,640]{4,3,2,1,0:T(8,128)(2,1)S(1)}, bf16[4,8,2,40,640]{4,3,2,1,0:T(8,128)(2,1)}, u32[]{:S(2)}) %copy-start.2) | copy-done | bytes 3276824
  92.1 11.9 %shard_map.133 = (bf16[2,2,4,40,640]{4,3,2,1,0:T(8,128)(2,1)S(1)}, bf16[2,2,4,40,640]{4,3,2,1,0:T(8,128)(2,1)S(1)}, f32[1,128]{1,0:T(1,128)S(1)}, f32[320,128]{1...) custom-call(s32[5]{0:T(128)S(1)} %stack.23.place, ...), custom_call_target="tpu_custom_call" | custom-call | tf_op jit(solution)/shard_map/pallas_call | solution.py:428
  108.0 5.5 %shard_map.135 = bf16[8,40,640]{2,1,0:T(8,128)(2,1)} custom-call(f32[320,640]{1,0:T(8,128)S(1)} %get-tuple-element.60.d_qn, f32[320,640]{1,0:T(8,128)S(1)} %get-tuple-element.61.d_kn, f32[320,640]{1,0:T(8,128)S(1)} %get-tuple-element.56.q_hat, f32[320,640]{1,0:T(8,128)S(1)} %get-tuple-element.57.k_hat, f32[320,128]{1,0:T(8,128)S(1)} %get-tuple-element.62.q_rstd, ...), custom_call_target="tpu_custom_call" | custom-call | tf_op jit(solution)/shard_map/pallas_call | solution.py:428
  113.5 4.7 %all-to-all-start.3 = ((bf16[8,40,640]{2,1,0:T(8,128)(2,1)}), bf16[8,40,640]{2,1,0:T(8,128)(2,1)S(1)}, u32[]{:S(2)}, u32[]{:S(2)}) async-start(bf16[8,40,640]{2,1,0:T(8,128)(2,1)} %shard_map.135), calls=%async_computation.3 | async-start | bytes 819200 | tf_op jit(solution)/shard_map/all_to_all | solution.py:590
  119.1 6.8 %collective-permute-done.21 = bf16[4,40,640]{2,1,0:T(8,128)(2,1)S(1)} collective-permute-done((bf16[4,40,640]{2,1,0:T(8,128)(2,1)S(1)}, bf16[4,40,640]{2,1,0:T(8,128)(2,1)S(1)}, u32[]{:S(2)}, u32[]{:S(2)}) %collective-permute-start.21) | collective-permute-done | bytes 204832 | tf_op jit(solution)/shard_map/ppermute | solution.py:19
  125.9 5.2 %all-to-all-done.3 = bf16[8,40,640]{2,1,0:T(8,128)(2,1)S(1)} async-done(((bf16[8,40,640]{2,1,0:T(8,128)(2,1)}), bf16[8,40,640]{2,1,0:T(8,128)(2,1)S(1)}, u32[]{:S(2)}, u32[]{:S(2)}) %all-to-all-start.3) | async-done | bytes 409632 | tf_op jit(solution)/shard_map/all_to_all | solution.py:590
  133.0 2.1 %collective-permute-done.26 = f32[640]{0:T(1024)S(1)} collective-permute-done((f32[640]{0:T(1024)S(1)}, f32[640]{0:T(1024)S(1)}, u32[]{:S(2)}, u32[]{:S(2)}) %collective-permute-start.26) | collective-permute-done | bytes 2592 | tf_op jit(solution)/shard_map/ppermute | solution.py:19
  135.1 2.9 %collective-permute-done.22 = bf16[2,40,640]{2,1,0:T(8,128)(2,1)S(1)} collective-permute-done((bf16[2,40,640]{2,1,0:T(8,128)(2,1)S(1)}, bf16[2,40,640]{2,1,0:T(8,128)(2,1)S(1)}, u32[]{:S(2)}, u32[]{:S(2)}) %collective-permute-start.22) | collective-permute-done | bytes 102432 | tf_op jit(solution)/shard_map/ppermute | solution.py:598
  138.9 2.7 %collective-permute-start.25 = (bf16[40,640]{1,0:T(8,128)(2,1)S(1)}, bf16[40,640]{1,0:T(8,128)(2,1)S(1)}, u32[]{:S(2)}, u32[]{:S(2)}) collective-permute-start(bf16[40,640]{1,0:T(8,128)(2,1)S(1)} %get-tuple-element.73), channel_id=1, source_target_pairs={{0,20},{2,22},{4,16},{6,18},{8,28},{10,30},{12,24},{14,26},{16,4},... | collective-permute-start | bytes 153608 | tf_op jit(solution)/shard_map/ppermute | solution.py:29
  (124 shorter events, 40.8 us)
Async XLA Ops:
  0.6 12.9 %collective-permute-start.1 = (bf16[288,640]{1,0:T(8,128)(2,1)}, bf16[288,640]{1,0:T(8,128)(2,1)S(1)}, u32[]{:S(2)}, u32[]{:S(2)}) collective-permute-start(bf16[288,640]{1,0:T(8,128)(2,1)} %bitcast.38), channel_id=1, source_target_pairs={{0,16},{16,0},{1,17},{17,1},{2,18},{18,2},{3,19},{19,3},{4,20},{20... | collective-permute-start | bytes 1105928 | tf_op jit(solution)/shard_map/ppermute | solution.py:19
  3.7 10.7 %collective-permute-start = (bf16[288,640]{1,0:T(8,128)(2,1)}, bf16[288,640]{1,0:T(8,128)(2,1)S(1)}, u32[]{:S(2)}, u32[]{:S(2)}) collective-permute-start(bf16[288,640]{1,0:T(8,128)(2,1)} %bitcast.39), channel_id=1, source_target_pairs={{0,1},{1,0},{2,3},{3,2},{4,5},{5,4},{6,7},{7,6},{8,9},{9,8},{10,11... | collective-permute-start | bytes 1105928 | tf_op jit(solution)/shard_map/ppermute | solution.py:19
  8.6 21.3 %all-to-all-start = ((bf16[8,56,640]{2,1,0:T(8,128)(2,1)}), bf16[8,56,640]{2,1,0:T(8,128)(2,1)S(1)}, u32[]{:S(2)}, u32[]{:S(2)}) async-start(bf16[8,56,640]{2,1,0:T(8,128)(2,1)} %shard_map.127), calls=%async_computation | async-start | bytes 1146880 | tf_op jit(solution)/shard_map/all_to_all | solution.py:470
  13.5 7.1 %collective-permute-start.2 = (bf16[144,640]{1,0:T(8,128)(2,1)S(1)}, bf16[144,640]{1,0:T(8,128)(2,1)S(1)}, u32[]{:S(2)}, u32[]{:S(2)}) collective-permute-start(bf16[144,640]{1,0:T(8,128)(2,1)S(1)} %slice.74), channel_id=1, source_target_pairs={{0,1},{1,0},{2,3},{3,2},{4,5},{5,4},{6,7},{7,6},{8,9},{9,8},{10,11... | collective-permute-start | bytes 552968 | tf_op jit(solution)/shard_map/ppermute | solution.py:19
  14.3 6.6 %collective-permute-start.3 = (bf16[144,640]{1,0:T(8,128)(2,1)S(1)}, bf16[144,640]{1,0:T(8,128)(2,1)S(1)}, u32[]{:S(2)}, u32[]{:S(2)}) collective-permute-start(bf16[144,640]{1,0:T(8,128)(2,1)S(1)} %slice.75), channel_id=1, source_target_pairs={{0,16},{16,0},{1,17},{17,1},{2,18},{18,2},{3,19},{19,3},{4,20},{20... | collective-permute-start | bytes 552968 | tf_op jit(solution)/shard_map/ppermute | solution.py:19
  15.9 11.6 %collective-permute-start.4 = (bf16[288,640]{1,0:T(8,128)(2,1)S(1)}, bf16[288,640]{1,0:T(8,128)(2,1)S(1)}, u32[]{:S(2)}, u32[]{:S(2)}) collective-permute-start(bf16[288,640]{1,0:T(8,128)(2,1)S(1)} %bitcast.40), channel_id=1, source_target_pairs={{0,2},{2,0},{4,6},{6,4},{8,10},{10,8},{12,14},{14,12},{1,3},{3,1},... | collective-permute-start | bytes 1105928 | tf_op jit(solution)/shard_map/ppermute | solution.py:19
  15.9 11.7 %collective-permute-start.5 = (bf16[288,640]{1,0:T(8,128)(2,1)S(1)}, bf16[288,640]{1,0:T(8,128)(2,1)S(1)}, u32[]{:S(2)}, u32[]{:S(2)}) collective-permute-start(bf16[288,640]{1,0:T(8,128)(2,1)S(1)} %collective-permute-done.refs_1_), channel_id=1, source_target_pairs={{0,2},{2,0},{4,6},{6,4},{8,10},{10,8},{12,14},{14,12},{1,3},{3,1},... | collective-permute-start | bytes 1105928 | tf_op jit(solution)/shard_map/ppermute | solution.py:19
  16.4 11.2 %collective-permute-start.6 = (bf16[288,640]{1,0:T(8,128)(2,1)S(1)}, bf16[288,640]{1,0:T(8,128)(2,1)}, u32[]{:S(2)}, u32[]{:S(2)}) collective-permute-start(bf16[288,640]{1,0:T(8,128)(2,1)S(1)} %collective-permute-done.1.refs_2_), channel_id=1, source_target_pairs={{0,2},{2,0},{4,6},{6,4},{8,10},{10,8},{12,14},{14,12},{1,3},{3,1},... | collective-permute-start | bytes 1105928 | tf_op jit(solution)/shard_map/ppermute | solution.py:19
  21.0 6.6 %collective-permute-start.7 = (bf16[288,640]{1,0:T(8,128)(2,1)S(1)}, bf16[288,640]{1,0:T(8,128)(2,1)}, u32[]{:S(2)}, u32[]{:S(2)}) collective-permute-start(bf16[288,640]{1,0:T(8,128)(2,1)S(1)} %constant_dynamic-update-slice_fusion.refs_3_), channel_id=1, source_target_pairs={{0,2},{2,0},{4,6},{6,4},{8,10},{10,8},{12,14},{14,12},{1,3},{3,1},... | collective-permute-start | bytes 1105928 | tf_op jit(solution)/shard_map/ppermute | solution.py:19
  30.8 18.2 %all-to-all-start.1 = ((bf16[16,60,240]{2,1,0:T(8,128)(2,1)}), bf16[16,60,240]{2,1,0:T(8,128)(2,1)S(1)}, u32[]{:S(2)}, u32[]{:S(2)}) async-start(bf16[16,60,240]{2,1,0:T(8,128)(2,1)} %bitcast.42), calls=%async_computation.1 | async-start | bytes 1048576 | tf_op jit(solution)/shard_map/all_to_all | solution.py:487
  34.5 16.8 %collective-permute-start.9 = (bf16[8,20,640]{2,1,0:T(8,128)(2,1)S(1)}, bf16[8,20,640]{2,1,0:T(8,128)(2,1)S(1)}, u32[]{:S(2)}, u32[]{:S(2)}) collective-permute-start(bf16[8,20,640]{2,1,0:T(8,128)(2,1)S(1)} %slice.58.mine), channel_id=1, source_target_pairs={{0,4},{2,6},{4,0},{6,2},{8,12},{10,14},{12,8},{14,10},{1,5},{3,7},... | collective-permute-start | bytes 614408 | tf_op jit(solution)/shard_map/ppermute | solution.py:489
  49.0 14.4 %collective-permute-start.8 = (bf16[16,60,240]{2,1,0:T(8,128)(2,1)S(1)}, bf16[16,60,240]{2,1,0:T(8,128)(2,1)S(1)}, u32[]{:S(2)}, u32[]{:S(2)}) collective-permute-start(bf16[16,60,240]{2,1,0:T(8,128)(2,1)S(1)} %all-to-all-done.1.mine), channel_id=1, source_target_pairs={{0,4},{2,6},{4,0},{6,2},{8,12},{10,14},{12,8},{14,10},{1,5},{3,7},... | collective-permute-start | bytes 1382408 | tf_op jit(solution)/shard_map/ppermute | solution.py:490
  51.9 17.2 %collective-permute-start.10 = (bf16[8,40,640]{2,1,0:T(8,128)(2,1)S(1)}, bf16[8,40,640]{2,1,0:T(8,128)(2,1)S(1)}, u32[]{:S(2)}, u32[]{:S(2)}) collective-permute-start(bf16[8,40,640]{2,1,0:T(8,128)(2,1)S(1)} %shard_map.131.refs_0_), channel_id=1, source_target_pairs={{0,1},{1,0},{2,3},{3,2},{4,5},{5,4},{6,7},{7,6},{8,9},{9,8},{10,11... | collective-permute-start | bytes 1228808 | tf_op jit(solution)/shard_map/ppermute | solution.py:19
  53.4 15.7 %collective-permute-start.11 = (bf16[8,40,640]{2,1,0:T(8,128)(2,1)S(1)}, bf16[8,40,640]{2,1,0:T(8,128)(2,1)S(1)}, u32[]{:S(2)}, u32[]{:S(2)}) collective-permute-start(bf16[8,40,640]{2,1,0:T(8,128)(2,1)S(1)} %shard_map.131.refs_0_), channel_id=1, source_target_pairs={{0,16},{16,0},{1,17},{17,1},{2,18},{18,2},{3,19},{19,3},{4,20},{20... | collective-permute-start | bytes 1228808 | tf_op jit(solution)/shard_map/ppermute | solution.py:19
  69.1 21.1 %all-to-all-start.2 = ((bf16[32,24,240]{2,1,0:T(8,128)(2,1)}), bf16[32,24,240]{2,1,0:T(8,128)(2,1)S(1)}, u32[]{:S(2)}, u32[]{:S(2)}) async-start(bf16[32,24,240]{2,1,0:T(8,128)(2,1)} %shard_map.130), calls=%async_computation.2 | async-start | bytes 786432 | tf_op jit(solution)/shard_map/all_to_all | solution.py:526
  72.7 12.1 %collective-permute-start.14 = (bf16[8,40,640]{2,1,0:T(8,128)(2,1)S(1)}, bf16[8,40,640]{2,1,0:T(8,128)(2,1)S(1)}, u32[]{:S(2)}, u32[]{:S(2)}) collective-permute-start(bf16[8,40,640]{2,1,0:T(8,128)(2,1)S(1)} %shard_map.131.refs_0_), channel_id=1, source_target_pairs={{0,2},{2,0},{4,6},{6,4},{8,10},{10,8},{12,14},{14,12},{1,3},{3,1},... | collective-permute-start | bytes 1228808 | tf_op jit(solution)/shard_map/ppermute | solution.py:19
  73.0 11.8 %collective-permute-start.15 = (bf16[8,40,640]{2,1,0:T(8,128)(2,1)S(1)}, bf16[8,40,640]{2,1,0:T(8,128)(2,1)}, u32[]{:S(2)}, u32[]{:S(2)}) collective-permute-start(bf16[8,40,640]{2,1,0:T(8,128)(2,1)S(1)} %collective-permute-done.10.refs_1_), channel_id=1, source_target_pairs={{0,2},{2,0},{4,6},{6,4},{8,10},{10,8},{12,14},{14,12},{1,3},{3,1},... | collective-permute-start | bytes 1228808 | tf_op jit(solution)/shard_map/ppermute | solution.py:19
  73.4 10.0 %collective-permute-start.12 = (bf16[4,40,640]{2,1,0:T(8,128)(2,1)S(1)}, bf16[4,40,640]{2,1,0:T(8,128)(2,1)S(1)}, u32[]{:S(2)}, u32[]{:S(2)}) collective-permute-start(bf16[4,40,640]{2,1,0:T(8,128)(2,1)S(1)} %slice.59), channel_id=1, source_target_pairs={{0,1},{1,0},{2,3},{3,2},{4,5},{5,4},{6,7},{7,6},{8,9},{9,8},{10,11... | collective-permute-start | bytes 614408 | tf_op jit(solution)/shard_map/ppermute | solution.py:19
  75.2 9.6 %collective-permute-start.16 = (bf16[8,40,640]{2,1,0:T(8,128)(2,1)S(1)}, bf16[8,40,640]{2,1,0:T(8,128)(2,1)}, u32[]{:S(2)}, u32[]{:S(2)}) collective-permute-start(bf16[8,40,640]{2,1,0:T(8,128)(2,1)S(1)} %collective-permute-done.11.refs_2_), channel_id=1, source_target_pairs={{0,2},{2,0},{4,6},{6,4},{8,10},{10,8},{12,14},{14,12},{1,3},{3,1},... | collective-permute-start | bytes 1228808 | tf_op jit(solution)/shard_map/ppermute | solution.py:19
  75.2 9.3 %collective-permute-start.13 = (bf16[4,40,640]{2,1,0:T(8,128)(2,1)S(1)}, bf16[4,40,640]{2,1,0:T(8,128)(2,1)}, u32[]{:S(2)}, u32[]{:S(2)}) collective-permute-start(bf16[4,40,640]{2,1,0:T(8,128)(2,1)S(1)} %slice.60), channel_id=1, source_target_pairs={{0,16},{16,0},{1,17},{17,1},{2,18},{18,2},{3,19},{19,3},{4,20},{20... | collective-permute-start | bytes 614408 | tf_op jit(solution)/shard_map/ppermute | solution.py:19
  106.7 11.6 %collective-permute-start.20 = (bf16[2,4,40,640]{3,2,1,0:T(8,128)(2,1)S(1)}, bf16[2,4,40,640]{3,2,1,0:T(8,128)(2,1)S(1)}, u32[]{:S(2)}, u32[]{:S(2)}) collective-permute-start(bf16[2,4,40,640]{3,2,1,0:T(8,128)(2,1)S(1)} %slice_bitcast_fusion), channel_id=1, source_target_pairs={{0,16},{16,0},{1,17},{17,1},{2,18},{18,2},{3,19},{19,3},{4,20},{20... | collective-permute-start | bytes 1228808 | tf_op jit(solution)/shard_map/ppermute | solution.py:19
  113.5 17.6 %all-to-all-start.3 = ((bf16[8,40,640]{2,1,0:T(8,128)(2,1)}), bf16[8,40,640]{2,1,0:T(8,128)(2,1)S(1)}, u32[]{:S(2)}, u32[]{:S(2)}) async-start(bf16[8,40,640]{2,1,0:T(8,128)(2,1)} %shard_map.135), calls=%async_computation.3 | async-start | bytes 819200 | tf_op jit(solution)/shard_map/all_to_all | solution.py:590
  118.4 7.5 %collective-permute-start.21 = (bf16[4,40,640]{2,1,0:T(8,128)(2,1)S(1)}, bf16[4,40,640]{2,1,0:T(8,128)(2,1)S(1)}, u32[]{:S(2)}, u32[]{:S(2)}) collective-permute-start(bf16[4,40,640]{2,1,0:T(8,128)(2,1)S(1)} %slice_bitcast_fusion.1), channel_id=1, source_target_pairs={{0,1},{1,0},{2,3},{3,2},{4,5},{5,4},{6,7},{7,6},{8,9},{9,8},{10,11... | collective-permute-start | bytes 614408 | tf_op jit(solution)/shard_map/ppermute | solution.py:19
  131.3 6.6 %collective-permute-start.22 = (bf16[2,40,640]{2,1,0:T(8,128)(2,1)S(1)}, bf16[2,40,640]{2,1,0:T(8,128)(2,1)S(1)}, u32[]{:S(2)}, u32[]{:S(2)}) collective-permute-start(bf16[2,40,640]{2,1,0:T(8,128)(2,1)S(1)} %slice.67), channel_id=1, source_target_pairs={{0,8},{2,10},{4,12},{6,14},{8,0},{10,2},{12,4},{14,6},{1,9},{3,11}... | collective-permute-start | bytes 307208 | tf_op jit(solution)/shard_map/ppermute | solution.py:598
  (26 other events, 169.0 us)
